TPU v7x, 32 devices: a whole 2x2x4 slice. The times are simulated.
32 devices in a mesh: dp: 8 (over z, core), tensor: 4 (over y, x).
Axes of the slice: x: 2, y: 2, z: 4, core: 2. Of those that a mesh axis runs over, the one named last changes fastest.
Arguments:
- tokens: bfloat16 [8192, 1536], P(('dp', 'tensor')), may hold values from -6 to 6
- segments: int32 [8192], P('dp'), may hold values from 0 to 2, as said below
- attn_gain: float32 [1536], replicated, may hold values from 0.1 to 1.9
- w_query: bfloat16 [1536, 1536], P('dp', 'tensor'), may hold values from -0.15625 to 0.15625
- key_weight: bfloat16 [1536, 512], P('dp', 'tensor'), may hold values from -0.15625 to 0.15625
- value_weight: bfloat16 [1536, 512], P('dp', 'tensor'), may hold values from -0.15625 to 0.15625
- query_gain: float32 [64], replicated, may hold values from 0.1 to 1.9
- key_gain: float32 [64], replicated, may hold values from 0.1 to 1.9
- w_out: bfloat16 [1536, 1536], P('tensor', 'dp'), may hold values from -0.625 to 0.625
- ffn_gain: float32 [1536], replicated, may hold values from 0.1 to 1.9
- w_gate: bfloat16 [1536, 6912], P('dp', 'tensor'), may hold values from -0.15625 to 0.15625
- w_up: bfloat16 [1536, 6912], P('dp', 'tensor'), may hold values from -0.15625 to 0.15625
- w_down: bfloat16 [6912, 1536], P('tensor', 'dp'), may hold values from -0.078125 to 0.078125
- cotangent: bfloat16 [8192, 1536], P(('dp', 'tensor')), may hold values from -6 to 6
Outputs:
- output: float32 [8192, 1536], P(('dp', 'tensor'))
- tokens_grad: float32 [8192, 1536], P(('dp', 'tensor'))
- attn_gain_grad: float32 [1536], replicated
- w_query_grad: float32 [1536, 1536], P('dp', 'tensor')
- w_key_grad: float32 [1536, 512], P('dp', 'tensor')
- w_value_grad: float32 [1536, 512], P('dp', 'tensor')
- query_gain_grad: float32 [64], replicated
- key_gain_grad: float32 [64], replicated
- w_out_grad: float32 [1536, 1536], P('tensor', 'dp')
- ffn_gain_grad: float32 [1536], replicated
- w_gate_grad: float32 [1536, 6912], P('dp', 'tensor')
- w_up_grad: float32 [1536, 6912], P('dp', 'tensor')
- w_down_grad: float32 [6912, 1536], P('tensor', 'dp')
Inputs may be any that keep to these rules, and one draw needn't show every extreme that they name: `segments`: within each sequence of 1024 tokens the segment numbers are 0, 1, 2 in order, never falling, each present; documents 0 and 2 have fewer than 256 tokens each.
All inputs are finite; a program needn't handle non-finite values.
Results may differ from a plain program's by a relative error of at most 0.02.
Values may be sent and summed in bfloat16 or wider, within the bound.
No kernel may reach another device: no remote copies, remote signals or barrier semaphores. Data moves between devices by JAX's collectives and lax.ppermute only.
A program may use at most 192 MiB of HBM per device.

v0:
```python
import jax
import jax.numpy as jnp
from jax import lax
from jax.sharding import PartitionSpec as P

QUERY_HEADS = 24
KEY_VALUE_HEADS = 8
HEAD_SIZE = 64


EPSILON = 1e-05
ROTARY_BASE = 1000000.0
NEGATIVE_FILL = -1e30


def norm_rows(values_in, gain):
    return (
        values_in
        * lax.rsqrt(jnp.mean(values_in * values_in, axis=-1, keepdims=True) + EPSILON)
        * gain
    )


def rotate(heads, positions):
    half_size = heads.shape[-1] // 2
    freqs = ROTARY_BASE ** (-2.0 * jnp.arange(half_size, dtype=jnp.float32) / heads.shape[-1])
    angles = positions.astype(jnp.float32)[:, None] * freqs[None, :]
    cosine = jnp.cos(angles)[:, None, :]
    sine = jnp.sin(angles)[:, None, :]
    first_half = heads[..., :half_size]
    second_half = heads[..., half_size:]
    return jnp.concatenate(
        [first_half * cosine - second_half * sine, second_half * cosine + first_half * sine],
        axis=-1,
    )


def position_table(seq_segments):
    length_total = seq_segments.shape[0]
    indices = jnp.arange(length_total, dtype=jnp.int32)
    boundary = jnp.concatenate([jnp.ones((1,), jnp.bool_), seq_segments[1:] != seq_segments[:-1]])
    starts = lax.cummax(jnp.where(boundary, indices, jnp.zeros_like(indices)), axis=0)
    return indices - starts


def cross_rows(left, right):
    return lax.dot_general(
        left, right, (((1,), (1,)), ((), ())), preferred_element_type=jnp.float32
    )


def cross_cols(left, right):
    return lax.dot_general(
        left, right, (((0,), (0,)), ((), ())), preferred_element_type=jnp.float32
    )


def swiglu(gating, lifted):
    return jax.nn.silu(gating) * lifted


def shards(
    tokens,
    segments,
    attn_gain,
    w_query,
    key_weight,
    value_weight,
    query_gain,
    key_gain,
    w_out,
    ffn_gain,
    w_gate,
    w_up,
    w_down,
    cotangent,
):
    query_full, key_full, value_full, out_full, gate_full, up_full, down_full = (
        lax.all_gather(w_query, "dp", axis=0, tiled=True),
        lax.all_gather(key_weight, "dp", axis=0, tiled=True),
        lax.all_gather(value_weight, "dp", axis=0, tiled=True),
        lax.all_gather(w_out, "dp", axis=1, tiled=True),
        lax.all_gather(w_gate, "dp", axis=0, tiled=True),
        lax.all_gather(w_up, "dp", axis=0, tiled=True),
        lax.all_gather(w_down, "dp", axis=1, tiled=True),
    )
    tokens_wide = tokens.astype(jnp.float32)
    length_total = segments.shape[0]
    group_width = QUERY_HEADS // KEY_VALUE_HEADS
    score_scale = HEAD_SIZE ** (-0.5)
    positions = position_table(segments)
    first_normalized = norm_rows(tokens_wide, attn_gain).astype(jnp.bfloat16)
    normed_all = lax.all_gather(first_normalized, "tensor", axis=0, tiled=True)
    query_raw = jnp.dot(normed_all, query_full, preferred_element_type=jnp.float32)
    key_unrotated = jnp.dot(normed_all, key_full, preferred_element_type=jnp.float32)
    value_raw = jnp.dot(normed_all, value_full, preferred_element_type=jnp.float32)

    def head_prepare(raw_rows, gain):
        return rotate(norm_rows(raw_rows.reshape(length_total, -1, HEAD_SIZE), gain), positions)

    query_rot, query_pull = jax.vjp(head_prepare, query_raw, query_gain)
    key_rot, key_pull = jax.vjp(head_prepare, key_unrotated, key_gain)
    kv_heads = key_rot.shape[1]
    query_low = query_rot.astype(jnp.bfloat16).reshape(
        length_total, kv_heads, group_width, HEAD_SIZE
    )
    key_low = key_rot.astype(jnp.bfloat16)
    value_low = value_raw.astype(jnp.bfloat16).reshape(length_total, kv_heads, HEAD_SIZE)
    block_rows = min(512, length_total)
    block_count = length_total // block_rows
    indices = jnp.arange(length_total, dtype=jnp.int32)

    def block_scores(block_index):
        first_row = block_index * block_rows
        query_block = lax.dynamic_slice_in_dim(query_low, first_row, block_rows, 0)
        row_ids = first_row + jnp.arange(block_rows, dtype=jnp.int32)
        row_segments = lax.dynamic_slice_in_dim(segments, first_row, block_rows, 0)
        allowed = (indices[None, :] <= row_ids[:, None]) & (
            row_segments[:, None] == segments[None, :]
        )
        scores = (
            jnp.einsum("ikgd,jkd->kgij", query_block, key_low, preferred_element_type=jnp.float32)
            * score_scale
        )
        return (query_block, jnp.where(allowed[None, None], scores, NEGATIVE_FILL))

    def forward_block(block_index):
        query_block, scores = block_scores(block_index)
        row_peak = jnp.max(scores, axis=-1, keepdims=True)
        exps = jnp.exp(scores - row_peak)
        row_totals = jnp.sum(exps, axis=-1, keepdims=True)
        softmax_rows = (exps / row_totals).astype(jnp.bfloat16)
        mixed = jnp.einsum(
            "kgij,jkd->ikgd", softmax_rows, value_low, preferred_element_type=jnp.float32
        )
        return (mixed.reshape(block_rows, -1), (row_peak + jnp.log(row_totals))[..., 0])

    attended_rows, log_totals = lax.map(forward_block, jnp.arange(block_count))
    attended_low = attended_rows.reshape(length_total, -1).astype(jnp.bfloat16)
    attn_part = lax.psum_scatter(
        jnp.dot(attended_low, out_full, preferred_element_type=jnp.float32).astype(jnp.bfloat16),
        "tensor",
        scatter_dimension=0,
        tiled=True,
    ).astype(jnp.float32)
    hidden = tokens_wide + attn_part
    normed_two = norm_rows(hidden, ffn_gain).astype(jnp.bfloat16)
    normed_all_two = lax.all_gather(normed_two, "tensor", axis=0, tiled=True)
    gating = jnp.dot(normed_all_two, gate_full, preferred_element_type=jnp.float32)
    lifted = jnp.dot(normed_all_two, up_full, preferred_element_type=jnp.float32)
    product, swiglu_pull = jax.vjp(swiglu, gating, lifted)
    activation = product.astype(jnp.bfloat16)
    ffn_part = lax.psum_scatter(
        jnp.dot(activation, down_full, preferred_element_type=jnp.float32).astype(jnp.bfloat16),
        "tensor",
        scatter_dimension=0,
        tiled=True,
    ).astype(jnp.float32)
    output = hidden + ffn_part
    grad_all = lax.all_gather(cotangent, "tensor", axis=0, tiled=True)
    fresh = lax.optimization_barrier(
        (w_query, key_weight, value_weight, w_out, w_gate, w_up, w_down, grad_all)
    )
    query_back, key_back, value_back, out_back, gate_back, up_back, down_back = (
        lax.all_gather(fresh[0], "dp", axis=0, tiled=True),
        lax.all_gather(fresh[1], "dp", axis=0, tiled=True),
        lax.all_gather(fresh[2], "dp", axis=0, tiled=True),
        lax.all_gather(fresh[3], "dp", axis=1, tiled=True),
        lax.all_gather(fresh[4], "dp", axis=0, tiled=True),
        lax.all_gather(fresh[5], "dp", axis=0, tiled=True),
        lax.all_gather(fresh[6], "dp", axis=1, tiled=True),
    )
    d_activation = cross_rows(grad_all, down_back)
    d_gating, d_lifted = swiglu_pull(d_activation)
    gate_grad_low = d_gating.astype(jnp.bfloat16)
    lift_grad_low = d_lifted.astype(jnp.bfloat16)
    down_term = cross_cols(grad_all, activation)
    gate_term = cross_cols(normed_all_two, gate_grad_low)
    lift_term = cross_cols(normed_all_two, lift_grad_low)
    d_normed_two = lax.psum_scatter(
        (cross_rows(gate_grad_low, gate_back) + cross_rows(lift_grad_low, up_back)).astype(
            jnp.bfloat16
        ),
        "tensor",
        scatter_dimension=0,
        tiled=True,
    ).astype(jnp.float32)
    gate_grad, lift_grad, down_grad_flip = (
        lax.psum_scatter(
            gate_term.astype(jnp.bfloat16), "dp", scatter_dimension=0, tiled=True
        ).astype(jnp.float32),
        lax.psum_scatter(
            lift_term.astype(jnp.bfloat16), "dp", scatter_dimension=0, tiled=True
        ).astype(jnp.float32),
        lax.psum_scatter(
            down_term.astype(jnp.bfloat16), "dp", scatter_dimension=0, tiled=True
        ).astype(jnp.float32),
    )
    _, norm_two_pull = jax.vjp(norm_rows, hidden, ffn_gain)
    d_hidden_norm, ffn_gain_part = norm_two_pull(d_normed_two)
    d_hidden = cotangent.astype(jnp.float32) + d_hidden_norm
    hidden_grad_all = lax.all_gather(d_hidden.astype(jnp.bfloat16), "tensor", axis=0, tiled=True)
    d_attended = cross_rows(hidden_grad_all, out_back).astype(jnp.bfloat16)
    out_term = cross_cols(hidden_grad_all, attended_low)
    d_attended_heads = d_attended.reshape(length_total, kv_heads, group_width, HEAD_SIZE)

    def backward_block(carried, block_index):
        key_sum, value_sum = carried
        query_block, scores = block_scores(block_index)
        softmax_rows = jnp.exp(scores - log_totals[block_index][..., None])
        grad_block = lax.dynamic_slice_in_dim(
            d_attended_heads, block_index * block_rows, block_rows, 0
        )
        grad_soft = jnp.einsum(
            "ikgd,jkd->kgij", grad_block, value_low, preferred_element_type=jnp.float32
        )
        row_inner = jnp.sum(softmax_rows * grad_soft, axis=-1, keepdims=True)
        grad_scores = (softmax_rows * (grad_soft - row_inner)).astype(jnp.bfloat16)
        query_piece = (
            jnp.einsum("kgij,jkd->ikgd", grad_scores, key_low, preferred_element_type=jnp.float32)
            * score_scale
        )
        key_sum = (
            key_sum
            + jnp.einsum(
                "kgij,ikgd->jkd", grad_scores, query_block, preferred_element_type=jnp.float32
            )
            * score_scale
        )
        value_sum = value_sum + jnp.einsum(
            "kgij,ikgd->jkd",
            softmax_rows.astype(jnp.bfloat16),
            grad_block,
            preferred_element_type=jnp.float32,
        )
        return ((key_sum, value_sum), query_piece)

    empty_state = jnp.zeros((length_total, kv_heads, HEAD_SIZE), jnp.float32)
    (d_keys, d_values), d_queries = lax.scan(
        backward_block, (empty_state, empty_state), jnp.arange(block_count)
    )
    d_queries = d_queries.reshape(length_total, kv_heads * group_width, HEAD_SIZE)
    d_query_raw, query_gain_part = query_pull(d_queries)
    d_key_raw, key_gain_part = key_pull(d_keys)
    query_grad_low = d_query_raw.astype(jnp.bfloat16)
    key_grad_low = d_key_raw.astype(jnp.bfloat16)
    value_grad_low = d_values.reshape(length_total, -1).astype(jnp.bfloat16)
    query_term = cross_cols(normed_all, query_grad_low)
    key_term = cross_cols(normed_all, key_grad_low)
    value_term = cross_cols(normed_all, value_grad_low)
    d_normed_one = lax.psum_scatter(
        (
            cross_rows(query_grad_low, query_back)
            + cross_rows(key_grad_low, key_back)
            + cross_rows(value_grad_low, value_back)
        ).astype(jnp.bfloat16),
        "tensor",
        scatter_dimension=0,
        tiled=True,
    ).astype(jnp.float32)
    query_grad, key_grad, value_grad, out_grad_flip = (
        lax.psum_scatter(
            query_term.astype(jnp.bfloat16), "dp", scatter_dimension=0, tiled=True
        ).astype(jnp.float32),
        lax.psum_scatter(
            key_term.astype(jnp.bfloat16), "dp", scatter_dimension=0, tiled=True
        ).astype(jnp.float32),
        lax.psum_scatter(
            value_term.astype(jnp.bfloat16), "dp", scatter_dimension=0, tiled=True
        ).astype(jnp.float32),
        lax.psum_scatter(
            out_term.astype(jnp.bfloat16), "dp", scatter_dimension=0, tiled=True
        ).astype(jnp.float32),
    )
    _, norm_one_pull = jax.vjp(norm_rows, tokens_wide, attn_gain)
    d_tokens_norm, attn_gain_part = norm_one_pull(d_normed_one)
    tokens_grad = d_hidden + d_tokens_norm
    attn_gain_grad, query_gain_grad, key_gain_grad, ffn_gain_grad = lax.psum(
        (attn_gain_part, query_gain_part, key_gain_part, ffn_gain_part), ("dp", "tensor")
    )
    return (
        output,
        tokens_grad,
        attn_gain_grad,
        query_grad,
        key_grad,
        value_grad,
        query_gain_grad,
        key_gain_grad,
        out_grad_flip.T,
        ffn_gain_grad,
        gate_grad,
        lift_grad,
        down_grad_flip.T,
    )


def solution(mesh):
    in_specs = (
        P(("dp", "tensor"), None),
        P("dp"),
        P(),
        P("dp", "tensor"),
        P("dp", "tensor"),
        P("dp", "tensor"),
        P(),
        P(),
        P("tensor", "dp"),
        P(),
        P("dp", "tensor"),
        P("dp", "tensor"),
        P("tensor", "dp"),
        P(("dp", "tensor"), None),
    )
    out_specs = (
        P(("dp", "tensor"), None),
        P(("dp", "tensor"), None),
        P(),
        P("dp", "tensor"),
        P("dp", "tensor"),
        P("dp", "tensor"),
        P(),
        P(),
        P("tensor", "dp"),
        P(),
        P("dp", "tensor"),
        P("dp", "tensor"),
        P("tensor", "dp"),
    )
    return jax.shard_map(shards, mesh=mesh, in_specs=in_specs, out_specs=out_specs, check_vma=False)
```

profile of v0, /device:TPU:0, one launch (start us, length us, event | category | flops | bytes accessed | tf_op | source)
XLA Modules:
  0.0 1188.5 jit_solution(7854833175363345280)
XLA Ops:
  13.3 17.2 %all_gather.56 = bf16[1536,128]{1,0:T(8,128)(2,1)S(1)} all-gather(bf16[192,128]{1,0:T(8,128)(2,1)S(1)} %copy-done.32), channel_id=1, replica_groups=mesh['dp'=8,'tensor'=4] {'dp'}, dimensions={0}, use_global_device_ids=true | all-gather | bytes 442368 | tf_op jit(solution)/shard_map/all_gather | solution.py:80
  30.4 14.5 %all_gather.57 = bf16[1536,128]{1,0:T(8,128)(2,1)S(1)} all-gather(bf16[192,128]{1,0:T(8,128)(2,1)S(1)} %copy-done.34), channel_id=1, replica_groups=mesh['dp'=8,'tensor'=4] {'dp'}, dimensions={0}, use_global_device_ids=true | all-gather | bytes 442368 | tf_op jit(solution)/shard_map/all_gather | solution.py:81
  45.5 37.5 %all-gather.15.cloned.1.call-done = bf16[1024,1536]{1,0:T(8,128)(2,1)} async-done(((bf16[256,1536]{1,0:T(8,128)(2,1)}), bf16[1024,1536]{1,0:T(8,128)(2,1)}) %all-gather.15.cloned.1.call-update) | async-done | bytes 3145744 | tf_op jit(solution)/shard_map/all_gather | solution.py:93
  82.9 3.8 fusion.75
  90.5 24.7 %while.28 = (s32[]{:T(128)}, bf16[2,512,384]{2,1,0:T(8,128)(2,1)S(1)}, f32[2,2,3,512]{3,2,1,0:T(4,128)S(1)}, s32[2]{0:T(128)S(1)}, s32[1024]{0:T(1024)S(1)}, /*i...) while((s32[]{:T(128)}, ...), condition=%wide.region_8.9_spmd.clone, body=%wide.region_5.8_spmd.clone.sunk | while | flops 844625408 | bytes 42854592 | solution.py:138
  94.6 3.6 fusion.146
  98.3 4.3 fusion.147
  107.0 3.6 fusion.146
  110.6 4.3 fusion.147
  116.1 4.8 convolution_convert_fusion.4
  122.3 42.7 %reduce-scatter.14.cloned.1.call-done = bf16[256,1536]{1,0:T(8,128)(2,1)} async-done(((bf16[1024,1536]{1,0:T(8,128)(2,1)}), bf16[256,1536]{1,0:T(8,128)(2,1)}) %reduce-scatter.14.cloned.1.call-update) | async-done | bytes 786448 | tf_op jit(solution)/shard_map/reduce_scatter | solution.py:140
  169.7 41.0 %all-gather.29.cloned.1.call-done = bf16[1024,1536]{1,0:T(8,128)(2,1)} async-done(((bf16[256,1536]{1,0:T(8,128)(2,1)}), bf16[1024,1536]{1,0:T(8,128)(2,1)}) %all-gather.29.cloned.1.call-update) | async-done | bytes 3145744 | tf_op jit(solution)/shard_map/all_gather | solution.py:160
  212.1 58.4 %all-gather.23.cloned.1.call-done = bf16[1536,1728]{1,0:T(8,128)(2,1)} async-done(((bf16[192,1728]{1,0:T(8,128)(2,1)}), bf16[1536,1728]{1,0:T(8,128)(2,1)}) %all-gather.23.cloned.1.call-update) | async-done | bytes 5308432 | tf_op jit(solution)/shard_map/all_gather | solution.py:83
  270.5 45.2 %all-gather.21.cloned.1.call-done = bf16[1024,1536]{1,0:T(8,128)(2,1)} async-done(((bf16[256,1536]{1,0:T(8,128)(2,1)}), bf16[1024,1536]{1,0:T(8,128)(2,1)}) %all-gather.21.cloned.1.call-update) | async-done | bytes 3145744 | tf_op jit(solution)/shard_map/all_gather | solution.py:148
  315.6 10.9 fusion.76
  326.5 49.0 %all-gather.25.cloned.1.call-done = bf16[1536,1728]{1,0:T(8,128)(2,1)} async-done(((bf16[192,1728]{1,0:T(8,128)(2,1)}), bf16[1536,1728]{1,0:T(8,128)(2,1)}) %all-gather.25.cloned.1.call-update) | async-done | bytes 5308432 | tf_op jit(solution)/shard_map/all_gather | solution.py:84
  375.5 10.9 fusion.77
  386.4 47.8 %all-gather.31.cloned.1.call-done = bf16[1728,1536]{0,1:T(8,128)(2,1)} async-done(((bf16[1728,192]{0,1:T(8,128)(2,1)}), bf16[1728,1536]{0,1:T(8,128)(2,1)}) %all-gather.31.cloned.1.call-update) | async-done | bytes 5308432 | tf_op jit(solution)/shard_map/all_gather | solution.py:171
  434.2 18.3 %fusion.52 = (bf16[1024,1728]{0,1:T(8,128)(2,1)}, bf16[1024,1728]{0,1:T(8,128)(2,1)}, bf16[1024,1728]{0,1:T(8,128)(2,1)}) fusion(f32[1024,1728]{0,1:T(8,128)} %fusion.76, f32[1024,1728]{0,1:T(8,128)} %fusion.77, bf16[1728,1536]{0,1:T(8,128)(2,1)} %all-gather.31.cloned.1.call-done, bf16[1024,1536]{1,0:T(8,128)(2,1)} %all-gather.29.cloned.1.call-done), kind=kOutput, calls=%fused_computation.67 | convolution fusion | flops 5464129536 | bytes 33226752 | tf_op jit(solution)/shard_map/dot_general | solution.py:47
  452.5 40.2 %all-gather.33.cloned.1.call-done = bf16[1536,1728]{1,0:T(8,128)(2,1)} async-done(((bf16[192,1728]{1,0:T(8,128)(2,1)}), bf16[1536,1728]{1,0:T(8,128)(2,1)}) %all-gather.33.cloned.1.call-update) | async-done | bytes 5308432 | tf_op jit(solution)/shard_map/all_gather | solution.py:169
  492.7 10.9 fusion.78
  503.6 47.7 %all-gather.35.cloned.1.call-done = bf16[1536,1728]{1,0:T(8,128)(2,1)} async-done(((bf16[192,1728]{1,0:T(8,128)(2,1)}), bf16[1536,1728]{1,0:T(8,128)(2,1)}) %all-gather.35.cloned.1.call-update) | async-done | bytes 5308432 | tf_op jit(solution)/shard_map/all_gather | solution.py:170
  551.3 11.3 add_convert_fusion.1
  563.4 42.0 %reduce-scatter.18.cloned.1.call-done = bf16[256,1536]{1,0:T(8,128)(2,1)} async-done(((bf16[1024,1536]{1,0:T(8,128)(2,1)}), bf16[256,1536]{1,0:T(8,128)(2,1)}) %reduce-scatter.18.cloned.1.call-update) | async-done | bytes 786448 | tf_op jit(solution)/shard_map/reduce_scatter | solution.py:180
  605.4 2.7 fusion.61
  608.1 3.1 fusion.74
  612.5 10.0 fusion.54
  622.5 8.1 copy.40
  630.7 10.6 convolution_convert_fusion.2
  641.4 10.1 convolution_convert_fusion.1
  651.7 24.1 %all-gather.37.cloned.1.call-done = bf16[1024,1536]{1,0:T(8,128)(2,1)} async-done(((bf16[256,1536]{1,0:T(8,128)(2,1)}), bf16[1024,1536]{1,0:T(8,128)(2,1)}) %all-gather.37.cloned.1.call-update) | async-done | bytes 3145744 | tf_op jit(solution)/shard_map/all_gather | solution.py:202
  675.8 3.6 convolution_convert_fusion.9
  679.5 120.3 %while.29 = (s32[]{:T(128)}, f32[1024,2,64]{0,2,1:T(8,128)S(1)}, f32[1024,2,64]{0,2,1:T(8,128)}, f32[2,512,2,3,64]{1,0,4,3,2:T(2,128)}, s32[2]{0:T(128)S(1)}, /*...) while((s32[]{:T(128)}, f32[1024,2,64]{0,2,1:T(8,128)S(1)}, ...), condition=%wide.region_16.17_spmd.clone, body=%wide.region_14.16_spmd.clone.sunk | while | flops 2062874112 | bytes 174172592 | solution.py:239
  681.6 6.4 fusion.156
  690.0 11.3 fusion.158
  702.8 7.0 fusion.159
  713.2 15.0 %dynamic_update_slice.22 = f32[2,512,2,3,64]{1,0,4,3,2:T(2,128)} dynamic-update-slice(f32[2,512,2,3,64]{1,0,4,3,2:T(2,128)} %get-tuple-element.489, f32[1,512,2,3,64]{1,0,4,3,2:T(1,128)S(1)} %copy.65, s32[]{:T(128)} %get-tuple-element.486, s32[]{:T(128)} %constant.48.clone.1..sunk.1, s32[]{:T(128)} %constant.48.clone.1..sunk.1, s32[]{:T(128)} %constant.48.clone.1..sunk.1, s32[]{:T(128)} %constant.48.clone.1..sunk.1) | dynamic-update-slice | bytes 1572868 | tf_op jit(solution)/shard_map/while/body/jit(dynamic_update_index_in_dim)/dynamic_update_slice | solution.py:239
  728.2 4.2 fusion.160
  732.4 7.3 fusion.161
  741.6 6.5 fusion.156
  750.0 11.3 fusion.158
  762.8 7.0 fusion.159
  773.2 15.0 %dynamic_update_slice.22 = f32[2,512,2,3,64]{1,0,4,3,2:T(2,128)} dynamic-update-slice(f32[2,512,2,3,64]{1,0,4,3,2:T(2,128)} %get-tuple-element.489, f32[1,512,2,3,64]{1,0,4,3,2:T(1,128)S(1)} %copy.65, s32[]{:T(128)} %get-tuple-element.486, s32[]{:T(128)} %constant.48.clone.1..sunk.1, s32[]{:T(128)} %constant.48.clone.1..sunk.1, s32[]{:T(128)} %constant.48.clone.1..sunk.1, s32[]{:T(128)} %constant.48.clone.1..sunk.1) | dynamic-update-slice | bytes 1572868 | tf_op jit(solution)/shard_map/while/body/jit(dynamic_update_index_in_dim)/dynamic_update_slice | solution.py:239
  788.2 4.2 fusion.160
  792.4 7.4 fusion.161
  800.6 3.6 reshape.369
  818.9 2.9 convolution_convert_fusion.6
  821.9 5.0 convolution_convert_fusion.5
  827.0 15.9 %all_gather.70 = bf16[1536,128]{1,0:T(8,128)(2,1)S(1)} all-gather(bf16[192,128]{1,0:T(8,128)(2,1)S(1)} %copy-done.33), channel_id=1, replica_groups=mesh['dp'=8,'tensor'=4] {'dp'}, dimensions={0}, use_global_device_ids=true | all-gather | bytes 442368 | tf_op jit(solution)/shard_map/all_gather | solution.py:166
  842.8 17.1 %all_gather.71 = bf16[1536,128]{1,0:T(8,128)(2,1)S(1)} all-gather(bf16[192,128]{1,0:T(8,128)(2,1)S(1)} %copy-done.35), channel_id=1, replica_groups=mesh['dp'=8,'tensor'=4] {'dp'}, dimensions={0}, use_global_device_ids=true | all-gather | bytes 442368 | tf_op jit(solution)/shard_map/all_gather | solution.py:167
  859.9 3.6 fusion.80
  863.6 3.3 fusion.79
  866.9 2.7 add_convert_fusion
  869.7 10.3 convolution_convert_fusion.3
  883.3 8.4 reduce-scatter.30.cloned.1.call-done
  893.9 60.7 %reduce-scatter.32.cloned.1.call-done = bf16[192,1728]{1,0:T(8,128)(2,1)} async-done(((bf16[1536,1728]{1,0:T(8,128)(2,1)}), bf16[192,1728]{1,0:T(8,128)(2,1)}) %reduce-scatter.32.cloned.1.call-update) | async-done | bytes 663568 | tf_op jit(solution)/shard_map/reduce_scatter | solution.py:192
  956.9 28.9 %reduce-scatter.24.cloned.1.call-done = bf16[192,128]{1,0:T(8,128)(2,1)} async-done(((bf16[1536,128]{1,0:T(8,128)(2,1)}), bf16[192,128]{1,0:T(8,128)(2,1)}) %reduce-scatter.24.cloned.1.call-update) | async-done | bytes 49168 | tf_op jit(solution)/shard_map/reduce_scatter | solution.py:265
  987.2 29.8 %reduce-scatter.26.cloned.1.call-done = bf16[192,128]{1,0:T(8,128)(2,1)} async-done(((bf16[1536,128]{1,0:T(8,128)(2,1)}), bf16[192,128]{1,0:T(8,128)(2,1)}) %reduce-scatter.26.cloned.1.call-update) | async-done | bytes 49168 | tf_op jit(solution)/shard_map/reduce_scatter | solution.py:268
  1018.4 32.5 %reduce-scatter.22.cloned.1.call-done = bf16[192,384]{1,0:T(8,128)(2,1)} async-done(((bf16[1536,384]{1,0:T(8,128)(2,1)}), bf16[192,384]{1,0:T(8,128)(2,1)}) %reduce-scatter.22.cloned.1.call-update) | async-done | bytes 147472 | tf_op jit(solution)/shard_map/reduce_scatter | solution.py:262
  1052.5 32.2 %reduce-scatter.28.cloned.1.call-done = bf16[192,384]{1,0:T(8,128)(2,1)} async-done(((bf16[1536,384]{1,0:T(8,128)(2,1)}), bf16[192,384]{1,0:T(8,128)(2,1)}) %reduce-scatter.28.cloned.1.call-update) | async-done | bytes 147472 | tf_op jit(solution)/shard_map/reduce_scatter | solution.py:271
  1086.4 43.3 %reduce-scatter.20.cloned.1.call-done = bf16[256,1536]{1,0:T(8,128)(2,1)} async-done(((bf16[1024,1536]{1,0:T(8,128)(2,1)}), bf16[256,1536]{1,0:T(8,128)(2,1)}) %reduce-scatter.20.cloned.1.call-update) | async-done | bytes 786448 | tf_op jit(solution)/shard_map/reduce_scatter | solution.py:251
  1131.5 40.0 %all-reduce.4 = (f32[1536]{0:T(1024)}, f32[64]{0:T(128)}, f32[64]{0:T(128)}, f32[1536]{0:T(1024)}) all-reduce(f32[1536]{0:T(1024)S(1)} %get-tuple-element.243, f32[64]{0:T(128)S(1)} %get-tuple-element.239, f32[64]{0:T(128)S(1)} %get-tuple-element.245, f32[1536]{0:T(1024)S(1)} %copy-done.43), channel_id=1, replica_groups=mesh['dp'=8,'tensor'=4] {'dp','tensor'}, use_global_device_ids=true, to_apply=%region_22.23 | all-reduce | flops 3200 | bytes 25600 | tf_op jit(solution)/shard_map/psum | solution.py:278
  1171.6 5.8 reduce-scatter.16.cloned.1.call-done
  1177.4 4.1 fusion.65
  (278 shorter events, 71.4 us)
Async XLA Ops:
  7.2 5.3 copy-start.26
  7.2 6.1 copy-start.32
  7.2 23.2 %copy-start.34 = (bf16[192,128]{1,0:T(8,128)(2,1)S(1)}, bf16[192,128]{1,0:T(8,128)(2,1)}, u32[]{:S(2)}) copy-start(bf16[192,128]{1,0:T(8,128)(2,1)} %param.23) | copy-start | bytes 147460
  7.2 38.3 %all-gather.17.cloned.1.call-start = ((), (), s32[]{:S(2)}) async-start(), calls=%async_computation.12 | async-start | bytes 1327104 | tf_op jit(solution)/shard_map/all_gather | solution.py:79
  7.9 75.0 %all-gather.15.cloned.1.call-start = ((), (), s32[]{:S(2)}) async-start(), calls=%async_computation.11 | async-start | bytes 3932160 | tf_op jit(solution)/shard_map/all_gather | solution.py:93
  11.7 103.5 %all-gather.19.cloned.1.call-start = ((), (), s32[]{:S(2)}) async-start(), calls=%async_computation.13 | async-start | bytes 1327104 | tf_op jit(solution)/shard_map/all_gather | solution.py:82
  12.4 152.6 %reduce-scatter.14.cloned.1.call-start = ((), (), s32[]{:S(2)}) async-start(), calls=%async_computation.14 | async-start | bytes 3932160 | tf_op jit(solution)/shard_map/reduce_scatter | solution.py:140
  45.4 43.6 %copy-start.20 = (f32[1024,32]{0,1:T(8,128)}, f32[1024,32]{0,1:T(8,128)S(1)}, u32[]{:S(2)}) copy-start(f32[1024,32]{0,1:T(8,128)S(1)} %get-tuple-element.306) | copy-start | bytes 393220
  45.4 43.6 %copy-start.22 = (f32[1024,32]{0,1:T(8,128)}, f32[1024,32]{0,1:T(8,128)S(1)}, u32[]{:S(2)}) copy-start(f32[1024,32]{0,1:T(8,128)S(1)} %get-tuple-element.307) | copy-start | bytes 393220
  120.9 44.1 %copy-start.4 = (bf16[256,1536]{1,0:T(8,128)(2,1)S(1)}, bf16[256,1536]{1,0:T(8,128)(2,1)}, u32[]{:S(2)}) copy-start(bf16[256,1536]{1,0:T(8,128)(2,1)} %param.18) | copy-start | bytes 2359300
  120.9 45.6 %copy-start.36 = (f32[1536]{0:T(1024)S(1)}, f32[1536]{0:T(1024)}, u32[]{:S(2)}) copy-start(f32[1536]{0:T(1024)} %param.27) | copy-start | bytes 18436
  120.9 89.8 %all-gather.29.cloned.1.call-start = ((), (), s32[]{:S(2)}) async-start(), calls=%async_computation.20 | async-start | bytes 3932160 | tf_op jit(solution)/shard_map/all_gather | solution.py:160
  121.5 149.0 %all-gather.23.cloned.1.call-start = ((), (), s32[]{:S(2)}) async-start(), calls=%async_computation.16 | async-start | bytes 6193152 | tf_op jit(solution)/shard_map/all_gather | solution.py:83
  122.1 193.5 %all-gather.21.cloned.1.call-start = ((), (), s32[]{:S(2)}) async-start(), calls=%async_computation.15 | async-start | bytes 3932160 | tf_op jit(solution)/shard_map/all_gather | solution.py:148
  166.5 441.6 %copy-start.44 = (f32[256]{0:T(256)}, f32[256]{0:T(256)S(1)}, u32[]{:S(2)}) copy-start(f32[256]{0:T(256)S(1)} %fusion.73) | copy-start | bytes 3076
  168.9 206.7 %all-gather.25.cloned.1.call-start = ((), (), s32[]{:S(2)}) async-start(), calls=%async_computation.17 | async-start | bytes 6193152 | tf_op jit(solution)/shard_map/all_gather | solution.py:84
  169.6 264.6 %all-gather.31.cloned.1.call-start = ((), (), s32[]{:S(2)}) async-start(), calls=%async_computation.21 | async-start | bytes 6193152 | tf_op jit(solution)/shard_map/all_gather | solution.py:171
  210.7 281.9 %all-gather.33.cloned.1.call-start = ((), (), s32[]{:S(2)}) async-start(), calls=%async_computation.22 | async-start | bytes 6193152 | tf_op jit(solution)/shard_map/all_gather | solution.py:169
  211.3 340.0 %all-gather.35.cloned.1.call-start = ((), (), s32[]{:S(2)}) async-start(), calls=%async_computation.23 | async-start | bytes 6193152 | tf_op jit(solution)/shard_map/all_gather | solution.py:170
  212.1 393.4 %reduce-scatter.18.cloned.1.call-start = ((), (), s32[]{:S(2)}) async-start(), calls=%async_computation.24 | async-start | bytes 3932160 | tf_op jit(solution)/shard_map/reduce_scatter | solution.py:180
  562.6 89.1 %all-gather.39.cloned.1.call-start = ((), (), s32[]{:S(2)}) async-start(), calls=%async_computation.26 | async-start | bytes 1327104 | tf_op jit(solution)/shard_map/all_gather | solution.py:168
  563.4 112.5 %all-gather.37.cloned.1.call-start = ((), (), s32[]{:S(2)}) async-start(), calls=%async_computation.25 | async-start | bytes 3932160 | tf_op jit(solution)/shard_map/all_gather | solution.py:202
  608.1 14.4 %copy-start.48 = (f32[256]{0:T(256)}, f32[256]{0:T(256)S(1)}, u32[]{:S(2)}) copy-start(f32[256]{0:T(256)S(1)} %multiply_multiply_fusion.5) | copy-start | bytes 3076
  611.3 252.3 %all-gather.41.cloned.1.call-start = ((), (), s32[]{:S(2)}) async-start(), calls=%async_computation.27 | async-start | bytes 1327104 | tf_op jit(solution)/shard_map/all_gather | solution.py:165
  611.8 257.8 %all-gather.27.cloned.1.call-start = ((), (), s32[]{:S(2)}) async-start(), calls=%async_computation.18 | async-start | bytes 6193152 | tf_op jit(solution)/shard_map/all_gather | solution.py:85
  612.4 267.6 %reduce-scatter.34.cloned.1.call-start = ((), (), s32[]{:S(2)}) async-start(), calls=%async_computation.35 | async-start | bytes 6193152
  630.7 261.0 %reduce-scatter.30.cloned.1.call-start = ((), (), s32[]{:S(2)}) async-start(), calls=%async_computation.33 | async-start | bytes 6193152 | tf_op jit(solution)/shard_map/reduce_scatter | solution.py:189
  641.4 313.2 %reduce-scatter.32.cloned.1.call-start = ((), (), s32[]{:S(2)}) async-start(), calls=%async_computation.34 | async-start | bytes 6193152 | tf_op jit(solution)/shard_map/reduce_scatter | solution.py:192
  651.6 334.1 %reduce-scatter.24.cloned.1.call-start = ((), (), s32[]{:S(2)}) async-start(), calls=%async_computation.30 | async-start | bytes 442368 | tf_op jit(solution)/shard_map/reduce_scatter | solution.py:265
  679.7 10.3 copy-start.16
  690.0 11.3 slice-start
  690.0 11.3 slice-start.1
  690.0 12.7 %slice-start.2 = ((s8[12582912]{0:T(1024)(128)(4,1)}), s8[4194304]{0:T(1024)(128)(4,1)S(1)}, s32[]{:S(2)}) async-start(s8[12582912]{0:T(1024)(128)(4,1)} %bitcast.223), calls=%async_computation.38 | async-start | bytes 8388608 | tf_op jit(solution)/shard_map/while
  728.2 4.2 copy-start.17
  739.7 10.3 copy-start.16
  750.0 11.3 slice-start
  750.0 11.3 slice-start.1
  750.0 12.7 %slice-start.2 = ((s8[12582912]{0:T(1024)(128)(4,1)}), s8[4194304]{0:T(1024)(128)(4,1)S(1)}, s32[]{:S(2)}) async-start(s8[12582912]{0:T(1024)(128)(4,1)} %bitcast.223), calls=%async_computation.38 | async-start | bytes 8388608 | tf_op jit(solution)/shard_map/while
  788.2 4.2 copy-start.17
  799.8 6.4 copy-start.21
  799.8 6.4 copy-start.23
  799.8 7.5 copy-start.39
  799.8 7.5 copy-start.53
  800.6 8.2 copy-start.42
  804.2 4.6 copy-start.11
  804.2 4.8 copy-start.2
  810.8 206.1 %reduce-scatter.26.cloned.1.call-start = ((), (), s32[]{:S(2)}) async-start(), calls=%async_computation.31 | async-start | bytes 442368 | tf_op jit(solution)/shard_map/reduce_scatter | solution.py:268
  815.6 235.2 %reduce-scatter.22.cloned.1.call-start = ((), (), s32[]{:S(2)}) async-start(), calls=%async_computation.29 | async-start | bytes 1327104 | tf_op jit(solution)/shard_map/reduce_scatter | solution.py:262
  821.8 5.1 copy-start.33
  821.8 21.0 %copy-start.35 = (bf16[192,128]{1,0:T(8,128)(2,1)S(1)}, bf16[192,128]{1,0:T(8,128)(2,1)}, u32[]{:S(2)}) copy-start(bf16[192,128]{1,0:T(8,128)(2,1)} %param.23) | copy-start | bytes 147460
  821.8 262.9 %reduce-scatter.28.cloned.1.call-start = ((), (), s32[]{:S(2)}) async-start(), calls=%async_computation.32 | async-start | bytes 1327104 | tf_op jit(solution)/shard_map/reduce_scatter | solution.py:271
  826.9 302.8 %reduce-scatter.20.cloned.1.call-start = ((), (), s32[]{:S(2)}) async-start(), calls=%async_computation.28 | async-start | bytes 3932160 | tf_op jit(solution)/shard_map/reduce_scatter | solution.py:251
  869.6 307.8 %reduce-scatter.16.cloned.1.call-start = ((), (), s32[]{:S(2)}) async-start(), calls=%async_computation.19 | async-start | bytes 3932160 | tf_op jit(solution)/shard_map/reduce_scatter | solution.py:153
  883.2 246.5 %copy-start.5 = (bf16[256,1536]{1,0:T(8,128)(2,1)S(1)}, bf16[256,1536]{1,0:T(8,128)(2,1)}, u32[]{:S(2)}) copy-start(bf16[256,1536]{1,0:T(8,128)(2,1)} %param.18) | copy-start | bytes 2359300
  883.2 246.5 %copy-start.40 = (f32[1536]{0:T(1024)S(1)}, f32[1536]{0:T(1024)}, u32[]{:S(2)}) copy-start(f32[1536]{0:T(1024)} %param.20) | copy-start | bytes 18436
  883.2 246.5 %copy-start.47 = (f32[256]{0:T(256)S(1)}, f32[256]{0:T(256)}, u32[]{:S(2)}) copy-start(f32[256]{0:T(256)} %copy-done.46) | copy-start | bytes 3076
  883.2 248.3 %copy-start.43 = (f32[1536]{0:T(1024)S(1)}, f32[1536]{0:T(1024)}, u32[]{:S(2)}) copy-start(f32[1536]{0:T(1024)} %get-tuple-element.241) | copy-start | bytes 18436
  883.2 288.4 %copy-start.51 = (f32[256]{0:T(256)S(1)}, f32[256]{0:T(256)}, u32[]{:S(2)}) copy-start(f32[256]{0:T(256)} %copy-done.50) | copy-start | bytes 3076
  883.2 294.2 %copy-start.9 = (bf16[256,1536]{1,0:T(8,128)(2,1)S(1)}, bf16[256,1536]{1,0:T(8,128)(2,1)}, u32[]{:S(2)}) copy-start(bf16[256,1536]{1,0:T(8,128)(2,1)} %reduce-scatter.14.cloned.1.call-done) | copy-start | bytes 2359300
  883.2 294.2 %copy-start.12 = (bf16[256,1536]{1,0:T(8,128)(2,1)S(1)}, bf16[256,1536]{1,0:T(8,128)(2,1)}, u32[]{:S(2)}) copy-start(bf16[256,1536]{1,0:T(8,128)(2,1)} %param.31) | copy-start | bytes 2359300
  883.2 294.1 %copy-start.13 = (bf16[256,1536]{1,0:T(8,128)(2,1)S(1)}, bf16[256,1536]{1,0:T(8,128)(2,1)}, u32[]{:S(2)}) copy-start(bf16[256,1536]{1,0:T(8,128)(2,1)} %reduce-scatter.18.cloned.1.call-done) | copy-start | bytes 2359300
  883.2 294.1 %copy-start.37 = (f32[1536]{0:T(1024)S(1)}, f32[1536]{0:T(1024)}, u32[]{:S(2)}) copy-start(f32[1536]{0:T(1024)} %param.27) | copy-start | bytes 18436
  883.3 294.1 %copy-start.45 = (f32[256]{0:T(256)S(1)}, f32[256]{0:T(256)}, u32[]{:S(2)}) copy-start(f32[256]{0:T(256)} %copy-done.44) | copy-start | bytes 3076
  883.3 294.1 %copy-start.49 = (f32[256]{0:T(256)S(1)}, f32[256]{0:T(256)}, u32[]{:S(2)}) copy-start(f32[256]{0:T(256)} %copy-done.48) | copy-start | bytes 3076
  (28 other events, 55.1 us)
Sparse Core Ops, SparseCore 0:
  9.7 27.5 all-gather.16
  39.6 43.2 all-gather.14
  84.6 22.6 all-gather.18
  121.0 43.9 reduce-scatter.13
  166.7 43.9 all-gather.28
  212.2 58.2 all-gather.22
  272.9 42.6 all-gather.20
  317.3 58.2 all-gather.24
  377.2 56.9 all-gather.30
  435.7 56.9 all-gather.32
  494.3 56.9 all-gather.34
  562.7 42.6 reduce-scatter.17
  607.1 22.6 all-gather.38
  632.0 43.7 all-gather.36
  677.3 22.6 all-gather.40
  701.5 57.9 all-gather.26
  761.7 61.1 reduce-scatter.33
  825.0 66.5 reduce-scatter.29
  894.0 60.6 reduce-scatter.31
  956.7 28.9 reduce-scatter.23
  988.1 28.8 reduce-scatter.25
  1019.8 31.0 reduce-scatter.21
  1053.8 30.9 reduce-scatter.27
  1087.6 42.0 reduce-scatter.19
  1132.6 44.6 reduce-scatter.15
where the time goes:
time: 1200 us; the launch traced here: 1190 us
  waiting for transfers between devices  724 us (60%)
  matrix products  215 us (18%)
  blocking collectives  105 us (9%)
  other arithmetic  64.8 us (5%)
  local copies, waits for them, and re-layouts  57.3 us (5%)
  between operations  15.4 us (1%)
    reduce_scatter x1, waiting for transfers between devices, shards(): lax.psum_scatter(lift_term.astype(jnp.bfloat16), 'dp', scatter_dimension=...  60.7 us
    all_gather x1, waiting for transfers between devices, shards(): lax.all_gather(w_gate, 'dp', axis=0, tiled=True)  58.4 us
    dot_general x7, matrix products, cross_rows(): lax.dot_general(left, right, (((1,), (1,)), ((), ())), preferred_element_...  53.8 us
    all_gather x1, waiting for transfers between devices, shards(): lax.all_gather(w_up, 'dp', axis=0, tiled=True)  49 us
    all_gather x1, waiting for transfers between devices, shards(): lax.all_gather(fresh[6], 'dp', axis=1, tiled=True)  47.8 us
    all_gather x1, waiting for transfers between devices, shards(): lax.all_gather(fresh[5], 'dp', axis=0, tiled=True)  47.7 us
    all_gather x1, waiting for transfers between devices, shards(): normed_all_two = lax.all_gather(normed_two, 'tensor', axis=0, tiled=True)  45.2 us
    reduce_scatter x1, waiting for transfers between devices, shards(): lax.psum_scatter((cross_rows(query_grad_low, query_back) + cross_rows(key...  43.3 us
  transfers between devices with their start and end apart: 25, of which 19 were waited for; matrix products, arithmetic and copies ran while one was open for 26% of the time, Pallas kernels for 0%

commit v1 on v0

v1 whole, which is shorter than its diff:
```python
import functools

import jax
import jax.numpy as jnp
from jax import lax
from jax.experimental import pallas as pl
from jax.experimental.pallas import tpu as pltpu
from jax.sharding import PartitionSpec as P

QUERY_HEADS = 24
KEY_VALUE_HEADS = 8
HEAD_SIZE = 64
GROUP = QUERY_HEADS // KEY_VALUE_HEADS
EPSILON = 1e-05
ROTARY_BASE = 1000000.0
NEGATIVE_FILL = -1e30
F32 = jnp.float32
LOW = jnp.bfloat16
SCALE = HEAD_SIZE ** (-0.5)


def norm_rows(values_in, gain):
    return (
        values_in
        * lax.rsqrt(jnp.mean(values_in * values_in, axis=-1, keepdims=True) + EPSILON)
        * gain
    )


def norm_back(values, gain, grad):
    inverse = lax.rsqrt(jnp.mean(values * values, axis=-1, keepdims=True) + EPSILON)
    hat = values * inverse
    scaled = grad * gain
    inner = jnp.mean(scaled * hat, axis=-1, keepdims=True)
    return (scaled - hat * inner) * inverse, jnp.sum(grad * hat, axis=0)


def mm(left, right):
    return jnp.dot(left, right, preferred_element_type=F32)


def cross_rows(left, right):
    return lax.dot_general(left, right, (((1,), (1,)), ((), ())), preferred_element_type=F32)


def cross_cols(left, right):
    return lax.dot_general(left, right, (((0,), (0,)), ((), ())), preferred_element_type=F32)


NT = (((1,), (1,)), ((), ()))
NN = (((1,), (0,)), ((), ()))
TN = (((0,), (0,)), ((), ()))


def kdot(left, right, dims):
    return lax.dot_general(left, right, dims, preferred_element_type=F32)


def stack_heads(block, head):
    first = head * GROUP * HEAD_SIZE
    return jnp.concatenate(
        [block[:, first + g * HEAD_SIZE : first + (g + 1) * HEAD_SIZE] for g in range(GROUP)], axis=0
    )


def attend_kernel(heads, rows, me_ref, q_ref, k_ref, v_ref, lo_ref, out_ref, lse_ref):
    me = me_ref[0]
    block = pl.program_id(0) ^ me
    low_bound = jnp.concatenate([lo_ref[0]] * GROUP, axis=1)
    row_ids = block * rows + lax.broadcasted_iota(jnp.int32, (1, rows), 1)
    row_ids = jnp.concatenate([row_ids] * GROUP, axis=1)
    width = GROUP * rows
    queries = q_ref[...] * SCALE
    pieces = []
    for head in range(heads):
        q3 = stack_heads(queries, head)
        cols = slice(head * HEAD_SIZE, (head + 1) * HEAD_SIZE)

        def step(other, carry, q3=q3, cols=cols):
            peak, total, acc = carry
            first = pl.multiple_of((other ^ me) * rows, rows)
            keys = k_ref[pl.ds(first, rows), cols]
            vals = v_ref[pl.ds(first, rows), cols]
            ids = other * rows + lax.broadcasted_iota(jnp.int32, (rows, 1), 0)
            scores = kdot(keys, q3, NT)
            scores = jnp.where((ids <= row_ids) & (ids >= low_bound), scores, NEGATIVE_FILL)
            higher = jnp.maximum(peak, jnp.max(scores, axis=0, keepdims=True))
            fade = jnp.exp(peak - higher)
            exps = jnp.exp(scores - higher)
            total = total * fade + jnp.sum(exps, axis=0, keepdims=True)
            acc = acc * fade + kdot(vals, exps.astype(LOW), TN)
            return higher, total, acc

        start = (
            jnp.full((1, width), NEGATIVE_FILL, F32),
            jnp.zeros((1, width), F32),
            jnp.zeros((HEAD_SIZE, width), F32),
        )
        start = step(block, start)
        peak, total, acc = lax.fori_loop(0, block, step, start)
        acc = acc / total
        lse_ref[0, head : head + 1, :] = peak + jnp.log(total)
        pieces += [acc[:, g * rows : (g + 1) * rows] for g in range(GROUP)]
    out_ref[...] = jnp.concatenate(pieces, axis=0).T.astype(LOW)


def attend_back_kernel(
    heads, rows, me_ref, q_ref, k_ref, v_ref, lo_ref, o_ref, do_ref, lse_ref, dq_ref, dk_ref, dv_ref
):
    me = me_ref[0]

    @pl.when(pl.program_id(0) == 0)
    def _():
        dk_ref[...] = jnp.zeros_like(dk_ref)
        dv_ref[...] = jnp.zeros_like(dv_ref)

    block = pl.program_id(0) ^ me
    low_bound = jnp.concatenate([lo_ref[0]] * GROUP, axis=1)
    row_ids = block * rows + lax.broadcasted_iota(jnp.int32, (1, rows), 1)
    row_ids = jnp.concatenate([row_ids] * GROUP, axis=1)
    width = GROUP * rows
    queries = q_ref[...] * SCALE
    grads = do_ref[...]
    product = (grads.astype(F32) * o_ref[...].astype(F32)).T
    pieces = []
    for head in range(heads):
        q3 = stack_heads(queries, head)
        do3 = stack_heads(grads, head)
        cols = slice(head * HEAD_SIZE, (head + 1) * HEAD_SIZE)
        first_row = head * GROUP * HEAD_SIZE
        inner = jnp.concatenate(
            [
                jnp.sum(
                    product[first_row + g * HEAD_SIZE : first_row + (g + 1) * HEAD_SIZE],
                    axis=0,
                    keepdims=True,
                )
                for g in range(GROUP)
            ],
            axis=1,
        )
        lse = lse_ref[0, head : head + 1, :]

        def step(other, acc, q3=q3, do3=do3, cols=cols, inner=inner, lse=lse):
            first = pl.multiple_of((other ^ me) * rows, rows)
            place = pl.ds(first, rows)
            keys = k_ref[place, cols]
            vals = v_ref[place, cols]
            ids = other * rows + lax.broadcasted_iota(jnp.int32, (rows, 1), 0)
            scores = kdot(keys, q3, NT)
            scores = jnp.where((ids <= row_ids) & (ids >= low_bound), scores, NEGATIVE_FILL)
            probs = jnp.exp(scores - lse)
            d_probs = kdot(vals, do3, NT)
            d_scores = (probs * (d_probs - inner)).astype(LOW)
            dk_ref[place, cols] += kdot(d_scores, q3, NN)
            dv_ref[place, cols] += kdot(probs.astype(LOW), do3, NN)
            return acc + kdot(keys, d_scores, TN)

        acc = lax.fori_loop(0, block + 1, step, jnp.zeros((HEAD_SIZE, width), F32))
        pieces += [acc[:, g * rows : (g + 1) * rows] for g in range(GROUP)]
    dq_ref[...] = jnp.concatenate(pieces, axis=0).T * SCALE


def attention_specs(ranks, rows, heads):
    length = ranks * rows
    q_spec = pl.BlockSpec((rows, heads * GROUP * HEAD_SIZE), lambda i, me: (i, 0))
    kv_spec = pl.BlockSpec((length, heads * HEAD_SIZE), lambda i, me: (0, 0))
    lo_spec = pl.BlockSpec((1, 1, rows), lambda i, me: (i, 0, 0))
    lse_spec = pl.BlockSpec((1, heads, GROUP * rows), lambda i, me: (i, 0, 0))
    return q_spec, kv_spec, lo_spec, lse_spec


def attend(me, queries, keys, values, bounds, ranks, heads):
    length = queries.shape[0]
    rows = length // ranks
    q_spec, kv_spec, lo_spec, lse_spec = attention_specs(ranks, rows, heads)
    return pl.pallas_call(
        functools.partial(attend_kernel, heads, rows),
        grid_spec=pltpu.PrefetchScalarGridSpec(
            num_scalar_prefetch=1,
            grid=(ranks,),
            in_specs=[q_spec, kv_spec, kv_spec, lo_spec],
            out_specs=[q_spec, lse_spec],
        ),
        out_shape=[
            jax.ShapeDtypeStruct(queries.shape, LOW),
            jax.ShapeDtypeStruct((ranks, heads, GROUP * rows), F32),
        ],
        compiler_params=pltpu.CompilerParams(vmem_limit_bytes=48 * 2**20),
        cost_estimate=pl.CostEstimate(
            flops=8 * length * length * heads * GROUP * HEAD_SIZE,
            bytes_accessed=8 * length * heads * GROUP * HEAD_SIZE,
            transcendentals=length * length * heads * GROUP,
        ),
        name="attend",
    )(me, queries, keys, values, bounds)


def attend_back(me, queries, keys, values, bounds, attended, d_attended, lse, ranks, heads):
    length = queries.shape[0]
    rows = length // ranks
    q_spec, kv_spec, lo_spec, lse_spec = attention_specs(ranks, rows, heads)
    return pl.pallas_call(
        functools.partial(attend_back_kernel, heads, rows),
        grid_spec=pltpu.PrefetchScalarGridSpec(
            num_scalar_prefetch=1,
            grid=(ranks,),
            in_specs=[q_spec, kv_spec, kv_spec, lo_spec, q_spec, q_spec, lse_spec],
            out_specs=[q_spec, kv_spec, kv_spec],
        ),
        out_shape=[
            jax.ShapeDtypeStruct(queries.shape, F32),
            jax.ShapeDtypeStruct(keys.shape, F32),
            jax.ShapeDtypeStruct(keys.shape, F32),
        ],
        compiler_params=pltpu.CompilerParams(vmem_limit_bytes=48 * 2**20),
        cost_estimate=pl.CostEstimate(
            flops=20 * length * length * heads * GROUP * HEAD_SIZE,
            bytes_accessed=16 * length * heads * GROUP * HEAD_SIZE,
            transcendentals=length * length * heads * GROUP,
        ),
        name="attend_back",
    )(me, queries, keys, values, bounds, attended, d_attended, lse)


def rotate(heads, cosine, sine):
    half_size = heads.shape[-1] // 2
    first_half = heads[..., :half_size]
    second_half = heads[..., half_size:]
    return jnp.concatenate(
        [first_half * cosine - second_half * sine, second_half * cosine + first_half * sine],
        axis=-1,
    )


def shards(
    dp_size,
    ranks,
    tokens,
    segments,
    attn_gain,
    w_query,
    key_weight,
    value_weight,
    query_gain,
    key_gain,
    w_out,
    ffn_gain,
    w_gate,
    w_up,
    w_down,
    cotangent,
):
    ring = dp_size // 2
    place = lax.axis_index("dp")
    stage = place // 2
    core = place % 2
    me = lax.axis_index("tensor")
    swap_pairs = [(i, i ^ 1) for i in range(dp_size)]
    ring_pairs = [(i, (i + 2) % dp_size) for i in range(dp_size)]
    heads = KEY_VALUE_HEADS // ranks
    rows = tokens.shape[0]
    length = segments.shape[0]
    q_cols = w_query.shape[1]
    kv_cols = key_weight.shape[1]

    def swap(v):
        return lax.ppermute(v, "dp", swap_pairs)

    def onward(v):
        return lax.ppermute(v, "dp", ring_pairs)

    def gather_dp(weight):
        depth, cols = weight.shape
        full = jnp.zeros((dp_size * depth, cols), weight.dtype)
        block = weight
        for hop in range(ring):
            owner = lax.rem(stage - hop + ring, ring)
            full = lax.dynamic_update_slice(full, block, ((owner * 2 + core) * depth, 0))
            full = lax.dynamic_update_slice(full, swap(block), ((owner * 2 + 1 - core) * depth, 0))
            if hop < ring - 1:
                block = onward(block)
        return full

    def by_core(matrix):
        count = matrix.shape[0]
        split = matrix.reshape(count, ring, 2, -1)
        even = split[:, :, 0].reshape(count, -1)
        odd = split[:, :, 1].reshape(count, -1)
        return jnp.where(core == 0, odd, even), jnp.where(core == 0, even, odd)

    def reduce_dp(left_pair, right):
        far = swap(cross_cols(left_pair[0], right).astype(LOW))
        near = (cross_cols(left_pair[1], right) + far.astype(F32)).astype(LOW)
        near = near.reshape(ring, -1, right.shape[1])

        def mine(hop):
            owner = lax.rem(stage - 1 - hop + 2 * ring, ring)
            return lax.dynamic_index_in_dim(near, owner, 0, keepdims=False)

        block = mine(0)
        for hop in range(1, ring):
            block = onward(block).astype(F32) + mine(hop).astype(F32)
            if hop < ring - 1:
                block = block.astype(LOW)
        return block

    def spread(block):
        return [block] + [
            lax.ppermute(block, "tensor", [(i, i ^ j) for i in range(ranks)]) for j in range(1, ranks)
        ]

    def collect(parts):
        total = parts[0].astype(F32)
        for j in range(1, ranks):
            total = total + lax.ppermute(
                parts[j].astype(LOW), "tensor", [(i, i ^ j) for i in range(ranks)]
            ).astype(F32)
        return total

    def cut(matrix):
        return [matrix[j * rows : (j + 1) * rows] for j in range(ranks)]

    tokens_wide = tokens.astype(F32)
    normed_own = norm_rows(tokens_wide, attn_gain).astype(LOW)
    normed_one = spread(normed_own)
    w_qkv = gather_dp(jnp.concatenate([w_query, key_weight, value_weight], axis=1))
    out_t = gather_dp(w_out.T)
    down_t = gather_dp(w_down.T)
    gate_full = gather_dp(w_gate)
    up_full = gather_dp(w_up)
    grad_blocks = spread(cotangent)

    first_start = jnp.sum((segments < 1).astype(jnp.int32))
    second_start = jnp.sum((segments < 2).astype(jnp.int32))
    ids = jnp.arange(length, dtype=jnp.int32).reshape(ranks, rows)
    begins = jnp.where(segments == 0, 0, jnp.where(segments == 1, first_start, second_start))
    begins = begins.astype(jnp.int32).reshape(ranks, rows)
    order = [me ^ j for j in range(ranks)]
    bounds = jnp.stack([lax.dynamic_index_in_dim(begins, o, 0, keepdims=False) for o in order])
    here = jnp.stack([lax.dynamic_index_in_dim(ids, o, 0, keepdims=False) for o in order])
    positions = (here - bounds).reshape(length).astype(F32)
    bounds = bounds.reshape(ranks, 1, rows)
    half = HEAD_SIZE // 2
    freqs = ROTARY_BASE ** (-2.0 * jnp.arange(half, dtype=F32) / HEAD_SIZE)
    angles = positions[:, None] * freqs[None, :]
    cosine = jnp.cos(angles)[:, None, :]
    sine = jnp.sin(angles)[:, None, :]

    raw = jnp.concatenate([mm(block, w_qkv) for block in normed_one], axis=0)
    normed_all = jnp.concatenate(normed_one, axis=0)

    def head_prepare(raw_rows, gain):
        return rotate(norm_rows(raw_rows.reshape(length, -1, HEAD_SIZE), gain), cosine, sine)

    query_rot, query_pull = jax.vjp(head_prepare, raw[:, :q_cols], query_gain)
    key_rot, key_pull = jax.vjp(head_prepare, raw[:, q_cols : q_cols + kv_cols], key_gain)
    query_low = query_rot.astype(LOW).reshape(length, -1)
    key_low = key_rot.astype(LOW).reshape(length, -1)
    value_low = raw[:, q_cols + kv_cols :].astype(LOW)
    me_array = me.astype(jnp.int32).reshape(1)
    attended, lse = attend(me_array, query_low, key_low, value_low, bounds, ranks, heads)

    attn_sum = collect([cross_rows(block, out_t) for block in cut(attended)])
    hidden = tokens_wide + attn_sum
    normed_two = spread(norm_rows(hidden, ffn_gain).astype(LOW))
    normed_two_all = jnp.concatenate(normed_two, axis=0)
    grad_all = jnp.concatenate(grad_blocks, axis=0)

    d_activation = mm(grad_all, down_t)
    gating = mm(normed_two_all, gate_full)
    lifted = mm(normed_two_all, up_full)
    gate_sig = jax.nn.sigmoid(gating)
    silu = gating * gate_sig
    activation = (silu * lifted).astype(LOW)
    d_gating = (d_activation * lifted * gate_sig * (1.0 + gating * (1.0 - gate_sig))).astype(LOW)
    d_lifted = (d_activation * silu).astype(LOW)

    d_normed_two = collect(
        [
            cross_rows(g, gate_full) + cross_rows(u, up_full)
            for g, u in zip(cut(d_gating), cut(d_lifted))
        ]
    )
    output = hidden + collect([cross_rows(block, down_t) for block in cut(activation)])
    grad_pair = by_core(grad_all)
    normed_two_pair = by_core(normed_two_all)
    down_grad = reduce_dp(grad_pair, activation)
    gate_grad = reduce_dp(normed_two_pair, d_gating)
    lift_grad = reduce_dp(normed_two_pair, d_lifted)

    d_hidden_norm, ffn_gain_part = norm_back(hidden, ffn_gain, d_normed_two)
    d_hidden = cotangent.astype(F32) + d_hidden_norm
    hidden_grad = spread(d_hidden.astype(LOW))
    d_attended = jnp.concatenate([mm(block, out_t) for block in hidden_grad], axis=0).astype(LOW)
    hidden_grad_pair = by_core(jnp.concatenate(hidden_grad, axis=0))
    d_queries, d_keys, d_values = attend_back(
        me_array, query_low, key_low, value_low, bounds, attended, d_attended, lse, ranks, heads
    )
    d_query_raw, query_gain_part = query_pull(d_queries.reshape(length, -1, HEAD_SIZE))
    d_key_raw, key_gain_part = key_pull(d_keys.reshape(length, -1, HEAD_SIZE))
    d_raw = jnp.concatenate(
        [d_query_raw.astype(LOW), d_key_raw.astype(LOW), d_values.astype(LOW)], axis=1
    )
    d_normed_one = collect([cross_rows(block, w_qkv) for block in cut(d_raw)])
    qkv_grad = reduce_dp(by_core(normed_all), d_raw)
    out_grad = reduce_dp(hidden_grad_pair, attended)
    d_tokens_norm, attn_gain_part = norm_back(tokens_wide, attn_gain, d_normed_one)
    tokens_grad = d_hidden + d_tokens_norm

    sizes = [attn_gain.shape[0], ffn_gain.shape[0], HEAD_SIZE, HEAD_SIZE]
    gains = jnp.concatenate([attn_gain_part, ffn_gain_part, query_gain_part, key_gain_part])
    gains = gains.reshape(1, -1)
    total = gains
    span = 1
    while span < ranks:
        total = total + lax.ppermute(total, "tensor", [(i, i ^ span) for i in range(ranks)])
        span *= 2
    span = 1
    while span < dp_size:
        total = total + lax.ppermute(total, "dp", [(i, i ^ span) for i in range(dp_size)])
        span *= 2
    total = total.reshape(-1)
    a, b = sizes[0], sizes[0] + sizes[1]
    return (
        output,
        tokens_grad,
        total[:a],
        qkv_grad[:, :q_cols],
        qkv_grad[:, q_cols : q_cols + kv_cols],
        qkv_grad[:, q_cols + kv_cols :],
        total[b : b + HEAD_SIZE],
        total[b + HEAD_SIZE :],
        out_grad.T,
        total[a:b],
        gate_grad,
        lift_grad,
        down_grad.T,
    )


def solution(mesh):
    in_specs = (
        P(("dp", "tensor"), None),
        P("dp"),
        P(),
        P("dp", "tensor"),
        P("dp", "tensor"),
        P("dp", "tensor"),
        P(),
        P(),
        P("tensor", "dp"),
        P(),
        P("dp", "tensor"),
        P("dp", "tensor"),
        P("tensor", "dp"),
        P(("dp", "tensor"), None),
    )
    out_specs = (
        P(("dp", "tensor"), None),
        P(("dp", "tensor"), None),
        P(),
        P("dp", "tensor"),
        P("dp", "tensor"),
        P("dp", "tensor"),
        P(),
        P(),
        P("tensor", "dp"),
        P(),
        P("dp", "tensor"),
        P("dp", "tensor"),
        P("tensor", "dp"),
    )
    body = functools.partial(shards, mesh.shape["dp"], mesh.shape["tensor"])
    return jax.shard_map(body, mesh=mesh, in_specs=in_specs, out_specs=out_specs, check_vma=False)
```

time: 1200 us -> 733 us (0.61)
  waiting for transfers between devices: 724 us -> 317 us
  blocking collectives: 105 us -> 0 us
  starting transfers between devices: 1.17 us -> 63.8 us
  matrix products: 215 us -> 156 us
  local copies, waits for them, and re-layouts: 57.3 us -> 111 us
  Pallas kernels: 0 us -> 29.7 us
  other arithmetic: 64.8 us -> 45.4 us
  between operations: 15.4 us -> 2.97 us
    all_gather x14 -> x0, waiting for transfers between devices: 391 us -> none  [the longest x1 58.4 us: shards(): lax.all_gather(w_gate, 'dp', axis=0, tiled=True)]
    reduce_scatter x10 -> x0, waiting for transfers between devices: 326 us -> none  [the longest x1 60.7 us: shards(): lax.psum_scatter(lift_term.astype(jnp.bfloat16), 'dp', scatter_dimension=...]
    ppermute x0 -> x84, waiting for transfers between devices: none -> 317 us  [the longest x30 188 us: onward(): return lax.ppermute(v, 'dp', ring_pairs)]
    dot_general x21 -> x11, matrix products: 119 us -> 46.1 us  [mm(): return jnp.dot(left, right, preferred_element_type=F32)]
    all_gather x4 -> x0, blocking collectives: 64.6 us -> none  [the longest x1 17.2 us: shards(): lax.all_gather(key_weight, 'dp', axis=0, tiled=True)]
    ppermute x0 -> x84, starting transfers between devices: none -> 63.8 us  [the longest x30 21.6 us: onward(): return lax.ppermute(v, 'dp', ring_pairs)]
    psum x1 -> x0, blocking collectives: 40 us -> none  [shards(): lax.psum((attn_gain_part, query_gain_part, key_gain_part, ffn_gain_part),...]
    pallas_call x0 -> x2, Pallas kernels: none -> 29.7 us  [the longest x1 16.9 us: attend_back(): pl.pallas_call(functools.partial(attend_back_kernel, heads, rows), grid_s...]
  transfers between devices with their start and end apart: 25 -> 84, of which waited for: 19 -> 35; matrix products, arithmetic and copies ran while one was open for 26% -> 33% of each run, Pallas kernels for 0% -> 4%
where the time goes in v1:
time: 733 us; the launch traced here: 726 us
  waiting for transfers between devices  317 us (43%)
  matrix products  156 us (21%)
  local copies, waits for them, and re-layouts  111 us (15%)
  starting transfers between devices  63.8 us (9%)
  other arithmetic  45.4 us (6%)
  Pallas kernels  29.7 us (4%)
    ppermute x30, waiting for transfers between devices, onward(): return lax.ppermute(v, 'dp', ring_pairs)  188 us
    dot_general x20, matrix products, cross_rows(): lax.dot_general(left, right, (((1,), (1,)), ((), ())), preferred_element_...  66.4 us
    ppermute x12, waiting for transfers between devices, collect(): lax.ppermute(parts[j].astype(LOW), 'tensor', [(i, i ^ j) for i in range(r...  63.9 us
    ppermute x12, waiting for transfers between devices, spread(): lax.ppermute(block, 'tensor', [(i, i ^ j) for i in range(ranks)])  59.5 us
    dot_general x11, matrix products, mm(): return jnp.dot(left, right, preferred_element_type=F32)  46.1 us
    dot_general x10, matrix products, cross_cols(): lax.dot_general(left, right, (((0,), (0,)), ((), ())), preferred_element_...  43.2 us
    ppermute x30, starting transfers between devices, onward(): return lax.ppermute(v, 'dp', ring_pairs)  21.6 us
    dynamic_update_slice x20, local copies, waits for them, and re-layouts, gather_dp(): lax.dynamic_update_slice(full, swap(block), ((owner * 2 + 1 - core) * dep...  21.2 us
  transfers between devices with their start and end apart: 84, of which 35 were waited for; matrix products, arithmetic and copies ran while one was open for 33% of the time, Pallas kernels for 4%

profile of v1, /device:TPU:0, one launch (start us, length us, event | category | flops | bytes accessed | tf_op | source)
XLA Modules:
  0.0 725.8 jit_solution(1973627336941063873)
XLA Ops:
  35.4 16.8 %collective-permute-done.13 = bf16[192,384]{1,0:T(8,128)(2,1)S(1)} collective-permute-done((bf16[192,384]{1,0:T(8,128)(2,1)}, bf16[192,384]{1,0:T(8,128)(2,1)S(1)}, u32[]{:S(2)}, u32[]{:S(2)}) %collective-permute-start.13) | collective-permute-done | bytes 147488 | tf_op jit(solution)/shard_map/ppermute | solution.py:271
  53.7 7.0 collective-permute-done.15
  61.3 4.2 collective-permute-done.3
  74.1 11.6 %collective-permute-done.38 = bf16[192,1728]{1,0:T(8,128)(2,1)S(1)} collective-permute-done((bf16[192,1728]{1,0:T(8,128)(2,1)S(1)}, bf16[192,1728]{1,0:T(8,128)(2,1)S(1)}, u32[]{:S(2)}, u32[]{:S(2)}) %collective-permute-start.38) | collective-permute-done | bytes 663584 | tf_op jit(solution)/shard_map/ppermute | solution.py:271
  88.2 11.1 %collective-permute-done.24 = bf16[192,1728]{1,0:T(8,128)(2,1)} collective-permute-done((bf16[192,1728]{1,0:T(8,128)(2,1)S(1)}, bf16[192,1728]{1,0:T(8,128)(2,1)}, u32[]{:S(2)}, u32[]{:S(2)}) %collective-permute-start.24) | collective-permute-done | bytes 663584 | tf_op jit(solution)/shard_map/ppermute | solution.py:271
  102.6 5.2 collective-permute-done.5
  115.9 4.7 copy.52
  120.6 3.5 collective-permute-done.47
  124.0 18.3 %collective-permute-done.48 = bf16[256,1536]{0,1:T(8,128)(2,1)} collective-permute-done((bf16[256,1536]{0,1:T(8,128)(2,1)}, bf16[256,1536]{0,1:T(8,128)(2,1)}, u32[]{:S(2)}, u32[]{:S(2)}) %collective-permute-start.48) | collective-permute-done | bytes 786464 | tf_op jit(solution)/shard_map/ppermute | solution.py:310
  162.2 12.8 %attend.1 = (bf16[1024,384]{1,0:T(8,128)(2,1)S(1)}, f32[4,2,768]{2,1,0:T(2,128)S(1)}) custom-call(s32[1]{0:T(128)} %bitcast.me_ref, bf16[1024,384]{1,0:T(8,128)(2,1)S(1)} %copy.41.q_ref, bf16[1024,128]{1,0:T(8,128)(2,1)S(1)} %copy.42.k_ref, bf16[1024,128]{1,0:T(8,128)(2,1)S(1)} %slice.292.v_ref, s32[4,1,256]{2,1,0:T(1,128)S(1)} %reshape.297.lo_ref), custom_call_target="tpu_custom_call" | custom-call | flops 3221225472 | bytes 3145728 | tf_op jit(solution)/shard_map/attend/pallas_call | solution.py:177
  176.8 4.0 collective-permute-start.26
  200.0 3.3 collective-permute-done.17
  203.3 18.6 %collective-permute-done.18 = bf16[256,1536]{1,0:T(8,128)(2,1)S(1)} collective-permute-done((bf16[256,1536]{1,0:T(8,128)(2,1)S(1)}, bf16[256,1536]{1,0:T(8,128)(2,1)S(1)}, u32[]{:S(2)}, u32[]{:S(2)}) %collective-permute-start.18) | collective-permute-done | bytes 786464 | tf_op jit(solution)/shard_map/ppermute | solution.py:316
  230.2 12.2 %collective-permute-done.42 = bf16[192,1728]{1,0:T(8,128)(2,1)} collective-permute-done((bf16[192,1728]{1,0:T(8,128)(2,1)}, bf16[192,1728]{1,0:T(8,128)(2,1)}, u32[]{:S(2)}, u32[]{:S(2)}) %collective-permute-start.42) | collective-permute-done | bytes 663584 | tf_op jit(solution)/shard_map/ppermute | solution.py:271
  248.7 6.6 collective-permute-done.28
  257.9 7.3 %collective-permute-done.21 = bf16[256,1536]{1,0:T(8,128)(2,1)S(1)} collective-permute-done((bf16[256,1536]{1,0:T(8,128)(2,1)S(1)}, bf16[256,1536]{1,0:T(8,128)(2,1)S(1)}, u32[]{:S(2)}, u32[]{:S(2)}) %collective-permute-start.21) | collective-permute-done | bytes 786464 | tf_op jit(solution)/shard_map/ppermute | solution.py:310
  268.8 4.7 copy.54
  273.5 3.9 broadcast_select_fusion.2
  279.5 12.4 %fusion.71 = f32[1024,1728]{0,1:T(8,128)} fusion(bf16[1536,1728]{1,0:T(8,128)(2,1)} %constant_dynamic-update-slice_fusion.8, bf16[256,1536]{1,0:T(8,128)(2,1)S(1)} %copy-done.63, bf16[256,1536]{1,0:T(8,128)(2,1)S(1)} %copy-done.61, bf16[256,1536]{1,0:T(8,128)(2,1)S(1)} %copy-done.59, bf16[256,1536]{1,0:T(8,128)(2,1)S(1)} %copy-done.34), kind=kOutput, calls=%fused_computation.242 | convolution fusion | flops 5448400896 | bytes 15532032 | tf_op jit(solution)/shard_map/dot_general | solution.py:39
  293.8 10.9 %fusion.70 = f32[1024,1728]{0,1:T(8,128)} fusion(bf16[1536,1728]{1,0:T(8,128)(2,1)} %constant_dynamic-update-slice_fusion, bf16[256,1536]{0,1:T(8,128)(2,1)} %collective-permute-done.49, bf16[256,1536]{0,1:T(8,128)(2,1)} %collective-permute-done.48, bf16[256,1536]{0,1:T(8,128)(2,1)S(1)} %copy-done.51, bf16[256,1536]{0,1:T(8,128)(2,1)} %copy.46), kind=kOutput, calls=%fused_computation.241 | convolution fusion | flops 5448400896 | bytes 15532032 | tf_op jit(solution)/shard_map/dot_general | solution.py:39
  306.8 17.4 %multiply_convert_fusion.1 = (bf16[1024,1728]{0,1:T(8,128)(2,1)}, bf16[1024,1728]{0,1:T(8,128)(2,1)}, bf16[1024,1728]{0,1:T(8,128)(2,1)}) fusion(f32[1024,1728]{0,1:T(8,128)} %fusion.70, f32[1024,1728]{0,1:T(8,128)} %fusion.71, bf16[1536,1728]{1,0:T(8,128)(2,1)} %constant_dynamic-update-slice_fusion.16, bf16[256,1536]{1,0:T(8,128)(2,1)} %copy-done.62, ...), kind=kOutput, calls=%fused_computation.1 | convolution fusion | flops 5474942976 | bytes 33226752 | tf_op jit(solution)/shard_map/dot_general | solution.py:39
  324.2 4.6 fusion.43
  328.9 4.2 fusion.40
  333.1 4.2 fusion.37
  337.3 4.4 fusion.34
  341.7 5.3 convolution_convert_fusion.11
  347.0 4.3 convolution_convert_fusion
  351.3 4.6 convolution_convert_fusion.1
  356.0 4.2 fusion.12
  361.4 4.3 fusion.13
  367.3 4.2 fusion.14
  372.4 5.1 convolution_convert_fusion.10
  378.7 4.4 convolution_convert_fusion.2
  383.1 17.8 %collective-permute-done.51 = bf16[256,1536]{1,0:T(8,128)(2,1)S(1)} collective-permute-done((bf16[256,1536]{1,0:T(8,128)(2,1)S(1)}, bf16[256,1536]{1,0:T(8,128)(2,1)S(1)}, u32[]{:S(2)}, u32[]{:S(2)}) %collective-permute-start.51) | collective-permute-done | bytes 786464 | tf_op jit(solution)/shard_map/ppermute | solution.py:316
  400.9 4.9 multiply_reduce_fusion.1
  410.5 5.1 convolution_convert_fusion.9
  416.2 15.2 %collective-permute-done.53 = bf16[256,1536]{1,0:T(8,128)(2,1)S(1)} collective-permute-done((bf16[256,1536]{1,0:T(8,128)(2,1)S(1)}, bf16[256,1536]{1,0:T(8,128)(2,1)S(1)}, u32[]{:S(2)}, u32[]{:S(2)}) %collective-permute-start.53) | collective-permute-done | bytes 786464 | tf_op jit(solution)/shard_map/ppermute | solution.py:310
  434.0 15.3 %collective-permute-done.55 = bf16[256,1536]{1,0:T(8,128)(2,1)S(1)} collective-permute-done((bf16[256,1536]{1,0:T(8,128)(2,1)S(1)}, bf16[256,1536]{1,0:T(8,128)(2,1)S(1)}, u32[]{:S(2)}, u32[]{:S(2)}) %collective-permute-start.55) | collective-permute-done | bytes 786464 | tf_op jit(solution)/shard_map/ppermute | solution.py:310
  452.0 4.7 copy.53
  456.8 3.2 broadcast_select_fusion.4
  464.5 16.9 %attend_back.1 = (f32[1024,384]{1,0:T(8,128)S(1)}, f32[1024,128]{1,0:T(8,128)S(1)}, f32[1024,128]{1,0:T(8,128)S(1)}) custom-call(s32[1]{0:T(128)} %bitcast.me_ref, bf16[1024,384]{1,0:T(8,128)(2,1)S(1)} %copy.41.q_ref, bf16[1024,128]{1,0:T(8,128)(2,1)S(1)} %copy-done.5, bf16[1024,128]{1,0:T(8,128)(2,1)S(1)} %slice.292.v_ref, ...), custom_call_target="tpu_custom_call" | custom-call | flops 8053063680 | bytes 6291456 | tf_op jit(solution)/shard_map/attend_back/pallas_call | solution.py:203
  499.4 6.5 fusion.10
  505.9 2.9 add_convert_fusion.4
  508.9 7.4 %collective-permute-done.56 = bf16[256,1536]{1,0:T(8,128)(2,1)S(1)} collective-permute-done((bf16[256,1536]{1,0:T(8,128)(2,1)S(1)}, bf16[256,1536]{1,0:T(8,128)(2,1)S(1)}, u32[]{:S(2)}, u32[]{:S(2)}) %collective-permute-start.56) | collective-permute-done | bytes 786464 | tf_op jit(solution)/shard_map/ppermute | solution.py:316
  516.3 16.7 %collective-permute-done.57 = bf16[256,1536]{1,0:T(8,128)(2,1)S(1)} collective-permute-done((bf16[256,1536]{1,0:T(8,128)(2,1)S(1)}, bf16[256,1536]{1,0:T(8,128)(2,1)S(1)}, u32[]{:S(2)}, u32[]{:S(2)}) %collective-permute-start.57) | collective-permute-done | bytes 786464 | tf_op jit(solution)/shard_map/ppermute | solution.py:316
  540.0 3.3 convolution_convert_fusion.12
  549.8 3.3 collective-permute-start.63
  557.5 4.5 collective-permute-done.70
  567.2 3.7 collective-permute-done.71
  571.6 5.6 add_convert_fusion
  577.2 3.3 copy.57
  583.3 7.4 %add_convert_fusion.1 = bf16[768,1728]{0,1:T(8,128)(2,1)} fusion(bf16[768,1728]{0,1:T(8,128)(2,1)} %collective-permute-done.76, bf16[1024,768]{0,1:T(8,128)(2,1)S(1)} %bitcast.187, bf16[1024,1728]{0,1:T(8,128)(2,1)} %get-tuple-element.36), kind=kOutput, calls=%fused_computation.6 | convolution fusion | flops 2721890304 | bytes 10420224 | tf_op jit(solution)/shard_map/dot_general | solution.py:47
  590.7 4.5 copy.56
  597.9 6.0 collective-permute-done.66
  605.7 7.4 %add_convert_fusion.2 = bf16[768,1728]{0,1:T(8,128)(2,1)} fusion(bf16[768,1728]{0,1:T(8,128)(2,1)} %collective-permute-done.72, bf16[1024,768]{0,1:T(8,128)(2,1)S(1)} %bitcast.188, bf16[1024,1728]{0,1:T(8,128)(2,1)} %get-tuple-element.35), kind=kOutput, calls=%fused_computation.7 | convolution fusion | flops 2721890304 | bytes 10420224 | tf_op jit(solution)/shard_map/dot_general | solution.py:47
  613.1 4.6 copy.55
  619.0 5.0 collective-permute-done.67
  630.3 8.9 %collective-permute-done.73 = bf16[192,1728]{1,0:T(8,128)(2,1)S(1)} collective-permute-done((bf16[192,1728]{1,0:T(8,128)(2,1)S(1)}, bf16[192,1728]{1,0:T(8,128)(2,1)S(1)}, u32[]{:S(2)}, u32[]{:S(2)}) %collective-permute-start.73) | collective-permute-done | bytes 663584 | tf_op jit(solution)/shard_map/ppermute | solution.py:271
  639.4 14.5 %collective-permute-done.82 = bf16[192,1728]{1,0:T(8,128)(2,1)S(1)} collective-permute-done((bf16[192,1728]{1,0:T(8,128)(2,1)S(1)}, bf16[192,1728]{1,0:T(8,128)(2,1)S(1)}, u32[]{:S(2)}, u32[]{:S(2)}) %collective-permute-start.82) | collective-permute-done | bytes 663584 | tf_op jit(solution)/shard_map/ppermute | solution.py:271
  654.1 14.5 %collective-permute-done.78 = bf16[192,1728]{1,0:T(8,128)(2,1)S(1)} collective-permute-done((bf16[192,1728]{1,0:T(8,128)(2,1)S(1)}, bf16[192,1728]{1,0:T(8,128)(2,1)S(1)}, u32[]{:S(2)}, u32[]{:S(2)}) %collective-permute-start.78) | collective-permute-done | bytes 663584 | tf_op jit(solution)/shard_map/ppermute | solution.py:271
  668.9 14.5 %collective-permute-done.74 = bf16[192,1728]{1,0:T(8,128)(2,1)S(1)} collective-permute-done((bf16[192,1728]{1,0:T(8,128)(2,1)S(1)}, bf16[192,1728]{1,0:T(8,128)(2,1)S(1)}, u32[]{:S(2)}, u32[]{:S(2)}) %collective-permute-start.74) | collective-permute-done | bytes 663584 | tf_op jit(solution)/shard_map/ppermute | solution.py:271
  683.6 14.5 %collective-permute-done.83 = bf16[192,1728]{1,0:T(8,128)(2,1)S(1)} collective-permute-done((bf16[192,1728]{1,0:T(8,128)(2,1)S(1)}, bf16[192,1728]{1,0:T(8,128)(2,1)S(1)}, u32[]{:S(2)}, u32[]{:S(2)}) %collective-permute-start.83) | collective-permute-done | bytes 663584 | tf_op jit(solution)/shard_map/ppermute | solution.py:271
  699.3 13.5 %collective-permute-done.79 = bf16[192,1728]{1,0:T(8,128)(2,1)S(1)} collective-permute-done((bf16[192,1728]{1,0:T(8,128)(2,1)S(1)}, bf16[192,1728]{1,0:T(8,128)(2,1)S(1)}, u32[]{:S(2)}, u32[]{:S(2)}) %collective-permute-start.79) | collective-permute-done | bytes 663584 | tf_op jit(solution)/shard_map/ppermute | solution.py:271
  714.1 10.0 %collective-permute-done.75 = bf16[192,1728]{1,0:T(8,128)(2,1)S(1)} collective-permute-done((bf16[192,1728]{1,0:T(8,128)(2,1)S(1)}, bf16[192,1728]{1,0:T(8,128)(2,1)S(1)}, u32[]{:S(2)}, u32[]{:S(2)}) %collective-permute-start.75) | collective-permute-done | bytes 663584 | tf_op jit(solution)/shard_map/ppermute | solution.py:271
  (489 shorter events, 206.7 us)
Async XLA Ops:
  3.3 29.7 %collective-permute-start = (bf16[192,640]{1,0:T(8,128)(2,1)S(1)}, bf16[192,640]{1,0:T(8,128)(2,1)}, u32[]{:S(2)}, u32[]{:S(2)}) collective-permute-start(bf16[192,640]{1,0:T(8,128)(2,1)S(1)} %constant_dynamic-update-slice_fusion.40), channel_id=1, source_target_pairs={{0,4},{4,0},{8,12},{12,8},{16,20},{20,16},{24,28},{28,24},{1,5},{5... | collective-permute-start | bytes 737288 | tf_op jit(solution)/shard_map/ppermute | solution.py:268
  3.8 29.6 %collective-permute-start.1 = (bf16[192,640]{1,0:T(8,128)(2,1)S(1)}, bf16[192,640]{1,0:T(8,128)(2,1)}, u32[]{:S(2)}, u32[]{:S(2)}) collective-permute-start(bf16[192,640]{1,0:T(8,128)(2,1)S(1)} %constant_dynamic-update-slice_fusion.40), channel_id=1, source_target_pairs={{0,8},{4,12},{8,16},{12,20},{16,24},{20,28},{24,0},{28,4},{1,9},{5... | collective-permute-start | bytes 737288 | tf_op jit(solution)/shard_map/ppermute | solution.py:271
  6.4 22.8 %collective-permute-start.10 = (bf16[192,384]{1,0:T(8,128)(2,1)}, bf16[192,384]{1,0:T(8,128)(2,1)}, u32[]{:S(2)}, u32[]{:S(2)}) collective-permute-start(bf16[192,384]{1,0:T(8,128)(2,1)} %bitcast.208), channel_id=1, source_target_pairs={{0,4},{4,0},{8,12},{12,8},{16,20},{20,16},{24,28},{28,24},{1,5},{5... | collective-permute-start | bytes 442376 | tf_op jit(solution)/shard_map/ppermute | solution.py:268
  6.6 24.3 %collective-permute-start.11 = (bf16[192,384]{1,0:T(8,128)(2,1)}, bf16[192,384]{1,0:T(8,128)(2,1)}, u32[]{:S(2)}, u32[]{:S(2)}) collective-permute-start(bf16[192,384]{1,0:T(8,128)(2,1)} %bitcast.209), channel_id=1, source_target_pairs={{0,8},{4,12},{8,16},{12,20},{16,24},{20,28},{24,0},{28,4},{1,9},{5... | collective-permute-start | bytes 442376 | tf_op jit(solution)/shard_map/ppermute | solution.py:271
  8.2 57.6 %collective-permute-start.30 = (bf16[192,1728]{1,0:T(8,128)(2,1)}, bf16[192,1728]{1,0:T(8,128)(2,1)}, u32[]{:S(2)}, u32[]{:S(2)}) collective-permute-start(bf16[192,1728]{1,0:T(8,128)(2,1)} %param.25), channel_id=1, source_target_pairs={{0,4},{4,0},{8,12},{12,8},{16,20},{20,16},{24,28},{28,24},{1,5},{5... | collective-permute-start | bytes 1990664 | tf_op jit(solution)/shard_map/ppermute | solution.py:268
  29.2 39.0 %collective-permute-start.31 = (bf16[192,1728]{1,0:T(8,128)(2,1)}, bf16[192,1728]{1,0:T(8,128)(2,1)}, u32[]{:S(2)}, u32[]{:S(2)}) collective-permute-start(bf16[192,1728]{1,0:T(8,128)(2,1)} %param.25), channel_id=1, source_target_pairs={{0,8},{4,12},{8,16},{12,20},{16,24},{20,28},{24,0},{28,4},{1,9},{5... | collective-permute-start | bytes 1990664 | tf_op jit(solution)/shard_map/ppermute | solution.py:271
  30.9 21.4 %collective-permute-start.12 = (bf16[192,384]{1,0:T(8,128)(2,1)}, bf16[192,384]{1,0:T(8,128)(2,1)S(1)}, u32[]{:S(2)}, u32[]{:S(2)}) collective-permute-start(bf16[192,384]{1,0:T(8,128)(2,1)} %collective-permute-done.11), channel_id=1, source_target_pairs={{0,4},{4,0},{8,12},{12,8},{16,20},{20,16},{24,28},{28,24},{1,5},{5... | collective-permute-start | bytes 442376 | tf_op jit(solution)/shard_map/ppermute | solution.py:268
  33.4 27.4 %collective-permute-start.2 = (bf16[192,640]{1,0:T(8,128)(2,1)}, bf16[192,640]{1,0:T(8,128)(2,1)S(1)}, u32[]{:S(2)}, u32[]{:S(2)}) collective-permute-start(bf16[192,640]{1,0:T(8,128)(2,1)} %collective-permute-done.1), channel_id=1, source_target_pairs={{0,4},{4,0},{8,12},{12,8},{16,20},{20,16},{24,28},{28,24},{1,5},{5... | collective-permute-start | bytes 737288 | tf_op jit(solution)/shard_map/ppermute | solution.py:268
  65.6 20.1 %collective-permute-start.38 = (bf16[192,1728]{1,0:T(8,128)(2,1)S(1)}, bf16[192,1728]{1,0:T(8,128)(2,1)S(1)}, u32[]{:S(2)}, u32[]{:S(2)}) collective-permute-start(bf16[192,1728]{1,0:T(8,128)(2,1)S(1)} %bitcast.203), channel_id=1, source_target_pairs={{0,8},{4,12},{8,16},{12,20},{16,24},{20,28},{24,0},{28,4},{1,9},{5... | collective-permute-start | bytes 1990664 | tf_op jit(solution)/shard_map/ppermute | solution.py:271
  65.6 22.5 %collective-permute-start.23 = (bf16[192,1728]{1,0:T(8,128)(2,1)S(1)}, bf16[192,1728]{1,0:T(8,128)(2,1)S(1)}, u32[]{:S(2)}, u32[]{:S(2)}) collective-permute-start(bf16[192,1728]{1,0:T(8,128)(2,1)S(1)} %copy-done.74), channel_id=1, source_target_pairs={{0,4},{4,0},{8,12},{12,8},{16,20},{20,16},{24,28},{28,24},{1,5},{5... | collective-permute-start | bytes 1990664 | tf_op jit(solution)/shard_map/ppermute | solution.py:268
  65.8 33.5 %collective-permute-start.24 = (bf16[192,1728]{1,0:T(8,128)(2,1)S(1)}, bf16[192,1728]{1,0:T(8,128)(2,1)}, u32[]{:S(2)}, u32[]{:S(2)}) collective-permute-start(bf16[192,1728]{1,0:T(8,128)(2,1)S(1)} %copy-done.74), channel_id=1, source_target_pairs={{0,8},{4,12},{8,16},{12,20},{16,24},{20,28},{24,0},{28,4},{1,9},{5... | collective-permute-start | bytes 1990664 | tf_op jit(solution)/shard_map/ppermute | solution.py:271
  68.2 41.1 %collective-permute-start.7 = (bf16[256,1536]{1,0:T(8,128)(2,1)S(1)}, bf16[256,1536]{1,0:T(8,128)(2,1)S(1)}, u32[]{:S(2)}, u32[]{:S(2)}) collective-permute-start(bf16[256,1536]{1,0:T(8,128)(2,1)S(1)} %copy-done.31), channel_id=1, source_target_pairs={{0,1},{1,0},{2,3},{3,2},{4,5},{5,4},{6,7},{7,6},{8,9},{9,8},{10,11... | collective-permute-start | bytes 2359304 | tf_op jit(solution)/shard_map/ppermute | solution.py:310
  71.7 41.1 %collective-permute-start.8 = (bf16[256,1536]{1,0:T(8,128)(2,1)S(1)}, bf16[256,1536]{1,0:T(8,128)(2,1)S(1)}, u32[]{:S(2)}, u32[]{:S(2)}) collective-permute-start(bf16[256,1536]{1,0:T(8,128)(2,1)S(1)} %copy-done.31), channel_id=1, source_target_pairs={{0,2},{1,3},{2,0},{3,1},{4,6},{5,7},{6,4},{7,5},{8,10},{9,11},{10,... | collective-permute-start | bytes 2359304 | tf_op jit(solution)/shard_map/ppermute | solution.py:310
  85.7 27.2 %collective-permute-start.9 = (bf16[256,1536]{1,0:T(8,128)(2,1)S(1)}, bf16[256,1536]{1,0:T(8,128)(2,1)S(1)}, u32[]{:S(2)}, u32[]{:S(2)}) collective-permute-start(bf16[256,1536]{1,0:T(8,128)(2,1)S(1)} %copy-done.31), channel_id=1, source_target_pairs={{0,3},{1,2},{2,1},{3,0},{4,7},{5,6},{6,5},{7,4},{8,11},{9,10},{10,... | collective-permute-start | bytes 2359304 | tf_op jit(solution)/shard_map/ppermute | solution.py:310
  101.1 22.9 %collective-permute-start.47 = (bf16[256,1536]{0,1:T(8,128)(2,1)}, bf16[256,1536]{0,1:T(8,128)(2,1)S(1)}, u32[]{:S(2)}, u32[]{:S(2)}) collective-permute-start(bf16[256,1536]{0,1:T(8,128)(2,1)} %copy.46), channel_id=1, source_target_pairs={{0,1},{1,0},{2,3},{3,2},{4,5},{5,4},{6,7},{7,6},{8,9},{9,8},{10,11... | collective-permute-start | bytes 2359304 | tf_op jit(solution)/shard_map/ppermute | solution.py:310
  107.8 34.5 %collective-permute-start.48 = (bf16[256,1536]{0,1:T(8,128)(2,1)}, bf16[256,1536]{0,1:T(8,128)(2,1)}, u32[]{:S(2)}, u32[]{:S(2)}) collective-permute-start(bf16[256,1536]{0,1:T(8,128)(2,1)} %copy.46), channel_id=1, source_target_pairs={{0,2},{1,3},{2,0},{3,1},{4,6},{5,7},{6,4},{7,5},{8,10},{9,11},{10,... | collective-permute-start | bytes 2359304 | tf_op jit(solution)/shard_map/ppermute | solution.py:310
  109.3 33.5 %collective-permute-start.49 = (bf16[256,1536]{0,1:T(8,128)(2,1)}, bf16[256,1536]{0,1:T(8,128)(2,1)}, u32[]{:S(2)}, u32[]{:S(2)}) collective-permute-start(bf16[256,1536]{0,1:T(8,128)(2,1)} %copy.46), channel_id=1, source_target_pairs={{0,3},{1,2},{2,1},{3,0},{4,7},{5,6},{6,5},{7,4},{8,11},{9,10},{10,... | collective-permute-start | bytes 2359304 | tf_op jit(solution)/shard_map/ppermute | solution.py:310
  112.9 64.0 %collective-permute-start.32 = (bf16[192,1728]{1,0:T(8,128)(2,1)}, bf16[192,1728]{1,0:T(8,128)(2,1)}, u32[]{:S(2)}, u32[]{:S(2)}) collective-permute-start(bf16[192,1728]{1,0:T(8,128)(2,1)} %collective-permute-done.31), channel_id=1, source_target_pairs={{0,4},{4,0},{8,12},{12,8},{16,20},{20,16},{24,28},{28,24},{1,5},{5... | collective-permute-start | bytes 1990664 | tf_op jit(solution)/shard_map/ppermute | solution.py:268
  113.0 69.9 %collective-permute-start.33 = (bf16[192,1728]{1,0:T(8,128)(2,1)}, bf16[192,1728]{1,0:T(8,128)(2,1)}, u32[]{:S(2)}, u32[]{:S(2)}) collective-permute-start(bf16[192,1728]{1,0:T(8,128)(2,1)} %collective-permute-done.31), channel_id=1, source_target_pairs={{0,8},{4,12},{8,16},{12,20},{16,24},{20,28},{24,0},{28,4},{1,9},{5... | collective-permute-start | bytes 1990664 | tf_op jit(solution)/shard_map/ppermute | solution.py:271
  124.0 61.5 %collective-permute-start.39 = (bf16[192,1728]{1,0:T(8,128)(2,1)}, bf16[192,1728]{1,0:T(8,128)(2,1)}, u32[]{:S(2)}, u32[]{:S(2)}) collective-permute-start(bf16[192,1728]{1,0:T(8,128)(2,1)} %copy-done.75), channel_id=1, source_target_pairs={{0,4},{4,0},{8,12},{12,8},{16,20},{20,16},{24,28},{28,24},{1,5},{5... | collective-permute-start | bytes 1990664 | tf_op jit(solution)/shard_map/ppermute | solution.py:268
  142.3 44.7 %collective-permute-start.40 = (bf16[192,1728]{1,0:T(8,128)(2,1)}, bf16[192,1728]{1,0:T(8,128)(2,1)}, u32[]{:S(2)}, u32[]{:S(2)}) collective-permute-start(bf16[192,1728]{1,0:T(8,128)(2,1)} %copy-done.75), channel_id=1, source_target_pairs={{0,8},{4,12},{8,16},{12,20},{16,24},{20,28},{24,0},{28,4},{1,9},{5... | collective-permute-start | bytes 1990664 | tf_op jit(solution)/shard_map/ppermute | solution.py:271
  149.6 43.0 %collective-permute-start.25 = (bf16[192,1728]{1,0:T(8,128)(2,1)}, bf16[192,1728]{1,0:T(8,128)(2,1)}, u32[]{:S(2)}, u32[]{:S(2)}) collective-permute-start(bf16[192,1728]{1,0:T(8,128)(2,1)} %collective-permute-done.24), channel_id=1, source_target_pairs={{0,4},{4,0},{8,12},{12,8},{16,20},{20,16},{24,28},{28,24},{1,5},{5... | collective-permute-start | bytes 1990664 | tf_op jit(solution)/shard_map/ppermute | solution.py:268
  176.8 20.3 %collective-permute-start.26 = (bf16[192,1728]{1,0:T(8,128)(2,1)}, bf16[192,1728]{1,0:T(8,128)(2,1)S(1)}, u32[]{:S(2)}, u32[]{:S(2)}) collective-permute-start(bf16[192,1728]{1,0:T(8,128)(2,1)} %collective-permute-done.24), channel_id=1, source_target_pairs={{0,8},{4,12},{8,16},{12,20},{16,24},{20,28},{24,0},{28,4},{1,9},{5... | collective-permute-start | bytes 1990664 | tf_op jit(solution)/shard_map/ppermute | solution.py:271
  182.9 20.4 %collective-permute-start.17 = (bf16[256,1536]{1,0:T(8,128)(2,1)S(1)}, bf16[256,1536]{1,0:T(8,128)(2,1)S(1)}, u32[]{:S(2)}, u32[]{:S(2)}) collective-permute-start(bf16[256,1536]{1,0:T(8,128)(2,1)S(1)} %convolution_convert_fusion.8), channel_id=1, source_target_pairs={{0,1},{1,0},{2,3},{3,2},{4,5},{5,4},{6,7},{7,6},{8,9},{9,8},{10,11... | collective-permute-start | bytes 2359304 | tf_op jit(solution)/shard_map/ppermute | solution.py:316
  185.5 36.4 %collective-permute-start.18 = (bf16[256,1536]{1,0:T(8,128)(2,1)S(1)}, bf16[256,1536]{1,0:T(8,128)(2,1)S(1)}, u32[]{:S(2)}, u32[]{:S(2)}) collective-permute-start(bf16[256,1536]{1,0:T(8,128)(2,1)S(1)} %convolution_convert_fusion.7), channel_id=1, source_target_pairs={{0,2},{1,3},{2,0},{3,1},{4,6},{5,7},{6,4},{7,5},{8,10},{9,11},{10,... | collective-permute-start | bytes 2359304 | tf_op jit(solution)/shard_map/ppermute | solution.py:316
  187.1 35.5 %collective-permute-start.19 = (bf16[256,1536]{1,0:T(8,128)(2,1)S(1)}, bf16[256,1536]{1,0:T(8,128)(2,1)S(1)}, u32[]{:S(2)}, u32[]{:S(2)}) collective-permute-start(bf16[256,1536]{1,0:T(8,128)(2,1)S(1)} %convolution_convert_fusion.6), channel_id=1, source_target_pairs={{0,3},{1,2},{2,1},{3,0},{4,7},{5,6},{6,5},{7,4},{8,11},{9,10},{10,... | collective-permute-start | bytes 2359304 | tf_op jit(solution)/shard_map/ppermute | solution.py:316
  192.6 31.1 %collective-permute-start.34 = (bf16[192,1728]{1,0:T(8,128)(2,1)}, bf16[192,1728]{1,0:T(8,128)(2,1)S(1)}, u32[]{:S(2)}, u32[]{:S(2)}) collective-permute-start(bf16[192,1728]{1,0:T(8,128)(2,1)} %collective-permute-done.33), channel_id=1, source_target_pairs={{0,4},{4,0},{8,12},{12,8},{16,20},{20,16},{24,28},{28,24},{1,5},{5... | collective-permute-start | bytes 1990664 | tf_op jit(solution)/shard_map/ppermute | solution.py:268
  197.1 29.0 %collective-permute-start.35 = (bf16[192,1728]{1,0:T(8,128)(2,1)}, bf16[192,1728]{1,0:T(8,128)(2,1)}, u32[]{:S(2)}, u32[]{:S(2)}) collective-permute-start(bf16[192,1728]{1,0:T(8,128)(2,1)} %collective-permute-done.33), channel_id=1, source_target_pairs={{0,8},{4,12},{8,16},{12,20},{16,24},{20,28},{24,0},{28,4},{1,9},{5... | collective-permute-start | bytes 1990664 | tf_op jit(solution)/shard_map/ppermute | solution.py:271
  203.3 25.4 %collective-permute-start.41 = (bf16[192,1728]{1,0:T(8,128)(2,1)}, bf16[192,1728]{1,0:T(8,128)(2,1)S(1)}, u32[]{:S(2)}, u32[]{:S(2)}) collective-permute-start(bf16[192,1728]{1,0:T(8,128)(2,1)} %collective-permute-done.40), channel_id=1, source_target_pairs={{0,4},{4,0},{8,12},{12,8},{16,20},{20,16},{24,28},{28,24},{1,5},{5... | collective-permute-start | bytes 1990664 | tf_op jit(solution)/shard_map/ppermute | solution.py:268
  221.9 20.5 %collective-permute-start.42 = (bf16[192,1728]{1,0:T(8,128)(2,1)}, bf16[192,1728]{1,0:T(8,128)(2,1)}, u32[]{:S(2)}, u32[]{:S(2)}) collective-permute-start(bf16[192,1728]{1,0:T(8,128)(2,1)} %collective-permute-done.40), channel_id=1, source_target_pairs={{0,8},{4,12},{8,16},{12,20},{16,24},{20,28},{24,0},{28,4},{1,9},{5... | collective-permute-start | bytes 1990664 | tf_op jit(solution)/shard_map/ppermute | solution.py:271
  222.5 25.3 %collective-permute-start.27 = (bf16[192,1728]{1,0:T(8,128)(2,1)S(1)}, bf16[192,1728]{1,0:T(8,128)(2,1)S(1)}, u32[]{:S(2)}, u32[]{:S(2)}) collective-permute-start(bf16[192,1728]{1,0:T(8,128)(2,1)S(1)} %collective-permute-done.26), channel_id=1, source_target_pairs={{0,4},{4,0},{8,12},{12,8},{16,20},{20,16},{24,28},{28,24},{1,5},{5... | collective-permute-start | bytes 1990664 | tf_op jit(solution)/shard_map/ppermute | solution.py:268
  223.7 31.6 %collective-permute-start.28 = (bf16[192,1728]{1,0:T(8,128)(2,1)S(1)}, bf16[192,1728]{1,0:T(8,128)(2,1)}, u32[]{:S(2)}, u32[]{:S(2)}) collective-permute-start(bf16[192,1728]{1,0:T(8,128)(2,1)S(1)} %collective-permute-done.26), channel_id=1, source_target_pairs={{0,8},{4,12},{8,16},{12,20},{16,24},{20,28},{24,0},{28,4},{1,9},{5... | collective-permute-start | bytes 1990664 | tf_op jit(solution)/shard_map/ppermute | solution.py:271
  226.1 31.3 %collective-permute-start.20 = (bf16[256,1536]{1,0:T(8,128)(2,1)S(1)}, bf16[256,1536]{1,0:T(8,128)(2,1)S(1)}, u32[]{:S(2)}, u32[]{:S(2)}) collective-permute-start(bf16[256,1536]{1,0:T(8,128)(2,1)S(1)} %multiply_convert_fusion.3), channel_id=1, source_target_pairs={{0,1},{1,0},{2,3},{3,2},{4,5},{5,4},{6,7},{7,6},{8,9},{9,8},{10,11... | collective-permute-start | bytes 2359304 | tf_op jit(solution)/shard_map/ppermute | solution.py:310
  228.7 36.5 %collective-permute-start.21 = (bf16[256,1536]{1,0:T(8,128)(2,1)S(1)}, bf16[256,1536]{1,0:T(8,128)(2,1)S(1)}, u32[]{:S(2)}, u32[]{:S(2)}) collective-permute-start(bf16[256,1536]{1,0:T(8,128)(2,1)S(1)} %multiply_convert_fusion.3), channel_id=1, source_target_pairs={{0,2},{1,3},{2,0},{3,1},{4,6},{5,7},{6,4},{7,5},{8,10},{9,11},{10,... | collective-permute-start | bytes 2359304 | tf_op jit(solution)/shard_map/ppermute | solution.py:310
  242.4 22.8 %collective-permute-start.22 = (bf16[256,1536]{1,0:T(8,128)(2,1)S(1)}, bf16[256,1536]{1,0:T(8,128)(2,1)S(1)}, u32[]{:S(2)}, u32[]{:S(2)}) collective-permute-start(bf16[256,1536]{1,0:T(8,128)(2,1)S(1)} %multiply_convert_fusion.3), channel_id=1, source_target_pairs={{0,3},{1,2},{2,1},{3,0},{4,7},{5,6},{6,5},{7,4},{8,11},{9,10},{10,... | collective-permute-start | bytes 2359304 | tf_op jit(solution)/shard_map/ppermute | solution.py:310
  247.8 29.6 %collective-permute-start.36 = (bf16[192,1728]{1,0:T(8,128)(2,1)}, bf16[192,1728]{1,0:T(8,128)(2,1)}, u32[]{:S(2)}, u32[]{:S(2)}) collective-permute-start(bf16[192,1728]{1,0:T(8,128)(2,1)} %collective-permute-done.35), channel_id=1, source_target_pairs={{0,4},{4,0},{8,12},{12,8},{16,20},{20,16},{24,28},{28,24},{1,5},{5... | collective-permute-start | bytes 1990664 | tf_op jit(solution)/shard_map/ppermute | solution.py:268
  255.3 36.5 %collective-permute-start.43 = (bf16[192,1728]{1,0:T(8,128)(2,1)}, bf16[192,1728]{1,0:T(8,128)(2,1)}, u32[]{:S(2)}, u32[]{:S(2)}) collective-permute-start(bf16[192,1728]{1,0:T(8,128)(2,1)} %collective-permute-done.42), channel_id=1, source_target_pairs={{0,4},{4,0},{8,12},{12,8},{16,20},{20,16},{24,28},{28,24},{1,5},{5... | collective-permute-start | bytes 1990664 | tf_op jit(solution)/shard_map/ppermute | solution.py:268
  257.4 47.4 %collective-permute-start.29 = (bf16[192,1728]{1,0:T(8,128)(2,1)}, bf16[192,1728]{1,0:T(8,128)(2,1)}, u32[]{:S(2)}, u32[]{:S(2)}) collective-permute-start(bf16[192,1728]{1,0:T(8,128)(2,1)} %collective-permute-done.28), channel_id=1, source_target_pairs={{0,4},{4,0},{8,12},{12,8},{16,20},{20,16},{24,28},{28,24},{1,5},{5... | collective-permute-start | bytes 1990664 | tf_op jit(solution)/shard_map/ppermute | solution.py:268
  360.2 22.9 %collective-permute-start.50 = (bf16[256,1536]{1,0:T(8,128)(2,1)S(1)}, bf16[256,1536]{1,0:T(8,128)(2,1)S(1)}, u32[]{:S(2)}, u32[]{:S(2)}) collective-permute-start(bf16[256,1536]{1,0:T(8,128)(2,1)S(1)} %fusion.12), channel_id=1, source_target_pairs={{0,1},{1,0},{2,3},{3,2},{4,5},{5,4},{6,7},{7,6},{8,9},{9,8},{10,11... | collective-permute-start | bytes 2359304 | tf_op jit(solution)/shard_map/ppermute | solution.py:316
  365.7 35.2 %collective-permute-start.51 = (bf16[256,1536]{1,0:T(8,128)(2,1)S(1)}, bf16[256,1536]{1,0:T(8,128)(2,1)S(1)}, u32[]{:S(2)}, u32[]{:S(2)}) collective-permute-start(bf16[256,1536]{1,0:T(8,128)(2,1)S(1)} %fusion.13), channel_id=1, source_target_pairs={{0,2},{1,3},{2,0},{3,1},{4,6},{5,7},{6,4},{7,5},{8,10},{9,11},{10,... | collective-permute-start | bytes 2359304 | tf_op jit(solution)/shard_map/ppermute | solution.py:316
  371.5 29.3 %collective-permute-start.52 = (bf16[256,1536]{1,0:T(8,128)(2,1)S(1)}, bf16[256,1536]{1,0:T(8,128)(2,1)S(1)}, u32[]{:S(2)}, u32[]{:S(2)}) collective-permute-start(bf16[256,1536]{1,0:T(8,128)(2,1)S(1)} %fusion.14), channel_id=1, source_target_pairs={{0,3},{1,2},{2,1},{3,0},{4,7},{5,6},{6,5},{7,4},{8,11},{9,10},{10,... | collective-permute-start | bytes 2359304 | tf_op jit(solution)/shard_map/ppermute | solution.py:316
  377.5 194.1 %collective-permute-start.80 = (bf16[768,1728]{0,1:T(8,128)(2,1)}, bf16[768,1728]{0,1:T(8,128)(2,1)}, u32[]{:S(2)}, u32[]{:S(2)}) collective-permute-start(bf16[768,1728]{0,1:T(8,128)(2,1)} %convolution_convert_fusion), channel_id=1, source_target_pairs={{0,4},{4,0},{8,12},{12,8},{16,20},{20,16},{24,28},{28,24},{1,5},{5... | collective-permute-start | bytes 7962632 | tf_op jit(solution)/shard_map/ppermute | solution.py:268
  377.5 118.3 %collective-permute-start.44 = (bf16[256,1536]{1,0:T(8,128)(2,1)}, bf16[256,1536]{1,0:T(8,128)(2,1)}, u32[]{:S(2)}, u32[]{:S(2)}) collective-permute-start(bf16[256,1536]{1,0:T(8,128)(2,1)} %convolution_convert_fusion.11), channel_id=1, source_target_pairs={{0,1},{1,0},{2,3},{3,2},{4,5},{5,4},{6,7},{7,6},{8,9},{9,8},{10,11... | collective-permute-start | bytes 2359304 | tf_op jit(solution)/shard_map/ppermute | solution.py:316
  407.0 24.4 %collective-permute-start.53 = (bf16[256,1536]{1,0:T(8,128)(2,1)S(1)}, bf16[256,1536]{1,0:T(8,128)(2,1)S(1)}, u32[]{:S(2)}, u32[]{:S(2)}) collective-permute-start(bf16[256,1536]{1,0:T(8,128)(2,1)S(1)} %fusion.68), channel_id=1, source_target_pairs={{0,1},{1,0},{2,3},{3,2},{4,5},{5,4},{6,7},{7,6},{8,9},{9,8},{10,11... | collective-permute-start | bytes 2359304 | tf_op jit(solution)/shard_map/ppermute | solution.py:310
  408.2 24.7 %collective-permute-start.54 = (bf16[256,1536]{1,0:T(8,128)(2,1)S(1)}, bf16[256,1536]{1,0:T(8,128)(2,1)S(1)}, u32[]{:S(2)}, u32[]{:S(2)}) collective-permute-start(bf16[256,1536]{1,0:T(8,128)(2,1)S(1)} %fusion.68), channel_id=1, source_target_pairs={{0,2},{1,3},{2,0},{3,1},{4,6},{5,7},{6,4},{7,5},{8,10},{9,11},{10,... | collective-permute-start | bytes 2359304 | tf_op jit(solution)/shard_map/ppermute | solution.py:310
  409.7 39.6 %collective-permute-start.55 = (bf16[256,1536]{1,0:T(8,128)(2,1)S(1)}, bf16[256,1536]{1,0:T(8,128)(2,1)S(1)}, u32[]{:S(2)}, u32[]{:S(2)}) collective-permute-start(bf16[256,1536]{1,0:T(8,128)(2,1)S(1)} %fusion.68), channel_id=1, source_target_pairs={{0,3},{1,2},{2,1},{3,0},{4,7},{5,6},{6,5},{7,4},{8,11},{9,10},{10,... | collective-permute-start | bytes 2359304 | tf_op jit(solution)/shard_map/ppermute | solution.py:310
  431.4 65.7 %collective-permute-start.45 = (bf16[256,1536]{1,0:T(8,128)(2,1)}, bf16[256,1536]{1,0:T(8,128)(2,1)}, u32[]{:S(2)}, u32[]{:S(2)}) collective-permute-start(bf16[256,1536]{1,0:T(8,128)(2,1)} %convolution_convert_fusion.10), channel_id=1, source_target_pairs={{0,2},{1,3},{2,0},{3,1},{4,6},{5,7},{6,4},{7,5},{8,10},{9,11},{10,... | collective-permute-start | bytes 2359304 | tf_op jit(solution)/shard_map/ppermute | solution.py:316
  432.9 64.7 %collective-permute-start.46 = (bf16[256,1536]{1,0:T(8,128)(2,1)}, bf16[256,1536]{1,0:T(8,128)(2,1)}, u32[]{:S(2)}, u32[]{:S(2)}) collective-permute-start(bf16[256,1536]{1,0:T(8,128)(2,1)} %convolution_convert_fusion.9), channel_id=1, source_target_pairs={{0,3},{1,2},{2,1},{3,0},{4,7},{5,6},{6,5},{7,4},{8,11},{9,10},{10,... | collective-permute-start | bytes 2359304 | tf_op jit(solution)/shard_map/ppermute | solution.py:316
  461.8 44.1 %collective-permute-start.68 = (bf16[768,384]{1,0:T(8,128)(2,1)}, bf16[768,384]{1,0:T(8,128)(2,1)}, u32[]{:S(2)}, u32[]{:S(2)}) collective-permute-start(bf16[768,384]{1,0:T(8,128)(2,1)} %convolution_convert_fusion.13), channel_id=1, source_target_pairs={{0,4},{4,0},{8,12},{12,8},{16,20},{20,16},{24,28},{28,24},{1,5},{5... | collective-permute-start | bytes 1769480 | tf_op jit(solution)/shard_map/ppermute | solution.py:268
  495.8 20.5 %collective-permute-start.56 = (bf16[256,1536]{1,0:T(8,128)(2,1)S(1)}, bf16[256,1536]{1,0:T(8,128)(2,1)S(1)}, u32[]{:S(2)}, u32[]{:S(2)}) collective-permute-start(bf16[256,1536]{1,0:T(8,128)(2,1)S(1)} %convolution_convert_fusion.5), channel_id=1, source_target_pairs={{0,1},{1,0},{2,3},{3,2},{4,5},{5,4},{6,7},{7,6},{8,9},{9,8},{10,11... | collective-permute-start | bytes 2359304 | tf_op jit(solution)/shard_map/ppermute | solution.py:316
  497.1 36.0 %collective-permute-start.57 = (bf16[256,1536]{1,0:T(8,128)(2,1)S(1)}, bf16[256,1536]{1,0:T(8,128)(2,1)S(1)}, u32[]{:S(2)}, u32[]{:S(2)}) collective-permute-start(bf16[256,1536]{1,0:T(8,128)(2,1)S(1)} %convolution_convert_fusion.4), channel_id=1, source_target_pairs={{0,2},{1,3},{2,0},{3,1},{4,6},{5,7},{6,4},{7,5},{8,10},{9,11},{10,... | collective-permute-start | bytes 2359304 | tf_op jit(solution)/shard_map/ppermute | solution.py:316
  497.6 35.5 %collective-permute-start.58 = (bf16[256,1536]{1,0:T(8,128)(2,1)S(1)}, bf16[256,1536]{1,0:T(8,128)(2,1)S(1)}, u32[]{:S(2)}, u32[]{:S(2)}) collective-permute-start(bf16[256,1536]{1,0:T(8,128)(2,1)S(1)} %convolution_convert_fusion.3), channel_id=1, source_target_pairs={{0,3},{1,2},{2,1},{3,0},{4,7},{5,6},{6,5},{7,4},{8,11},{9,10},{10,... | collective-permute-start | bytes 2359304 | tf_op jit(solution)/shard_map/ppermute | solution.py:316
  505.9 77.4 %collective-permute-start.76 = (bf16[768,1728]{0,1:T(8,128)(2,1)}, bf16[768,1728]{0,1:T(8,128)(2,1)}, u32[]{:S(2)}, u32[]{:S(2)}) collective-permute-start(bf16[768,1728]{0,1:T(8,128)(2,1)} %convolution_convert_fusion.1), channel_id=1, source_target_pairs={{0,4},{4,0},{8,12},{12,8},{16,20},{20,16},{24,28},{28,24},{1,5},{5... | collective-permute-start | bytes 7962632 | tf_op jit(solution)/shard_map/ppermute | solution.py:268
  516.3 89.4 %collective-permute-start.72 = (bf16[768,1728]{0,1:T(8,128)(2,1)}, bf16[768,1728]{0,1:T(8,128)(2,1)}, u32[]{:S(2)}, u32[]{:S(2)}) collective-permute-start(bf16[768,1728]{0,1:T(8,128)(2,1)} %convolution_convert_fusion.2), channel_id=1, source_target_pairs={{0,4},{4,0},{8,12},{12,8},{16,20},{20,16},{24,28},{28,24},{1,5},{5... | collective-permute-start | bytes 7962632 | tf_op jit(solution)/shard_map/ppermute | solution.py:268
  581.4 45.0 %collective-permute-start.81 = (bf16[192,1728]{1,0:T(8,128)(2,1)}, bf16[192,1728]{1,0:T(8,128)(2,1)S(1)}, u32[]{:S(2)}, u32[]{:S(2)}) collective-permute-start(bf16[192,1728]{1,0:T(8,128)(2,1)} %dynamic-slice_bitcast_fusion), channel_id=1, source_target_pairs={{0,8},{4,12},{8,16},{12,20},{16,24},{20,28},{24,0},{28,4},{1,9},{5... | collective-permute-start | bytes 1990664 | tf_op jit(solution)/shard_map/ppermute | solution.py:271
  583.3 20.7 %collective-permute-start.66 = (bf16[192,640]{1,0:T(8,128)(2,1)}, bf16[192,640]{1,0:T(8,128)(2,1)}, u32[]{:S(2)}, u32[]{:S(2)}) collective-permute-start(bf16[192,640]{1,0:T(8,128)(2,1)} %fusion.52), channel_id=1, source_target_pairs={{0,8},{4,12},{8,16},{12,20},{16,24},{20,28},{24,0},{28,4},{1,9},{5... | collective-permute-start | bytes 737288 | tf_op jit(solution)/shard_map/ppermute | solution.py:271
  597.3 29.4 %collective-permute-start.77 = (bf16[192,1728]{1,0:T(8,128)(2,1)}, bf16[192,1728]{1,0:T(8,128)(2,1)}, u32[]{:S(2)}, u32[]{:S(2)}) collective-permute-start(bf16[192,1728]{1,0:T(8,128)(2,1)} %dynamic-slice_bitcast_fusion.1), channel_id=1, source_target_pairs={{0,8},{4,12},{8,16},{12,20},{16,24},{20,28},{24,0},{28,4},{1,9},{5... | collective-permute-start | bytes 1990664 | tf_op jit(solution)/shard_map/ppermute | solution.py:271
  618.9 20.2 %collective-permute-start.73 = (bf16[192,1728]{1,0:T(8,128)(2,1)S(1)}, bf16[192,1728]{1,0:T(8,128)(2,1)S(1)}, u32[]{:S(2)}, u32[]{:S(2)}) collective-permute-start(bf16[192,1728]{1,0:T(8,128)(2,1)S(1)} %dynamic-slice_bitcast_fusion.2), channel_id=1, source_target_pairs={{0,8},{4,12},{8,16},{12,20},{16,24},{20,28},{24,0},{28,4},{1,9},{5... | collective-permute-start | bytes 1990664 | tf_op jit(solution)/shard_map/ppermute | solution.py:271
  626.6 27.2 %collective-permute-start.82 = (bf16[192,1728]{1,0:T(8,128)(2,1)S(1)}, bf16[192,1728]{1,0:T(8,128)(2,1)S(1)}, u32[]{:S(2)}, u32[]{:S(2)}) collective-permute-start(bf16[192,1728]{1,0:T(8,128)(2,1)S(1)} %fusion.29), channel_id=1, source_target_pairs={{0,8},{4,12},{8,16},{12,20},{16,24},{20,28},{24,0},{28,4},{1,9},{5... | collective-permute-start | bytes 1990664 | tf_op jit(solution)/shard_map/ppermute | solution.py:271
  628.1 40.5 %collective-permute-start.78 = (bf16[192,1728]{1,0:T(8,128)(2,1)S(1)}, bf16[192,1728]{1,0:T(8,128)(2,1)S(1)}, u32[]{:S(2)}, u32[]{:S(2)}) collective-permute-start(bf16[192,1728]{1,0:T(8,128)(2,1)S(1)} %fusion.31), channel_id=1, source_target_pairs={{0,8},{4,12},{8,16},{12,20},{16,24},{20,28},{24,0},{28,4},{1,9},{5... | collective-permute-start | bytes 1990664 | tf_op jit(solution)/shard_map/ppermute | solution.py:271
  639.3 44.1 %collective-permute-start.74 = (bf16[192,1728]{1,0:T(8,128)(2,1)S(1)}, bf16[192,1728]{1,0:T(8,128)(2,1)S(1)}, u32[]{:S(2)}, u32[]{:S(2)}) collective-permute-start(bf16[192,1728]{1,0:T(8,128)(2,1)S(1)} %fusion.33), channel_id=1, source_target_pairs={{0,8},{4,12},{8,16},{12,20},{16,24},{20,28},{24,0},{28,4},{1,9},{5... | collective-permute-start | bytes 1990664 | tf_op jit(solution)/shard_map/ppermute | solution.py:271
  654.1 44.1 %collective-permute-start.83 = (bf16[192,1728]{1,0:T(8,128)(2,1)S(1)}, bf16[192,1728]{1,0:T(8,128)(2,1)S(1)}, u32[]{:S(2)}, u32[]{:S(2)}) collective-permute-start(bf16[192,1728]{1,0:T(8,128)(2,1)S(1)} %fusion.28), channel_id=1, source_target_pairs={{0,8},{4,12},{8,16},{12,20},{16,24},{20,28},{24,0},{28,4},{1,9},{5... | collective-permute-start | bytes 1990664 | tf_op jit(solution)/shard_map/ppermute | solution.py:271
  668.8 44.1 %collective-permute-start.79 = (bf16[192,1728]{1,0:T(8,128)(2,1)S(1)}, bf16[192,1728]{1,0:T(8,128)(2,1)S(1)}, u32[]{:S(2)}, u32[]{:S(2)}) collective-permute-start(bf16[192,1728]{1,0:T(8,128)(2,1)S(1)} %fusion.30), channel_id=1, source_target_pairs={{0,8},{4,12},{8,16},{12,20},{16,24},{20,28},{24,0},{28,4},{1,9},{5... | collective-permute-start | bytes 1990664 | tf_op jit(solution)/shard_map/ppermute | solution.py:271
  683.6 40.6 %collective-permute-start.75 = (bf16[192,1728]{1,0:T(8,128)(2,1)S(1)}, bf16[192,1728]{1,0:T(8,128)(2,1)S(1)}, u32[]{:S(2)}, u32[]{:S(2)}) collective-permute-start(bf16[192,1728]{1,0:T(8,128)(2,1)S(1)} %fusion.32), channel_id=1, source_target_pairs={{0,8},{4,12},{8,16},{12,20},{16,24},{20,28},{24,0},{28,4},{1,9},{5... | collective-permute-start | bytes 1990664 | tf_op jit(solution)/shard_map/ppermute | solution.py:271
  (118 other events, 1272.1 us)

commit v2 on v1

--- a/solution.py
+++ b/solution.py
@@ -17,6 +17,7 @@
 F32 = jnp.float32
 LOW = jnp.bfloat16
 SCALE = HEAD_SIZE ** (-0.5)
+FREE = pl.CostEstimate(flops=0, bytes_accessed=0, transcendentals=0)
 
 
 def norm_rows(values_in, gain):
@@ -187,11 +188,7 @@
             jax.ShapeDtypeStruct((ranks, heads, GROUP * rows), F32),
         ],
         compiler_params=pltpu.CompilerParams(vmem_limit_bytes=48 * 2**20),
-        cost_estimate=pl.CostEstimate(
-            flops=8 * length * length * heads * GROUP * HEAD_SIZE,
-            bytes_accessed=8 * length * heads * GROUP * HEAD_SIZE,
-            transcendentals=length * length * heads * GROUP,
-        ),
+        cost_estimate=FREE,
         name="attend",
     )(me, queries, keys, values, bounds)
 
@@ -214,23 +211,451 @@
             jax.ShapeDtypeStruct(keys.shape, F32),
         ],
         compiler_params=pltpu.CompilerParams(vmem_limit_bytes=48 * 2**20),
-        cost_estimate=pl.CostEstimate(
-            flops=20 * length * length * heads * GROUP * HEAD_SIZE,
-            bytes_accessed=16 * length * heads * GROUP * HEAD_SIZE,
-            transcendentals=length * length * heads * GROUP,
-        ),
+        cost_estimate=FREE,
         name="attend_back",
     )(me, queries, keys, values, bounds, attended, d_attended, lse)
 
 
-def rotate(heads, cosine, sine):
-    half_size = heads.shape[-1] // 2
-    first_half = heads[..., :half_size]
-    second_half = heads[..., half_size:]
-    return jnp.concatenate(
-        [first_half * cosine - second_half * sine, second_half * cosine + first_half * sine],
-        axis=-1,
-    )
+def fold_kernel(ranks, ring, rows, split, core_ref, *refs):
+    blocks, all_ref, outs = refs[:ranks], refs[ranks], refs[ranks + 1 :]
+    core = core_ref[0]
+    turned = outs[-1]
+    depth = turned.shape[0] // (2 * ring)
+    for j in range(ranks):
+        block = blocks[j][...]
+        span = slice(j * rows, (j + 1) * rows)
+        all_ref[span, :] = block
+        if not split:
+            turned[:, span] = block.T
+            continue
+        turned[...] = block.T
+        for i in range(ring):
+            to = slice(i * depth, (i + 1) * depth)
+            for side_ref, side in zip(outs[:2], (1 - core, core)):
+                first = pl.multiple_of((2 * i + side) * depth, 16)
+                side_ref[to, span] = turned[pl.ds(first, depth), :]
+
+
+def fold(core, blocks, ring, split=False):
+    ranks = len(blocks)
+    rows, width = blocks[0].shape
+    length = ranks * rows
+    whole = lambda shape: pl.BlockSpec(shape, lambda i: (0, 0))
+    shapes = [(length, width)] + ([(width // 2, length)] * 2 if split else [(width, length)])
+    return pl.pallas_call(
+        functools.partial(fold_kernel, ranks, ring, rows, split),
+        grid=(1,),
+        in_specs=[pl.BlockSpec(memory_space=pltpu.SMEM)] + [whole((rows, width))] * ranks,
+        out_specs=[whole(shape) for shape in shapes],
+        out_shape=[jax.ShapeDtypeStruct(shape, LOW) for shape in shapes],
+        scratch_shapes=[pltpu.VMEM((width, rows), LOW)] if split else [],
+        compiler_params=pltpu.CompilerParams(vmem_limit_bytes=40 * 2**20),
+        cost_estimate=FREE,
+        name="fold",
+    )(core, *blocks)
+
+
+def place_kernel(ring, depth, at_ref, *refs):
+    blocks = refs[: 2 * ring]
+    full_ref, sems = refs[2 * ring :]
+    stage, core = at_ref[0], at_ref[1]
+    copies = []
+    for hop in range(ring):
+        owner = lax.rem(stage - hop + ring, ring)
+        for half, side in enumerate((core, 1 - core)):
+            first = pl.multiple_of((owner * 2 + side) * depth, 16)
+            copies.append(
+                pltpu.make_async_copy(
+                    blocks[2 * hop + half], full_ref.at[pl.ds(first, depth)], sems.at[2 * hop + half]
+                )
+            )
+    for copy in copies:
+        copy.start()
+    for copy in copies:
+        copy.wait()
+
+
+def place(at, blocks, ring):
+    depth, cols = blocks[0].shape
+    return pl.pallas_call(
+        functools.partial(place_kernel, ring, depth),
+        in_specs=[pl.BlockSpec(memory_space=pltpu.SMEM)]
+        + [pl.BlockSpec(memory_space=pl.ANY)] * (2 * ring),
+        grid=(1,),
+        out_specs=pl.BlockSpec((2 * ring * depth, cols), lambda i: (0, 0)),
+        out_shape=jax.ShapeDtypeStruct((2 * ring * depth, cols), LOW),
+        scratch_shapes=[pltpu.SemaphoreType.DMA((2 * ring,))],
+        compiler_params=pltpu.CompilerParams(vmem_limit_bytes=24 * 2**20),
+        cost_estimate=FREE,
+        name="place",
+    )(at, *blocks)
+
+
+def product_kernel(tiles, left_ref, *refs):
+    for k, right in enumerate(refs[:-1]):
+
+        @pl.when(pl.program_id(0) // tiles == k)
+        def _(right=right):
+            refs[-1][...] = jnp.dot(
+                left_ref[...], right[...], preferred_element_type=F32
+            ).astype(LOW)
+
+
+def product(left, rights):
+    depth, length = left.shape
+    cols = rights[0].shape[1]
+    tile = 256 if cols % 256 == 0 else 128
+    tiles = cols // tile
+    return pl.pallas_call(
+        functools.partial(product_kernel, tiles),
+        grid=(tiles * len(rights),),
+        in_specs=[pl.BlockSpec((depth, length), lambda i: (0, 0))]
+        + [
+            pl.BlockSpec((length, tile), lambda i, k=k: (0, jnp.clip(i - k * tiles, 0, tiles - 1)))
+            for k in range(len(rights))
+        ],
+        out_specs=pl.BlockSpec((depth, tile), lambda i: (0, i)),
+        out_shape=jax.ShapeDtypeStruct((depth, cols * len(rights)), LOW),
+        compiler_params=pltpu.CompilerParams(vmem_limit_bytes=32 * 2**20),
+        cost_estimate=FREE,
+        name="product",
+    )(left, *rights)
+
+
+def attn_products_kernel(*refs):
+    lefts, rights, out_ref = refs[:2], refs[2:4], refs[4]
+    first = 0
+    for left, right in zip(lefts, rights):
+        cols = right.shape[1]
+        out_ref[:, first : first + cols] = jnp.dot(
+            left[...], right[...], preferred_element_type=F32
+        ).astype(LOW)
+        first += cols
+
+
+def attn_products(lefts, rights):
+    depth = lefts[0].shape[0]
+    tiles = 4
+    part = lambda a: pl.BlockSpec((depth // tiles, a.shape[1]), lambda i: (i, 0))
+    whole = lambda a: pl.BlockSpec(a.shape, lambda i: (0, 0))
+    shape = jax.ShapeDtypeStruct((depth, sum(a.shape[1] for a in rights)), LOW)
+    return pl.pallas_call(
+        attn_products_kernel,
+        grid=(tiles,),
+        in_specs=[part(a) for a in lefts] + [whole(a) for a in rights],
+        out_specs=part(shape),
+        out_shape=shape,
+        compiler_params=pltpu.CompilerParams(vmem_limit_bytes=40 * 2**20),
+        cost_estimate=FREE,
+        name="attn_products",
+    )(*lefts, *rights)
+
+
+def back_parts_kernel(rows, count, *refs):
+    total = sum(kdot(refs[k][...], refs[count + k][0], NT) for k in range(count))
+    for j, out_ref in enumerate(refs[2 * count :]):
+        out_ref[...] = total[j * rows : (j + 1) * rows].astype(LOW)
+
+
+def back_parts(lefts, weights, which, ranks):
+    length, cols = lefts[0].shape
+    width = weights.shape[1]
+    rows = length // ranks
+    tile = 256
+    return pl.pallas_call(
+        functools.partial(back_parts_kernel, rows, len(lefts)),
+        grid=(width // tile,),
+        in_specs=[pl.BlockSpec((length, cols), lambda i: (0, 0))] * len(lefts)
+        + [pl.BlockSpec((1, tile, cols), lambda i, k=k: (k, i, 0)) for k in which],
+        out_specs=[pl.BlockSpec((rows, tile), lambda i: (0, i))] * ranks,
+        out_shape=[jax.ShapeDtypeStruct((rows, width), LOW)] * ranks,
+        compiler_params=pltpu.CompilerParams(vmem_limit_bytes=40 * 2**20),
+        cost_estimate=FREE,
+        name="back_parts",
+    )(*lefts, *([weights] * len(which)))
+
+
+def join_kernel(flows, at_ref, *refs):
+    total = refs[flows][...].astype(F32) + refs[flows + 1][...].astype(F32)
+    if flows:
+        total = total + refs[0][...].astype(F32)
+    refs[-1][...] = total.astype(refs[-1].dtype)
+
+
+def join(owner, flow, near, other, ring, dtype):
+    depth, cols = near.shape[0] // ring, near.shape[1]
+    flows = [] if flow is None else [flow]
+    half = cols // 2 if cols % 256 == 0 else cols
+    row = pl.BlockSpec((depth, half), lambda i, at: (0, i))
+    chosen = pl.BlockSpec((depth, half), lambda i, at: (at[0], i))
+    return pl.pallas_call(
+        functools.partial(join_kernel, len(flows)),
+        grid_spec=pltpu.PrefetchScalarGridSpec(
+            num_scalar_prefetch=1,
+            grid=(cols // half,),
+            in_specs=[row] * len(flows) + [chosen] * 2,
+            out_specs=row,
+        ),
+        out_shape=jax.ShapeDtypeStruct((depth, cols), dtype),
+        compiler_params=pltpu.CompilerParams(vmem_limit_bytes=24 * 2**20),
+        cost_estimate=FREE,
+        name="join",
+    )(owner.astype(jnp.int32).reshape(1), *flows, near, other)
+
+
+def sum_kernel(count, base_ref, *refs):
+    total = base_ref[...].astype(F32)
+    arrived = refs[0][...].astype(F32)
+    for ref in refs[1:count]:
+        arrived = arrived + ref[...].astype(F32)
+    total = total + arrived
+    refs[-1 if len(refs) == count + 1 else -2][...] = total
+    if len(refs) > count + 1:
+        gain_ref = refs[count]
+        inverse = lax.rsqrt(jnp.mean(total * total, axis=-1, keepdims=True) + EPSILON)
+        refs[-1][...] = (total * inverse * gain_ref[...]).astype(LOW)
+
+
+def sum_up(base, parts, gain=None):
+    rows, width = base.shape
+    step = rows // 2
+    by_row = pl.BlockSpec((step, width), lambda i: (i, 0))
+    gains = [] if gain is None else [gain.reshape(1, -1)]
+    outs = [jax.ShapeDtypeStruct((rows, width), F32)]
+    if gains:
+        outs.append(jax.ShapeDtypeStruct((rows, width), LOW))
+    return pl.pallas_call(
+        functools.partial(sum_kernel, len(parts)),
+        grid=(2,),
+        in_specs=[by_row] * (1 + len(parts)) + [pl.BlockSpec((1, width), lambda i: (0, 0))] * len(gains),
+        out_specs=[by_row] * len(outs),
+        out_shape=outs,
+        compiler_params=pltpu.CompilerParams(vmem_limit_bytes=24 * 2**20),
+        cost_estimate=FREE,
+        name="sum_up",
+    )(base, *parts, *gains)
+
+
+def norm_back_kernel(count, value_ref, gain_ref, rest_ref, *refs):
+    parts, outs = refs[:count], refs[count:]
+    value = value_ref[...].astype(F32)
+    grad = parts[0][...].astype(F32)
+    for ref in parts[1:]:
+        grad = grad + ref[...].astype(F32)
+    inverse = lax.rsqrt(jnp.mean(value * value, axis=-1, keepdims=True) + EPSILON)
+    hat = value * inverse
+    scaled = grad * gain_ref[...]
+    inner = jnp.mean(scaled * hat, axis=-1, keepdims=True)
+    total = rest_ref[...].astype(F32) + (scaled - hat * inner) * inverse
+    outs[0][...] = total
+    if len(outs) > 1:
+        outs[1][...] = total.astype(LOW)
+
+        @pl.when(pl.program_id(0) == 0)
+        def _():
+            outs[2][...] = jnp.zeros_like(outs[2])
+
+        outs[2][...] += jnp.sum(grad * hat, axis=0, keepdims=True)
+
+
+def norm_back_sum(value, gain, rest, parts, more):
+    rows, width = value.shape
+    step = rows // 2
+    by_row = pl.BlockSpec((step, width), lambda i: (i, 0))
+    fixed = pl.BlockSpec((1, width), lambda i: (0, 0))
+    shapes = [jax.ShapeDtypeStruct((rows, width), F32)]
+    if more:
+        shapes += [jax.ShapeDtypeStruct((rows, width), LOW), jax.ShapeDtypeStruct((1, width), F32)]
+    return pl.pallas_call(
+        functools.partial(norm_back_kernel, len(parts)),
+        grid=(2,),
+        in_specs=[by_row, fixed, by_row] + [by_row] * len(parts),
+        out_specs=[by_row, by_row, fixed][: len(shapes)],
+        out_shape=shapes,
+        compiler_params=pltpu.CompilerParams(vmem_limit_bytes=24 * 2**20),
+        cost_estimate=FREE,
+        name="norm_back_sum",
+    )(value, gain.reshape(1, -1), rest, *parts)
+
+
+def rows_product_kernel(left_ref, right_ref, out_ref):
+    out_ref[...] = jnp.dot(left_ref[...], right_ref[...], preferred_element_type=F32).astype(LOW)
+
+
+def rows_product(left, right, ranks):
+    length, depth = left.shape
+    rows = length // ranks
+    return pl.pallas_call(
+        rows_product_kernel,
+        grid=(ranks,),
+        in_specs=[
+            pl.BlockSpec((rows, depth), lambda i: (i, 0)),
+            pl.BlockSpec(right.shape, lambda i: (0, 0)),
+        ],
+        out_specs=pl.BlockSpec((rows, right.shape[1]), lambda i: (i, 0)),
+        out_shape=jax.ShapeDtypeStruct((length, right.shape[1]), LOW),
+        compiler_params=pltpu.CompilerParams(vmem_limit_bytes=24 * 2**20),
+        cost_estimate=FREE,
+        name="rows_product",
+    )(left, right)
+
+
+def gain_part_kernel(normed_ref, gain_ref, *refs):
+    rows = refs[0].shape[0]
+    total = jnp.zeros(refs[-1].shape, F32)
+    for j, ref in enumerate(refs[:-1]):
+        block = normed_ref[j * rows : (j + 1) * rows, :].astype(F32)
+        total = total + jnp.sum(block * ref[...].astype(F32), axis=0, keepdims=True)
+    refs[-1][...] = total / gain_ref[...]
+
+
+def gain_part(normed, gain, parts):
+    width = normed.shape[1]
+    tile = 512
+    column = lambda a: pl.BlockSpec((a.shape[0], tile), lambda i: (0, i))
+    row = gain.reshape(1, -1)
+    return pl.pallas_call(
+        gain_part_kernel,
+        grid=(width // tile,),
+        in_specs=[column(normed), column(row)] + [column(part) for part in parts],
+        out_specs=column(row),
+        out_shape=jax.ShapeDtypeStruct((1, width), F32),
+        compiler_params=pltpu.CompilerParams(vmem_limit_bytes=24 * 2**20),
+        cost_estimate=FREE,
+        name="gain_part",
+    )(normed, row, *parts)
+
+
+def group_mean(values):
+    width = values.shape[1]
+    part = 2 * HEAD_SIZE
+    left = lax.broadcasted_iota(jnp.int32, (part, part), 0) // HEAD_SIZE
+    right = lax.broadcasted_iota(jnp.int32, (part, part), 1) // HEAD_SIZE
+    spread = jnp.where(left == right, 1.0 / HEAD_SIZE, 0.0).astype(F32)
+    pieces = []
+    for first in range(0, width, part):
+        size = min(part, width - first)
+        pieces.append(
+            lax.dot_general(
+                values[:, first : first + size],
+                spread[:size, :size],
+                NN,
+                precision=lax.Precision.HIGHEST,
+                preferred_element_type=F32,
+            )
+        )
+    return jnp.concatenate(pieces, axis=1) if len(pieces) > 1 else pieces[0]
+
+
+def across(table, width):
+    part = table.shape[1]
+    if width < part:
+        return table[:, :width]
+    return jnp.concatenate([table] * (width // part) + ([table[:, : width % part]] if width % part else []), axis=1)
+
+
+def partner(values):
+    width = values.shape[1]
+    half = HEAD_SIZE // 2
+    lane = lax.broadcasted_iota(jnp.int32, values.shape, 1) % HEAD_SIZE
+    return jnp.where(lane < half, pltpu.roll(values, width - half, 1), pltpu.roll(values, half, 1))
+
+
+def prepare_kernel(q_cols, kv_cols, x_ref, w_ref, cos_ref, sin_ref, gain_ref, q_ref, k_ref, v_ref, raw_ref):
+    product = jnp.dot(x_ref[...], w_ref[...], preferred_element_type=F32)
+    for first, cols, to in ((0, q_cols, q_ref), (q_cols, kv_cols, k_ref)):
+        raw = product[:, first : first + cols]
+        scaled = raw * lax.rsqrt(group_mean(raw * raw) + EPSILON) * gain_ref[:, first : first + cols]
+        cos = across(cos_ref[...], cols)
+        sin = across(sin_ref[...], cols)
+        to[...] = (scaled * cos + partner(scaled) * sin).astype(LOW)
+        raw_ref[:, first : first + cols] = raw
+    v_ref[...] = product[:, q_cols + kv_cols :].astype(LOW)
+
+
+def prepare(normed, weight, cosine, sine, gains, q_cols, kv_cols, ranks):
+    length, width = normed.shape
+    rows = length // ranks
+    at_row = lambda i: (i, 0)
+    fixed = lambda i: (0, 0)
+    return pl.pallas_call(
+        functools.partial(prepare_kernel, q_cols, kv_cols),
+        grid=(ranks,),
+        in_specs=[
+            pl.BlockSpec((rows, width), at_row),
+            pl.BlockSpec(weight.shape, fixed),
+            pl.BlockSpec((rows, cosine.shape[1]), at_row),
+            pl.BlockSpec((rows, cosine.shape[1]), at_row),
+            pl.BlockSpec((1, q_cols + kv_cols), fixed),
+        ],
+        out_specs=[
+            pl.BlockSpec((rows, q_cols), at_row),
+            pl.BlockSpec((rows, kv_cols), at_row),
+            pl.BlockSpec((rows, kv_cols), at_row),
+            pl.BlockSpec((rows, q_cols + kv_cols), at_row),
+        ],
+        out_shape=[
+            jax.ShapeDtypeStruct((length, q_cols), LOW),
+            jax.ShapeDtypeStruct((length, kv_cols), LOW),
+            jax.ShapeDtypeStruct((length, kv_cols), LOW),
+            jax.ShapeDtypeStruct((length, q_cols + kv_cols), F32),
+        ],
+        compiler_params=pltpu.CompilerParams(vmem_limit_bytes=40 * 2**20),
+        cost_estimate=FREE,
+        name="prepare",
+    )(normed, weight, cosine, sine, gains)
+
+
+def prepare_back_kernel(
+    q_cols, kv_cols, dq_ref, dk_ref, dv_ref, raw_ref, cos_ref, sin_ref, gain_ref, out_ref, gain_grad_ref
+):
+    @pl.when(pl.program_id(0) == 0)
+    def _():
+        gain_grad_ref[...] = jnp.zeros_like(gain_grad_ref)
+
+    for first, cols, grad_ref in ((0, q_cols, dq_ref), (q_cols, kv_cols, dk_ref)):
+        span = slice(first, first + cols)
+        grad = grad_ref[...]
+        turned = grad * across(cos_ref[...], cols) - partner(grad) * across(sin_ref[...], cols)
+        raw = raw_ref[:, span]
+        inverse = lax.rsqrt(group_mean(raw * raw) + EPSILON)
+        hat = raw * inverse
+        gain_grad_ref[:, span] += jnp.sum(turned * hat, axis=0, keepdims=True)
+        scaled = turned * gain_ref[:, span]
+        out_ref[:, span] = ((scaled - hat * group_mean(scaled * hat)) * inverse).astype(LOW)
+    out_ref[:, q_cols + kv_cols :] = dv_ref[...].astype(LOW)
+
+
+def prepare_back(d_queries, d_keys, d_values, raw, cosine, sine, gains, ranks):
+    length, q_cols = d_queries.shape
+    kv_cols = d_keys.shape[1]
+    rows = length // ranks
+    at_row = lambda i: (i, 0)
+    fixed = lambda i: (0, 0)
+    return pl.pallas_call(
+        functools.partial(prepare_back_kernel, q_cols, kv_cols),
+        grid=(ranks,),
+        in_specs=[
+            pl.BlockSpec((rows, q_cols), at_row),
+            pl.BlockSpec((rows, kv_cols), at_row),
+            pl.BlockSpec((rows, kv_cols), at_row),
+            pl.BlockSpec((rows, q_cols + kv_cols), at_row),
+            pl.BlockSpec((rows, cosine.shape[1]), at_row),
+            pl.BlockSpec((rows, cosine.shape[1]), at_row),
+            pl.BlockSpec((1, q_cols + kv_cols), fixed),
+        ],
+        out_specs=[
+            pl.BlockSpec((rows, q_cols + 2 * kv_cols), at_row),
+            pl.BlockSpec((1, q_cols + kv_cols), fixed),
+        ],
+        out_shape=[
+            jax.ShapeDtypeStruct((length, q_cols + 2 * kv_cols), LOW),
+            jax.ShapeDtypeStruct((1, q_cols + kv_cols), F32),
+        ],
+        compiler_params=pltpu.CompilerParams(vmem_limit_bytes=40 * 2**20),
+        cost_estimate=FREE,
+        name="prepare_back",
+    )(d_queries, d_keys, d_values, raw, cosine, sine, gains)
 
 
 def shards(
@@ -252,9 +677,9 @@
     cotangent,
 ):
     ring = dp_size // 2
-    place = lax.axis_index("dp")
-    stage = place // 2
-    core = place % 2
+    index = lax.axis_index("dp")
+    stage = index // 2
+    core = index % 2
     me = lax.axis_index("tensor")
     swap_pairs = [(i, i ^ 1) for i in range(dp_size)]
     ring_pairs = [(i, (i + 2) % dp_size) for i in range(dp_size)]
@@ -264,72 +689,74 @@
     q_cols = w_query.shape[1]
     kv_cols = key_weight.shape[1]
 
+    hidden_cols = w_gate.shape[1]
+    hidden_pad = -hidden_cols % 128
+
+    def widen(weight):
+        return jnp.pad(weight, ((0, 0), (0, hidden_pad)))
+
     def swap(v):
         return lax.ppermute(v, "dp", swap_pairs)
 
     def onward(v):
         return lax.ppermute(v, "dp", ring_pairs)
 
-    def gather_dp(weight):
-        depth, cols = weight.shape
-        full = jnp.zeros((dp_size * depth, cols), weight.dtype)
-        block = weight
+    core_array = core.astype(jnp.int32).reshape(1)
+    at = jnp.stack([stage, core]).astype(jnp.int32)
+
+    def ring_gather(label, block):
+        blocks = []
         for hop in range(ring):
-            owner = lax.rem(stage - hop + ring, ring)
-            full = lax.dynamic_update_slice(full, block, ((owner * 2 + core) * depth, 0))
-            full = lax.dynamic_update_slice(full, swap(block), ((owner * 2 + 1 - core) * depth, 0))
+            with jax.named_scope(f"{label}_swap{hop}"):
+                blocks += [block, swap(block)]
             if hop < ring - 1:
-                block = onward(block)
-        return full
-
-    def by_core(matrix):
-        count = matrix.shape[0]
-        split = matrix.reshape(count, ring, 2, -1)
-        even = split[:, :, 0].reshape(count, -1)
-        odd = split[:, :, 1].reshape(count, -1)
-        return jnp.where(core == 0, odd, even), jnp.where(core == 0, even, odd)
-
-    def reduce_dp(left_pair, right):
-        far = swap(cross_cols(left_pair[0], right).astype(LOW))
-        near = (cross_cols(left_pair[1], right) + far.astype(F32)).astype(LOW)
-        near = near.reshape(ring, -1, right.shape[1])
-
-        def mine(hop):
-            owner = lax.rem(stage - 1 - hop + 2 * ring, ring)
-            return lax.dynamic_index_in_dim(near, owner, 0, keepdims=False)
-
-        block = mine(0)
-        for hop in range(1, ring):
-            block = onward(block).astype(F32) + mine(hop).astype(F32)
-            if hop < ring - 1:
-                block = block.astype(LOW)
-        return block
-
-    def spread(block):
-        return [block] + [
-            lax.ppermute(block, "tensor", [(i, i ^ j) for i in range(ranks)]) for j in range(1, ranks)
-        ]
-
-    def collect(parts):
-        total = parts[0].astype(F32)
-        for j in range(1, ranks):
-            total = total + lax.ppermute(
-                parts[j].astype(LOW), "tensor", [(i, i ^ j) for i in range(ranks)]
-            ).astype(F32)
+                with jax.named_scope(f"{label}_hop{hop + 1}"):
+                    block = onward(block)
+        return blocks
+
+    def hop(label, block):
+        with jax.named_scope(label):
+            return onward(block)
+
+    def owner_after(count):
+        return lax.rem(stage - 1 - count + 2 * ring, ring)
+
+    def spread(label, block):
+        with jax.named_scope(label):
+            return [block] + [
+                lax.ppermute(block, "tensor", [(i, i ^ j) for i in range(ranks)])
+                for j in range(1, ranks)
+            ]
+
+    def send_parts(label, parts):
+        with jax.named_scope(label):
+            return [
+                lax.ppermute(parts[j], "tensor", [(i, i ^ j) for i in range(ranks)])
+                for j in range(1, ranks)
+            ]
+
+    def add_up(own, arrived):
+        total = own.astype(F32)
+        for piece in arrived:
+            total = total + piece.astype(F32)
         return total
 
     def cut(matrix):
         return [matrix[j * rows : (j + 1) * rows] for j in range(ranks)]
 
+    def tie(value, *others):
+        return lax.optimization_barrier((value,) + others)[0]
+
     tokens_wide = tokens.astype(F32)
     normed_own = norm_rows(tokens_wide, attn_gain).astype(LOW)
-    normed_one = spread(normed_own)
-    w_qkv = gather_dp(jnp.concatenate([w_query, key_weight, value_weight], axis=1))
-    out_t = gather_dp(w_out.T)
-    down_t = gather_dp(w_down.T)
-    gate_full = gather_dp(w_gate)
-    up_full = gather_dp(w_up)
-    grad_blocks = spread(cotangent)
+    normed_one = spread("one_spread", normed_own)
+    a_blocks = ring_gather("attn", jnp.concatenate([w_query, key_weight, value_weight, w_out.T], axis=1))
+    ffn_full = lax.all_gather(
+        jnp.stack([widen(w_down.T), widen(w_gate), widen(w_up)]), "dp", axis=1, tiled=True
+    )
+    grad_blocks = spread("cot_spread", tie(cotangent, *normed_one))
+    wide = hidden_cols + hidden_pad
+    down_t, gate_full, up_full = ffn_full[0], ffn_full[1], ffn_full[2]
 
     first_start = jnp.sum((segments < 1).astype(jnp.int32))
     second_start = jnp.sum((segments < 2).astype(jnp.int32))
@@ -343,79 +770,127 @@
     bounds = bounds.reshape(ranks, 1, rows)
     half = HEAD_SIZE // 2
     freqs = ROTARY_BASE ** (-2.0 * jnp.arange(half, dtype=F32) / HEAD_SIZE)
-    angles = positions[:, None] * freqs[None, :]
-    cosine = jnp.cos(angles)[:, None, :]
-    sine = jnp.sin(angles)[:, None, :]
-
-    raw = jnp.concatenate([mm(block, w_qkv) for block in normed_one], axis=0)
-    normed_all = jnp.concatenate(normed_one, axis=0)
-
-    def head_prepare(raw_rows, gain):
-        return rotate(norm_rows(raw_rows.reshape(length, -1, HEAD_SIZE), gain), cosine, sine)
-
-    query_rot, query_pull = jax.vjp(head_prepare, raw[:, :q_cols], query_gain)
-    key_rot, key_pull = jax.vjp(head_prepare, raw[:, q_cols : q_cols + kv_cols], key_gain)
-    query_low = query_rot.astype(LOW).reshape(length, -1)
-    key_low = key_rot.astype(LOW).reshape(length, -1)
-    value_low = raw[:, q_cols + kv_cols :].astype(LOW)
+    angles = positions[:, None] * jnp.concatenate([freqs] * 4)[None, :]
+    signs = jnp.concatenate([-jnp.ones(half, F32), jnp.ones(half, F32)] * 2)
+    cosine = jnp.cos(angles)
+    sine = jnp.sin(angles) * signs[None, :]
+    head_gains = jnp.concatenate(
+        [query_gain] * (q_cols // HEAD_SIZE) + [key_gain] * (kv_cols // HEAD_SIZE)
+    ).reshape(1, -1)
+
+    normed_all, normed_one_t = fold(core_array, normed_one, ring)
+    a_blocks[-2] = tie(a_blocks[-2], normed_all, cosine, sine)
+    attn_full = place(at, a_blocks, ring)
+    w_qkv = attn_full[:, : q_cols + 2 * kv_cols]
+    out_t = attn_full[:, q_cols + 2 * kv_cols :]
+    query_low, key_low, value_low, raw = prepare(
+        normed_all, w_qkv, cosine, sine, head_gains, q_cols, kv_cols, ranks
+    )
     me_array = me.astype(jnp.int32).reshape(1)
     attended, lse = attend(me_array, query_low, key_low, value_low, bounds, ranks, heads)
 
-    attn_sum = collect([cross_rows(block, out_t) for block in cut(attended)])
-    hidden = tokens_wide + attn_sum
-    normed_two = spread(norm_rows(hidden, ffn_gain).astype(LOW))
-    normed_two_all = jnp.concatenate(normed_two, axis=0)
-    grad_all = jnp.concatenate(grad_blocks, axis=0)
-
-    d_activation = mm(grad_all, down_t)
-    gating = mm(normed_two_all, gate_full)
+    attended_go = tie(attended, *grad_blocks)
+    attn_parts = back_parts([attended_go], out_t[None], (0,), ranks)
+    attn_arrived = send_parts("attn_sum", attn_parts)
+    grad_all, *grad_pair = fold(
+        core_array, [tie(grad_blocks[0], *attn_parts)] + grad_blocks[1:], ring, True
+    )
+    attn_arrived[0] = tie(attn_arrived[0], grad_all)
+    hidden, normed_two_own = sum_up(tokens, [attn_parts[0]] + attn_arrived, ffn_gain)
+    normed_two = spread("two_spread", normed_two_own)
+    d_activation = mm(grad_all, down_t).astype(LOW)
+    normed_two[-1] = tie(normed_two[-1], d_activation)
+    normed_two_all, *normed_two_pair = fold(core_array, normed_two, ring, True)
+
+    gating = mm(normed_two_all, gate_full).astype(LOW).astype(F32)
     lifted = mm(normed_two_all, up_full)
     gate_sig = jax.nn.sigmoid(gating)
     silu = gating * gate_sig
     activation = (silu * lifted).astype(LOW)
-    d_gating = (d_activation * lifted * gate_sig * (1.0 + gating * (1.0 - gate_sig))).astype(LOW)
-    d_lifted = (d_activation * silu).astype(LOW)
-
-    d_normed_two = collect(
-        [
-            cross_rows(g, gate_full) + cross_rows(u, up_full)
-            for g, u in zip(cut(d_gating), cut(d_lifted))
-        ]
-    )
-    output = hidden + collect([cross_rows(block, down_t) for block in cut(activation)])
-    grad_pair = by_core(grad_all)
-    normed_two_pair = by_core(normed_two_all)
-    down_grad = reduce_dp(grad_pair, activation)
-    gate_grad = reduce_dp(normed_two_pair, d_gating)
-    lift_grad = reduce_dp(normed_two_pair, d_lifted)
-
-    d_hidden_norm, ffn_gain_part = norm_back(hidden, ffn_gain, d_normed_two)
-    d_hidden = cotangent.astype(F32) + d_hidden_norm
-    hidden_grad = spread(d_hidden.astype(LOW))
-    d_attended = jnp.concatenate([mm(block, out_t) for block in hidden_grad], axis=0).astype(LOW)
-    hidden_grad_pair = by_core(jnp.concatenate(hidden_grad, axis=0))
+    d_act_wide = d_activation.astype(F32)
+    d_gating = (d_act_wide * lifted * gate_sig * (1.0 + gating * (1.0 - gate_sig))).astype(LOW)
+    d_lifted = (d_act_wide * silu).astype(LOW)
+
+    last = ring - 1
+
+    def advance(label, flow, near, other, count):
+        if count == last:
+            return join(owner_after(count), flow, near, other, ring, F32), None
+        block = join(owner_after(count), flow, near, other, ring, LOW)
+        return block, hop(f"{label}_hop{count + 1}", block)
+
+    def several(label, block, flow, near, other, first, end, *after):
+        for count in range(first, end):
+            block, flow = advance(label, tie(flow, *after), near, other, count)
+        return block, flow
+
+    down_far = product(grad_pair[0], [activation])
+    down_other = swap(down_far)
+    down_near = product(grad_pair[1], [tie(activation, down_far)])
+    down_block, down_flow = advance("down_grad", None, down_near, down_other, 0)
+    both_far = product(normed_two_pair[0], [tie(d_gating, down_block), d_lifted])
+    both_other = swap(both_far)
+    both_near = product(normed_two_pair[1], [tie(d_gating, both_far), d_lifted])
+    two_parts = back_parts([tie(d_gating, both_near), d_lifted], ffn_full, (1, 2), ranks)
+    down_block, down_flow = advance("down_grad", tie(down_flow, *two_parts), down_near, down_other, 1)
+    two_go = lax.optimization_barrier(tuple(two_parts) + (down_block,))[:-1]
+    two_arrived = send_parts("two_sum", two_go)
+    both_block, both_flow = advance("both_grad", None, tie(both_near, *two_go), both_other, 0)
+    ffn_parts = back_parts([tie(activation, both_block)], ffn_full, (0,), ranks)
+    two_arrived = list(lax.optimization_barrier(tuple(two_arrived) + (ffn_parts[0],))[:-1])
+    d_hidden, d_hidden_low, ffn_gain_part = norm_back_sum(
+        hidden, ffn_gain, cotangent, [two_parts[0]] + two_arrived, True
+    )
+    hidden_grad = spread("dh_spread", d_hidden_low)
+    down_block, down_flow = several(
+        "down_grad", down_block, down_flow, down_near, down_other, 2, last, hidden_grad[1]
+    )
+    both_block, both_flow = several(
+        "both_grad", both_block, both_flow, both_near, both_other, 1, last - 1, hidden_grad[1], down_block
+    )
+    hidden_grad[-1] = tie(hidden_grad[-1], both_block)
+    hidden_grad_all, hidden_grad_t = fold(core_array, hidden_grad, ring)
+    ffn_go = lax.optimization_barrier(tuple(ffn_parts) + tuple(hidden_grad))[:ranks]
+    ffn_arrived = send_parts("ffn_sum", ffn_go)
+    d_attended = rows_product(hidden_grad_all, out_t, ranks)
     d_queries, d_keys, d_values = attend_back(
         me_array, query_low, key_low, value_low, bounds, attended, d_attended, lse, ranks, heads
     )
-    d_query_raw, query_gain_part = query_pull(d_queries.reshape(length, -1, HEAD_SIZE))
-    d_key_raw, key_gain_part = key_pull(d_keys.reshape(length, -1, HEAD_SIZE))
-    d_raw = jnp.concatenate(
-        [d_query_raw.astype(LOW), d_key_raw.astype(LOW), d_values.astype(LOW)], axis=1
-    )
-    d_normed_one = collect([cross_rows(block, w_qkv) for block in cut(d_raw)])
-    qkv_grad = reduce_dp(by_core(normed_all), d_raw)
-    out_grad = reduce_dp(hidden_grad_pair, attended)
-    d_tokens_norm, attn_gain_part = norm_back(tokens_wide, attn_gain, d_normed_one)
-    tokens_grad = d_hidden + d_tokens_norm
-
+    d_raw, head_gain_parts = prepare_back(
+        d_queries, d_keys, d_values, raw, cosine, sine, head_gains, ranks
+    )
+    down_grad, _ = advance("down_grad", tie(down_flow, *ffn_arrived), down_near, down_other, last)
+    both_block, both_flow = advance(
+        "both_grad", tie(both_flow, down_grad), both_near, both_other, last - 1
+    )
+    one_parts = back_parts([tie(d_raw, both_block, *ffn_arrived)], w_qkv[None], (0,), ranks)
+    one_arrived = send_parts("one_sum", one_parts)
+    attn_full_grad = attn_products([normed_one_t, hidden_grad_t], [tie(d_raw, *one_parts), attended])
+    attn_grad = lax.psum_scatter(attn_full_grad, "dp", scatter_dimension=0, tiled=True).astype(F32)
+    attn_gain_part = gain_part(tie(normed_all, attn_full_grad), attn_gain, one_parts).reshape(-1)
+    (output,) = sum_up(tie(hidden, attn_gain_part), [ffn_parts[0]] + ffn_arrived)
+    one_arrived[-1] = tie(one_arrived[-1], output)
+    (tokens_grad,) = norm_back_sum(tokens, attn_gain, d_hidden, [one_parts[0]] + one_arrived, False)
+    both_grad, _ = advance("both_grad", tie(both_flow, tokens_grad), both_near, both_other, last)
+    qkv_cols = q_cols + 2 * kv_cols
+    qkv_grad = attn_grad[:, :qkv_cols]
+    out_grad = attn_grad[:, qkv_cols:]
+    down_grad = down_grad[:, :hidden_cols]
+    gate_grad = both_grad[:, :hidden_cols]
+    lift_grad = both_grad[:, wide : wide + hidden_cols]
+
+    head_gain_parts = head_gain_parts.reshape(-1, HEAD_SIZE)
+    query_gain_part = jnp.sum(head_gain_parts[: q_cols // HEAD_SIZE], axis=0)
+    key_gain_part = jnp.sum(head_gain_parts[q_cols // HEAD_SIZE :], axis=0)
     sizes = [attn_gain.shape[0], ffn_gain.shape[0], HEAD_SIZE, HEAD_SIZE]
-    gains = jnp.concatenate([attn_gain_part, ffn_gain_part, query_gain_part, key_gain_part])
+    gains = jnp.concatenate([attn_gain_part, ffn_gain_part.reshape(-1), query_gain_part, key_gain_part])
     gains = gains.reshape(1, -1)
     total = gains
     span = 1
     while span < ranks:
         total = total + lax.ppermute(total, "tensor", [(i, i ^ span) for i in range(ranks)])
         span *= 2
+    total = tie(total, both_grad, tokens_grad)
     span = 1
     while span < dp_size:
         total = total + lax.ppermute(total, "dp", [(i, i ^ span) for i in range(dp_size)])

time: 733 us -> 513 us (0.70)
  waiting for transfers between devices: 317 us -> 190 us
  matrix products: 156 us -> 31.3 us
  Pallas kernels: 29.7 us -> 150 us
  local copies, waits for them, and re-layouts: 111 us -> 49.5 us
  other arithmetic: 45.4 us -> 8.49 us
  between operations: 2.97 us -> 15.5 us
    ppermute x30 -> x9, waiting for transfers between devices: 188 us -> 63 us  [onward(): return lax.ppermute(v, 'dp', ring_pairs)]
    pallas_call x0 -> x30, Pallas kernels: none -> 121 us  [the longest x4 32.5 us: back_parts(): pl.pallas_call(functools.partial(back_parts_kernel, rows, len(lefts)), gr...]
    dot_general x30 -> x0, matrix products: 110 us -> none  [the longest x20 66.4 us: cross_rows(): lax.dot_general(left, right, (((1,), (1,)), ((), ())), preferred_element_...]
    dynamic_update_slice x40 -> x0, local copies, waits for them, and re-layouts: 42 us -> none  [the longest x20 21.2 us: gather_dp(): lax.dynamic_update_slice(full, swap(block), ((owner * 2 + 1 - core) * dep...]
    ppermute x12, waiting for transfers between devices: 59.5 us -> 24.1 us  [spread(): lax.ppermute(block, 'tensor', [(i, i ^ j) for i in range(ranks)])]
    ppermute x2, waiting for transfers between devices: 1.53 us -> 23 us  [shards(): lax.ppermute(total, 'tensor', [(i, i ^ span) for i in range(ranks)])]
    all_gather x0 -> x1, waiting for transfers between devices: none -> 21 us  [shards(): lax.all_gather(jnp.stack([widen(w_down.T), widen(w_gate), widen(w_up)]),...]
    unnamed x200 -> x155, local copies, waits for them, and re-layouts: 17.6 us -> 35 us
  transfers between devices with their start and end apart: 84 -> 46, of which waited for: 35 -> 24; matrix products, arithmetic and copies ran while one was open for 33% -> 5% of each run, Pallas kernels for 4% -> 23%
where the time goes in v2:
time: 513 us; the launch traced here: 507 us
  waiting for transfers between devices  190 us (37%)
  Pallas kernels  150 us (29%)
  starting transfers between devices  62.6 us (12%)
  local copies, waits for them, and re-layouts  49.5 us (10%)
  matrix products  31.3 us (6%)
  between operations  15.5 us (3%)
  other arithmetic  8.49 us (2%)
    ppermute x9, waiting for transfers between devices, onward(): return lax.ppermute(v, 'dp', ring_pairs)  63 us
    ppermute x12, waiting for transfers between devices, send_parts(): lax.ppermute(parts[j], 'tensor', [(i, i ^ j) for i in range(ranks)])  52.3 us
    unnamed x155, local copies, waits for them, and re-layouts  35 us
    pallas_call x4, Pallas kernels, back_parts(): pl.pallas_call(functools.partial(back_parts_kernel, rows, len(lefts)), gr...  32.5 us
    dot_general x3, matrix products, mm(): return jnp.dot(left, right, preferred_element_type=F32)  31.3 us
    pallas_call x4, Pallas kernels, product(): pl.pallas_call(functools.partial(product_kernel, tiles), grid=(tiles * le...  30.8 us
    ppermute x9, starting transfers between devices, onward(): return lax.ppermute(v, 'dp', ring_pairs)  30.2 us
    ppermute x12, waiting for transfers between devices, spread(): lax.ppermute(block, 'tensor', [(i, i ^ j) for i in range(ranks)])  24.1 us
  transfers between devices with their start and end apart: 46, of which 24 were waited for; matrix products, arithmetic and copies ran while one was open for 5% of the time, Pallas kernels for 23%

profile of v2, /device:TPU:0, one launch (start us, length us, event | category | flops | bytes accessed | tf_op | source)
XLA Modules:
  0.0 507.5 jit_solution(13619534531914331648)
XLA Ops:
  11.6 3.1 collective-permute-start.4
  16.7 9.2 %collective-permute-done.4.refs_2_ = bf16[192,1024]{1,0:T(8,128)(2,1)} collective-permute-done((bf16[192,1024]{1,0:T(8,128)(2,1)S(1)}, bf16[192,1024]{1,0:T(8,128)(2,1)}, u32[]{:S(2)}, u32[]{:S(2)}) %collective-permute-start.4) | collective-permute-done | bytes 393248 | tf_op jit(solution)/shard_map/attn_hop1/ppermute | solution.py:702
  30.8 17.0 %collective-permute-done.6.refs_4_ = bf16[192,1024]{1,0:T(8,128)(2,1)} collective-permute-done((bf16[192,1024]{1,0:T(8,128)(2,1)}, bf16[192,1024]{1,0:T(8,128)(2,1)}, u32[]{:S(2)}, u32[]{:S(2)}) %collective-permute-start.6) | collective-permute-done | bytes 393248 | tf_op jit(solution)/shard_map/attn_hop2/ppermute | solution.py:702
  47.8 5.9 %collective-permute-start.8 = (bf16[192,1024]{1,0:T(8,128)(2,1)}, bf16[192,1024]{1,0:T(8,128)(2,1)}, u32[]{:S(2)}, u32[]{:S(2)}) collective-permute-start(bf16[192,1024]{1,0:T(8,128)(2,1)} %collective-permute-done.6.refs_4_), channel_id=1, source_target_pairs={{0,8},{4,12},{8,16},{12,20},{16,24},{20,28},{24,0},{28,4},{1,9},{5... | collective-permute-start | bytes 1179656 | tf_op jit(solution)/shard_map/attn_hop3/ppermute | solution.py:702
  53.9 7.7 %collective-permute-done.1.refs_2_ = bf16[256,1536]{1,0:T(8,128)(2,1)} collective-permute-done((bf16[256,1536]{1,0:T(8,128)(2,1)S(1)}, bf16[256,1536]{1,0:T(8,128)(2,1)}, u32[]{:S(2)}, u32[]{:S(2)}) %collective-permute-start.1) | collective-permute-done | bytes 786464 | tf_op jit(solution)/shard_map/one_spread/ppermute | solution.py:727
  61.6 11.0 %collective-permute-done.8.refs_6_ = bf16[192,1024]{1,0:T(8,128)(2,1)} collective-permute-done((bf16[192,1024]{1,0:T(8,128)(2,1)}, bf16[192,1024]{1,0:T(8,128)(2,1)}, u32[]{:S(2)}, u32[]{:S(2)}) %collective-permute-start.8) | collective-permute-done | bytes 393248 | tf_op jit(solution)/shard_map/attn_hop3/ppermute | solution.py:702
  77.6 2.6 fusion.16
  80.2 2.8 fold.4
  82.9 1.7 copy-done.30
  84.6 2.9 place.1
  89.2 5.5 %prepare.1 = (bf16[1024,384]{1,0:T(8,128)(2,1)S(1)}, bf16[1024,128]{1,0:T(8,128)(2,1)S(1)}, bf16[1024,128]{1,0:T(8,128)(2,1)S(1)}, f32[1024,512]{1,0:T(8,128)S(1)}) custom-call(bf16[1024,1536]{1,0:T(8,128)(2,1)S(1)} %get-tuple-element.157.x_ref.normed_ref, bf16[1536,640]{1,0:T(8,128)(2,1)S(1)} %get-tuple-element.173.w_ref, ...), custom_call_target="tpu_custom_call" | custom-call | tf_op jit(solution)/shard_map/prepare/pallas_call | solution.py:581
  96.0 12.8 %attend.1 = (bf16[1024,384]{1,0:T(8,128)(2,1)S(1)}, f32[4,2,768]{2,1,0:T(2,128)S(1)}) custom-call(s32[1]{0:T(128)} %bitcast.me_ref, bf16[1024,384]{1,0:T(8,128)(2,1)S(1)} %get-tuple-element.91.q_ref, bf16[1024,128]{1,0:T(8,128)(2,1)S(1)} %get-tuple-element.92.k_ref, bf16[1024,128]{1,0:T(8,128)(2,1)S(1)} %get-tuple-element.93.v_ref, ...), custom_call_target="tpu_custom_call" | custom-call | tf_op jit(solution)/shard_map/attend/pallas_call | solution.py:178
  108.8 3.0 collective-permute-done.11.refs_2_
  113.1 3.0 back_parts.4
  122.6 14.0 %collective-permute-done.13.refs_1_ = bf16[256,1536]{1,0:T(8,128)(2,1)S(1)} collective-permute-done((bf16[256,1536]{1,0:T(8,128)(2,1)S(1)}, bf16[256,1536]{1,0:T(8,128)(2,1)S(1)}, u32[]{:S(2)}, u32[]{:S(2)}) %collective-permute-start.13) | collective-permute-done | bytes 786464 | tf_op jit(solution)/shard_map/attn_sum/ppermute | solution.py:734
  136.7 16.7 %collective-permute-done.14.refs_2_ = bf16[256,1536]{1,0:T(8,128)(2,1)S(1)} collective-permute-done((bf16[256,1536]{1,0:T(8,128)(2,1)S(1)}, bf16[256,1536]{1,0:T(8,128)(2,1)S(1)}, u32[]{:S(2)}, u32[]{:S(2)}) %collective-permute-start.14) | collective-permute-done | bytes 786464 | tf_op jit(solution)/shard_map/attn_sum/ppermute | solution.py:734
  158.9 21.0 %all-gather.2.cloned.1.call-done.refs_2_.refs_3_.refs_1_ = bf16[3,1536,1792]{2,1,0:T(8,128)(2,1)} async-done(((bf16[3,192,1792]{2,1,0:T(8,128)(2,1)}), bf16[3,1536,1792]{2,1,0:T(8,128)(2,1)}) %all-gather.2.cloned.1.call-update) | async-done | bytes 16515088 | tf_op jit(solution)/shard_map/all_gather | solution.py:754
  180.0 9.1 %fusion.11 = bf16[1024,1792]{1,0:T(8,128)(2,1)S(1)} fusion(bf16[1024,1536]{1,0:T(8,128)(2,1)} %copy-done.63, bf16[3,1536,1792]{2,1,0:T(8,128)(2,1)} %all-gather.2.cloned.1.call-done.refs_2_.refs_3_.refs_1_), kind=kOutput, calls=%fused_computation.20 | convolution fusion | flops 5638979584 | bytes 12320768 | tf_op jit(solution)/shard_map/dot_general | solution.py:40
  190.6 2.4 fold.6
  195.2 8.6 %fusion.12 = bf16[1024,1792]{1,0:T(8,128)(2,1)S(1)} fusion(bf16[1024,1536]{1,0:T(8,128)(2,1)S(1)} %get-tuple-element.108, bf16[3,1536,1792]{2,1,0:T(8,128)(2,1)} %all-gather.2.cloned.1.call-done.refs_2_.refs_3_.refs_1_), kind=kOutput, calls=%fused_computation.21 | convolution fusion | flops 5638979584 | bytes 12320768 | tf_op jit(solution)/shard_map/dot_general | solution.py:40
  203.9 13.6 %multiply_convert_fusion = (bf16[1024,1792]{1,0:T(8,128)(2,1)S(1)}, bf16[1024,1792]{1,0:T(8,128)(2,1)}, bf16[1024,1792]{1,0:T(8,128)(2,1)}) fusion(bf16[1024,1792]{1,0:T(8,128)(2,1)S(1)} %fusion.12, bf16[1024,1792]{1,0:T(8,128)(2,1)S(1)} %fusion.11, bf16[1024,1536]{1,0:T(8,128)(2,1)S(1)} %get-tuple-element.108, ...), kind=kOutput, calls=%fused_computation.13 | convolution fusion | flops 5668339712 | bytes 27000832 | tf_op jit(solution)/shard_map/dot_general | solution.py:40
  217.4 6.1 %product.4 = bf16[768,1792]{1,0:T(8,128)(2,1)} custom-call(bf16[768,1024]{1,0:T(8,128)(2,1)S(1)} %copy-done.45, bf16[1024,1792]{1,0:T(8,128)(2,1)S(1)} %get-tuple-element.126.refs_0_), custom_call_target="tpu_custom_call" | custom-call | tf_op jit(solution)/shard_map/product/pallas_call | solution.py:309
  223.6 2.0 copy-done.9
  227.0 4.6 product.5.refs_0_.refs_1_
  231.7 2.1 join.8
  234.6 10.6 %product.6 = bf16[768,3584]{1,0:T(8,128)(2,1)} custom-call(bf16[768,1024]{1,0:T(8,128)(2,1)S(1)} %copy-done.41, bf16[1024,1792]{1,0:T(8,128)(2,1)S(1)} %copy-done.2, bf16[1024,1792]{1,0:T(8,128)(2,1)S(1)} %copy-done.5), custom_call_target="tpu_custom_call" | custom-call | tf_op jit(solution)/shard_map/product/pallas_call | solution.py:309
  245.8 12.5 %collective-permute-start.20 = (bf16[192,1792]{1,0:T(8,128)(2,1)}, bf16[192,1792]{1,0:T(8,128)(2,1)}, u32[]{:S(2)}, u32[]{:S(2)}) collective-permute-start(bf16[192,1792]{1,0:T(8,128)(2,1)} %join.8), channel_id=1, source_target_pairs={{0,8},{4,12},{8,16},{12,20},{16,24},{20,28},{24,0},{28,4},{1,9},{5... | collective-permute-start | bytes 2064392 | tf_op jit(solution)/shard_map/down_grad_hop1/ppermute | solution.py:702
  258.3 2.0 copy-done.3
  260.3 2.0 copy-done.6
  263.8 9.4 %product.7.refs_0_.refs_1_ = bf16[768,3584]{1,0:T(8,128)(2,1)S(1)} custom-call(bf16[768,1024]{1,0:T(8,128)(2,1)S(1)} %copy-done.39, bf16[1024,1792]{1,0:T(8,128)(2,1)S(1)} %copy-done.3, bf16[1024,1792]{1,0:T(8,128)(2,1)S(1)} %copy-done.6), custom_call_target="tpu_custom_call" | custom-call | tf_op jit(solution)/shard_map/product/pallas_call | solution.py:309
  273.3 16.3 %back_parts.5 = (bf16[256,1536]{1,0:T(8,128)(2,1)S(1)}, bf16[256,1536]{1,0:T(8,128)(2,1)}, bf16[256,1536]{1,0:T(8,128)(2,1)S(1)}, bf16[256,1536]{1,0:T(8,128)(2,1)S(1)}) custom-call(bf16[1024,1792]{1,0:T(8,128)(2,1)S(1)} %copy-done.4, bf16[1024,1792]{1,0:T(8,128)(2,1)S(1)} %copy-done.7, ...), custom_call_target="tpu_custom_call" | custom-call | tf_op jit(solution)/shard_map/back_parts/pallas_call | solution.py:365
  289.6 2.2 join.9
  295.3 2.4 join.10
  297.7 2.5 collective-permute-start.28
  300.2 9.3 %back_parts.6 = (bf16[256,1536]{1,0:T(8,128)(2,1)S(1)}, bf16[256,1536]{1,0:T(8,128)(2,1)}, bf16[256,1536]{1,0:T(8,128)(2,1)}, bf16[256,1536]{1,0:T(8,128)(2,1)}) custom-call(bf16[1024,1792]{1,0:T(8,128)(2,1)S(1)} %copy-done.10, bf16[3,1536,1792]{2,1,0:T(8,128)(2,1)} %all-gather.2.cloned.1.call-done.refs_2_.refs_3_.refs_1_), custom_call_target="tpu_custom_call" | custom-call | tf_op jit(solution)/shard_map/back_parts/pallas_call | solution.py:365
  309.5 3.0 collective-permute-done.21.refs_1_
  313.4 15.8 %collective-permute-done.23.refs_3_ = bf16[256,1536]{1,0:T(8,128)(2,1)S(1)} collective-permute-done((bf16[256,1536]{1,0:T(8,128)(2,1)S(1)}, bf16[256,1536]{1,0:T(8,128)(2,1)S(1)}, u32[]{:S(2)}, u32[]{:S(2)}) %collective-permute-start.23) | collective-permute-done | bytes 786464 | tf_op jit(solution)/shard_map/two_sum/ppermute | solution.py:734
  329.2 2.2 norm_back_sum.2
  333.6 2.5 collective-permute-start.29
  339.1 12.5 %collective-permute-done.29.refs_0_ = bf16[192,1792]{1,0:T(8,128)(2,1)} collective-permute-done((bf16[192,1792]{1,0:T(8,128)(2,1)}, bf16[192,1792]{1,0:T(8,128)(2,1)}, u32[]{:S(2)}, u32[]{:S(2)}) %collective-permute-start.29) | collective-permute-done | bytes 688160 | tf_op jit(solution)/shard_map/down_grad_hop2/ppermute | solution.py:702
  351.7 2.3 collective-permute-done.25.refs_1_
  354.0 2.3 join.11
  357.2 2.9 join.12
  360.1 2.5 collective-permute-start.30
  362.5 6.1 %collective-permute-done.27.refs_3_ = bf16[256,1536]{1,0:T(8,128)(2,1)} collective-permute-done((bf16[256,1536]{1,0:T(8,128)(2,1)}, bf16[256,1536]{1,0:T(8,128)(2,1)}, u32[]{:S(2)}, u32[]{:S(2)}) %collective-permute-start.27) | collective-permute-done | bytes 786464 | tf_op jit(solution)/shard_map/dh_spread/ppermute | solution.py:727
  368.6 3.4 collective-permute-done.26.refs_2_
  376.8 2.9 fold.7
  379.9 2.4 rows_product.1.do_ref
  382.3 16.7 %attend_back.1 = (f32[1024,384]{1,0:T(8,128)S(1)}, f32[1024,128]{1,0:T(8,128)S(1)}, f32[1024,128]{1,0:T(8,128)S(1)}) custom-call(s32[1]{0:T(128)} %bitcast.me_ref, bf16[1024,384]{1,0:T(8,128)(2,1)S(1)} %copy-done.29, bf16[1024,128]{1,0:T(8,128)(2,1)S(1)} %copy-done.48, bf16[1024,128]{1,0:T(8,128)(2,1)S(1)} %copy-done.50, s32[4,1,256]{2,1,0:T(1,128)S(1)} %reshape.131.lo_ref, ...), custom_call_target="tpu_custom_call" | custom-call | tf_op jit(solution)/shard_map/attend_back/pallas_call | solution.py:200
  399.0 5.6 %prepare_back.1 = (bf16[1024,640]{1,0:T(8,128)(2,1)S(1)}, f32[1,512]{1,0:T(1,128)S(1)}) custom-call(f32[1024,384]{1,0:T(8,128)S(1)} %get-tuple-element.138.dq_ref, f32[1024,128]{1,0:T(8,128)S(1)} %get-tuple-element.139.dk_ref, f32[1024,128]{1,0:T(8,128)S(1)} %get-tuple-element.140.dv_ref, f32[1024,512]{1,0:T(8,128)S(1)} %copy-done.35, ...), custom_call_target="tpu_custom_call" | custom-call | tf_op jit(solution)/shard_map/prepare_back/pallas_call | solution.py:635
  405.1 1.8 collective-permute-done.34.refs_3_
  409.6 2.2 join.14
  412.9 3.9 back_parts.7
  418.8 4.8 attn_products.1
  426.2 1.9 copy-done.14
  436.8 1.7 collective-permute-start.39
  441.1 2.8 sum_up.3
  443.9 23.0 %collective-permute-done.39 = f32[1,3200]{1,0:T(1,128)S(1)} collective-permute-done((f32[1,3200]{1,0:T(1,128)S(1)}, f32[1,3200]{1,0:T(1,128)S(1)}, u32[]{:S(2)}, u32[]{:S(2)}) %collective-permute-start.39) | collective-permute-done | bytes 12832 | tf_op jit(solution)/shard_map/ppermute | solution.py:891
  467.0 2.1 norm_back_sum.3
  469.1 13.0 %collective-permute-done.40.refs_0_ = bf16[192,3584]{1,0:T(8,128)(2,1)} collective-permute-done((bf16[192,3584]{1,0:T(8,128)(2,1)}, bf16[192,3584]{1,0:T(8,128)(2,1)}, u32[]{:S(2)}, u32[]{:S(2)}) %collective-permute-start.40) | collective-permute-done | bytes 1376288 | tf_op jit(solution)/shard_map/both_grad_hop3/ppermute | solution.py:702
  482.1 2.1 join.15
  486.8 2.5 collective-permute-done.42
  489.4 1.7 fusion.20
  491.1 2.9 collective-permute-done.43
  (268 shorter events, 84.8 us)
Async XLA Ops:
  7.2 172.8 %all-gather.2.cloned.1.call-start = ((), (), s32[]{:S(2)}) async-start(), calls=%async_computation.1 | async-start | bytes 18579456 | tf_op jit(solution)/shard_map/all_gather | solution.py:754
  11.4 61.8 %copy-start.70 = (f32[64]{0:T(128)S(1)}, f32[64]{0:T(128)}, u32[]{:S(2)}) copy-start(f32[64]{0:T(128)} %param.20) | copy-start | bytes 772
  11.4 62.7 %copy-start.32 = (bf16[256,1536]{1,0:T(8,128)(2,1)S(1)}, bf16[256,1536]{1,0:T(8,128)(2,1)}, u32[]{:S(2)}) copy-start(bf16[256,1536]{1,0:T(8,128)(2,1)} %rest_ref.1) | copy-start | bytes 2359300
  11.4 483.8 %reduce-scatter.2.cloned.1.call-start = ((), (), s32[]{:S(2)}) async-start(), calls=%async_computation.2 | async-start | bytes 3538944 | tf_op jit(solution)/shard_map/reduce_scatter | solution.py:869
  11.6 14.3 %collective-permute-start.4 = (bf16[192,1024]{1,0:T(8,128)(2,1)S(1)}, bf16[192,1024]{1,0:T(8,128)(2,1)}, u32[]{:S(2)}, u32[]{:S(2)}) collective-permute-start(bf16[192,1024]{1,0:T(8,128)(2,1)S(1)} %pad_maximum_fusion.1.refs_0_), channel_id=1, source_target_pairs={{0,8},{4,12},{8,16},{12,20},{16,24},{20,28},{24,0},{28,4},{1,9},{5... | collective-permute-start | bytes 1179656 | tf_op jit(solution)/shard_map/attn_hop1/ppermute | solution.py:702
  15.2 38.6 %collective-permute-start = (bf16[256,1536]{1,0:T(8,128)(2,1)S(1)}, bf16[256,1536]{1,0:T(8,128)(2,1)S(1)}, u32[]{:S(2)}, u32[]{:S(2)}) collective-permute-start(bf16[256,1536]{1,0:T(8,128)(2,1)S(1)} %fusion.15.refs_0_), channel_id=1, source_target_pairs={{0,1},{1,0},{2,3},{3,2},{4,5},{5,4},{6,7},{7,6},{8,9},{9,8},{10,11... | collective-permute-start | bytes 2359304 | tf_op jit(solution)/shard_map/one_spread/ppermute | solution.py:727
  25.9 21.9 %collective-permute-start.6 = (bf16[192,1024]{1,0:T(8,128)(2,1)}, bf16[192,1024]{1,0:T(8,128)(2,1)}, u32[]{:S(2)}, u32[]{:S(2)}) collective-permute-start(bf16[192,1024]{1,0:T(8,128)(2,1)} %collective-permute-done.4.refs_2_), channel_id=1, source_target_pairs={{0,8},{4,12},{8,16},{12,20},{16,24},{20,28},{24,0},{28,4},{1,9},{5... | collective-permute-start | bytes 1179656 | tf_op jit(solution)/shard_map/attn_hop2/ppermute | solution.py:702
  25.9 35.7 %collective-permute-start.1 = (bf16[256,1536]{1,0:T(8,128)(2,1)S(1)}, bf16[256,1536]{1,0:T(8,128)(2,1)}, u32[]{:S(2)}, u32[]{:S(2)}) collective-permute-start(bf16[256,1536]{1,0:T(8,128)(2,1)S(1)} %fusion.15.refs_0_), channel_id=1, source_target_pairs={{0,2},{1,3},{2,0},{3,1},{4,6},{5,7},{6,4},{7,5},{8,10},{9,11},{10,... | collective-permute-start | bytes 2359304 | tf_op jit(solution)/shard_map/one_spread/ppermute | solution.py:727
  27.4 46.6 %collective-permute-start.2 = (bf16[256,1536]{1,0:T(8,128)(2,1)S(1)}, bf16[256,1536]{1,0:T(8,128)(2,1)}, u32[]{:S(2)}, u32[]{:S(2)}) collective-permute-start(bf16[256,1536]{1,0:T(8,128)(2,1)S(1)} %fusion.15.refs_0_), channel_id=1, source_target_pairs={{0,3},{1,2},{2,1},{3,0},{4,7},{5,6},{6,5},{7,4},{8,11},{9,10},{10,... | collective-permute-start | bytes 2359304 | tf_op jit(solution)/shard_map/one_spread/ppermute | solution.py:727
  28.9 46.5 %collective-permute-start.3 = (bf16[192,1024]{1,0:T(8,128)(2,1)S(1)}, bf16[192,1024]{1,0:T(8,128)(2,1)}, u32[]{:S(2)}, u32[]{:S(2)}) collective-permute-start(bf16[192,1024]{1,0:T(8,128)(2,1)S(1)} %pad_maximum_fusion.1.refs_0_), channel_id=1, source_target_pairs={{0,4},{4,0},{8,12},{12,8},{16,20},{20,16},{24,28},{28,24},{1,5},{5... | collective-permute-start | bytes 1179656 | tf_op jit(solution)/shard_map/attn_swap0/ppermute | solution.py:699
  47.8 24.8 %collective-permute-start.8 = (bf16[192,1024]{1,0:T(8,128)(2,1)}, bf16[192,1024]{1,0:T(8,128)(2,1)}, u32[]{:S(2)}, u32[]{:S(2)}) collective-permute-start(bf16[192,1024]{1,0:T(8,128)(2,1)} %collective-permute-done.6.refs_4_), channel_id=1, source_target_pairs={{0,8},{4,12},{8,16},{12,20},{16,24},{20,28},{24,0},{28,4},{1,9},{5... | collective-permute-start | bytes 1179656 | tf_op jit(solution)/shard_map/attn_hop3/ppermute | solution.py:702
  53.8 23.2 %collective-permute-start.5 = (bf16[192,1024]{1,0:T(8,128)(2,1)}, bf16[192,1024]{1,0:T(8,128)(2,1)}, u32[]{:S(2)}, u32[]{:S(2)}) collective-permute-start(bf16[192,1024]{1,0:T(8,128)(2,1)} %collective-permute-done.4.refs_2_), channel_id=1, source_target_pairs={{0,4},{4,0},{8,12},{12,8},{16,20},{20,16},{24,28},{28,24},{1,5},{5... | collective-permute-start | bytes 1179656 | tf_op jit(solution)/shard_map/attn_swap1/ppermute | solution.py:699
  61.6 23.0 %collective-permute-start.7 = (bf16[192,1024]{1,0:T(8,128)(2,1)}, bf16[192,1024]{1,0:T(8,128)(2,1)}, u32[]{:S(2)}, u32[]{:S(2)}) collective-permute-start(bf16[192,1024]{1,0:T(8,128)(2,1)} %collective-permute-done.6.refs_4_), channel_id=1, source_target_pairs={{0,4},{4,0},{8,12},{12,8},{16,20},{20,16},{24,28},{28,24},{1,5},{5... | collective-permute-start | bytes 1179656 | tf_op jit(solution)/shard_map/attn_swap2/ppermute | solution.py:699
  72.6 12.1 %collective-permute-start.9 = (bf16[192,1024]{1,0:T(8,128)(2,1)}, bf16[192,1024]{1,0:T(8,128)(2,1)}, u32[]{:S(2)}, u32[]{:S(2)}) collective-permute-start(bf16[192,1024]{1,0:T(8,128)(2,1)} %collective-permute-done.8.refs_6_), channel_id=1, source_target_pairs={{0,4},{4,0},{8,12},{12,8},{16,20},{20,16},{24,28},{28,24},{1,5},{5... | collective-permute-start | bytes 1179656 | tf_op jit(solution)/shard_map/attn_swap3/ppermute | solution.py:699
  74.1 34.7 %collective-permute-start.10 = (bf16[256,1536]{1,0:T(8,128)(2,1)S(1)}, bf16[256,1536]{1,0:T(8,128)(2,1)S(1)}, u32[]{:S(2)}, u32[]{:S(2)}) collective-permute-start(bf16[256,1536]{1,0:T(8,128)(2,1)S(1)} %copy-done.32), channel_id=1, source_target_pairs={{0,1},{1,0},{2,3},{3,2},{4,5},{5,4},{6,7},{7,6},{8,9},{9,8},{10,11... | collective-permute-start | bytes 2359304 | tf_op jit(solution)/shard_map/cot_spread/ppermute | solution.py:727
  75.3 36.5 %collective-permute-start.11 = (bf16[256,1536]{1,0:T(8,128)(2,1)S(1)}, bf16[256,1536]{1,0:T(8,128)(2,1)S(1)}, u32[]{:S(2)}, u32[]{:S(2)}) collective-permute-start(bf16[256,1536]{1,0:T(8,128)(2,1)S(1)} %copy-done.32), channel_id=1, source_target_pairs={{0,2},{1,3},{2,0},{3,1},{4,6},{5,7},{6,4},{7,5},{8,10},{9,11},{10,... | collective-permute-start | bytes 2359304 | tf_op jit(solution)/shard_map/cot_spread/ppermute | solution.py:727
  76.9 34.9 %collective-permute-start.12 = (bf16[256,1536]{1,0:T(8,128)(2,1)S(1)}, bf16[256,1536]{1,0:T(8,128)(2,1)S(1)}, u32[]{:S(2)}, u32[]{:S(2)}) collective-permute-start(bf16[256,1536]{1,0:T(8,128)(2,1)S(1)} %copy-done.32), channel_id=1, source_target_pairs={{0,3},{1,2},{2,1},{3,0},{4,7},{5,6},{6,5},{7,4},{8,11},{9,10},{10,... | collective-permute-start | bytes 2359304 | tf_op jit(solution)/shard_map/cot_spread/ppermute | solution.py:727
  96.0 20.1 %copy-start.28 = (bf16[1024,384]{1,0:T(8,128)(2,1)}, bf16[1024,384]{1,0:T(8,128)(2,1)S(1)}, u32[]{:S(2)}) copy-start(bf16[1024,384]{1,0:T(8,128)(2,1)S(1)} %get-tuple-element.91.q_ref) | copy-start | bytes 2359300
  96.0 20.1 %copy-start.47 = (bf16[1024,128]{1,0:T(8,128)(2,1)}, bf16[1024,128]{1,0:T(8,128)(2,1)S(1)}, u32[]{:S(2)}) copy-start(bf16[1024,128]{1,0:T(8,128)(2,1)S(1)} %get-tuple-element.92.k_ref) | copy-start | bytes 786436
  96.0 20.1 %copy-start.49 = (bf16[1024,128]{1,0:T(8,128)(2,1)}, bf16[1024,128]{1,0:T(8,128)(2,1)S(1)}, u32[]{:S(2)}) copy-start(bf16[1024,128]{1,0:T(8,128)(2,1)S(1)} %get-tuple-element.93.v_ref) | copy-start | bytes 786436
  96.0 23.7 %copy-start.72 = (f32[1536]{0:T(1024)S(1)}, f32[1536]{0:T(1024)}, u32[]{:S(2)}) copy-start(f32[1536]{0:T(1024)} %param.23) | copy-start | bytes 18436
  116.1 20.5 %collective-permute-start.13 = (bf16[256,1536]{1,0:T(8,128)(2,1)S(1)}, bf16[256,1536]{1,0:T(8,128)(2,1)S(1)}, u32[]{:S(2)}, u32[]{:S(2)}) collective-permute-start(bf16[256,1536]{1,0:T(8,128)(2,1)S(1)} %get-tuple-element.98), channel_id=1, source_target_pairs={{0,1},{1,0},{2,3},{3,2},{4,5},{5,4},{6,7},{7,6},{8,9},{9,8},{10,11... | collective-permute-start | bytes 2359304 | tf_op jit(solution)/shard_map/attn_sum/ppermute | solution.py:734
  117.5 35.8 %collective-permute-start.14 = (bf16[256,1536]{1,0:T(8,128)(2,1)S(1)}, bf16[256,1536]{1,0:T(8,128)(2,1)S(1)}, u32[]{:S(2)}, u32[]{:S(2)}) collective-permute-start(bf16[256,1536]{1,0:T(8,128)(2,1)S(1)} %get-tuple-element.99), channel_id=1, source_target_pairs={{0,2},{1,3},{2,0},{3,1},{4,6},{5,7},{6,4},{7,5},{8,10},{9,11},{10,... | collective-permute-start | bytes 2359304 | tf_op jit(solution)/shard_map/attn_sum/ppermute | solution.py:734
  118.3 35.1 %collective-permute-start.15 = (bf16[256,1536]{1,0:T(8,128)(2,1)S(1)}, bf16[256,1536]{1,0:T(8,128)(2,1)S(1)}, u32[]{:S(2)}, u32[]{:S(2)}) collective-permute-start(bf16[256,1536]{1,0:T(8,128)(2,1)S(1)} %get-tuple-element.100), channel_id=1, source_target_pairs={{0,3},{1,2},{2,1},{3,0},{4,7},{5,6},{6,5},{7,4},{8,11},{9,10},{10,... | collective-permute-start | bytes 2359304 | tf_op jit(solution)/shard_map/attn_sum/ppermute | solution.py:734
  122.6 31.7 %copy-start.42 = (bf16[768,1024]{1,0:T(8,128)(2,1)}, bf16[768,1024]{1,0:T(8,128)(2,1)S(1)}, u32[]{:S(2)}) copy-start(bf16[768,1024]{1,0:T(8,128)(2,1)S(1)} %get-tuple-element.111.left_ref) | copy-start | bytes 4718596
  122.6 32.8 %copy-start.44 = (bf16[768,1024]{1,0:T(8,128)(2,1)}, bf16[768,1024]{1,0:T(8,128)(2,1)S(1)}, u32[]{:S(2)}) copy-start(bf16[768,1024]{1,0:T(8,128)(2,1)S(1)} %get-tuple-element.112.left_ref) | copy-start | bytes 4718596
  155.5 35.1 %collective-permute-start.16 = (bf16[256,1536]{1,0:T(8,128)(2,1)S(1)}, bf16[256,1536]{1,0:T(8,128)(2,1)S(1)}, u32[]{:S(2)}, u32[]{:S(2)}) collective-permute-start(bf16[256,1536]{1,0:T(8,128)(2,1)S(1)} %get-tuple-element.106.refs_0_), channel_id=1, source_target_pairs={{0,1},{1,0},{2,3},{3,2},{4,5},{5,4},{6,7},{7,6},{8,9},{9,8},{10,11... | collective-permute-start | bytes 2359304 | tf_op jit(solution)/shard_map/two_spread/ppermute | solution.py:727
  156.0 34.6 %collective-permute-start.17 = (bf16[256,1536]{1,0:T(8,128)(2,1)S(1)}, bf16[256,1536]{1,0:T(8,128)(2,1)S(1)}, u32[]{:S(2)}, u32[]{:S(2)}) collective-permute-start(bf16[256,1536]{1,0:T(8,128)(2,1)S(1)} %get-tuple-element.106.refs_0_), channel_id=1, source_target_pairs={{0,2},{1,3},{2,0},{3,1},{4,6},{5,7},{6,4},{7,5},{8,10},{9,11},{10,... | collective-permute-start | bytes 2359304 | tf_op jit(solution)/shard_map/two_spread/ppermute | solution.py:727
  157.5 33.1 %collective-permute-start.18 = (bf16[256,1536]{1,0:T(8,128)(2,1)S(1)}, bf16[256,1536]{1,0:T(8,128)(2,1)}, u32[]{:S(2)}, u32[]{:S(2)}) collective-permute-start(bf16[256,1536]{1,0:T(8,128)(2,1)S(1)} %get-tuple-element.106.refs_0_), channel_id=1, source_target_pairs={{0,3},{1,2},{2,1},{3,0},{4,7},{5,6},{6,5},{7,4},{8,11},{9,10},{10,... | collective-permute-start | bytes 2359304 | tf_op jit(solution)/shard_map/two_spread/ppermute | solution.py:727
  223.6 8.1 %collective-permute-start.19 = (bf16[768,1792]{1,0:T(8,128)(2,1)}, bf16[768,1792]{1,0:T(8,128)(2,1)}, u32[]{:S(2)}, u32[]{:S(2)}) collective-permute-start(bf16[768,1792]{1,0:T(8,128)(2,1)} %product.4), channel_id=1, source_target_pairs={{0,4},{4,0},{8,12},{12,8},{16,20},{20,16},{24,28},{28,24},{1,5},{5... | collective-permute-start | bytes 8257544 | tf_op jit(solution)/shard_map/ppermute | solution.py:699
  245.2 50.0 %collective-permute-start.24 = (bf16[768,3584]{1,0:T(8,128)(2,1)}, bf16[768,3584]{1,0:T(8,128)(2,1)}, u32[]{:S(2)}, u32[]{:S(2)}) collective-permute-start(bf16[768,3584]{1,0:T(8,128)(2,1)} %product.6), channel_id=1, source_target_pairs={{0,4},{4,0},{8,12},{12,8},{16,20},{20,16},{24,28},{28,24},{1,5},{5... | collective-permute-start | bytes 16515080 | tf_op jit(solution)/shard_map/ppermute | solution.py:699
  245.8 43.8 %collective-permute-start.20 = (bf16[192,1792]{1,0:T(8,128)(2,1)}, bf16[192,1792]{1,0:T(8,128)(2,1)}, u32[]{:S(2)}, u32[]{:S(2)}) collective-permute-start(bf16[192,1792]{1,0:T(8,128)(2,1)} %join.8), channel_id=1, source_target_pairs={{0,8},{4,12},{8,16},{12,20},{16,24},{20,28},{24,0},{28,4},{1,9},{5... | collective-permute-start | bytes 2064392 | tf_op jit(solution)/shard_map/down_grad_hop1/ppermute | solution.py:702
  273.3 22.0 %copy-start = (bf16[768,3584]{1,0:T(8,128)(2,1)}, bf16[768,3584]{1,0:T(8,128)(2,1)S(1)}, u32[]{:S(2)}) copy-start(bf16[768,3584]{1,0:T(8,128)(2,1)S(1)} %product.7.refs_0_.refs_1_) | copy-start | bytes 16515076
  291.8 20.7 %collective-permute-start.21 = (bf16[256,1536]{1,0:T(8,128)(2,1)}, bf16[256,1536]{1,0:T(8,128)(2,1)S(1)}, u32[]{:S(2)}, u32[]{:S(2)}) collective-permute-start(bf16[256,1536]{1,0:T(8,128)(2,1)} %get-tuple-element.122), channel_id=1, source_target_pairs={{0,1},{1,0},{2,3},{3,2},{4,5},{5,4},{6,7},{7,6},{8,9},{9,8},{10,11... | collective-permute-start | bytes 2359304 | tf_op jit(solution)/shard_map/two_sum/ppermute | solution.py:734
  293.4 20.1 %collective-permute-start.22 = (bf16[256,1536]{1,0:T(8,128)(2,1)S(1)}, bf16[256,1536]{1,0:T(8,128)(2,1)S(1)}, u32[]{:S(2)}, u32[]{:S(2)}) collective-permute-start(bf16[256,1536]{1,0:T(8,128)(2,1)S(1)} %get-tuple-element.123), channel_id=1, source_target_pairs={{0,2},{1,3},{2,0},{3,1},{4,6},{5,7},{6,4},{7,5},{8,10},{9,11},{10,... | collective-permute-start | bytes 2359304 | tf_op jit(solution)/shard_map/two_sum/ppermute | solution.py:734
  293.9 35.4 %collective-permute-start.23 = (bf16[256,1536]{1,0:T(8,128)(2,1)S(1)}, bf16[256,1536]{1,0:T(8,128)(2,1)S(1)}, u32[]{:S(2)}, u32[]{:S(2)}) collective-permute-start(bf16[256,1536]{1,0:T(8,128)(2,1)S(1)} %get-tuple-element.124), channel_id=1, source_target_pairs={{0,3},{1,2},{2,1},{3,0},{4,7},{5,6},{6,5},{7,4},{8,11},{9,10},{10,... | collective-permute-start | bytes 2359304 | tf_op jit(solution)/shard_map/two_sum/ppermute | solution.py:734
  297.7 31.5 %copy-start.19 = (f32[256,1536]{1,0:T(8,128)S(1)}, f32[256,1536]{1,0:T(8,128)}, u32[]{:S(2)}) copy-start(f32[256,1536]{1,0:T(8,128)} %copy-done.18) | copy-start | bytes 4718596
  297.7 31.5 %copy-start.33 = (bf16[256,1536]{1,0:T(8,128)(2,1)S(1)}, bf16[256,1536]{1,0:T(8,128)(2,1)}, u32[]{:S(2)}) copy-start(bf16[256,1536]{1,0:T(8,128)(2,1)} %rest_ref.1) | copy-start | bytes 2359300
  297.7 58.6 %collective-permute-start.28 = (bf16[192,3584]{1,0:T(8,128)(2,1)}, bf16[192,3584]{1,0:T(8,128)(2,1)}, u32[]{:S(2)}, u32[]{:S(2)}) collective-permute-start(bf16[192,3584]{1,0:T(8,128)(2,1)} %join.10), channel_id=1, source_target_pairs={{0,8},{4,12},{8,16},{12,20},{16,24},{20,28},{24,0},{28,4},{1,9},{5... | collective-permute-start | bytes 4128776 | tf_op jit(solution)/shard_map/both_grad_hop1/ppermute | solution.py:702
  309.5 21.9 %copy-start.51 = (bf16[256,1536]{1,0:T(8,128)(2,1)}, bf16[256,1536]{1,0:T(8,128)(2,1)S(1)}, u32[]{:S(2)}) copy-start(bf16[256,1536]{1,0:T(8,128)(2,1)S(1)} %get-tuple-element.127.refs_0_) | copy-start | bytes 2359300
  333.2 20.8 %collective-permute-start.25 = (bf16[256,1536]{1,0:T(8,128)(2,1)}, bf16[256,1536]{1,0:T(8,128)(2,1)}, u32[]{:S(2)}, u32[]{:S(2)}) collective-permute-start(bf16[256,1536]{1,0:T(8,128)(2,1)} %get-tuple-element.131.refs_0_), channel_id=1, source_target_pairs={{0,1},{1,0},{2,3},{3,2},{4,5},{5,4},{6,7},{7,6},{8,9},{9,8},{10,11... | collective-permute-start | bytes 2359304 | tf_op jit(solution)/shard_map/dh_spread/ppermute | solution.py:727
  333.6 18.1 %collective-permute-start.29 = (bf16[192,1792]{1,0:T(8,128)(2,1)}, bf16[192,1792]{1,0:T(8,128)(2,1)}, u32[]{:S(2)}, u32[]{:S(2)}) collective-permute-start(bf16[192,1792]{1,0:T(8,128)(2,1)} %join.9), channel_id=1, source_target_pairs={{0,8},{4,12},{8,16},{12,20},{16,24},{20,28},{24,0},{28,4},{1,9},{5... | collective-permute-start | bytes 2064392 | tf_op jit(solution)/shard_map/down_grad_hop2/ppermute | solution.py:702
  336.0 32.6 %collective-permute-start.27 = (bf16[256,1536]{1,0:T(8,128)(2,1)}, bf16[256,1536]{1,0:T(8,128)(2,1)}, u32[]{:S(2)}, u32[]{:S(2)}) collective-permute-start(bf16[256,1536]{1,0:T(8,128)(2,1)} %get-tuple-element.131.refs_0_), channel_id=1, source_target_pairs={{0,3},{1,2},{2,1},{3,0},{4,7},{5,6},{6,5},{7,4},{8,11},{9,10},{10,... | collective-permute-start | bytes 2359304 | tf_op jit(solution)/shard_map/dh_spread/ppermute | solution.py:727
  337.6 34.5 %collective-permute-start.26 = (bf16[256,1536]{1,0:T(8,128)(2,1)}, bf16[256,1536]{1,0:T(8,128)(2,1)}, u32[]{:S(2)}, u32[]{:S(2)}) collective-permute-start(bf16[256,1536]{1,0:T(8,128)(2,1)} %get-tuple-element.131.refs_0_), channel_id=1, source_target_pairs={{0,2},{1,3},{2,0},{3,1},{4,6},{5,7},{6,4},{7,5},{8,10},{9,11},{10,... | collective-permute-start | bytes 2359304 | tf_op jit(solution)/shard_map/dh_spread/ppermute | solution.py:727
  360.1 49.5 %collective-permute-start.30 = (bf16[192,3584]{1,0:T(8,128)(2,1)}, bf16[192,3584]{1,0:T(8,128)(2,1)}, u32[]{:S(2)}, u32[]{:S(2)}) collective-permute-start(bf16[192,3584]{1,0:T(8,128)(2,1)} %join.12), channel_id=1, source_target_pairs={{0,8},{4,12},{8,16},{12,20},{16,24},{20,28},{24,0},{28,4},{1,9},{5... | collective-permute-start | bytes 4128776 | tf_op jit(solution)/shard_map/both_grad_hop2/ppermute | solution.py:702
  372.1 32.9 %collective-permute-start.32 = (bf16[256,1536]{1,0:T(8,128)(2,1)}, bf16[256,1536]{1,0:T(8,128)(2,1)}, u32[]{:S(2)}, u32[]{:S(2)}) collective-permute-start(bf16[256,1536]{1,0:T(8,128)(2,1)} %get-tuple-element.146), channel_id=1, source_target_pairs={{0,1},{1,0},{2,3},{3,2},{4,5},{5,4},{6,7},{7,6},{8,9},{9,8},{10,11... | collective-permute-start | bytes 2359304 | tf_op jit(solution)/shard_map/ffn_sum/ppermute | solution.py:734
  373.7 31.4 %collective-permute-start.33 = (bf16[256,1536]{1,0:T(8,128)(2,1)}, bf16[256,1536]{1,0:T(8,128)(2,1)}, u32[]{:S(2)}, u32[]{:S(2)}) collective-permute-start(bf16[256,1536]{1,0:T(8,128)(2,1)} %get-tuple-element.147), channel_id=1, source_target_pairs={{0,2},{1,3},{2,0},{3,1},{4,6},{5,7},{6,4},{7,5},{8,10},{9,11},{10,... | collective-permute-start | bytes 2359304 | tf_op jit(solution)/shard_map/ffn_sum/ppermute | solution.py:734
  374.1 32.7 %collective-permute-start.34 = (bf16[256,1536]{1,0:T(8,128)(2,1)}, bf16[256,1536]{1,0:T(8,128)(2,1)}, u32[]{:S(2)}, u32[]{:S(2)}) collective-permute-start(bf16[256,1536]{1,0:T(8,128)(2,1)} %get-tuple-element.148), channel_id=1, source_target_pairs={{0,3},{1,2},{2,1},{3,0},{4,7},{5,6},{6,5},{7,4},{8,11},{9,10},{10,... | collective-permute-start | bytes 2359304 | tf_op jit(solution)/shard_map/ffn_sum/ppermute | solution.py:734
  375.6 29.4 %collective-permute-start.31 = (bf16[192,1792]{1,0:T(8,128)(2,1)}, bf16[192,1792]{1,0:T(8,128)(2,1)}, u32[]{:S(2)}, u32[]{:S(2)}) collective-permute-start(bf16[192,1792]{1,0:T(8,128)(2,1)} %join.11), channel_id=1, source_target_pairs={{0,8},{4,12},{8,16},{12,20},{16,24},{20,28},{24,0},{28,4},{1,9},{5... | collective-permute-start | bytes 2064392 | tf_op jit(solution)/shard_map/down_grad_hop3/ppermute | solution.py:702
  379.8 19.1 %copy-start.25 = (f32[1024,128]{1,0:T(8,128)S(1)}, f32[1024,128]{1,0:T(8,128)}, u32[]{:S(2)}) copy-start(f32[1024,128]{1,0:T(8,128)} %copy-done.24) | copy-start | bytes 1572868
  379.8 19.1 %copy-start.27 = (f32[1024,128]{1,0:T(8,128)S(1)}, f32[1024,128]{1,0:T(8,128)}, u32[]{:S(2)}) copy-start(f32[1024,128]{1,0:T(8,128)} %copy-done.26) | copy-start | bytes 1572868
  379.9 19.1 %copy-start.35 = (f32[1024,512]{1,0:T(8,128)S(1)}, f32[1024,512]{1,0:T(8,128)}, u32[]{:S(2)}) copy-start(f32[1024,512]{1,0:T(8,128)} %copy-done.34) | copy-start | bytes 6291460
  425.2 56.9 %collective-permute-start.40 = (bf16[192,3584]{1,0:T(8,128)(2,1)}, bf16[192,3584]{1,0:T(8,128)(2,1)}, u32[]{:S(2)}, u32[]{:S(2)}) collective-permute-start(bf16[192,3584]{1,0:T(8,128)(2,1)} %copy-done.46), channel_id=1, source_target_pairs={{0,8},{4,12},{8,16},{12,20},{16,24},{20,28},{24,0},{28,4},{1,9},{5... | collective-permute-start | bytes 4128776 | tf_op jit(solution)/shard_map/both_grad_hop3/ppermute | solution.py:702
  431.6 50.5 %slice-start.2 = ((s8[5505024]{0:T(1024)(128)(4,1)}), s8[1310720]{0:T(1024)(128)(4,1)S(1)}, s32[]{:S(2)}) async-start(s8[5505024]{0:T(1024)(128)(4,1)} %bitcast.51), calls=%async_computation.5 | async-start | bytes 2621440
  432.5 4.2 collective-permute-start.38
  433.2 33.7 %collective-permute-start.35 = (bf16[256,1536]{1,0:T(8,128)(2,1)}, bf16[256,1536]{1,0:T(8,128)(2,1)S(1)}, u32[]{:S(2)}, u32[]{:S(2)}) collective-permute-start(bf16[256,1536]{1,0:T(8,128)(2,1)} %copy-done.55), channel_id=1, source_target_pairs={{0,1},{1,0},{2,3},{3,2},{4,5},{5,4},{6,7},{7,6},{8,9},{9,8},{10,11... | collective-permute-start | bytes 2359304 | tf_op jit(solution)/shard_map/one_sum/ppermute | solution.py:734
  434.6 32.3 %collective-permute-start.36 = (bf16[256,1536]{1,0:T(8,128)(2,1)}, bf16[256,1536]{1,0:T(8,128)(2,1)S(1)}, u32[]{:S(2)}, u32[]{:S(2)}) collective-permute-start(bf16[256,1536]{1,0:T(8,128)(2,1)} %copy-done.53), channel_id=1, source_target_pairs={{0,2},{1,3},{2,0},{3,1},{4,6},{5,7},{6,4},{7,5},{8,10},{9,11},{10,... | collective-permute-start | bytes 2359304 | tf_op jit(solution)/shard_map/one_sum/ppermute | solution.py:734
  435.3 31.6 %collective-permute-start.37 = (bf16[256,1536]{1,0:T(8,128)(2,1)}, bf16[256,1536]{1,0:T(8,128)(2,1)S(1)}, u32[]{:S(2)}, u32[]{:S(2)}) collective-permute-start(bf16[256,1536]{1,0:T(8,128)(2,1)} %copy-done.57), channel_id=1, source_target_pairs={{0,3},{1,2},{2,1},{3,0},{4,7},{5,6},{6,5},{7,4},{8,11},{9,10},{10,... | collective-permute-start | bytes 2359304 | tf_op jit(solution)/shard_map/one_sum/ppermute | solution.py:734
  436.8 45.4 %slice-start.3 = ((s8[5505024]{0:T(1024)(128)(4,1)}), s8[4194304]{0:T(1024)(128)(4,1)S(1)}, s32[]{:S(2)}) async-start(s8[5505024]{0:T(1024)(128)(4,1)} %bitcast.51), calls=%async_computation.6 | async-start | bytes 8388608
  436.8 30.1 %collective-permute-start.39 = (f32[1,3200]{1,0:T(1,128)S(1)}, f32[1,3200]{1,0:T(1,128)S(1)}, u32[]{:S(2)}, u32[]{:S(2)}) collective-permute-start(f32[1,3200]{1,0:T(1,128)S(1)} %reshape_add_fusion), channel_id=1, source_target_pairs={{0,2},{1,3},{2,0},{3,1},{4,6},{5,7},{6,4},{7,5},{8,10},{9,11},{10,... | collective-permute-start | bytes 38408 | tf_op jit(solution)/shard_map/ppermute | solution.py:891
  441.1 25.9 %copy-start.37 = (f32[256,1536]{1,0:T(8,128)S(1)}, f32[256,1536]{1,0:T(8,128)}, u32[]{:S(2)}) copy-start(f32[256,1536]{1,0:T(8,128)} %copy-done.36) | copy-start | bytes 4718596
  484.3 1.2 collective-permute-start.41
  485.5 3.8 collective-permute-start.42
  489.3 4.7 collective-permute-start.43
  (59 other events, 233.5 us)
Sparse Core Ops, SparseCore 0:
  11.6 168.3 all-gather.1
  425.4 60.6 reduce-scatter.1

commit v3 on v2

--- a/solution.py
+++ b/solution.py
@@ -188,7 +188,11 @@
             jax.ShapeDtypeStruct((ranks, heads, GROUP * rows), F32),
         ],
         compiler_params=pltpu.CompilerParams(vmem_limit_bytes=48 * 2**20),
-        cost_estimate=FREE,
+        cost_estimate=pl.CostEstimate(
+            flops=16 * length * length * heads * GROUP * HEAD_SIZE,
+            bytes_accessed=32 * 2**20,
+            transcendentals=length * length * heads * GROUP,
+        ),
         name="attend",
     )(me, queries, keys, values, bounds)
 
@@ -316,7 +320,7 @@
         ],
         out_specs=pl.BlockSpec((depth, tile), lambda i: (0, i)),
         out_shape=jax.ShapeDtypeStruct((depth, cols * len(rights)), LOW),
-        compiler_params=pltpu.CompilerParams(vmem_limit_bytes=32 * 2**20),
+        compiler_params=pltpu.CompilerParams(vmem_limit_bytes=40 * 2**20),
         cost_estimate=FREE,
         name="product",
     )(left, *rights)
@@ -369,7 +373,7 @@
         + [pl.BlockSpec((1, tile, cols), lambda i, k=k: (k, i, 0)) for k in which],
         out_specs=[pl.BlockSpec((rows, tile), lambda i: (0, i))] * ranks,
         out_shape=[jax.ShapeDtypeStruct((rows, width), LOW)] * ranks,
-        compiler_params=pltpu.CompilerParams(vmem_limit_bytes=40 * 2**20),
+        compiler_params=pltpu.CompilerParams(vmem_limit_bytes=56 * 2**20),
         cost_estimate=FREE,
         name="back_parts",
     )(*lefts, *([weights] * len(which)))
@@ -397,10 +401,60 @@
             out_specs=row,
         ),
         out_shape=jax.ShapeDtypeStruct((depth, cols), dtype),
-        compiler_params=pltpu.CompilerParams(vmem_limit_bytes=24 * 2**20),
+        compiler_params=pltpu.CompilerParams(vmem_limit_bytes=56 * 2**20),
         cost_estimate=FREE,
         name="join",
     )(owner.astype(jnp.int32).reshape(1), *flows, near, other)
+
+
+def last_join_kernel(at_ref, flow_ref, near_ref, other_ref, *out_refs):
+    total = flow_ref[...].astype(F32) + near_ref[...].astype(F32) + other_ref[...].astype(F32)
+    width = total.shape[1] // len(out_refs)
+    for k, out_ref in enumerate(out_refs):
+        cols = out_ref.shape[1]
+        out_ref[...] = total[:, k * width : k * width + cols]
+
+
+def last_join(owner, flow, near, other, ring, cols, count):
+    depth, wide = near.shape[0] // ring, near.shape[1]
+    chosen = pl.BlockSpec((depth, wide), lambda i, at: (at[0], 0))
+    return pl.pallas_call(
+        last_join_kernel,
+        grid_spec=pltpu.PrefetchScalarGridSpec(
+            num_scalar_prefetch=1,
+            grid=(1,),
+            in_specs=[pl.BlockSpec((depth, wide), lambda i, at: (0, 0)), chosen, chosen],
+            out_specs=[pl.BlockSpec((depth, cols), lambda i, at: (0, 0))] * count,
+        ),
+        out_shape=[jax.ShapeDtypeStruct((depth, cols), F32)] * count,
+        compiler_params=pltpu.CompilerParams(vmem_limit_bytes=56 * 2**20),
+        cost_estimate=FREE,
+        name="last_join",
+    )(owner.astype(jnp.int32).reshape(1), flow, near, other)
+
+
+def cut_kernel(widths, grads_ref, *out_refs):
+    first = 0
+    for cols, out_ref in zip(widths[:-1], out_refs):
+        out_ref[...] = grads_ref[:, first : first + cols].astype(F32)
+        first += cols
+    out_refs[-1][...] = grads_ref[:, first : first + widths[-1]].astype(F32).T
+
+
+def cut_grads(grads, widths):
+    depth = grads.shape[0]
+    whole = lambda shape: pl.BlockSpec(shape, lambda i: (0, 0))
+    shapes = [(depth, cols) for cols in widths[:-1]] + [(widths[-1], depth)]
+    return pl.pallas_call(
+        functools.partial(cut_kernel, widths),
+        grid=(1,),
+        in_specs=[whole(grads.shape)],
+        out_specs=[whole(shape) for shape in shapes],
+        out_shape=[jax.ShapeDtypeStruct(shape, F32) for shape in shapes],
+        compiler_params=pltpu.CompilerParams(vmem_limit_bytes=24 * 2**20),
+        cost_estimate=FREE,
+        name="cut_grads",
+    )(grads)
 
 
 def sum_kernel(count, base_ref, *refs):
@@ -430,7 +484,7 @@
         in_specs=[by_row] * (1 + len(parts)) + [pl.BlockSpec((1, width), lambda i: (0, 0))] * len(gains),
         out_specs=[by_row] * len(outs),
         out_shape=outs,
-        compiler_params=pltpu.CompilerParams(vmem_limit_bytes=24 * 2**20),
+        compiler_params=pltpu.CompilerParams(vmem_limit_bytes=56 * 2**20),
         cost_estimate=FREE,
         name="sum_up",
     )(base, *parts, *gains)
@@ -472,14 +526,14 @@
         in_specs=[by_row, fixed, by_row] + [by_row] * len(parts),
         out_specs=[by_row, by_row, fixed][: len(shapes)],
         out_shape=shapes,
-        compiler_params=pltpu.CompilerParams(vmem_limit_bytes=24 * 2**20),
+        compiler_params=pltpu.CompilerParams(vmem_limit_bytes=56 * 2**20),
         cost_estimate=FREE,
         name="norm_back_sum",
     )(value, gain.reshape(1, -1), rest, *parts)
 
 
 def rows_product_kernel(left_ref, right_ref, out_ref):
-    out_ref[...] = jnp.dot(left_ref[...], right_ref[...], preferred_element_type=F32).astype(LOW)
+    out_ref[...] = jnp.dot(left_ref[...], right_ref[0], preferred_element_type=F32).astype(LOW)
 
 
 def rows_product(left, right, ranks):
@@ -490,40 +544,42 @@
         grid=(ranks,),
         in_specs=[
             pl.BlockSpec((rows, depth), lambda i: (i, 0)),
-            pl.BlockSpec(right.shape, lambda i: (0, 0)),
+            pl.BlockSpec((1,) + right.shape[1:], lambda i: (0, 0, 0)),
         ],
-        out_specs=pl.BlockSpec((rows, right.shape[1]), lambda i: (i, 0)),
-        out_shape=jax.ShapeDtypeStruct((length, right.shape[1]), LOW),
+        out_specs=pl.BlockSpec((rows, right.shape[2]), lambda i: (i, 0)),
+        out_shape=jax.ShapeDtypeStruct((length, right.shape[2]), LOW),
         compiler_params=pltpu.CompilerParams(vmem_limit_bytes=24 * 2**20),
         cost_estimate=FREE,
         name="rows_product",
     )(left, right)
 
 
-def gain_part_kernel(normed_ref, gain_ref, *refs):
-    rows = refs[0].shape[0]
-    total = jnp.zeros(refs[-1].shape, F32)
-    for j, ref in enumerate(refs[:-1]):
+def gain_parts_kernel(normed_ref, gain_ref, two_ref, heads_ref, *refs):
+    parts, out_ref = refs[:-1], refs[-1]
+    rows, width = parts[0].shape
+    total = jnp.zeros((1, width), F32)
+    for j, ref in enumerate(parts):
         block = normed_ref[j * rows : (j + 1) * rows, :].astype(F32)
         total = total + jnp.sum(block * ref[...].astype(F32), axis=0, keepdims=True)
-    refs[-1][...] = total / gain_ref[...]
-
-
-def gain_part(normed, gain, parts):
-    width = normed.shape[1]
-    tile = 512
-    column = lambda a: pl.BlockSpec((a.shape[0], tile), lambda i: (0, i))
-    row = gain.reshape(1, -1)
-    return pl.pallas_call(
-        gain_part_kernel,
-        grid=(width // tile,),
-        in_specs=[column(normed), column(row)] + [column(part) for part in parts],
-        out_specs=column(row),
-        out_shape=jax.ShapeDtypeStruct((1, width), F32),
-        compiler_params=pltpu.CompilerParams(vmem_limit_bytes=24 * 2**20),
-        cost_estimate=FREE,
-        name="gain_part",
-    )(normed, row, *parts)
+    out_ref[:, :width] = total / gain_ref[...]
+    out_ref[:, width : 2 * width] = two_ref[...]
+    out_ref[:, 2 * width :] = heads_ref[...]
+
+
+def gain_parts(normed, gain, parts, two, heads):
+    args = [normed, gain.reshape(1, -1), two, heads, *parts]
+    whole = lambda a: pl.BlockSpec(a.shape, lambda i: (0, 0))
+    shape = jax.ShapeDtypeStruct((1, 2 * normed.shape[1] + heads.shape[1]), F32)
+    return pl.pallas_call(
+        gain_parts_kernel,
+        grid=(1,),
+        in_specs=[whole(a) for a in args],
+        out_specs=whole(shape),
+        out_shape=shape,
+        compiler_params=pltpu.CompilerParams(vmem_limit_bytes=56 * 2**20),
+        cost_estimate=FREE,
+        name="gain_parts",
+    )(*args)
 
 
 def group_mean(values):
@@ -652,7 +708,7 @@
             jax.ShapeDtypeStruct((length, q_cols + 2 * kv_cols), LOW),
             jax.ShapeDtypeStruct((1, q_cols + kv_cols), F32),
         ],
-        compiler_params=pltpu.CompilerParams(vmem_limit_bytes=40 * 2**20),
+        compiler_params=pltpu.CompilerParams(vmem_limit_bytes=56 * 2**20),
         cost_estimate=FREE,
         name="prepare_back",
     )(d_queries, d_keys, d_values, raw, cosine, sine, gains)
@@ -704,16 +760,6 @@
     core_array = core.astype(jnp.int32).reshape(1)
     at = jnp.stack([stage, core]).astype(jnp.int32)
 
-    def ring_gather(label, block):
-        blocks = []
-        for hop in range(ring):
-            with jax.named_scope(f"{label}_swap{hop}"):
-                blocks += [block, swap(block)]
-            if hop < ring - 1:
-                with jax.named_scope(f"{label}_hop{hop + 1}"):
-                    block = onward(block)
-        return blocks
-
     def hop(label, block):
         with jax.named_scope(label):
             return onward(block)
@@ -750,14 +796,24 @@
     tokens_wide = tokens.astype(F32)
     normed_own = norm_rows(tokens_wide, attn_gain).astype(LOW)
     normed_one = spread("one_spread", normed_own)
-    a_blocks = ring_gather("attn", jnp.concatenate([w_query, key_weight, value_weight, w_out.T], axis=1))
+    wide = hidden_cols + hidden_pad
     ffn_full = lax.all_gather(
         jnp.stack([widen(w_down.T), widen(w_gate), widen(w_up)]), "dp", axis=1, tiled=True
     )
+    gate_full, up_full = ffn_full[1], ffn_full[2]
+    qkv_blocks = [jnp.concatenate([w_query, key_weight, value_weight], axis=1)]
+    for count in range(1, ring):
+        qkv_blocks.append(hop(f"qkv_hop{count}", qkv_blocks[-1]))
+    out_blocks = [w_out.T]
+    for count in range(1, ring):
+        out_flow = hop(f"out_hop{count}", out_blocks[-1])
+        if count < ring - 1:
+            out_blocks.append(tie(out_flow, qkv_blocks[count + 1]))
+
+    def complete(blocks):
+        return place(at, [b for block in blocks for b in (block, swap(block))], ring)
+
     grad_blocks = spread("cot_spread", tie(cotangent, *normed_one))
-    wide = hidden_cols + hidden_pad
-    down_t, gate_full, up_full = ffn_full[0], ffn_full[1], ffn_full[2]
-
     first_start = jnp.sum((segments < 1).astype(jnp.int32))
     second_start = jnp.sum((segments < 2).astype(jnp.int32))
     ids = jnp.arange(length, dtype=jnp.int32).reshape(ranks, rows)
@@ -779,10 +835,7 @@
     ).reshape(1, -1)
 
     normed_all, normed_one_t = fold(core_array, normed_one, ring)
-    a_blocks[-2] = tie(a_blocks[-2], normed_all, cosine, sine)
-    attn_full = place(at, a_blocks, ring)
-    w_qkv = attn_full[:, : q_cols + 2 * kv_cols]
-    out_t = attn_full[:, q_cols + 2 * kv_cols :]
+    w_qkv = complete(qkv_blocks)
     query_low, key_low, value_low, raw = prepare(
         normed_all, w_qkv, cosine, sine, head_gains, q_cols, kv_cols, ranks
     )
@@ -790,15 +843,15 @@
     attended, lse = attend(me_array, query_low, key_low, value_low, bounds, ranks, heads)
 
     attended_go = tie(attended, *grad_blocks)
+    out_blocks.append(tie(out_flow, attended))
+    out_t = complete(out_blocks)
     attn_parts = back_parts([attended_go], out_t[None], (0,), ranks)
     attn_arrived = send_parts("attn_sum", attn_parts)
-    grad_all, *grad_pair = fold(
-        core_array, [tie(grad_blocks[0], *attn_parts)] + grad_blocks[1:], ring, True
-    )
+    grad_all, grad_t = fold(core_array, [tie(grad_blocks[0], *attn_parts)] + grad_blocks[1:], ring)
     attn_arrived[0] = tie(attn_arrived[0], grad_all)
     hidden, normed_two_own = sum_up(tokens, [attn_parts[0]] + attn_arrived, ffn_gain)
     normed_two = spread("two_spread", normed_two_own)
-    d_activation = mm(grad_all, down_t).astype(LOW)
+    d_activation = rows_product(grad_all, ffn_full, ranks)
     normed_two[-1] = tie(normed_two[-1], d_activation)
     normed_two_all, *normed_two_pair = fold(core_array, normed_two, ring, True)
 
@@ -824,89 +877,82 @@
             block, flow = advance(label, tie(flow, *after), near, other, count)
         return block, flow
 
-    down_far = product(grad_pair[0], [activation])
-    down_other = swap(down_far)
-    down_near = product(grad_pair[1], [tie(activation, down_far)])
-    down_block, down_flow = advance("down_grad", None, down_near, down_other, 0)
-    both_far = product(normed_two_pair[0], [tie(d_gating, down_block), d_lifted])
+    down_full_grad = product(grad_t, [activation])
+    down_grad = lax.psum_scatter(down_full_grad, "dp", scatter_dimension=0, tiled=True)
+    two_parts = back_parts([tie(d_gating, down_full_grad), d_lifted], ffn_full, (1, 2), ranks)
+    two_arrived = send_parts("two_sum", two_parts)
+    both_far = product(normed_two_pair[0], [tie(d_gating, *two_parts), d_lifted])
+    both_near = product(normed_two_pair[1], [tie(d_gating, both_far), d_lifted])
+    *two_arrived, both_far, both_near = lax.optimization_barrier((*two_arrived, both_far, both_near))
     both_other = swap(both_far)
-    both_near = product(normed_two_pair[1], [tie(d_gating, both_far), d_lifted])
-    two_parts = back_parts([tie(d_gating, both_near), d_lifted], ffn_full, (1, 2), ranks)
-    down_block, down_flow = advance("down_grad", tie(down_flow, *two_parts), down_near, down_other, 1)
-    two_go = lax.optimization_barrier(tuple(two_parts) + (down_block,))[:-1]
-    two_arrived = send_parts("two_sum", two_go)
-    both_block, both_flow = advance("both_grad", None, tie(both_near, *two_go), both_other, 0)
-    ffn_parts = back_parts([tie(activation, both_block)], ffn_full, (0,), ranks)
-    two_arrived = list(lax.optimization_barrier(tuple(two_arrived) + (ffn_parts[0],))[:-1])
     d_hidden, d_hidden_low, ffn_gain_part = norm_back_sum(
         hidden, ffn_gain, cotangent, [two_parts[0]] + two_arrived, True
     )
     hidden_grad = spread("dh_spread", d_hidden_low)
-    down_block, down_flow = several(
-        "down_grad", down_block, down_flow, down_near, down_other, 2, last, hidden_grad[1]
-    )
+    both_block, both_flow = advance("both_grad", None, tie(both_near, d_hidden_low), both_other, 0)
+    ffn_parts = back_parts([tie(activation, d_hidden_low)], ffn_full, (0,), ranks)
+    hidden_grad[1] = tie(hidden_grad[1], *ffn_parts)
     both_block, both_flow = several(
-        "both_grad", both_block, both_flow, both_near, both_other, 1, last - 1, hidden_grad[1], down_block
+        "both_grad", both_block, both_flow, both_near, both_other, 1, last - 1, hidden_grad[1]
     )
     hidden_grad[-1] = tie(hidden_grad[-1], both_block)
     hidden_grad_all, hidden_grad_t = fold(core_array, hidden_grad, ring)
     ffn_go = lax.optimization_barrier(tuple(ffn_parts) + tuple(hidden_grad))[:ranks]
     ffn_arrived = send_parts("ffn_sum", ffn_go)
-    d_attended = rows_product(hidden_grad_all, out_t, ranks)
+    d_attended = rows_product(hidden_grad_all, out_t[None], ranks)
     d_queries, d_keys, d_values = attend_back(
         me_array, query_low, key_low, value_low, bounds, attended, d_attended, lse, ranks, heads
     )
     d_raw, head_gain_parts = prepare_back(
         d_queries, d_keys, d_values, raw, cosine, sine, head_gains, ranks
     )
-    down_grad, _ = advance("down_grad", tie(down_flow, *ffn_arrived), down_near, down_other, last)
     both_block, both_flow = advance(
-        "both_grad", tie(both_flow, down_grad), both_near, both_other, last - 1
+        "both_grad", tie(both_flow, *ffn_arrived), both_near, both_other, last - 1
     )
     one_parts = back_parts([tie(d_raw, both_block, *ffn_arrived)], w_qkv[None], (0,), ranks)
     one_arrived = send_parts("one_sum", one_parts)
     attn_full_grad = attn_products([normed_one_t, hidden_grad_t], [tie(d_raw, *one_parts), attended])
-    attn_grad = lax.psum_scatter(attn_full_grad, "dp", scatter_dimension=0, tiled=True).astype(F32)
-    attn_gain_part = gain_part(tie(normed_all, attn_full_grad), attn_gain, one_parts).reshape(-1)
-    (output,) = sum_up(tie(hidden, attn_gain_part), [ffn_parts[0]] + ffn_arrived)
-    one_arrived[-1] = tie(one_arrived[-1], output)
+    attn_grad = lax.psum_scatter(
+        tie(attn_full_grad, down_grad), "dp", scatter_dimension=0, tiled=True)
+    gains = gain_parts(
+        tie(normed_all, attn_full_grad), attn_gain, one_parts, ffn_gain_part, head_gain_parts
+    )
+    (output,) = sum_up(tie(hidden, gains), [ffn_parts[0]] + ffn_arrived)
+
+    def exchange_sum(own, axis, offsets, size):
+        pieces = [own] + [lax.ppermute(own, axis, [(i, i ^ j) for i in range(size)]) for j in offsets]
+        while len(pieces) > 1:
+            pieces = [a + b for a, b in zip(pieces[::2], pieces[1::2])]
+        return pieces[0]
+
+    total = exchange_sum(gains, "tensor", range(1, ranks), ranks)
+    one_arrived[-1] = tie(one_arrived[-1], output, total)
     (tokens_grad,) = norm_back_sum(tokens, attn_gain, d_hidden, [one_parts[0]] + one_arrived, False)
-    both_grad, _ = advance("both_grad", tie(both_flow, tokens_grad), both_near, both_other, last)
-    qkv_cols = q_cols + 2 * kv_cols
-    qkv_grad = attn_grad[:, :qkv_cols]
-    out_grad = attn_grad[:, qkv_cols:]
-    down_grad = down_grad[:, :hidden_cols]
-    gate_grad = both_grad[:, :hidden_cols]
-    lift_grad = both_grad[:, wide : wide + hidden_cols]
-
-    head_gain_parts = head_gain_parts.reshape(-1, HEAD_SIZE)
-    query_gain_part = jnp.sum(head_gain_parts[: q_cols // HEAD_SIZE], axis=0)
-    key_gain_part = jnp.sum(head_gain_parts[q_cols // HEAD_SIZE :], axis=0)
-    sizes = [attn_gain.shape[0], ffn_gain.shape[0], HEAD_SIZE, HEAD_SIZE]
-    gains = jnp.concatenate([attn_gain_part, ffn_gain_part.reshape(-1), query_gain_part, key_gain_part])
-    gains = gains.reshape(1, -1)
-    total = gains
-    span = 1
-    while span < ranks:
-        total = total + lax.ppermute(total, "tensor", [(i, i ^ span) for i in range(ranks)])
-        span *= 2
-    total = tie(total, both_grad, tokens_grad)
-    span = 1
-    while span < dp_size:
-        total = total + lax.ppermute(total, "dp", [(i, i ^ span) for i in range(dp_size)])
-        span *= 2
+    gate_grad, lift_grad = last_join(
+        owner_after(last), tie(both_flow, tokens_grad), both_near, both_other, ring, hidden_cols, 2
+    )
+    query_grad, key_grad, value_grad, out_grad = cut_grads(
+        attn_grad, (q_cols, kv_cols, kv_cols, q_cols)
+    )
+    down_grad = down_grad[:, :hidden_cols].astype(F32)
+
+    total = tie(total, gate_grad, tokens_grad)
+    total = exchange_sum(total, "dp", range(1, 2), dp_size)
+    total = exchange_sum(total, "dp", range(2, dp_size, 2), dp_size)
     total = total.reshape(-1)
-    a, b = sizes[0], sizes[0] + sizes[1]
+    a, b = attn_gain.shape[0], 2 * attn_gain.shape[0]
+    query_gain_grad = jnp.sum(total[b : b + q_cols].reshape(-1, HEAD_SIZE), axis=0)
+    key_gain_grad = jnp.sum(total[b + q_cols :].reshape(-1, HEAD_SIZE), axis=0)
     return (
         output,
         tokens_grad,
         total[:a],
-        qkv_grad[:, :q_cols],
-        qkv_grad[:, q_cols : q_cols + kv_cols],
-        qkv_grad[:, q_cols + kv_cols :],
-        total[b : b + HEAD_SIZE],
-        total[b + HEAD_SIZE :],
-        out_grad.T,
+        query_grad,
+        key_grad,
+        value_grad,
+        query_gain_grad,
+        key_gain_grad,
+        out_grad,
         total[a:b],
         gate_grad,
         lift_grad,

time: 513 us -> 489 us (0.953)
  waiting for transfers between devices: 190 us -> 155 us
  Pallas kernels: 150 us -> 175 us
  matrix products: 31.3 us -> 22.6 us
  local copies, waits for them, and re-layouts: 49.5 us -> 42.9 us
    ppermute x5 -> x7, waiting for transfers between devices: 29.6 us -> 2.88 us  [exchange_sum(): lax.ppermute(own, axis, [(i, i ^ j) for i in range(size)])]
    ppermute x12, waiting for transfers between devices: 52.3 us -> 67.4 us  [send_parts(): lax.ppermute(parts[j], 'tensor', [(i, i ^ j) for i in range(ranks)])]
    ppermute x9, waiting for transfers between devices: 63 us -> 51.3 us  [onward(): return lax.ppermute(v, 'dp', ring_pairs)]
    ppermute x12, waiting for transfers between devices: 24.1 us -> 14.8 us  [spread(): lax.ppermute(block, 'tensor', [(i, i ^ j) for i in range(ranks)])]
    dot_general x3 -> x2, matrix products: 31.3 us -> 22.6 us  [mm(): return jnp.dot(left, right, preferred_element_type=F32)]
    pallas_call x8 -> x3, Pallas kernels: 17.9 us -> 9.43 us  [join(): pl.pallas_call(functools.partial(join_kernel, len(flows)), grid_spec=pltp...]
    pallas_call x1 -> x3, Pallas kernels: 0.82 us -> 8.95 us  [the longest x1 4.1 us: gain_parts(): pl.pallas_call(gain_parts_kernel, grid=(1,), in_specs=[whole(a) for a in...]
    all_gather x1, waiting for transfers between devices: 21 us -> 13 us  [shards(): lax.all_gather(jnp.stack([widen(w_down.T), widen(w_gate), widen(w_up)]),...]
  transfers between devices with their start and end apart: 46 -> 52, of which waited for: 24 -> 21; matrix products, arithmetic and copies ran while one was open for 5% -> 2% of each run, Pallas kernels for 23% -> 34%
where the time goes in v3:
time: 489 us; the launch traced here: 483 us
  Pallas kernels  175 us (36%)
  waiting for transfers between devices  155 us (32%)
  starting transfers between devices  62.9 us (13%)
  local copies, waits for them, and re-layouts  42.9 us (9%)
  matrix products  22.6 us (5%)
  between operations  15.1 us (3%)
  other arithmetic  9.14 us (2%)
    ppermute x12, waiting for transfers between devices, send_parts(): lax.ppermute(parts[j], 'tensor', [(i, i ^ j) for i in range(ranks)])  67.4 us
    ppermute x9, waiting for transfers between devices, onward(): return lax.ppermute(v, 'dp', ring_pairs)  51.3 us
    pallas_call x4, Pallas kernels, back_parts(): pl.pallas_call(functools.partial(back_parts_kernel, rows, len(lefts)), gr...  40.5 us
    unnamed x146, local copies, waits for them, and re-layouts  37.5 us
    pallas_call x3, Pallas kernels, product(): pl.pallas_call(functools.partial(product_kernel, tiles), grid=(tiles * le...  27.8 us
    ppermute x9, starting transfers between devices, onward(): return lax.ppermute(v, 'dp', ring_pairs)  24.8 us
    dot_general x2, matrix products, mm(): return jnp.dot(left, right, preferred_element_type=F32)  22.6 us
    pallas_call x1, Pallas kernels, attend_back(): pl.pallas_call(functools.partial(attend_back_kernel, heads, rows), grid_s...  16.7 us
  transfers between devices with their start and end apart: 52, of which 21 were waited for; matrix products, arithmetic and copies ran while one was open for 2% of the time, Pallas kernels for 34%

profile of v3, /device:TPU:0, one launch (start us, length us, event | category | flops | bytes accessed | tf_op | source)
XLA Modules:
  0.0 482.8 jit_solution(14467578944591292036)
XLA Ops:
  11.6 3.1 collective-permute-start.4
  15.2 2.5 collective-permute-start.2
  21.0 2.5 collective-permute-done.4.refs_2_
  25.0 12.8 %collective-permute-done.6.refs_4_ = bf16[192,640]{1,0:T(8,128)(2,1)} collective-permute-done((bf16[192,640]{1,0:T(8,128)(2,1)}, bf16[192,640]{1,0:T(8,128)(2,1)}, u32[]{:S(2)}, u32[]{:S(2)}) %collective-permute-start.6) | collective-permute-done | bytes 245792 | tf_op jit(solution)/shard_map/qkv_hop2/ppermute | solution.py:758
  37.8 2.9 collective-permute-start.8
  40.7 2.5 collective-permute-start.16
  43.4 15.8 %collective-permute-done.16.refs_4_ = bf16[192,384]{1,0:T(8,128)(2,1)} collective-permute-done((bf16[192,384]{1,0:T(8,128)(2,1)S(1)}, bf16[192,384]{1,0:T(8,128)(2,1)}, u32[]{:S(2)}, u32[]{:S(2)}) %collective-permute-start.16) | collective-permute-done | bytes 147488 | tf_op jit(solution)/shard_map/out_hop2/ppermute | solution.py:758
  60.5 10.8 %collective-permute-start.18 = (bf16[192,384]{1,0:T(8,128)(2,1)}, bf16[192,384]{1,0:T(8,128)(2,1)S(1)}, u32[]{:S(2)}, u32[]{:S(2)}) collective-permute-start(bf16[192,384]{1,0:T(8,128)(2,1)} %collective-permute-done.16.refs_4_), channel_id=1, source_target_pairs={{0,8},{4,12},{8,16},{12,20},{16,24},{20,28},{24,0},{28,4},{1,9},{5... | collective-permute-start | bytes 442376 | tf_op jit(solution)/shard_map/out_hop3/ppermute | solution.py:758
  71.6 1.9 fusion.14
  73.6 2.6 collective-permute-start.12
  79.1 2.4 fold.4
  83.2 2.7 place.2.w_ref
  85.9 5.5 %prepare.1 = (bf16[1024,384]{1,0:T(8,128)(2,1)S(1)}, bf16[1024,128]{1,0:T(8,128)(2,1)S(1)}, bf16[1024,128]{1,0:T(8,128)(2,1)S(1)}, f32[1024,512]{1,0:T(8,128)S(1)}) custom-call(bf16[1024,1536]{1,0:T(8,128)(2,1)S(1)} %get-tuple-element.158.x_ref.normed_ref, bf16[1536,640]{1,0:T(8,128)(2,1)S(1)} %place.2.w_ref, f32[1024,128]{1,0:T(8,128)S(1)} %get-tuple-element.194.cos_ref, ...), custom_call_target="tpu_custom_call" | custom-call | tf_op jit(solution)/shard_map/prepare/pallas_call | solution.py:637
  94.7 12.8 %attend.1 = (bf16[1024,384]{1,0:T(8,128)(2,1)S(1)}, f32[4,2,768]{2,1,0:T(2,128)S(1)}) custom-call(s32[1]{0:T(128)} %bitcast.me_ref, bf16[1024,384]{1,0:T(8,128)(2,1)S(1)} %get-tuple-element.94.q_ref, bf16[1024,128]{1,0:T(8,128)(2,1)S(1)} %get-tuple-element.95.k_ref, bf16[1024,128]{1,0:T(8,128)(2,1)S(1)} %get-tuple-element.96.v_ref, ...), custom_call_target="tpu_custom_call" | custom-call | flops 6442450944 | bytes 33554432 | tf_op jit(solution)/shard_map/attend/pallas_call | solution.py:178
  109.2 2.3 place.3
  112.6 6.0 %back_parts.4 = (bf16[256,1536]{1,0:T(8,128)(2,1)}, bf16[256,1536]{1,0:T(8,128)(2,1)}, bf16[256,1536]{1,0:T(8,128)(2,1)}, bf16[256,1536]{1,0:T(8,128)(2,1)}) custom-call(bf16[1024,384]{1,0:T(8,128)(2,1)} %copy-done.10, bf16[1,1536,384]{2,1,0:T(8,128)(2,1)} %bitcast.36), custom_call_target="tpu_custom_call" | custom-call | tf_op jit(solution)/shard_map/back_parts/pallas_call | solution.py:369
  118.5 1.6 collective-permute-start.20
  122.6 2.6 fold.5
  126.9 12.2 %collective-permute-done.20.refs_1_ = bf16[256,1536]{1,0:T(8,128)(2,1)S(1)} collective-permute-done((bf16[256,1536]{1,0:T(8,128)(2,1)}, bf16[256,1536]{1,0:T(8,128)(2,1)S(1)}, u32[]{:S(2)}, u32[]{:S(2)}) %collective-permute-start.20) | collective-permute-done | bytes 786464 | tf_op jit(solution)/shard_map/attn_sum/ppermute | solution.py:780
  139.1 17.6 %collective-permute-done.21.refs_2_ = bf16[256,1536]{1,0:T(8,128)(2,1)S(1)} collective-permute-done((bf16[256,1536]{1,0:T(8,128)(2,1)}, bf16[256,1536]{1,0:T(8,128)(2,1)S(1)}, u32[]{:S(2)}, u32[]{:S(2)}) %collective-permute-start.21) | collective-permute-done | bytes 786464 | tf_op jit(solution)/shard_map/attn_sum/ppermute | solution.py:780
  158.5 3.6 sum_up.2
  163.8 1.7 collective-permute-start.23
  165.5 13.0 %all-gather.2.cloned.1.call-done.right_ref.refs_2_.refs_3_.refs_1_ = bf16[3,1536,1792]{2,1,0:T(8,128)(2,1)} async-done(((bf16[3,192,1792]{2,1,0:T(8,128)(2,1)}), bf16[3,1536,1792]{2,1,0:T(8,128)(2,1)}) %all-gather.2.cloned.1.call-update) | async-done | bytes 16515088 | tf_op jit(solution)/shard_map/all_gather | solution.py:800
  178.5 5.7 %copy-done = bf16[3,1536,1792]{2,1,0:T(8,128)(2,1)S(1)} copy-done((bf16[3,1536,1792]{2,1,0:T(8,128)(2,1)S(1)}, bf16[3,1536,1792]{2,1,0:T(8,128)(2,1)}, u32[]{:S(2)}) %copy-start) | copy-done | bytes 16515096
  184.2 1.9 copy-done.20
  186.1 6.4 %rows_product.2 = bf16[1024,1792]{1,0:T(8,128)(2,1)S(1)} custom-call(bf16[1024,1536]{1,0:T(8,128)(2,1)S(1)} %copy-done.20, bf16[3,1536,1792]{2,1,0:T(8,128)(2,1)S(1)} %copy-done), custom_call_target="tpu_custom_call" | custom-call | tf_op jit(solution)/shard_map/rows_product/pallas_call | solution.py:542
  192.5 5.5 %collective-permute-done.24.refs_2_ = bf16[256,1536]{1,0:T(8,128)(2,1)} collective-permute-done((bf16[256,1536]{1,0:T(8,128)(2,1)}, bf16[256,1536]{1,0:T(8,128)(2,1)}, u32[]{:S(2)}, u32[]{:S(2)}) %collective-permute-start.24) | collective-permute-done | bytes 786464 | tf_op jit(solution)/shard_map/two_spread/ppermute | solution.py:773
  198.8 2.9 fold.6
  202.9 9.2 %fusion.10 = bf16[1024,1792]{1,0:T(8,128)(2,1)S(1)} fusion(bf16[1024,1536]{1,0:T(8,128)(2,1)S(1)} %get-tuple-element.114, bf16[3,1536,1792]{2,1,0:T(8,128)(2,1)} %all-gather.2.cloned.1.call-done.right_ref.refs_2_.refs_3_.refs_1_), kind=kOutput, calls=%fused_computation.18 | convolution fusion | flops 5638979584 | bytes 12320768 | tf_op jit(solution)/shard_map/dot_general | solution.py:40
  212.0 13.5 %multiply_convert_fusion = (bf16[1024,1792]{1,0:T(8,128)(2,1)S(1)}, bf16[1024,1792]{1,0:T(8,128)(2,1)}, bf16[1024,1792]{1,0:T(8,128)(2,1)}) fusion(bf16[1024,1792]{1,0:T(8,128)(2,1)S(1)} %fusion.10, bf16[1024,1792]{1,0:T(8,128)(2,1)S(1)} %rows_product.2, bf16[1024,1536]{1,0:T(8,128)(2,1)S(1)} %get-tuple-element.114, ...), kind=kOutput, calls=%fused_computation.13 | convolution fusion | flops 5668339712 | bytes 27000832 | tf_op jit(solution)/shard_map/dot_general | solution.py:40
  225.5 7.7 %product.3 = bf16[1536,1792]{1,0:T(8,128)(2,1)S(1)} custom-call(bf16[1536,1024]{1,0:T(8,128)(2,1)S(1)} %get-tuple-element.115.left_ref, bf16[1024,1792]{1,0:T(8,128)(2,1)S(1)} %get-tuple-element.129.refs_0_), custom_call_target="tpu_custom_call" | custom-call | tf_op jit(solution)/shard_map/product/pallas_call | solution.py:313
  233.2 2.4 copy-done.4
  235.6 1.8 copy-done.6
  237.5 17.2 %back_parts.5 = (bf16[256,1536]{1,0:T(8,128)(2,1)}, bf16[256,1536]{1,0:T(8,128)(2,1)}, bf16[256,1536]{1,0:T(8,128)(2,1)}, bf16[256,1536]{1,0:T(8,128)(2,1)}) custom-call(bf16[1024,1792]{1,0:T(8,128)(2,1)} %get-tuple-element.124.refs_0_, bf16[1024,1792]{1,0:T(8,128)(2,1)} %get-tuple-element.192.refs_1_, ...), custom_call_target="tpu_custom_call" | custom-call | tf_op jit(solution)/shard_map/back_parts/pallas_call | solution.py:369
  255.9 2.3 collective-permute-start.28
  259.7 10.6 %product.4 = bf16[768,3584]{1,0:T(8,128)(2,1)} custom-call(bf16[768,1024]{1,0:T(8,128)(2,1)S(1)} %copy-done.27, bf16[1024,1792]{1,0:T(8,128)(2,1)S(1)} %copy-done.2, bf16[1024,1792]{1,0:T(8,128)(2,1)S(1)} %copy-done.3), custom_call_target="tpu_custom_call" | custom-call | tf_op jit(solution)/shard_map/product/pallas_call | solution.py:313
  270.3 9.5 %product.5.refs_0_.refs_1_.near_ref = bf16[768,3584]{1,0:T(8,128)(2,1)S(1)} custom-call(bf16[768,1024]{1,0:T(8,128)(2,1)S(1)} %copy-done.25, bf16[1024,1792]{1,0:T(8,128)(2,1)S(1)} %copy-done.2, bf16[1024,1792]{1,0:T(8,128)(2,1)S(1)} %copy-done.3), custom_call_target="tpu_custom_call" | custom-call | tf_op jit(solution)/shard_map/product/pallas_call | solution.py:313
  279.8 2.4 copy-done.1
  282.2 9.5 %collective-permute-done.27.refs_2_ = bf16[256,1536]{1,0:T(8,128)(2,1)} collective-permute-done((bf16[256,1536]{1,0:T(8,128)(2,1)}, bf16[256,1536]{1,0:T(8,128)(2,1)}, u32[]{:S(2)}, u32[]{:S(2)}) %collective-permute-start.27) | collective-permute-done | bytes 786464 | tf_op jit(solution)/shard_map/two_sum/ppermute | solution.py:780
  291.7 4.6 norm_back_sum.2
  296.3 4.8 collective-permute-done.32.refs_1_.refs_2_.other_ref
  301.1 2.8 join.3
  303.9 2.7 collective-permute-start.33
  310.0 10.4 %back_parts.6 = (bf16[256,1536]{1,0:T(8,128)(2,1)}, bf16[256,1536]{1,0:T(8,128)(2,1)}, bf16[256,1536]{1,0:T(8,128)(2,1)}, bf16[256,1536]{1,0:T(8,128)(2,1)}) custom-call(bf16[1024,1792]{1,0:T(8,128)(2,1)} %copy-done.6, bf16[3,1536,1792]{2,1,0:T(8,128)(2,1)} %all-gather.2.cloned.1.call-done.right_ref.refs_2_.refs_3_.refs_1_), custom_call_target="tpu_custom_call" | custom-call | tf_op jit(solution)/shard_map/back_parts/pallas_call | solution.py:369
  320.4 6.5 %collective-permute-done.29.refs_1_ = bf16[256,1536]{1,0:T(8,128)(2,1)S(1)} collective-permute-done((bf16[256,1536]{1,0:T(8,128)(2,1)S(1)}, bf16[256,1536]{1,0:T(8,128)(2,1)S(1)}, u32[]{:S(2)}, u32[]{:S(2)}) %collective-permute-start.29) | collective-permute-done | bytes 786464 | tf_op jit(solution)/shard_map/dh_spread/ppermute | solution.py:773
  327.0 11.2 %collective-permute-done.33.refs_0_ = bf16[192,3584]{1,0:T(8,128)(2,1)} collective-permute-done((bf16[192,3584]{1,0:T(8,128)(2,1)}, bf16[192,3584]{1,0:T(8,128)(2,1)}, u32[]{:S(2)}, u32[]{:S(2)}) %collective-permute-start.33) | collective-permute-done | bytes 1376288 | tf_op jit(solution)/shard_map/both_grad_hop1/ppermute | solution.py:758
  338.2 3.2 join.4
  347.8 2.1 fold.7
  350.0 2.6 rows_product.3.do_ref
  352.6 16.7 %attend_back.1 = (f32[1024,384]{1,0:T(8,128)S(1)}, f32[1024,128]{1,0:T(8,128)S(1)}, f32[1024,128]{1,0:T(8,128)S(1)}) custom-call(s32[1]{0:T(128)} %bitcast.me_ref, bf16[1024,384]{1,0:T(8,128)(2,1)S(1)} %copy-done.30, bf16[1024,128]{1,0:T(8,128)(2,1)S(1)} %copy-done.39, bf16[1024,128]{1,0:T(8,128)(2,1)S(1)} %copy-done.41, s32[4,1,256]{2,1,0:T(1,128)S(1)} %reshape.123.lo_ref, ...), custom_call_target="tpu_custom_call" | custom-call | tf_op jit(solution)/shard_map/attend_back/pallas_call | solution.py:204
  372.0 7.8 %prepare_back.1 = (bf16[1024,640]{1,0:T(8,128)(2,1)}, f32[1,512]{1,0:T(1,128)}) custom-call(f32[1024,384]{1,0:T(8,128)} %copy-done.28, f32[1024,128]{1,0:T(8,128)} %copy-done.35, f32[1024,128]{1,0:T(8,128)} %copy-done.36, f32[1024,512]{1,0:T(8,128)} %copy-done.23, f32[1024,128]{1,0:T(8,128)} %copy-done.14, f32[1024,128]{1,0:T(8,128)} %copy-done.13, ...), custom_call_target="tpu_custom_call" | custom-call | tf_op jit(solution)/shard_map/prepare_back/pallas_call | solution.py:691
  379.8 3.4 join.5
  383.2 6.9 %back_parts.7 = (bf16[256,1536]{1,0:T(8,128)(2,1)}, bf16[256,1536]{1,0:T(8,128)(2,1)}, bf16[256,1536]{1,0:T(8,128)(2,1)}, bf16[256,1536]{1,0:T(8,128)(2,1)}) custom-call(bf16[1024,640]{1,0:T(8,128)(2,1)} %get-tuple-element.157.refs_0_.refs_2_, bf16[1,1536,640]{2,1,0:T(8,128)(2,1)} %bitcast.35), custom_call_target="tpu_custom_call" | custom-call | tf_op jit(solution)/shard_map/back_parts/pallas_call | solution.py:369
  390.2 1.9 copy-done.18
  392.0 5.7 %attn_products.1 = bf16[1536,1024]{1,0:T(8,128)(2,1)} custom-call(bf16[1536,1024]{1,0:T(8,128)(2,1)S(1)} %copy-done.16, bf16[1536,1024]{1,0:T(8,128)(2,1)S(1)} %copy-done.18, bf16[1024,640]{1,0:T(8,128)(2,1)S(1)} %copy-done.12, bf16[1024,384]{1,0:T(8,128)(2,1)S(1)} %copy-done.11), custom_call_target="tpu_custom_call" | custom-call | tf_op jit(solution)/shard_map/attn_products/pallas_call | solution.py:346
  400.0 4.1 gain_parts.1
  408.7 3.4 sum_up.3
  413.0 1.7 collective-permute-start.40
  415.4 25.1 %collective-permute-done.40.refs_3_ = bf16[256,1536]{1,0:T(8,128)(2,1)S(1)} collective-permute-done((bf16[256,1536]{1,0:T(8,128)(2,1)S(1)}, bf16[256,1536]{1,0:T(8,128)(2,1)S(1)}, u32[]{:S(2)}, u32[]{:S(2)}) %collective-permute-start.40) | collective-permute-done | bytes 786464 | tf_op jit(solution)/shard_map/one_sum/ppermute | solution.py:780
  440.5 3.0 collective-permute-done.39.refs_2_
  444.5 4.2 norm_back_sum.3
  448.7 9.0 %collective-permute-done.44.flow_ref = bf16[192,3584]{1,0:T(8,128)(2,1)S(1)} collective-permute-done((bf16[192,3584]{1,0:T(8,128)(2,1)S(1)}, bf16[192,3584]{1,0:T(8,128)(2,1)S(1)}, u32[]{:S(2)}, u32[]{:S(2)}) %collective-permute-start.44) | collective-permute-done | bytes 1376288 | tf_op jit(solution)/shard_map/both_grad_hop3/ppermute | solution.py:758
  458.7 4.0 last_join.1
  464.1 4.3 collective-permute-start.46
  (253 shorter events, 65.9 us)
Async XLA Ops:
  7.2 171.3 %all-gather.2.cloned.1.call-start = ((), (), s32[]{:S(2)}) async-start(), calls=%async_computation.2 | async-start | bytes 18579456 | tf_op jit(solution)/shard_map/all_gather | solution.py:800
  11.5 60.1 %copy-start.70 = (f32[128]{0:T(128)S(1)}, f32[128]{0:T(128)}, u32[]{:S(2)}) copy-start(f32[128]{0:T(128)} %constant.100.clone.1) | copy-start | bytes 1540
  11.5 62.1 %copy-start.21 = (bf16[256,1536]{1,0:T(8,128)(2,1)S(1)}, bf16[256,1536]{1,0:T(8,128)(2,1)}, u32[]{:S(2)}) copy-start(bf16[256,1536]{1,0:T(8,128)(2,1)} %rest_ref.1) | copy-start | bytes 2359300
  11.5 65.7 %copy-start.67 = (f32[64]{0:T(128)S(1)}, f32[64]{0:T(128)}, u32[]{:S(2)}) copy-start(f32[64]{0:T(128)} %param.20) | copy-start | bytes 772
  11.5 386.2 %reduce-scatter.3.cloned.1.call-start = ((), (), s32[]{:S(2)}) async-start(), calls=%async_computation.3 | async-start | bytes 6193152 | tf_op jit(solution)/shard_map/reduce_scatter | solution.py:881
  11.6 11.9 %collective-permute-start.4 = (bf16[192,640]{1,0:T(8,128)(2,1)S(1)}, bf16[192,640]{1,0:T(8,128)(2,1)}, u32[]{:S(2)}, u32[]{:S(2)}) collective-permute-start(bf16[192,640]{1,0:T(8,128)(2,1)S(1)} %constant_dynamic-update-slice_fusion.refs_0_), channel_id=1, source_target_pairs={{0,8},{4,12},{8,16},{12,20},{16,24},{20,28},{24,0},{28,4},{1,9},{5... | collective-permute-start | bytes 737288 | tf_op jit(solution)/shard_map/qkv_hop1/ppermute | solution.py:758
  15.2 44.4 %collective-permute-start.2 = (bf16[256,1536]{1,0:T(8,128)(2,1)S(1)}, bf16[256,1536]{1,0:T(8,128)(2,1)S(1)}, u32[]{:S(2)}, u32[]{:S(2)}) collective-permute-start(bf16[256,1536]{1,0:T(8,128)(2,1)S(1)} %fusion.13.refs_0_), channel_id=1, source_target_pairs={{0,3},{1,2},{2,1},{3,0},{4,7},{5,6},{6,5},{7,4},{8,11},{9,10},{10,... | collective-permute-start | bytes 2359304 | tf_op jit(solution)/shard_map/one_spread/ppermute | solution.py:773
  17.7 42.8 %collective-permute-start.1 = (bf16[256,1536]{1,0:T(8,128)(2,1)S(1)}, bf16[256,1536]{1,0:T(8,128)(2,1)}, u32[]{:S(2)}, u32[]{:S(2)}) collective-permute-start(bf16[256,1536]{1,0:T(8,128)(2,1)S(1)} %fusion.13.refs_0_), channel_id=1, source_target_pairs={{0,2},{1,3},{2,0},{3,1},{4,6},{5,7},{6,4},{7,5},{8,10},{9,11},{10,... | collective-permute-start | bytes 2359304 | tf_op jit(solution)/shard_map/one_spread/ppermute | solution.py:773
  18.3 53.1 %collective-permute-start = (bf16[256,1536]{1,0:T(8,128)(2,1)S(1)}, bf16[256,1536]{1,0:T(8,128)(2,1)}, u32[]{:S(2)}, u32[]{:S(2)}) collective-permute-start(bf16[256,1536]{1,0:T(8,128)(2,1)S(1)} %fusion.13.refs_0_), channel_id=1, source_target_pairs={{0,1},{1,0},{2,3},{3,2},{4,5},{5,4},{6,7},{7,6},{8,9},{9,8},{10,11... | collective-permute-start | bytes 2359304 | tf_op jit(solution)/shard_map/one_spread/ppermute | solution.py:773
  18.8 21.9 %collective-permute-start.14 = (bf16[192,384]{1,0:T(8,128)(2,1)S(1)}, bf16[192,384]{1,0:T(8,128)(2,1)S(1)}, u32[]{:S(2)}, u32[]{:S(2)}) collective-permute-start(bf16[192,384]{1,0:T(8,128)(2,1)S(1)} %bitcast.38), channel_id=1, source_target_pairs={{0,8},{4,12},{8,16},{12,20},{16,24},{20,28},{24,0},{28,4},{1,9},{5... | collective-permute-start | bytes 442376 | tf_op jit(solution)/shard_map/out_hop1/ppermute | solution.py:758
  23.6 14.2 %collective-permute-start.6 = (bf16[192,640]{1,0:T(8,128)(2,1)}, bf16[192,640]{1,0:T(8,128)(2,1)}, u32[]{:S(2)}, u32[]{:S(2)}) collective-permute-start(bf16[192,640]{1,0:T(8,128)(2,1)} %collective-permute-done.4.refs_2_), channel_id=1, source_target_pairs={{0,8},{4,12},{8,16},{12,20},{16,24},{20,28},{24,0},{28,4},{1,9},{5... | collective-permute-start | bytes 737288 | tf_op jit(solution)/shard_map/qkv_hop2/ppermute | solution.py:758
  37.8 21.4 %collective-permute-start.8 = (bf16[192,640]{1,0:T(8,128)(2,1)}, bf16[192,640]{1,0:T(8,128)(2,1)}, u32[]{:S(2)}, u32[]{:S(2)}) collective-permute-start(bf16[192,640]{1,0:T(8,128)(2,1)} %collective-permute-done.6.refs_4_), channel_id=1, source_target_pairs={{0,8},{4,12},{8,16},{12,20},{16,24},{20,28},{24,0},{28,4},{1,9},{5... | collective-permute-start | bytes 737288 | tf_op jit(solution)/shard_map/qkv_hop3/ppermute | solution.py:758
  40.7 30.9 %copy-start.43 = (bf16[192,384]{1,0:T(8,128)(2,1)}, bf16[192,384]{1,0:T(8,128)(2,1)S(1)}, u32[]{:S(2)}) copy-start(bf16[192,384]{1,0:T(8,128)(2,1)S(1)} %collective-permute-done.14.refs_2_) | copy-start | bytes 442372
  40.7 18.4 %collective-permute-start.16 = (bf16[192,384]{1,0:T(8,128)(2,1)S(1)}, bf16[192,384]{1,0:T(8,128)(2,1)}, u32[]{:S(2)}, u32[]{:S(2)}) collective-permute-start(bf16[192,384]{1,0:T(8,128)(2,1)S(1)} %collective-permute-done.14.refs_2_), channel_id=1, source_target_pairs={{0,8},{4,12},{8,16},{12,20},{16,24},{20,28},{24,0},{28,4},{1,9},{5... | collective-permute-start | bytes 442376 | tf_op jit(solution)/shard_map/out_hop2/ppermute | solution.py:758
  59.1 14.4 %collective-permute-start.3 = (bf16[192,640]{1,0:T(8,128)(2,1)S(1)}, bf16[192,640]{1,0:T(8,128)(2,1)}, u32[]{:S(2)}, u32[]{:S(2)}) collective-permute-start(bf16[192,640]{1,0:T(8,128)(2,1)S(1)} %constant_dynamic-update-slice_fusion.refs_0_), channel_id=1, source_target_pairs={{0,4},{4,0},{8,12},{12,8},{16,20},{20,16},{24,28},{28,24},{1,5},{5... | collective-permute-start | bytes 737288 | tf_op jit(solution)/shard_map/ppermute | solution.py:755
  59.1 17.0 %collective-permute-start.5 = (bf16[192,640]{1,0:T(8,128)(2,1)}, bf16[192,640]{1,0:T(8,128)(2,1)}, u32[]{:S(2)}, u32[]{:S(2)}) collective-permute-start(bf16[192,640]{1,0:T(8,128)(2,1)} %collective-permute-done.4.refs_2_), channel_id=1, source_target_pairs={{0,4},{4,0},{8,12},{12,8},{16,20},{20,16},{24,28},{28,24},{1,5},{5... | collective-permute-start | bytes 737288 | tf_op jit(solution)/shard_map/ppermute | solution.py:755
  60.5 16.2 %collective-permute-start.7 = (bf16[192,640]{1,0:T(8,128)(2,1)}, bf16[192,640]{1,0:T(8,128)(2,1)S(1)}, u32[]{:S(2)}, u32[]{:S(2)}) collective-permute-start(bf16[192,640]{1,0:T(8,128)(2,1)} %collective-permute-done.6.refs_4_), channel_id=1, source_target_pairs={{0,4},{4,0},{8,12},{12,8},{16,20},{20,16},{24,28},{28,24},{1,5},{5... | collective-permute-start | bytes 737288 | tf_op jit(solution)/shard_map/ppermute | solution.py:755
  60.5 33.6 %collective-permute-start.18 = (bf16[192,384]{1,0:T(8,128)(2,1)}, bf16[192,384]{1,0:T(8,128)(2,1)S(1)}, u32[]{:S(2)}, u32[]{:S(2)}) collective-permute-start(bf16[192,384]{1,0:T(8,128)(2,1)} %collective-permute-done.16.refs_4_), channel_id=1, source_target_pairs={{0,8},{4,12},{8,16},{12,20},{16,24},{20,28},{24,0},{28,4},{1,9},{5... | collective-permute-start | bytes 442376 | tf_op jit(solution)/shard_map/out_hop3/ppermute | solution.py:758
  71.4 11.8 %collective-permute-start.9 = (bf16[192,640]{1,0:T(8,128)(2,1)}, bf16[192,640]{1,0:T(8,128)(2,1)}, u32[]{:S(2)}, u32[]{:S(2)}) collective-permute-start(bf16[192,640]{1,0:T(8,128)(2,1)} %collective-permute-done.8.refs_6_), channel_id=1, source_target_pairs={{0,4},{4,0},{8,12},{12,8},{16,20},{20,16},{24,28},{28,24},{1,5},{5... | collective-permute-start | bytes 737288 | tf_op jit(solution)/shard_map/ppermute | solution.py:755
  73.6 39.0 %collective-permute-start.12 = (bf16[256,1536]{1,0:T(8,128)(2,1)S(1)}, bf16[256,1536]{1,0:T(8,128)(2,1)}, u32[]{:S(2)}, u32[]{:S(2)}) collective-permute-start(bf16[256,1536]{1,0:T(8,128)(2,1)S(1)} %copy-done.21), channel_id=1, source_target_pairs={{0,3},{1,2},{2,1},{3,0},{4,7},{5,6},{6,5},{7,4},{8,11},{9,10},{10,... | collective-permute-start | bytes 2359304 | tf_op jit(solution)/shard_map/cot_spread/ppermute | solution.py:773
  76.2 36.4 %collective-permute-start.11 = (bf16[256,1536]{1,0:T(8,128)(2,1)S(1)}, bf16[256,1536]{1,0:T(8,128)(2,1)}, u32[]{:S(2)}, u32[]{:S(2)}) collective-permute-start(bf16[256,1536]{1,0:T(8,128)(2,1)S(1)} %copy-done.21), channel_id=1, source_target_pairs={{0,2},{1,3},{2,0},{3,1},{4,6},{5,7},{6,4},{7,5},{8,10},{9,11},{10,... | collective-permute-start | bytes 2359304 | tf_op jit(solution)/shard_map/cot_spread/ppermute | solution.py:773
  76.7 35.8 %collective-permute-start.10 = (bf16[256,1536]{1,0:T(8,128)(2,1)S(1)}, bf16[256,1536]{1,0:T(8,128)(2,1)}, u32[]{:S(2)}, u32[]{:S(2)}) collective-permute-start(bf16[256,1536]{1,0:T(8,128)(2,1)S(1)} %copy-done.21), channel_id=1, source_target_pairs={{0,1},{1,0},{2,3},{3,2},{4,5},{5,4},{6,7},{7,6},{8,9},{9,8},{10,11... | collective-permute-start | bytes 2359304 | tf_op jit(solution)/shard_map/cot_spread/ppermute | solution.py:773
  83.1 24.4 %collective-permute-start.13 = (bf16[192,384]{1,0:T(8,128)(2,1)S(1)}, bf16[192,384]{1,0:T(8,128)(2,1)S(1)}, u32[]{:S(2)}, u32[]{:S(2)}) collective-permute-start(bf16[192,384]{1,0:T(8,128)(2,1)S(1)} %bitcast.39), channel_id=1, source_target_pairs={{0,4},{4,0},{8,12},{12,8},{16,20},{20,16},{24,28},{28,24},{1,5},{5... | collective-permute-start | bytes 442376 | tf_op jit(solution)/shard_map/ppermute | solution.py:755
  94.1 13.3 %copy-start.29 = (bf16[1024,384]{1,0:T(8,128)(2,1)}, bf16[1024,384]{1,0:T(8,128)(2,1)S(1)}, u32[]{:S(2)}) copy-start(bf16[1024,384]{1,0:T(8,128)(2,1)S(1)} %get-tuple-element.94.q_ref) | copy-start | bytes 2359300
  94.1 13.3 %copy-start.38 = (bf16[1024,128]{1,0:T(8,128)(2,1)}, bf16[1024,128]{1,0:T(8,128)(2,1)S(1)}, u32[]{:S(2)}) copy-start(bf16[1024,128]{1,0:T(8,128)(2,1)S(1)} %get-tuple-element.95.k_ref) | copy-start | bytes 786436
  94.1 13.3 %copy-start.40 = (bf16[1024,128]{1,0:T(8,128)(2,1)}, bf16[1024,128]{1,0:T(8,128)(2,1)S(1)}, u32[]{:S(2)}) copy-start(bf16[1024,128]{1,0:T(8,128)(2,1)S(1)} %get-tuple-element.96.v_ref) | copy-start | bytes 786436
  94.1 13.5 %collective-permute-start.15 = (bf16[192,384]{1,0:T(8,128)(2,1)S(1)}, bf16[192,384]{1,0:T(8,128)(2,1)S(1)}, u32[]{:S(2)}, u32[]{:S(2)}) collective-permute-start(bf16[192,384]{1,0:T(8,128)(2,1)S(1)} %copy-done.44), channel_id=1, source_target_pairs={{0,4},{4,0},{8,12},{12,8},{16,20},{20,16},{24,28},{28,24},{1,5},{5... | collective-permute-start | bytes 442376 | tf_op jit(solution)/shard_map/ppermute | solution.py:755
  107.5 14.5 %copy-start.69 = (f32[1536]{0:T(1024)S(1)}, f32[1536]{0:T(1024)}, u32[]{:S(2)}) copy-start(f32[1536]{0:T(1024)} %param.23) | copy-start | bytes 18436
  107.5 15.1 %copy-start.22 = (bf16[256,1536]{1,0:T(8,128)(2,1)S(1)}, bf16[256,1536]{1,0:T(8,128)(2,1)}, u32[]{:S(2)}) copy-start(bf16[256,1536]{1,0:T(8,128)(2,1)} %rest_ref.1) | copy-start | bytes 2359300
  107.5 1.6 collective-permute-start.17
  107.6 1.5 collective-permute-start.19
  118.5 20.6 %collective-permute-start.20 = (bf16[256,1536]{1,0:T(8,128)(2,1)}, bf16[256,1536]{1,0:T(8,128)(2,1)S(1)}, u32[]{:S(2)}, u32[]{:S(2)}) collective-permute-start(bf16[256,1536]{1,0:T(8,128)(2,1)} %get-tuple-element.104), channel_id=1, source_target_pairs={{0,1},{1,0},{2,3},{3,2},{4,5},{5,4},{6,7},{7,6},{8,9},{9,8},{10,11... | collective-permute-start | bytes 2359304 | tf_op jit(solution)/shard_map/attn_sum/ppermute | solution.py:780
  120.2 36.5 %collective-permute-start.21 = (bf16[256,1536]{1,0:T(8,128)(2,1)}, bf16[256,1536]{1,0:T(8,128)(2,1)S(1)}, u32[]{:S(2)}, u32[]{:S(2)}) collective-permute-start(bf16[256,1536]{1,0:T(8,128)(2,1)} %get-tuple-element.105), channel_id=1, source_target_pairs={{0,2},{1,3},{2,0},{3,1},{4,6},{5,7},{6,4},{7,5},{8,10},{9,11},{10,... | collective-permute-start | bytes 2359304 | tf_op jit(solution)/shard_map/attn_sum/ppermute | solution.py:780
  121.7 35.0 %collective-permute-start.22 = (bf16[256,1536]{1,0:T(8,128)(2,1)}, bf16[256,1536]{1,0:T(8,128)(2,1)S(1)}, u32[]{:S(2)}, u32[]{:S(2)}) collective-permute-start(bf16[256,1536]{1,0:T(8,128)(2,1)} %get-tuple-element.106), channel_id=1, source_target_pairs={{0,3},{1,2},{2,1},{3,0},{4,7},{5,6},{6,5},{7,4},{8,11},{9,10},{10,... | collective-permute-start | bytes 2359304 | tf_op jit(solution)/shard_map/attn_sum/ppermute | solution.py:780
  139.1 17.6 %copy-start.54 = (bf16[256,1536]{1,0:T(8,128)(2,1)}, bf16[256,1536]{1,0:T(8,128)(2,1)S(1)}, u32[]{:S(2)}) copy-start(bf16[256,1536]{1,0:T(8,128)(2,1)S(1)} %collective-permute-done.20.refs_1_) | copy-start | bytes 2359300
  162.0 30.5 %collective-permute-start.25 = (bf16[256,1536]{1,0:T(8,128)(2,1)}, bf16[256,1536]{1,0:T(8,128)(2,1)}, u32[]{:S(2)}, u32[]{:S(2)}) collective-permute-start(bf16[256,1536]{1,0:T(8,128)(2,1)} %get-tuple-element.112.refs_0_), channel_id=1, source_target_pairs={{0,3},{1,2},{2,1},{3,0},{4,7},{5,6},{6,5},{7,4},{8,11},{9,10},{10,... | collective-permute-start | bytes 2359304 | tf_op jit(solution)/shard_map/two_spread/ppermute | solution.py:773
  163.5 34.5 %collective-permute-start.24 = (bf16[256,1536]{1,0:T(8,128)(2,1)}, bf16[256,1536]{1,0:T(8,128)(2,1)}, u32[]{:S(2)}, u32[]{:S(2)}) collective-permute-start(bf16[256,1536]{1,0:T(8,128)(2,1)} %get-tuple-element.112.refs_0_), channel_id=1, source_target_pairs={{0,2},{1,3},{2,0},{3,1},{4,6},{5,7},{6,4},{7,5},{8,10},{9,11},{10,... | collective-permute-start | bytes 2359304 | tf_op jit(solution)/shard_map/two_spread/ppermute | solution.py:773
  163.8 35.0 %collective-permute-start.23 = (bf16[256,1536]{1,0:T(8,128)(2,1)}, bf16[256,1536]{1,0:T(8,128)(2,1)}, u32[]{:S(2)}, u32[]{:S(2)}) collective-permute-start(bf16[256,1536]{1,0:T(8,128)(2,1)} %get-tuple-element.112.refs_0_), channel_id=1, source_target_pairs={{0,1},{1,0},{2,3},{3,2},{4,5},{5,4},{6,7},{7,6},{8,9},{9,8},{10,11... | collective-permute-start | bytes 2359304 | tf_op jit(solution)/shard_map/two_spread/ppermute | solution.py:773
  237.5 235.7 %reduce-scatter.5.cloned.1.call-start = ((), (), s32[]{:S(2)}) async-start(), calls=%async_computation.4 | async-start | bytes 3538944 | tf_op jit(solution)/shard_map/reduce_scatter | solution.py:915
  237.5 20.7 %copy-start.2 = (bf16[1024,1792]{1,0:T(8,128)(2,1)S(1)}, bf16[1024,1792]{1,0:T(8,128)(2,1)}, u32[]{:S(2)}) copy-start(bf16[1024,1792]{1,0:T(8,128)(2,1)} %get-tuple-element.124.refs_0_) | copy-start | bytes 11010052
  237.5 20.7 %copy-start.3 = (bf16[1024,1792]{1,0:T(8,128)(2,1)S(1)}, bf16[1024,1792]{1,0:T(8,128)(2,1)}, u32[]{:S(2)}) copy-start(bf16[1024,1792]{1,0:T(8,128)(2,1)} %get-tuple-element.192.refs_1_) | copy-start | bytes 11010052
  254.8 27.5 %collective-permute-start.26 = (bf16[256,1536]{1,0:T(8,128)(2,1)}, bf16[256,1536]{1,0:T(8,128)(2,1)S(1)}, u32[]{:S(2)}, u32[]{:S(2)}) collective-permute-start(bf16[256,1536]{1,0:T(8,128)(2,1)} %get-tuple-element.118), channel_id=1, source_target_pairs={{0,1},{1,0},{2,3},{3,2},{4,5},{5,4},{6,7},{7,6},{8,9},{9,8},{10,11... | collective-permute-start | bytes 2359304 | tf_op jit(solution)/shard_map/two_sum/ppermute | solution.py:780
  255.3 36.3 %collective-permute-start.27 = (bf16[256,1536]{1,0:T(8,128)(2,1)}, bf16[256,1536]{1,0:T(8,128)(2,1)}, u32[]{:S(2)}, u32[]{:S(2)}) collective-permute-start(bf16[256,1536]{1,0:T(8,128)(2,1)} %get-tuple-element.119), channel_id=1, source_target_pairs={{0,2},{1,3},{2,0},{3,1},{4,6},{5,7},{6,4},{7,5},{8,10},{9,11},{10,... | collective-permute-start | bytes 2359304 | tf_op jit(solution)/shard_map/two_sum/ppermute | solution.py:780
  255.9 35.8 %collective-permute-start.28 = (bf16[256,1536]{1,0:T(8,128)(2,1)}, bf16[256,1536]{1,0:T(8,128)(2,1)}, u32[]{:S(2)}, u32[]{:S(2)}) collective-permute-start(bf16[256,1536]{1,0:T(8,128)(2,1)} %get-tuple-element.120), channel_id=1, source_target_pairs={{0,3},{1,2},{2,1},{3,0},{4,7},{5,6},{6,5},{7,4},{8,11},{9,10},{10,... | collective-permute-start | bytes 2359304 | tf_op jit(solution)/shard_map/two_sum/ppermute | solution.py:780
  291.7 9.4 %collective-permute-start.32 = (bf16[768,3584]{1,0:T(8,128)(2,1)}, bf16[768,3584]{1,0:T(8,128)(2,1)}, u32[]{:S(2)}, u32[]{:S(2)}) collective-permute-start(bf16[768,3584]{1,0:T(8,128)(2,1)} %product.4), channel_id=1, source_target_pairs={{0,4},{4,0},{8,12},{12,8},{16,20},{20,16},{24,28},{28,24},{1,5},{5... | collective-permute-start | bytes 16515080 | tf_op jit(solution)/shard_map/ppermute | solution.py:755
  303.9 34.3 %collective-permute-start.33 = (bf16[192,3584]{1,0:T(8,128)(2,1)}, bf16[192,3584]{1,0:T(8,128)(2,1)}, u32[]{:S(2)}, u32[]{:S(2)}) collective-permute-start(bf16[192,3584]{1,0:T(8,128)(2,1)} %join.3), channel_id=1, source_target_pairs={{0,8},{4,12},{8,16},{12,20},{16,24},{20,28},{24,0},{28,4},{1,9},{5... | collective-permute-start | bytes 4128776 | tf_op jit(solution)/shard_map/both_grad_hop1/ppermute | solution.py:758
  306.6 20.4 %collective-permute-start.29 = (bf16[256,1536]{1,0:T(8,128)(2,1)S(1)}, bf16[256,1536]{1,0:T(8,128)(2,1)S(1)}, u32[]{:S(2)}, u32[]{:S(2)}) collective-permute-start(bf16[256,1536]{1,0:T(8,128)(2,1)S(1)} %copy-done.33), channel_id=1, source_target_pairs={{0,1},{1,0},{2,3},{3,2},{4,5},{5,4},{6,7},{7,6},{8,9},{9,8},{10,11... | collective-permute-start | bytes 2359304 | tf_op jit(solution)/shard_map/dh_spread/ppermute | solution.py:773
  307.1 35.7 %collective-permute-start.31 = (bf16[256,1536]{1,0:T(8,128)(2,1)S(1)}, bf16[256,1536]{1,0:T(8,128)(2,1)S(1)}, u32[]{:S(2)}, u32[]{:S(2)}) collective-permute-start(bf16[256,1536]{1,0:T(8,128)(2,1)S(1)} %copy-done.33), channel_id=1, source_target_pairs={{0,3},{1,2},{2,1},{3,0},{4,7},{5,6},{6,5},{7,4},{8,11},{9,10},{10,... | collective-permute-start | bytes 2359304 | tf_op jit(solution)/shard_map/dh_spread/ppermute | solution.py:773
  308.6 35.7 %collective-permute-start.30 = (bf16[256,1536]{1,0:T(8,128)(2,1)S(1)}, bf16[256,1536]{1,0:T(8,128)(2,1)}, u32[]{:S(2)}, u32[]{:S(2)}) collective-permute-start(bf16[256,1536]{1,0:T(8,128)(2,1)S(1)} %copy-done.33), channel_id=1, source_target_pairs={{0,2},{1,3},{2,0},{3,1},{4,6},{5,7},{6,4},{7,5},{8,10},{9,11},{10,... | collective-permute-start | bytes 2359304 | tf_op jit(solution)/shard_map/dh_spread/ppermute | solution.py:773
  341.4 38.4 %collective-permute-start.34 = (bf16[192,3584]{1,0:T(8,128)(2,1)}, bf16[192,3584]{1,0:T(8,128)(2,1)}, u32[]{:S(2)}, u32[]{:S(2)}) collective-permute-start(bf16[192,3584]{1,0:T(8,128)(2,1)} %join.4), channel_id=1, source_target_pairs={{0,8},{4,12},{8,16},{12,20},{16,24},{20,28},{24,0},{28,4},{1,9},{5... | collective-permute-start | bytes 4128776 | tf_op jit(solution)/shard_map/both_grad_hop2/ppermute | solution.py:758
  344.3 35.5 %collective-permute-start.35 = (bf16[256,1536]{1,0:T(8,128)(2,1)}, bf16[256,1536]{1,0:T(8,128)(2,1)}, u32[]{:S(2)}, u32[]{:S(2)}) collective-permute-start(bf16[256,1536]{1,0:T(8,128)(2,1)} %get-tuple-element.148), channel_id=1, source_target_pairs={{0,1},{1,0},{2,3},{3,2},{4,5},{5,4},{6,7},{7,6},{8,9},{9,8},{10,11... | collective-permute-start | bytes 2359304 | tf_op jit(solution)/shard_map/ffn_sum/ppermute | solution.py:780
  345.5 34.3 %collective-permute-start.36 = (bf16[256,1536]{1,0:T(8,128)(2,1)}, bf16[256,1536]{1,0:T(8,128)(2,1)}, u32[]{:S(2)}, u32[]{:S(2)}) collective-permute-start(bf16[256,1536]{1,0:T(8,128)(2,1)} %get-tuple-element.149), channel_id=1, source_target_pairs={{0,2},{1,3},{2,0},{3,1},{4,6},{5,7},{6,4},{7,5},{8,10},{9,11},{10,... | collective-permute-start | bytes 2359304 | tf_op jit(solution)/shard_map/ffn_sum/ppermute | solution.py:780
  346.3 33.5 %collective-permute-start.37 = (bf16[256,1536]{1,0:T(8,128)(2,1)}, bf16[256,1536]{1,0:T(8,128)(2,1)}, u32[]{:S(2)}, u32[]{:S(2)}) collective-permute-start(bf16[256,1536]{1,0:T(8,128)(2,1)} %get-tuple-element.150), channel_id=1, source_target_pairs={{0,3},{1,2},{2,1},{3,0},{4,7},{5,6},{6,5},{7,4},{8,11},{9,10},{10,... | collective-permute-start | bytes 2359304 | tf_op jit(solution)/shard_map/ffn_sum/ppermute | solution.py:780
  399.0 58.6 %collective-permute-start.44 = (bf16[192,3584]{1,0:T(8,128)(2,1)S(1)}, bf16[192,3584]{1,0:T(8,128)(2,1)S(1)}, u32[]{:S(2)}, u32[]{:S(2)}) collective-permute-start(bf16[192,3584]{1,0:T(8,128)(2,1)S(1)} %copy-done.50), channel_id=1, source_target_pairs={{0,8},{4,12},{8,16},{12,20},{16,24},{20,28},{24,0},{28,4},{1,9},{5... | collective-permute-start | bytes 4128776 | tf_op jit(solution)/shard_map/both_grad_hop3/ppermute | solution.py:758
  404.1 8.0 %collective-permute-start.43 = (f32[1,3584]{1,0:T(1,128)}, f32[1,3584]{1,0:T(1,128)S(1)}, u32[]{:S(2)}, u32[]{:S(2)}) collective-permute-start(f32[1,3584]{1,0:T(1,128)} %gain_parts.1), channel_id=1, source_target_pairs={{0,3},{1,2},{2,1},{3,0},{4,7},{5,6},{6,5},{7,4},{8,11},{9,10},{10,... | collective-permute-start | bytes 43016 | tf_op jit(solution)/shard_map/ppermute | solution.py:923
  405.3 7.7 %collective-permute-start.42 = (f32[1,3584]{1,0:T(1,128)}, f32[1,3584]{1,0:T(1,128)}, u32[]{:S(2)}, u32[]{:S(2)}) collective-permute-start(f32[1,3584]{1,0:T(1,128)} %gain_parts.1), channel_id=1, source_target_pairs={{0,2},{1,3},{2,0},{3,1},{4,6},{5,7},{6,4},{7,5},{8,10},{9,11},{10,... | collective-permute-start | bytes 43016 | tf_op jit(solution)/shard_map/ppermute | solution.py:923
  406.6 8.0 %collective-permute-start.41 = (f32[1,3584]{1,0:T(1,128)}, f32[1,3584]{1,0:T(1,128)}, u32[]{:S(2)}, u32[]{:S(2)}) collective-permute-start(f32[1,3584]{1,0:T(1,128)} %gain_parts.1), channel_id=1, source_target_pairs={{0,1},{1,0},{2,3},{3,2},{4,5},{5,4},{6,7},{7,6},{8,9},{9,8},{10,11... | collective-permute-start | bytes 43016 | tf_op jit(solution)/shard_map/ppermute | solution.py:923
  407.6 32.9 %collective-permute-start.38 = (bf16[256,1536]{1,0:T(8,128)(2,1)S(1)}, bf16[256,1536]{1,0:T(8,128)(2,1)S(1)}, u32[]{:S(2)}, u32[]{:S(2)}) collective-permute-start(bf16[256,1536]{1,0:T(8,128)(2,1)S(1)} %copy-done.58), channel_id=1, source_target_pairs={{0,1},{1,0},{2,3},{3,2},{4,5},{5,4},{6,7},{7,6},{8,9},{9,8},{10,11... | collective-permute-start | bytes 2359304 | tf_op jit(solution)/shard_map/one_sum/ppermute | solution.py:780
  412.1 31.4 %collective-permute-start.39 = (bf16[256,1536]{1,0:T(8,128)(2,1)S(1)}, bf16[256,1536]{1,0:T(8,128)(2,1)S(1)}, u32[]{:S(2)}, u32[]{:S(2)}) collective-permute-start(bf16[256,1536]{1,0:T(8,128)(2,1)S(1)} %copy-done.57), channel_id=1, source_target_pairs={{0,2},{1,3},{2,0},{3,1},{4,6},{5,7},{6,4},{7,5},{8,10},{9,11},{10,... | collective-permute-start | bytes 2359304 | tf_op jit(solution)/shard_map/one_sum/ppermute | solution.py:780
  413.0 27.5 %collective-permute-start.40 = (bf16[256,1536]{1,0:T(8,128)(2,1)S(1)}, bf16[256,1536]{1,0:T(8,128)(2,1)S(1)}, u32[]{:S(2)}, u32[]{:S(2)}) collective-permute-start(bf16[256,1536]{1,0:T(8,128)(2,1)S(1)} %copy-done.59), channel_id=1, source_target_pairs={{0,3},{1,2},{2,1},{3,0},{4,7},{5,6},{6,5},{7,4},{8,11},{9,10},{10,... | collective-permute-start | bytes 2359304 | tf_op jit(solution)/shard_map/one_sum/ppermute | solution.py:780
  462.7 1.2 collective-permute-start.45
  463.9 5.6 %collective-permute-start.48 = (f32[1,3584]{1,0:T(1,128)S(1)}, f32[1,3584]{1,0:T(1,128)S(1)}, u32[]{:S(2)}, u32[]{:S(2)}) collective-permute-start(f32[1,3584]{1,0:T(1,128)S(1)} %add.117), channel_id=1, source_target_pairs={{0,24},{4,28},{8,16},{12,20},{16,8},{20,12},{24,0},{28,4},{1,25},{... | collective-permute-start | bytes 43016 | tf_op jit(solution)/shard_map/ppermute | solution.py:923
  464.0 5.5 %collective-permute-start.47 = (f32[1,3584]{1,0:T(1,128)S(1)}, f32[1,3584]{1,0:T(1,128)S(1)}, u32[]{:S(2)}, u32[]{:S(2)}) collective-permute-start(f32[1,3584]{1,0:T(1,128)S(1)} %add.117), channel_id=1, source_target_pairs={{0,16},{4,20},{8,24},{12,28},{16,0},{20,4},{24,8},{28,12},{1,17},{... | collective-permute-start | bytes 43016 | tf_op jit(solution)/shard_map/ppermute | solution.py:923
  464.1 6.0 %collective-permute-start.46 = (f32[1,3584]{1,0:T(1,128)S(1)}, f32[1,3584]{1,0:T(1,128)S(1)}, u32[]{:S(2)}, u32[]{:S(2)}) collective-permute-start(f32[1,3584]{1,0:T(1,128)S(1)} %add.117), channel_id=1, source_target_pairs={{0,8},{4,12},{8,0},{12,4},{16,24},{20,28},{24,16},{28,20},{1,9},{5... | collective-permute-start | bytes 43016 | tf_op jit(solution)/shard_map/ppermute | solution.py:923
  (59 other events, 258.4 us)
Sparse Core Ops, SparseCore 0:
  11.6 166.8 all-gather.1
  237.6 61.1 reduce-scatter.2
  397.8 62.1 reduce-scatter.4

commit v4 on v3

--- a/solution.py
+++ b/solution.py
@@ -220,24 +220,21 @@
     )(me, queries, keys, values, bounds, attended, d_attended, lse)
 
 
-def fold_kernel(ranks, ring, rows, split, core_ref, *refs):
-    blocks, all_ref, outs = refs[:ranks], refs[ranks], refs[ranks + 1 :]
+def fold_kernel(ranks, ring, rows, core_ref, *refs):
+    blocks, (all_ref, turned_ref), split = refs[:ranks], refs[ranks : ranks + 2], refs[ranks + 2 :]
     core = core_ref[0]
-    turned = outs[-1]
-    depth = turned.shape[0] // (2 * ring)
+    depth = turned_ref.shape[0] // (2 * ring)
     for j in range(ranks):
         block = blocks[j][...]
         span = slice(j * rows, (j + 1) * rows)
         all_ref[span, :] = block
-        if not split:
-            turned[:, span] = block.T
-            continue
-        turned[...] = block.T
-        for i in range(ring):
-            to = slice(i * depth, (i + 1) * depth)
-            for side_ref, side in zip(outs[:2], (1 - core, core)):
-                first = pl.multiple_of((2 * i + side) * depth, 16)
-                side_ref[to, span] = turned[pl.ds(first, depth), :]
+        turned_ref[:, span] = block.T
+        if split:
+            for i in range(ring):
+                to = slice(i * depth, (i + 1) * depth)
+                for side_ref, side in zip(split, (1 - core, core)):
+                    first = pl.multiple_of((2 * i + side) * depth, 16)
+                    side_ref[to, span] = turned_ref[pl.ds(first, depth), span]
 
 
 def fold(core, blocks, ring, split=False):
@@ -245,14 +242,13 @@
     rows, width = blocks[0].shape
     length = ranks * rows
     whole = lambda shape: pl.BlockSpec(shape, lambda i: (0, 0))
-    shapes = [(length, width)] + ([(width // 2, length)] * 2 if split else [(width, length)])
-    return pl.pallas_call(
-        functools.partial(fold_kernel, ranks, ring, rows, split),
+    shapes = [(length, width), (width, length)] + ([(width // 2, length)] * 2 if split else [])
+    return pl.pallas_call(
+        functools.partial(fold_kernel, ranks, ring, rows),
         grid=(1,),
         in_specs=[pl.BlockSpec(memory_space=pltpu.SMEM)] + [whole((rows, width))] * ranks,
         out_specs=[whole(shape) for shape in shapes],
         out_shape=[jax.ShapeDtypeStruct(shape, LOW) for shape in shapes],
-        scratch_shapes=[pltpu.VMEM((width, rows), LOW)] if split else [],
         compiler_params=pltpu.CompilerParams(vmem_limit_bytes=40 * 2**20),
         cost_estimate=FREE,
         name="fold",
@@ -373,7 +369,7 @@
         + [pl.BlockSpec((1, tile, cols), lambda i, k=k: (k, i, 0)) for k in which],
         out_specs=[pl.BlockSpec((rows, tile), lambda i: (0, i))] * ranks,
         out_shape=[jax.ShapeDtypeStruct((rows, width), LOW)] * ranks,
-        compiler_params=pltpu.CompilerParams(vmem_limit_bytes=56 * 2**20),
+        compiler_params=pltpu.CompilerParams(vmem_limit_bytes=48 * 2**20),
         cost_estimate=FREE,
         name="back_parts",
     )(*lefts, *([weights] * len(which)))
@@ -401,7 +397,7 @@
             out_specs=row,
         ),
         out_shape=jax.ShapeDtypeStruct((depth, cols), dtype),
-        compiler_params=pltpu.CompilerParams(vmem_limit_bytes=56 * 2**20),
+        compiler_params=pltpu.CompilerParams(vmem_limit_bytes=24 * 2**20),
         cost_estimate=FREE,
         name="join",
     )(owner.astype(jnp.int32).reshape(1), *flows, near, other)
@@ -797,22 +793,16 @@
     normed_own = norm_rows(tokens_wide, attn_gain).astype(LOW)
     normed_one = spread("one_spread", normed_own)
     wide = hidden_cols + hidden_pad
-    ffn_full = lax.all_gather(
-        jnp.stack([widen(w_down.T), widen(w_gate), widen(w_up)]), "dp", axis=1, tiled=True
-    )
-    gate_full, up_full = ffn_full[1], ffn_full[2]
     qkv_blocks = [jnp.concatenate([w_query, key_weight, value_weight], axis=1)]
     for count in range(1, ring):
         qkv_blocks.append(hop(f"qkv_hop{count}", qkv_blocks[-1]))
-    out_blocks = [w_out.T]
-    for count in range(1, ring):
-        out_flow = hop(f"out_hop{count}", out_blocks[-1])
-        if count < ring - 1:
-            out_blocks.append(tie(out_flow, qkv_blocks[count + 1]))
-
-    def complete(blocks):
-        return place(at, [b for block in blocks for b in (block, swap(block))], ring)
-
+    ffn_full = lax.all_gather(
+        tie(jnp.stack([widen(w_down.T), widen(w_gate), widen(w_up)]), qkv_blocks[2]),
+        "dp",
+        axis=1,
+        tiled=True,
+    )
+    gate_full, up_full = ffn_full[1], ffn_full[2]
     grad_blocks = spread("cot_spread", tie(cotangent, *normed_one))
     first_start = jnp.sum((segments < 1).astype(jnp.int32))
     second_start = jnp.sum((segments < 2).astype(jnp.int32))
@@ -834,7 +824,17 @@
         [query_gain] * (q_cols // HEAD_SIZE) + [key_gain] * (kv_cols // HEAD_SIZE)
     ).reshape(1, -1)
 
+    out_blocks = [w_out.T]
     normed_all, normed_one_t = fold(core_array, normed_one, ring)
+    for count in range(1, ring):
+        out_flow = hop(f"out_hop{count}", out_blocks[-1])
+        if count < ring - 1:
+            before = (cosine, sine, head_gains, bounds) if count == 1 else (normed_all,)
+            out_blocks.append(tie(out_flow, qkv_blocks[count + 1], *before))
+
+    def complete(blocks):
+        return place(at, [b for block in blocks for b in (block, swap(block))], ring)
+
     w_qkv = complete(qkv_blocks)
     query_low, key_low, value_low, raw = prepare(
         normed_all, w_qkv, cosine, sine, head_gains, q_cols, kv_cols, ranks
@@ -853,7 +853,7 @@
     normed_two = spread("two_spread", normed_two_own)
     d_activation = rows_product(grad_all, ffn_full, ranks)
     normed_two[-1] = tie(normed_two[-1], d_activation)
-    normed_two_all, *normed_two_pair = fold(core_array, normed_two, ring, True)
+    normed_two_all, normed_two_t, *normed_two_pair = fold(core_array, normed_two, ring, True)
 
     gating = mm(normed_two_all, gate_full).astype(LOW).astype(F32)
     lifted = mm(normed_two_all, up_full)
@@ -881,21 +881,27 @@
     down_grad = lax.psum_scatter(down_full_grad, "dp", scatter_dimension=0, tiled=True)
     two_parts = back_parts([tie(d_gating, down_full_grad), d_lifted], ffn_full, (1, 2), ranks)
     two_arrived = send_parts("two_sum", two_parts)
-    both_far = product(normed_two_pair[0], [tie(d_gating, *two_parts), d_lifted])
-    both_near = product(normed_two_pair[1], [tie(d_gating, both_far), d_lifted])
-    *two_arrived, both_far, both_near = lax.optimization_barrier((*two_arrived, both_far, both_near))
-    both_other = swap(both_far)
+    gate_far = product(normed_two_pair[0], [tie(d_gating, *two_parts)])
+    gate_near = product(normed_two_pair[1], [tie(d_gating, gate_far)])
+    lift_full_grad = product(normed_two_t, [tie(d_lifted, gate_near)])
+    *two_arrived, gate_far, gate_near, lift_full_grad = lax.optimization_barrier(
+        (*two_arrived, gate_far, gate_near, lift_full_grad)
+    )
+    gate_other = swap(gate_far)
     d_hidden, d_hidden_low, ffn_gain_part = norm_back_sum(
         hidden, ffn_gain, cotangent, [two_parts[0]] + two_arrived, True
     )
     hidden_grad = spread("dh_spread", d_hidden_low)
-    both_block, both_flow = advance("both_grad", None, tie(both_near, d_hidden_low), both_other, 0)
+    lift_grad = lax.psum_scatter(
+        tie(lift_full_grad, down_grad, d_hidden_low), "dp", scatter_dimension=0, tiled=True
+    )
+    gate_block, gate_flow = advance("gate_grad", None, tie(gate_near, d_hidden_low), gate_other, 0)
     ffn_parts = back_parts([tie(activation, d_hidden_low)], ffn_full, (0,), ranks)
     hidden_grad[1] = tie(hidden_grad[1], *ffn_parts)
-    both_block, both_flow = several(
-        "both_grad", both_block, both_flow, both_near, both_other, 1, last - 1, hidden_grad[1]
-    )
-    hidden_grad[-1] = tie(hidden_grad[-1], both_block)
+    gate_block, gate_flow = several(
+        "gate_grad", gate_block, gate_flow, gate_near, gate_other, 1, last - 1, hidden_grad[1]
+    )
+    hidden_grad[-1] = tie(hidden_grad[-1], gate_block)
     hidden_grad_all, hidden_grad_t = fold(core_array, hidden_grad, ring)
     ffn_go = lax.optimization_barrier(tuple(ffn_parts) + tuple(hidden_grad))[:ranks]
     ffn_arrived = send_parts("ffn_sum", ffn_go)
@@ -906,14 +912,14 @@
     d_raw, head_gain_parts = prepare_back(
         d_queries, d_keys, d_values, raw, cosine, sine, head_gains, ranks
     )
-    both_block, both_flow = advance(
-        "both_grad", tie(both_flow, *ffn_arrived), both_near, both_other, last - 1
-    )
-    one_parts = back_parts([tie(d_raw, both_block, *ffn_arrived)], w_qkv[None], (0,), ranks)
+    gate_block, gate_flow = advance(
+        "gate_grad", tie(gate_flow, *ffn_arrived), gate_near, gate_other, last - 1
+    )
+    one_parts = back_parts([tie(d_raw, gate_block, *ffn_arrived)], w_qkv[None], (0,), ranks)
     one_arrived = send_parts("one_sum", one_parts)
     attn_full_grad = attn_products([normed_one_t, hidden_grad_t], [tie(d_raw, *one_parts), attended])
     attn_grad = lax.psum_scatter(
-        tie(attn_full_grad, down_grad), "dp", scatter_dimension=0, tiled=True)
+        tie(attn_full_grad, lift_grad), "dp", scatter_dimension=0, tiled=True)
     gains = gain_parts(
         tie(normed_all, attn_full_grad), attn_gain, one_parts, ffn_gain_part, head_gain_parts
     )
@@ -925,18 +931,18 @@
             pieces = [a + b for a, b in zip(pieces[::2], pieces[1::2])]
         return pieces[0]
 
-    total = exchange_sum(gains, "tensor", range(1, ranks), ranks)
-    one_arrived[-1] = tie(one_arrived[-1], output, total)
+    (gate_grad,) = last_join(
+        owner_after(last), tie(gate_flow, output), gate_near, gate_other, ring, hidden_cols, 1
+    )
+    one_arrived[-1] = tie(one_arrived[-1], output, gains, gate_grad)
     (tokens_grad,) = norm_back_sum(tokens, attn_gain, d_hidden, [one_parts[0]] + one_arrived, False)
-    gate_grad, lift_grad = last_join(
-        owner_after(last), tie(both_flow, tokens_grad), both_near, both_other, ring, hidden_cols, 2
-    )
+    lift_grad = lift_grad[:, :hidden_cols].astype(F32)
     query_grad, key_grad, value_grad, out_grad = cut_grads(
         attn_grad, (q_cols, kv_cols, kv_cols, q_cols)
     )
     down_grad = down_grad[:, :hidden_cols].astype(F32)
 
-    total = tie(total, gate_grad, tokens_grad)
+    total = exchange_sum(tie(gains, tokens_grad), "tensor", range(1, ranks), ranks)
     total = exchange_sum(total, "dp", range(1, 2), dp_size)
     total = exchange_sum(total, "dp", range(2, dp_size, 2), dp_size)
     total = total.reshape(-1)

time: 489 us -> 473 us (0.967)
  starting transfers between devices: 62.9 us -> 41 us
  local copies, waits for them, and re-layouts: 42.9 us -> 60.1 us
  Pallas kernels: 175 us -> 159 us
  waiting for transfers between devices: 155 us -> 163 us
    ppermute x12, waiting for transfers between devices: 67.4 us -> 42.1 us  [send_parts(): lax.ppermute(parts[j], 'tensor', [(i, i ^ j) for i in range(ranks)])]
    ppermute x9, waiting for transfers between devices: 51.3 us -> 75.2 us  [onward(): return lax.ppermute(v, 'dp', ring_pairs)]
    ppermute x9, starting transfers between devices: 24.8 us -> 3.15 us  [onward(): return lax.ppermute(v, 'dp', ring_pairs)]
    unnamed x146 -> x166, local copies, waits for them, and re-layouts: 37.5 us -> 53.4 us
    all_gather x1, waiting for transfers between devices: 13 us -> 22.1 us  [shards(): lax.all_gather(tie(jnp.stack([widen(w_down.T), widen(w_gate), widen(w_up)...]
    pallas_call x3 -> x4, Pallas kernels: 27.8 us -> 24.7 us  [product(): pl.pallas_call(functools.partial(product_kernel, tiles), grid=(tiles * le...]
  transfers between devices with their start and end apart: 52 -> 53, of which waited for: 21 -> 25; matrix products, arithmetic and copies ran while one was open for 2% -> 4% of each run, Pallas kernels for 34% -> 32%
where the time goes in v4:
time: 473 us; the launch traced here: 471 us
  waiting for transfers between devices  163 us (34%)
  Pallas kernels  159 us (34%)
  local copies, waits for them, and re-layouts  60.1 us (13%)
  starting transfers between devices  41 us (9%)
  matrix products  22.2 us (5%)
  between operations  14.6 us (3%)
  other arithmetic  11.3 us (2%)
    ppermute x9, waiting for transfers between devices, onward(): return lax.ppermute(v, 'dp', ring_pairs)  75.2 us
    unnamed x166, local copies, waits for them, and re-layouts  53.4 us
    ppermute x12, waiting for transfers between devices, send_parts(): lax.ppermute(parts[j], 'tensor', [(i, i ^ j) for i in range(ranks)])  42.1 us
    pallas_call x4, Pallas kernels, back_parts(): pl.pallas_call(functools.partial(back_parts_kernel, rows, len(lefts)), gr...  36.5 us
    pallas_call x4, Pallas kernels, product(): pl.pallas_call(functools.partial(product_kernel, tiles), grid=(tiles * le...  24.7 us
    dot_general x2, matrix products, mm(): return jnp.dot(left, right, preferred_element_type=F32)  22.2 us
    all_gather x1, waiting for transfers between devices, shards(): lax.all_gather(tie(jnp.stack([widen(w_down.T), widen(w_gate), widen(w_up)...  22.1 us
    pallas_call x1, Pallas kernels, attend_back(): pl.pallas_call(functools.partial(attend_back_kernel, heads, rows), grid_s...  16.7 us
  transfers between devices with their start and end apart: 53, of which 25 were waited for; matrix products, arithmetic and copies ran while one was open for 4% of the time, Pallas kernels for 32%

profile of v4, /device:TPU:0, one launch (start us, length us, event | category | flops | bytes accessed | tf_op | source)
XLA Modules:
  0.0 471.3 jit_solution(11383107768404072377)
XLA Ops:
  9.9 3.1 collective-permute-start.4
  14.4 6.5 %collective-permute-done.4.refs_2_ = bf16[192,640]{1,0:T(8,128)(2,1)S(1)} collective-permute-done((bf16[192,640]{1,0:T(8,128)(2,1)S(1)}, bf16[192,640]{1,0:T(8,128)(2,1)S(1)}, u32[]{:S(2)}, u32[]{:S(2)}) %collective-permute-start.4) | collective-permute-done | bytes 245792 | tf_op jit(solution)/shard_map/qkv_hop1/ppermute | solution.py:754
  20.9 1.5 pad_maximum_fusion
  22.4 7.4 %collective-permute-done.6.refs_4_ = bf16[192,640]{1,0:T(8,128)(2,1)S(1)} collective-permute-done((bf16[192,640]{1,0:T(8,128)(2,1)S(1)}, bf16[192,640]{1,0:T(8,128)(2,1)S(1)}, u32[]{:S(2)}, u32[]{:S(2)}) %collective-permute-start.6) | collective-permute-done | bytes 245792 | tf_op jit(solution)/shard_map/qkv_hop2/ppermute | solution.py:754
  30.8 2.3 collective-permute-start.2
  38.0 5.5 %collective-permute-done.14.refs_2_ = bf16[192,384]{1,0:T(8,128)(2,1)} collective-permute-done((bf16[192,384]{1,0:T(8,128)(2,1)S(1)}, bf16[192,384]{1,0:T(8,128)(2,1)}, u32[]{:S(2)}, u32[]{:S(2)}) %collective-permute-start.14) | collective-permute-done | bytes 147488 | tf_op jit(solution)/shard_map/out_hop1/ppermute | solution.py:754
  43.5 9.0 %collective-permute-done.8.refs_6_ = bf16[192,640]{1,0:T(8,128)(2,1)S(1)} collective-permute-done((bf16[192,640]{1,0:T(8,128)(2,1)}, bf16[192,640]{1,0:T(8,128)(2,1)S(1)}, u32[]{:S(2)}, u32[]{:S(2)}) %collective-permute-start.8) | collective-permute-done | bytes 245792 | tf_op jit(solution)/shard_map/qkv_hop3/ppermute | solution.py:754
  54.1 3.7 fusion.14
  58.8 7.7 %collective-permute-done.1.refs_2_ = bf16[256,1536]{1,0:T(8,128)(2,1)S(1)} collective-permute-done((bf16[256,1536]{1,0:T(8,128)(2,1)S(1)}, bf16[256,1536]{1,0:T(8,128)(2,1)S(1)}, u32[]{:S(2)}, u32[]{:S(2)}) %collective-permute-start.1) | collective-permute-done | bytes 786464 | tf_op jit(solution)/shard_map/one_spread/ppermute | solution.py:769
  74.0 1.7 copy-done.14
  75.6 3.4 collective-permute-done.16.refs_4_
  79.1 1.7 collective-permute-start.12
  85.6 2.9 place.2.w_ref
  88.6 5.5 %prepare.1 = (bf16[1024,384]{1,0:T(8,128)(2,1)S(1)}, bf16[1024,128]{1,0:T(8,128)(2,1)S(1)}, bf16[1024,128]{1,0:T(8,128)(2,1)S(1)}, f32[1024,512]{1,0:T(8,128)S(1)}) custom-call(bf16[1024,1536]{1,0:T(8,128)(2,1)S(1)} %get-tuple-element.164.x_ref.normed_ref, bf16[1536,640]{1,0:T(8,128)(2,1)S(1)} %place.2.w_ref, f32[1024,128]{1,0:T(8,128)S(1)} %copy-done.13, ...), custom_call_target="tpu_custom_call" | custom-call | tf_op jit(solution)/shard_map/prepare/pallas_call | solution.py:633
  97.3 12.8 %attend.1 = (bf16[1024,384]{1,0:T(8,128)(2,1)S(1)}, f32[4,2,768]{2,1,0:T(2,128)S(1)}) custom-call(s32[1]{0:T(128)} %bitcast.me_ref, bf16[1024,384]{1,0:T(8,128)(2,1)S(1)} %get-tuple-element.97.q_ref, bf16[1024,128]{1,0:T(8,128)(2,1)S(1)} %get-tuple-element.98.k_ref, bf16[1024,128]{1,0:T(8,128)(2,1)S(1)} %get-tuple-element.99.v_ref, ...), custom_call_target="tpu_custom_call" | custom-call | flops 6442450944 | bytes 33554432 | tf_op jit(solution)/shard_map/attend/pallas_call | solution.py:178
  112.0 2.3 place.3
  115.8 3.0 back_parts.4
  124.9 1.7 copy-done.16
  126.6 1.6 copy-done.23
  128.2 12.0 %collective-permute-done.20.refs_1_ = bf16[256,1536]{1,0:T(8,128)(2,1)S(1)} collective-permute-done((bf16[256,1536]{1,0:T(8,128)(2,1)S(1)}, bf16[256,1536]{1,0:T(8,128)(2,1)S(1)}, u32[]{:S(2)}, u32[]{:S(2)}) %collective-permute-start.20) | collective-permute-done | bytes 786464 | tf_op jit(solution)/shard_map/attn_sum/ppermute | solution.py:776
  140.2 16.7 %collective-permute-done.21.refs_2_ = bf16[256,1536]{1,0:T(8,128)(2,1)S(1)} collective-permute-done((bf16[256,1536]{1,0:T(8,128)(2,1)S(1)}, bf16[256,1536]{1,0:T(8,128)(2,1)S(1)}, u32[]{:S(2)}, u32[]{:S(2)}) %collective-permute-start.21) | collective-permute-done | bytes 786464 | tf_op jit(solution)/shard_map/attn_sum/ppermute | solution.py:776
  158.7 3.5 sum_up.2
  163.9 1.9 collective-permute-start.23
  165.8 22.1 %all-gather.2.cloned.1.call-done.right_ref.refs_2_.refs_3_.refs_1_ = bf16[3,1536,1792]{2,1,0:T(8,128)(2,1)} async-done(((bf16[3,192,1792]{2,1,0:T(8,128)(2,1)}), bf16[3,1536,1792]{2,1,0:T(8,128)(2,1)}) %all-gather.2.cloned.1.call-update) | async-done | bytes 16515088 | tf_op jit(solution)/shard_map/all_gather | solution.py:799
  187.9 5.7 %copy-done = bf16[3,1536,1792]{2,1,0:T(8,128)(2,1)S(1)} copy-done((bf16[3,1536,1792]{2,1,0:T(8,128)(2,1)S(1)}, bf16[3,1536,1792]{2,1,0:T(8,128)(2,1)}, u32[]{:S(2)}) %copy-start) | copy-done | bytes 16515096
  193.6 1.9 copy-done.24
  195.5 6.4 %rows_product.2 = bf16[1024,1792]{1,0:T(8,128)(2,1)S(1)} custom-call(bf16[1024,1536]{1,0:T(8,128)(2,1)S(1)} %copy-done.24, bf16[3,1536,1792]{2,1,0:T(8,128)(2,1)S(1)} %copy-done), custom_call_target="tpu_custom_call" | custom-call | tf_op jit(solution)/shard_map/rows_product/pallas_call | solution.py:538
  207.3 1.6 copy-done.18
  210.0 8.6 %fusion.10 = bf16[1024,1792]{1,0:T(8,128)(2,1)S(1)} fusion(bf16[1024,1536]{1,0:T(8,128)(2,1)S(1)} %get-tuple-element.118, bf16[3,1536,1792]{2,1,0:T(8,128)(2,1)} %all-gather.2.cloned.1.call-done.right_ref.refs_2_.refs_3_.refs_1_), kind=kOutput, calls=%fused_computation.18 | convolution fusion | flops 5638979584 | bytes 12320768 | tf_op jit(solution)/shard_map/dot_general | solution.py:40
  218.6 13.6 %multiply_convert_fusion = (bf16[1024,1792]{1,0:T(8,128)(2,1)S(1)}, bf16[1024,1792]{1,0:T(8,128)(2,1)}, bf16[1024,1792]{1,0:T(8,128)(2,1)}) fusion(bf16[1024,1792]{1,0:T(8,128)(2,1)S(1)} %fusion.10, bf16[1024,1792]{1,0:T(8,128)(2,1)S(1)} %rows_product.2, bf16[1024,1536]{1,0:T(8,128)(2,1)S(1)} %get-tuple-element.118, ...), kind=kOutput, calls=%fused_computation.13 | convolution fusion | flops 5668339712 | bytes 27000832 | tf_op jit(solution)/shard_map/dot_general | solution.py:40
  232.3 7.7 %product.4 = bf16[1536,1792]{1,0:T(8,128)(2,1)S(1)} custom-call(bf16[1536,1024]{1,0:T(8,128)(2,1)S(1)} %copy-done.17, bf16[1024,1792]{1,0:T(8,128)(2,1)S(1)} %get-tuple-element.135.refs_0_), custom_call_target="tpu_custom_call" | custom-call | tf_op jit(solution)/shard_map/product/pallas_call | solution.py:309
  240.0 2.4 copy-done.4
  242.4 1.8 copy-done.7
  244.3 17.3 %back_parts.5 = (bf16[256,1536]{1,0:T(8,128)(2,1)S(1)}, bf16[256,1536]{1,0:T(8,128)(2,1)}, bf16[256,1536]{1,0:T(8,128)(2,1)}, bf16[256,1536]{1,0:T(8,128)(2,1)}) custom-call(bf16[1024,1792]{1,0:T(8,128)(2,1)} %get-tuple-element.128.refs_0_, bf16[1024,1792]{1,0:T(8,128)(2,1)} %get-tuple-element.130.refs_1_.refs_0_, ...), custom_call_target="tpu_custom_call" | custom-call | tf_op jit(solution)/shard_map/back_parts/pallas_call | solution.py:365
  265.1 4.6 product.5
  269.8 1.5 copy-done.26
  271.3 4.6 product.6.refs_0_.refs_1_.near_ref
  276.0 7.7 %product.7 = bf16[1536,1792]{1,0:T(8,128)(2,1)S(1)} custom-call(bf16[1536,1024]{1,0:T(8,128)(2,1)S(1)} %copy-done.19, bf16[1024,1792]{1,0:T(8,128)(2,1)S(1)} %copy-done.6), custom_call_target="tpu_custom_call" | custom-call | tf_op jit(solution)/shard_map/product/pallas_call | solution.py:309
  283.7 2.4 copy-done.3
  286.1 13.3 %collective-permute-done.27.refs_2_ = bf16[256,1536]{1,0:T(8,128)(2,1)} collective-permute-done((bf16[256,1536]{1,0:T(8,128)(2,1)}, bf16[256,1536]{1,0:T(8,128)(2,1)}, u32[]{:S(2)}, u32[]{:S(2)}) %collective-permute-start.27) | collective-permute-done | bytes 786464 | tf_op jit(solution)/shard_map/two_sum/ppermute | solution.py:776
  299.5 4.5 norm_back_sum.2
  305.0 1.5 collective-permute-start.29
  308.5 1.9 collective-permute-done.32.refs_1_.refs_2_.other_ref
  310.4 2.1 join.3
  312.5 10.5 %back_parts.6 = (bf16[256,1536]{1,0:T(8,128)(2,1)S(1)}, bf16[256,1536]{1,0:T(8,128)(2,1)}, bf16[256,1536]{1,0:T(8,128)(2,1)}, bf16[256,1536]{1,0:T(8,128)(2,1)}) custom-call(bf16[1024,1792]{1,0:T(8,128)(2,1)} %copy-done.7, bf16[3,1536,1792]{2,1,0:T(8,128)(2,1)} %all-gather.2.cloned.1.call-done.right_ref.refs_2_.refs_3_.refs_1_), custom_call_target="tpu_custom_call" | custom-call | tf_op jit(solution)/shard_map/back_parts/pallas_call | solution.py:365
  322.9 2.8 collective-permute-done.29.refs_1_
  325.7 21.6 %collective-permute-done.33.refs_0_ = bf16[192,1792]{1,0:T(8,128)(2,1)} collective-permute-done((bf16[192,1792]{1,0:T(8,128)(2,1)}, bf16[192,1792]{1,0:T(8,128)(2,1)}, u32[]{:S(2)}, u32[]{:S(2)}) %collective-permute-start.33) | collective-permute-done | bytes 688160 | tf_op jit(solution)/shard_map/gate_grad_hop1/ppermute | solution.py:754
  347.3 2.2 join.4
  354.2 2.7 fold.7
  357.0 2.6 rows_product.3.do_ref
  359.6 16.7 %attend_back.1 = (f32[1024,384]{1,0:T(8,128)S(1)}, f32[1024,128]{1,0:T(8,128)S(1)}, f32[1024,128]{1,0:T(8,128)S(1)}) custom-call(s32[1]{0:T(128)} %bitcast.me_ref, bf16[1024,384]{1,0:T(8,128)(2,1)S(1)} %copy-done.33, bf16[1024,128]{1,0:T(8,128)(2,1)S(1)} %copy-done.57, bf16[1024,128]{1,0:T(8,128)(2,1)S(1)} %copy-done.59, s32[4,1,256]{2,1,0:T(1,128)S(1)} %reshape.123.lo_ref, ...), custom_call_target="tpu_custom_call" | custom-call | tf_op jit(solution)/shard_map/attend_back/pallas_call | solution.py:204
  379.0 7.7 %prepare_back.1 = (bf16[1024,640]{1,0:T(8,128)(2,1)}, f32[1,512]{1,0:T(1,128)}) custom-call(f32[1024,384]{1,0:T(8,128)} %copy-done.28, f32[1024,128]{1,0:T(8,128)} %copy-done.53, f32[1024,128]{1,0:T(8,128)} %copy-done.54, f32[1024,512]{1,0:T(8,128)} %copy-done.27, f32[1024,128]{1,0:T(8,128)} %get-tuple-element.200.cos_ref, ...), custom_call_target="tpu_custom_call" | custom-call | tf_op jit(solution)/shard_map/prepare_back/pallas_call | solution.py:687
  387.5 1.6 join.5
  390.0 5.7 %back_parts.7 = (bf16[256,1536]{1,0:T(8,128)(2,1)S(1)}, bf16[256,1536]{1,0:T(8,128)(2,1)S(1)}, bf16[256,1536]{1,0:T(8,128)(2,1)S(1)}, bf16[256,1536]{1,0:T(8,128)(2,1)S(1)}) custom-call(bf16[1024,640]{1,0:T(8,128)(2,1)S(1)} %copy-done.11, bf16[1,1536,640]{2,1,0:T(8,128)(2,1)} %bitcast.35), custom_call_target="tpu_custom_call" | custom-call | tf_op jit(solution)/shard_map/back_parts/pallas_call | solution.py:365
  396.6 5.7 %attn_products.1 = bf16[1536,1024]{1,0:T(8,128)(2,1)} custom-call(bf16[1536,1024]{1,0:T(8,128)(2,1)S(1)} %copy-done.15, bf16[1536,1024]{1,0:T(8,128)(2,1)S(1)} %get-tuple-element.146.refs_1_, bf16[1024,640]{1,0:T(8,128)(2,1)S(1)} %copy-done.11, bf16[1024,384]{1,0:T(8,128)(2,1)S(1)} %get-tuple-element.102.refs_0_.o_ref.refs_3_), custom_call_target="tpu_custom_call" | custom-call | tf_op jit(solution)/shard_map/attn_products/pallas_call | solution.py:342
  402.3 2.4 collective-permute-start.40
  406.5 4.0 gain_parts.1
  410.5 3.4 sum_up.3
  413.9 21.1 %collective-permute-done.41.flow_ref = bf16[192,1792]{1,0:T(8,128)(2,1)} collective-permute-done((bf16[192,1792]{1,0:T(8,128)(2,1)S(1)}, bf16[192,1792]{1,0:T(8,128)(2,1)}, u32[]{:S(2)}, u32[]{:S(2)}) %collective-permute-start.41) | collective-permute-done | bytes 688160 | tf_op jit(solution)/shard_map/gate_grad_hop3/ppermute | solution.py:754
  435.0 2.8 last_join.1
  437.9 4.3 norm_back_sum.3
  442.1 2.4 collective-permute-start.44
  450.1 3.1 collective-permute-start.48
  455.7 2.1 collective-permute-done.47
  (278 shorter events, 80.6 us)
Async XLA Ops:
  7.2 180.7 %all-gather.2.cloned.1.call-start = ((), (), s32[]{:S(2)}) async-start(), calls=%async_computation.3 | async-start | bytes 18579456 | tf_op jit(solution)/shard_map/all_gather | solution.py:799
  9.9 11.1 %collective-permute-start.4 = (bf16[192,640]{1,0:T(8,128)(2,1)S(1)}, bf16[192,640]{1,0:T(8,128)(2,1)S(1)}, u32[]{:S(2)}, u32[]{:S(2)}) collective-permute-start(bf16[192,640]{1,0:T(8,128)(2,1)S(1)} %constant_dynamic-update-slice_fusion.refs_0_), channel_id=1, source_target_pairs={{0,8},{4,12},{8,16},{12,20},{16,24},{20,28},{24,0},{28,4},{1,9},{5... | collective-permute-start | bytes 737288 | tf_op jit(solution)/shard_map/qkv_hop1/ppermute | solution.py:754
  14.4 15.5 %copy-start.70 = (bf16[256,1536]{1,0:T(8,128)(2,1)S(1)}, bf16[256,1536]{1,0:T(8,128)(2,1)}, u32[]{:S(2)}) copy-start(bf16[256,1536]{1,0:T(8,128)(2,1)} %value_ref.1) | copy-start | bytes 2359300
  20.9 8.9 %collective-permute-start.6 = (bf16[192,640]{1,0:T(8,128)(2,1)S(1)}, bf16[192,640]{1,0:T(8,128)(2,1)S(1)}, u32[]{:S(2)}, u32[]{:S(2)}) collective-permute-start(bf16[192,640]{1,0:T(8,128)(2,1)S(1)} %collective-permute-done.4.refs_2_), channel_id=1, source_target_pairs={{0,8},{4,12},{8,16},{12,20},{16,24},{20,28},{24,0},{28,4},{1,9},{5... | collective-permute-start | bytes 737288 | tf_op jit(solution)/shard_map/qkv_hop2/ppermute | solution.py:754
  29.9 274.9 %reduce-scatter.4.cloned.1.call-start = ((), (), s32[]{:S(2)}) async-start(), calls=%async_computation.4 | async-start | bytes 6193152 | tf_op jit(solution)/shard_map/reduce_scatter | solution.py:881
  30.8 37.5 %copy-start.21 = (bf16[256,1536]{1,0:T(8,128)(2,1)}, bf16[256,1536]{1,0:T(8,128)(2,1)S(1)}, u32[]{:S(2)}) copy-start(bf16[256,1536]{1,0:T(8,128)(2,1)S(1)} %fusion.13.refs_0_) | copy-start | bytes 2359300
  30.8 21.7 %collective-permute-start.2 = (bf16[256,1536]{1,0:T(8,128)(2,1)S(1)}, bf16[256,1536]{1,0:T(8,128)(2,1)S(1)}, u32[]{:S(2)}, u32[]{:S(2)}) collective-permute-start(bf16[256,1536]{1,0:T(8,128)(2,1)S(1)} %fusion.13.refs_0_), channel_id=1, source_target_pairs={{0,3},{1,2},{2,1},{3,0},{4,7},{5,6},{6,5},{7,4},{8,11},{9,10},{10,... | collective-permute-start | bytes 2359304 | tf_op jit(solution)/shard_map/one_spread/ppermute | solution.py:769
  33.1 33.4 %collective-permute-start.1 = (bf16[256,1536]{1,0:T(8,128)(2,1)S(1)}, bf16[256,1536]{1,0:T(8,128)(2,1)S(1)}, u32[]{:S(2)}, u32[]{:S(2)}) collective-permute-start(bf16[256,1536]{1,0:T(8,128)(2,1)S(1)} %fusion.13.refs_0_), channel_id=1, source_target_pairs={{0,2},{1,3},{2,0},{3,1},{4,6},{5,7},{6,4},{7,5},{8,10},{9,11},{10,... | collective-permute-start | bytes 2359304 | tf_op jit(solution)/shard_map/one_spread/ppermute | solution.py:769
  33.6 33.7 %collective-permute-start = (bf16[256,1536]{1,0:T(8,128)(2,1)S(1)}, bf16[256,1536]{1,0:T(8,128)(2,1)S(1)}, u32[]{:S(2)}, u32[]{:S(2)}) collective-permute-start(bf16[256,1536]{1,0:T(8,128)(2,1)S(1)} %fusion.13.refs_0_), channel_id=1, source_target_pairs={{0,1},{1,0},{2,3},{3,2},{4,5},{5,4},{6,7},{7,6},{8,9},{9,8},{10,11... | collective-permute-start | bytes 2359304 | tf_op jit(solution)/shard_map/one_spread/ppermute | solution.py:769
  34.4 9.1 %collective-permute-start.14 = (bf16[192,384]{1,0:T(8,128)(2,1)S(1)}, bf16[192,384]{1,0:T(8,128)(2,1)}, u32[]{:S(2)}, u32[]{:S(2)}) collective-permute-start(bf16[192,384]{1,0:T(8,128)(2,1)S(1)} %bitcast.38), channel_id=1, source_target_pairs={{0,8},{4,12},{8,16},{12,20},{16,24},{20,28},{24,0},{28,4},{1,9},{5... | collective-permute-start | bytes 442376 | tf_op jit(solution)/shard_map/out_hop1/ppermute | solution.py:754
  37.8 14.7 %collective-permute-start.8 = (bf16[192,640]{1,0:T(8,128)(2,1)}, bf16[192,640]{1,0:T(8,128)(2,1)S(1)}, u32[]{:S(2)}, u32[]{:S(2)}) collective-permute-start(bf16[192,640]{1,0:T(8,128)(2,1)} %copy-done.62), channel_id=1, source_target_pairs={{0,8},{4,12},{8,16},{12,20},{16,24},{20,28},{24,0},{28,4},{1,9},{5... | collective-permute-start | bytes 737288 | tf_op jit(solution)/shard_map/qkv_hop3/ppermute | solution.py:754
  43.5 35.6 %collective-permute-start.3 = (bf16[192,640]{1,0:T(8,128)(2,1)S(1)}, bf16[192,640]{1,0:T(8,128)(2,1)}, u32[]{:S(2)}, u32[]{:S(2)}) collective-permute-start(bf16[192,640]{1,0:T(8,128)(2,1)S(1)} %constant_dynamic-update-slice_fusion.refs_0_), channel_id=1, source_target_pairs={{0,4},{4,0},{8,12},{12,8},{16,20},{20,16},{24,28},{28,24},{1,5},{5... | collective-permute-start | bytes 737288 | tf_op jit(solution)/shard_map/ppermute | solution.py:751
  52.5 28.3 %collective-permute-start.5 = (bf16[192,640]{1,0:T(8,128)(2,1)}, bf16[192,640]{1,0:T(8,128)(2,1)}, u32[]{:S(2)}, u32[]{:S(2)}) collective-permute-start(bf16[192,640]{1,0:T(8,128)(2,1)} %copy-done.60), channel_id=1, source_target_pairs={{0,4},{4,0},{8,12},{12,8},{16,20},{20,16},{24,28},{28,24},{1,5},{5... | collective-permute-start | bytes 737288 | tf_op jit(solution)/shard_map/ppermute | solution.py:751
  54.1 27.5 %collective-permute-start.7 = (bf16[192,640]{1,0:T(8,128)(2,1)}, bf16[192,640]{1,0:T(8,128)(2,1)}, u32[]{:S(2)}, u32[]{:S(2)}) collective-permute-start(bf16[192,640]{1,0:T(8,128)(2,1)} %copy-done.62), channel_id=1, source_target_pairs={{0,4},{4,0},{8,12},{12,8},{16,20},{20,16},{24,28},{28,24},{1,5},{5... | collective-permute-start | bytes 737288 | tf_op jit(solution)/shard_map/ppermute | solution.py:751
  58.8 29.8 %copy-start.69 = (f32[512]{0:T(512)}, f32[512]{0:T(512)S(1)}, u32[]{:S(2)}) copy-start(f32[512]{0:T(512)S(1)} %concatenate.11) | copy-start | bytes 6148
  67.3 11.7 %collective-permute-start.16 = (bf16[192,384]{1,0:T(8,128)(2,1)}, bf16[192,384]{1,0:T(8,128)(2,1)}, u32[]{:S(2)}, u32[]{:S(2)}) collective-permute-start(bf16[192,384]{1,0:T(8,128)(2,1)} %collective-permute-done.14.refs_2_), channel_id=1, source_target_pairs={{0,8},{4,12},{8,16},{12,20},{16,24},{20,28},{24,0},{28,4},{1,9},{5... | collective-permute-start | bytes 442376 | tf_op jit(solution)/shard_map/out_hop2/ppermute | solution.py:754
  68.2 14.5 %collective-permute-start.9 = (bf16[192,640]{1,0:T(8,128)(2,1)}, bf16[192,640]{1,0:T(8,128)(2,1)}, u32[]{:S(2)}, u32[]{:S(2)}) collective-permute-start(bf16[192,640]{1,0:T(8,128)(2,1)} %copy-done.64), channel_id=1, source_target_pairs={{0,4},{4,0},{8,12},{12,8},{16,20},{20,16},{24,28},{28,24},{1,5},{5... | collective-permute-start | bytes 737288 | tf_op jit(solution)/shard_map/ppermute | solution.py:751
  75.6 18.5 %copy-start.8 = (bf16[1024,1536]{1,0:T(8,128)(2,1)}, bf16[1024,1536]{1,0:T(8,128)(2,1)S(1)}, u32[]{:S(2)}) copy-start(bf16[1024,1536]{1,0:T(8,128)(2,1)S(1)} %get-tuple-element.164.x_ref.normed_ref) | copy-start | bytes 9437188
  79.1 17.7 %collective-permute-start.18 = (bf16[192,384]{1,0:T(8,128)(2,1)}, bf16[192,384]{1,0:T(8,128)(2,1)}, u32[]{:S(2)}, u32[]{:S(2)}) collective-permute-start(bf16[192,384]{1,0:T(8,128)(2,1)} %collective-permute-done.16.refs_4_), channel_id=1, source_target_pairs={{0,8},{4,12},{8,16},{12,20},{16,24},{20,28},{24,0},{28,4},{1,9},{5... | collective-permute-start | bytes 442376 | tf_op jit(solution)/shard_map/out_hop3/ppermute | solution.py:754
  79.1 35.2 %collective-permute-start.12 = (bf16[256,1536]{1,0:T(8,128)(2,1)}, bf16[256,1536]{1,0:T(8,128)(2,1)S(1)}, u32[]{:S(2)}, u32[]{:S(2)}) collective-permute-start(bf16[256,1536]{1,0:T(8,128)(2,1)} %rest_ref.1), channel_id=1, source_target_pairs={{0,3},{1,2},{2,1},{3,0},{4,7},{5,6},{6,5},{7,4},{8,11},{9,10},{10,... | collective-permute-start | bytes 2359304 | tf_op jit(solution)/shard_map/cot_spread/ppermute | solution.py:769
  80.8 35.0 %collective-permute-start.11 = (bf16[256,1536]{1,0:T(8,128)(2,1)}, bf16[256,1536]{1,0:T(8,128)(2,1)S(1)}, u32[]{:S(2)}, u32[]{:S(2)}) collective-permute-start(bf16[256,1536]{1,0:T(8,128)(2,1)} %rest_ref.1), channel_id=1, source_target_pairs={{0,2},{1,3},{2,0},{3,1},{4,6},{5,7},{6,4},{7,5},{8,10},{9,11},{10,... | collective-permute-start | bytes 2359304 | tf_op jit(solution)/shard_map/cot_spread/ppermute | solution.py:769
  81.6 34.2 %collective-permute-start.10 = (bf16[256,1536]{1,0:T(8,128)(2,1)}, bf16[256,1536]{1,0:T(8,128)(2,1)S(1)}, u32[]{:S(2)}, u32[]{:S(2)}) collective-permute-start(bf16[256,1536]{1,0:T(8,128)(2,1)} %rest_ref.1), channel_id=1, source_target_pairs={{0,1},{1,0},{2,3},{3,2},{4,5},{5,4},{6,7},{7,6},{8,9},{9,8},{10,11... | collective-permute-start | bytes 2359304 | tf_op jit(solution)/shard_map/cot_spread/ppermute | solution.py:769
  82.7 27.4 %collective-permute-start.13 = (bf16[192,384]{1,0:T(8,128)(2,1)S(1)}, bf16[192,384]{1,0:T(8,128)(2,1)S(1)}, u32[]{:S(2)}, u32[]{:S(2)}) collective-permute-start(bf16[192,384]{1,0:T(8,128)(2,1)S(1)} %bitcast.39), channel_id=1, source_target_pairs={{0,4},{4,0},{8,12},{12,8},{16,20},{20,16},{24,28},{28,24},{1,5},{5... | collective-permute-start | bytes 442376 | tf_op jit(solution)/shard_map/ppermute | solution.py:751
  96.7 13.5 %collective-permute-start.15 = (bf16[192,384]{1,0:T(8,128)(2,1)}, bf16[192,384]{1,0:T(8,128)(2,1)S(1)}, u32[]{:S(2)}, u32[]{:S(2)}) collective-permute-start(bf16[192,384]{1,0:T(8,128)(2,1)} %collective-permute-done.14.refs_2_), channel_id=1, source_target_pairs={{0,4},{4,0},{8,12},{12,8},{16,20},{20,16},{24,28},{28,24},{1,5},{5... | collective-permute-start | bytes 442376 | tf_op jit(solution)/shard_map/ppermute | solution.py:751
  110.1 13.8 %copy-start.25 = (bf16[256,1536]{1,0:T(8,128)(2,1)S(1)}, bf16[256,1536]{1,0:T(8,128)(2,1)}, u32[]{:S(2)}) copy-start(bf16[256,1536]{1,0:T(8,128)(2,1)} %rest_ref.1) | copy-start | bytes 2359300
  110.1 1.6 collective-permute-start.17
  110.2 1.7 collective-permute-start.19
  119.8 20.4 %collective-permute-start.20 = (bf16[256,1536]{1,0:T(8,128)(2,1)S(1)}, bf16[256,1536]{1,0:T(8,128)(2,1)S(1)}, u32[]{:S(2)}, u32[]{:S(2)}) collective-permute-start(bf16[256,1536]{1,0:T(8,128)(2,1)S(1)} %get-tuple-element.107), channel_id=1, source_target_pairs={{0,1},{1,0},{2,3},{3,2},{4,5},{5,4},{6,7},{7,6},{8,9},{9,8},{10,11... | collective-permute-start | bytes 2359304 | tf_op jit(solution)/shard_map/attn_sum/ppermute | solution.py:776
  120.8 36.1 %collective-permute-start.21 = (bf16[256,1536]{1,0:T(8,128)(2,1)S(1)}, bf16[256,1536]{1,0:T(8,128)(2,1)S(1)}, u32[]{:S(2)}, u32[]{:S(2)}) collective-permute-start(bf16[256,1536]{1,0:T(8,128)(2,1)S(1)} %get-tuple-element.108), channel_id=1, source_target_pairs={{0,2},{1,3},{2,0},{3,1},{4,6},{5,7},{6,4},{7,5},{8,10},{9,11},{10,... | collective-permute-start | bytes 2359304 | tf_op jit(solution)/shard_map/attn_sum/ppermute | solution.py:776
  122.0 34.9 %collective-permute-start.22 = (bf16[256,1536]{1,0:T(8,128)(2,1)S(1)}, bf16[256,1536]{1,0:T(8,128)(2,1)S(1)}, u32[]{:S(2)}, u32[]{:S(2)}) collective-permute-start(bf16[256,1536]{1,0:T(8,128)(2,1)S(1)} %get-tuple-element.109), channel_id=1, source_target_pairs={{0,3},{1,2},{2,1},{3,0},{4,7},{5,6},{6,5},{7,4},{8,11},{9,10},{10,... | collective-permute-start | bytes 2359304 | tf_op jit(solution)/shard_map/attn_sum/ppermute | solution.py:776
  140.2 16.8 %copy-start.71 = (bf16[256,1536]{1,0:T(8,128)(2,1)}, bf16[256,1536]{1,0:T(8,128)(2,1)S(1)}, u32[]{:S(2)}) copy-start(bf16[256,1536]{1,0:T(8,128)(2,1)S(1)} %collective-permute-done.20.refs_1_) | copy-start | bytes 2359300
  162.3 39.6 %collective-permute-start.25 = (bf16[256,1536]{1,0:T(8,128)(2,1)}, bf16[256,1536]{1,0:T(8,128)(2,1)S(1)}, u32[]{:S(2)}, u32[]{:S(2)}) collective-permute-start(bf16[256,1536]{1,0:T(8,128)(2,1)} %get-tuple-element.116.refs_0_), channel_id=1, source_target_pairs={{0,3},{1,2},{2,1},{3,0},{4,7},{5,6},{6,5},{7,4},{8,11},{9,10},{10,... | collective-permute-start | bytes 2359304 | tf_op jit(solution)/shard_map/two_spread/ppermute | solution.py:769
  163.8 38.1 %collective-permute-start.24 = (bf16[256,1536]{1,0:T(8,128)(2,1)}, bf16[256,1536]{1,0:T(8,128)(2,1)S(1)}, u32[]{:S(2)}, u32[]{:S(2)}) collective-permute-start(bf16[256,1536]{1,0:T(8,128)(2,1)} %get-tuple-element.116.refs_0_), channel_id=1, source_target_pairs={{0,2},{1,3},{2,0},{3,1},{4,6},{5,7},{6,4},{7,5},{8,10},{9,11},{10,... | collective-permute-start | bytes 2359304 | tf_op jit(solution)/shard_map/two_spread/ppermute | solution.py:769
  163.9 38.8 %collective-permute-start.23 = (bf16[256,1536]{1,0:T(8,128)(2,1)}, bf16[256,1536]{1,0:T(8,128)(2,1)S(1)}, u32[]{:S(2)}, u32[]{:S(2)}) collective-permute-start(bf16[256,1536]{1,0:T(8,128)(2,1)} %get-tuple-element.116.refs_0_), channel_id=1, source_target_pairs={{0,1},{1,0},{2,3},{3,2},{4,5},{5,4},{6,7},{7,6},{8,9},{9,8},{10,11... | collective-permute-start | bytes 2359304 | tf_op jit(solution)/shard_map/two_spread/ppermute | solution.py:769
  244.2 158.1 %reduce-scatter.6.cloned.1.call-start = ((), (), s32[]{:S(2)}) async-start(), calls=%async_computation.5 | async-start | bytes 6193152 | tf_op jit(solution)/shard_map/reduce_scatter | solution.py:895
  244.2 20.9 %copy-start.2 = (bf16[1024,1792]{1,0:T(8,128)(2,1)S(1)}, bf16[1024,1792]{1,0:T(8,128)(2,1)}, u32[]{:S(2)}) copy-start(bf16[1024,1792]{1,0:T(8,128)(2,1)} %get-tuple-element.128.refs_0_) | copy-start | bytes 11010052
  261.6 24.5 %collective-permute-start.26 = (bf16[256,1536]{1,0:T(8,128)(2,1)}, bf16[256,1536]{1,0:T(8,128)(2,1)}, u32[]{:S(2)}, u32[]{:S(2)}) collective-permute-start(bf16[256,1536]{1,0:T(8,128)(2,1)} %get-tuple-element.122), channel_id=1, source_target_pairs={{0,1},{1,0},{2,3},{3,2},{4,5},{5,4},{6,7},{7,6},{8,9},{9,8},{10,11... | collective-permute-start | bytes 2359304 | tf_op jit(solution)/shard_map/two_sum/ppermute | solution.py:776
  262.9 36.6 %collective-permute-start.27 = (bf16[256,1536]{1,0:T(8,128)(2,1)}, bf16[256,1536]{1,0:T(8,128)(2,1)}, u32[]{:S(2)}, u32[]{:S(2)}) collective-permute-start(bf16[256,1536]{1,0:T(8,128)(2,1)} %get-tuple-element.123), channel_id=1, source_target_pairs={{0,2},{1,3},{2,0},{3,1},{4,6},{5,7},{6,4},{7,5},{8,10},{9,11},{10,... | collective-permute-start | bytes 2359304 | tf_op jit(solution)/shard_map/two_sum/ppermute | solution.py:776
  264.4 35.1 %collective-permute-start.28 = (bf16[256,1536]{1,0:T(8,128)(2,1)}, bf16[256,1536]{1,0:T(8,128)(2,1)}, u32[]{:S(2)}, u32[]{:S(2)}) collective-permute-start(bf16[256,1536]{1,0:T(8,128)(2,1)} %get-tuple-element.124), channel_id=1, source_target_pairs={{0,3},{1,2},{2,1},{3,0},{4,7},{5,6},{6,5},{7,4},{8,11},{9,10},{10,... | collective-permute-start | bytes 2359304 | tf_op jit(solution)/shard_map/two_sum/ppermute | solution.py:776
  276.0 111.6 %copy-start.1 = (bf16[768,1792]{1,0:T(8,128)(2,1)}, bf16[768,1792]{1,0:T(8,128)(2,1)S(1)}, u32[]{:S(2)}) copy-start(bf16[768,1792]{1,0:T(8,128)(2,1)S(1)} %product.6.refs_0_.refs_1_.near_ref) | copy-start | bytes 8257540
  304.9 157.2 %reduce-scatter.8.cloned.1.call-start = ((), (), s32[]{:S(2)}) async-start(), calls=%async_computation.6 | async-start | bytes 3538944 | tf_op jit(solution)/shard_map/reduce_scatter | solution.py:921
  304.9 5.5 %collective-permute-start.32 = (bf16[768,1792]{1,0:T(8,128)(2,1)}, bf16[768,1792]{1,0:T(8,128)(2,1)}, u32[]{:S(2)}, u32[]{:S(2)}) collective-permute-start(bf16[768,1792]{1,0:T(8,128)(2,1)} %copy-done.26), channel_id=1, source_target_pairs={{0,4},{4,0},{8,12},{12,8},{16,20},{20,16},{24,28},{28,24},{1,5},{5... | collective-permute-start | bytes 8257544 | tf_op jit(solution)/shard_map/ppermute | solution.py:751
  305.0 20.7 %collective-permute-start.29 = (bf16[256,1536]{1,0:T(8,128)(2,1)}, bf16[256,1536]{1,0:T(8,128)(2,1)}, u32[]{:S(2)}, u32[]{:S(2)}) collective-permute-start(bf16[256,1536]{1,0:T(8,128)(2,1)} %get-tuple-element.134.refs_0_), channel_id=1, source_target_pairs={{0,1},{1,0},{2,3},{3,2},{4,5},{5,4},{6,7},{7,6},{8,9},{9,8},{10,11... | collective-permute-start | bytes 2359304 | tf_op jit(solution)/shard_map/dh_spread/ppermute | solution.py:769
  306.5 43.0 %collective-permute-start.31 = (bf16[256,1536]{1,0:T(8,128)(2,1)}, bf16[256,1536]{1,0:T(8,128)(2,1)}, u32[]{:S(2)}, u32[]{:S(2)}) collective-permute-start(bf16[256,1536]{1,0:T(8,128)(2,1)} %get-tuple-element.134.refs_0_), channel_id=1, source_target_pairs={{0,3},{1,2},{2,1},{3,0},{4,7},{5,6},{6,5},{7,4},{8,11},{9,10},{10,... | collective-permute-start | bytes 2359304 | tf_op jit(solution)/shard_map/dh_spread/ppermute | solution.py:769
  308.0 41.5 %collective-permute-start.30 = (bf16[256,1536]{1,0:T(8,128)(2,1)}, bf16[256,1536]{1,0:T(8,128)(2,1)}, u32[]{:S(2)}, u32[]{:S(2)}) collective-permute-start(bf16[256,1536]{1,0:T(8,128)(2,1)} %get-tuple-element.134.refs_0_), channel_id=1, source_target_pairs={{0,2},{1,3},{2,0},{3,1},{4,6},{5,7},{6,4},{7,5},{8,10},{9,11},{10,... | collective-permute-start | bytes 2359304 | tf_op jit(solution)/shard_map/dh_spread/ppermute | solution.py:769
  312.5 34.8 %collective-permute-start.33 = (bf16[192,1792]{1,0:T(8,128)(2,1)}, bf16[192,1792]{1,0:T(8,128)(2,1)}, u32[]{:S(2)}, u32[]{:S(2)}) collective-permute-start(bf16[192,1792]{1,0:T(8,128)(2,1)} %join.3), channel_id=1, source_target_pairs={{0,8},{4,12},{8,16},{12,20},{16,24},{20,28},{24,0},{28,4},{1,9},{5... | collective-permute-start | bytes 2064392 | tf_op jit(solution)/shard_map/gate_grad_hop1/ppermute | solution.py:754
  322.9 26.5 %copy-start.31 = (bf16[256,1536]{1,0:T(8,128)(2,1)}, bf16[256,1536]{1,0:T(8,128)(2,1)S(1)}, u32[]{:S(2)}) copy-start(bf16[256,1536]{1,0:T(8,128)(2,1)S(1)} %get-tuple-element.136.refs_0_) | copy-start | bytes 2359300
  349.5 38.0 %collective-permute-start.35 = (bf16[256,1536]{1,0:T(8,128)(2,1)}, bf16[256,1536]{1,0:T(8,128)(2,1)}, u32[]{:S(2)}, u32[]{:S(2)}) collective-permute-start(bf16[256,1536]{1,0:T(8,128)(2,1)} %get-tuple-element.154), channel_id=1, source_target_pairs={{0,1},{1,0},{2,3},{3,2},{4,5},{5,4},{6,7},{7,6},{8,9},{9,8},{10,11... | collective-permute-start | bytes 2359304 | tf_op jit(solution)/shard_map/ffn_sum/ppermute | solution.py:776
  350.9 36.6 %collective-permute-start.36 = (bf16[256,1536]{1,0:T(8,128)(2,1)}, bf16[256,1536]{1,0:T(8,128)(2,1)}, u32[]{:S(2)}, u32[]{:S(2)}) collective-permute-start(bf16[256,1536]{1,0:T(8,128)(2,1)} %get-tuple-element.155), channel_id=1, source_target_pairs={{0,2},{1,3},{2,0},{3,1},{4,6},{5,7},{6,4},{7,5},{8,10},{9,11},{10,... | collective-permute-start | bytes 2359304 | tf_op jit(solution)/shard_map/ffn_sum/ppermute | solution.py:776
  352.4 35.1 %collective-permute-start.37 = (bf16[256,1536]{1,0:T(8,128)(2,1)}, bf16[256,1536]{1,0:T(8,128)(2,1)}, u32[]{:S(2)}, u32[]{:S(2)}) collective-permute-start(bf16[256,1536]{1,0:T(8,128)(2,1)} %get-tuple-element.156), channel_id=1, source_target_pairs={{0,3},{1,2},{2,1},{3,0},{4,7},{5,6},{6,5},{7,4},{8,11},{9,10},{10,... | collective-permute-start | bytes 2359304 | tf_op jit(solution)/shard_map/ffn_sum/ppermute | solution.py:776
  353.0 34.5 %collective-permute-start.34 = (bf16[192,1792]{1,0:T(8,128)(2,1)}, bf16[192,1792]{1,0:T(8,128)(2,1)}, u32[]{:S(2)}, u32[]{:S(2)}) collective-permute-start(bf16[192,1792]{1,0:T(8,128)(2,1)} %join.4), channel_id=1, source_target_pairs={{0,8},{4,12},{8,16},{12,20},{16,24},{20,28},{24,0},{28,4},{1,9},{5... | collective-permute-start | bytes 2064392 | tf_op jit(solution)/shard_map/gate_grad_hop2/ppermute | solution.py:754
  402.3 35.5 %collective-permute-start.40 = (bf16[256,1536]{1,0:T(8,128)(2,1)S(1)}, bf16[256,1536]{1,0:T(8,128)(2,1)}, u32[]{:S(2)}, u32[]{:S(2)}) collective-permute-start(bf16[256,1536]{1,0:T(8,128)(2,1)S(1)} %get-tuple-element.162.refs_3_), channel_id=1, source_target_pairs={{0,3},{1,2},{2,1},{3,0},{4,7},{5,6},{6,5},{7,4},{8,11},{9,10},{10,... | collective-permute-start | bytes 2359304 | tf_op jit(solution)/shard_map/one_sum/ppermute | solution.py:776
  404.7 33.1 %collective-permute-start.38 = (bf16[256,1536]{1,0:T(8,128)(2,1)S(1)}, bf16[256,1536]{1,0:T(8,128)(2,1)}, u32[]{:S(2)}, u32[]{:S(2)}) collective-permute-start(bf16[256,1536]{1,0:T(8,128)(2,1)S(1)} %get-tuple-element.160.refs_1_), channel_id=1, source_target_pairs={{0,1},{1,0},{2,3},{3,2},{4,5},{5,4},{6,7},{7,6},{8,9},{9,8},{10,11... | collective-permute-start | bytes 2359304 | tf_op jit(solution)/shard_map/one_sum/ppermute | solution.py:776
  405.3 32.5 %collective-permute-start.39 = (bf16[256,1536]{1,0:T(8,128)(2,1)S(1)}, bf16[256,1536]{1,0:T(8,128)(2,1)}, u32[]{:S(2)}, u32[]{:S(2)}) collective-permute-start(bf16[256,1536]{1,0:T(8,128)(2,1)S(1)} %get-tuple-element.161.refs_2_), channel_id=1, source_target_pairs={{0,2},{1,3},{2,0},{3,1},{4,6},{5,7},{6,4},{7,5},{8,10},{9,11},{10,... | collective-permute-start | bytes 2359304 | tf_op jit(solution)/shard_map/one_sum/ppermute | solution.py:776
  405.9 29.1 %collective-permute-start.41 = (bf16[192,1792]{1,0:T(8,128)(2,1)S(1)}, bf16[192,1792]{1,0:T(8,128)(2,1)}, u32[]{:S(2)}, u32[]{:S(2)}) collective-permute-start(bf16[192,1792]{1,0:T(8,128)(2,1)S(1)} %copy-done.52), channel_id=1, source_target_pairs={{0,8},{4,12},{8,16},{12,20},{16,24},{20,28},{24,0},{28,4},{1,9},{5... | collective-permute-start | bytes 2064392 | tf_op jit(solution)/shard_map/gate_grad_hop3/ppermute | solution.py:754
  437.8 21.9 %copy-start.75 = (bf16[192,1792]{1,0:T(8,128)(2,1)S(1)}, bf16[192,1792]{1,0:T(8,128)(2,1)}, u32[]{:S(2)}) copy-start(bf16[192,1792]{1,0:T(8,128)(2,1)} %reduce-scatter.4.cloned.1.call-done) | copy-start | bytes 2064388
  437.9 23.0 %copy-start.76 = (bf16[192,1792]{1,0:T(8,128)(2,1)S(1)}, bf16[192,1792]{1,0:T(8,128)(2,1)}, u32[]{:S(2)}) copy-start(bf16[192,1792]{1,0:T(8,128)(2,1)} %reduce-scatter.6.cloned.1.call-done) | copy-start | bytes 2064388
  442.1 4.7 collective-permute-start.44
  444.5 3.7 collective-permute-start.43
  445.1 3.7 collective-permute-start.42
  448.8 1.2 collective-permute-start.45
  450.1 5.6 %collective-permute-start.48 = (f32[1,3584]{1,0:T(1,128)S(1)}, f32[1,3584]{1,0:T(1,128)S(1)}, u32[]{:S(2)}, u32[]{:S(2)}) collective-permute-start(f32[1,3584]{1,0:T(1,128)S(1)} %add.119), channel_id=1, source_target_pairs={{0,24},{4,28},{8,16},{12,20},{16,8},{20,12},{24,0},{28,4},{1,25},{... | collective-permute-start | bytes 43016 | tf_op jit(solution)/shard_map/ppermute | solution.py:929
  453.2 4.6 collective-permute-start.47
  453.2 4.6 collective-permute-start.46
  (70 other events, 282.4 us)
Sparse Core Ops, SparseCore 0:
  30.0 157.8 all-gather.1
  244.3 60.4 reduce-scatter.3
  307.2 90.2 reduce-scatter.5
  402.5 49.6 reduce-scatter.7

commit v5 on v4

--- a/solution.py
+++ b/solution.py
@@ -316,7 +316,7 @@
         ],
         out_specs=pl.BlockSpec((depth, tile), lambda i: (0, i)),
         out_shape=jax.ShapeDtypeStruct((depth, cols * len(rights)), LOW),
-        compiler_params=pltpu.CompilerParams(vmem_limit_bytes=40 * 2**20),
+        compiler_params=pltpu.CompilerParams(vmem_limit_bytes=56 * 2**20),
         cost_estimate=FREE,
         name="product",
     )(left, *rights)
@@ -532,7 +532,7 @@
     out_ref[...] = jnp.dot(left_ref[...], right_ref[0], preferred_element_type=F32).astype(LOW)
 
 
-def rows_product(left, right, ranks):
+def rows_product(left, right, ranks, grant):
     length, depth = left.shape
     rows = length // ranks
     return pl.pallas_call(
@@ -544,7 +544,7 @@
         ],
         out_specs=pl.BlockSpec((rows, right.shape[2]), lambda i: (i, 0)),
         out_shape=jax.ShapeDtypeStruct((length, right.shape[2]), LOW),
-        compiler_params=pltpu.CompilerParams(vmem_limit_bytes=24 * 2**20),
+        compiler_params=pltpu.CompilerParams(vmem_limit_bytes=grant * 2**20),
         cost_estimate=FREE,
         name="rows_product",
     )(left, right)
@@ -851,7 +851,7 @@
     attn_arrived[0] = tie(attn_arrived[0], grad_all)
     hidden, normed_two_own = sum_up(tokens, [attn_parts[0]] + attn_arrived, ffn_gain)
     normed_two = spread("two_spread", normed_two_own)
-    d_activation = rows_product(grad_all, ffn_full, ranks)
+    d_activation = rows_product(grad_all, ffn_full, ranks, 56)
     normed_two[-1] = tie(normed_two[-1], d_activation)
     normed_two_all, normed_two_t, *normed_two_pair = fold(core_array, normed_two, ring, True)
 
@@ -905,7 +905,7 @@
     hidden_grad_all, hidden_grad_t = fold(core_array, hidden_grad, ring)
     ffn_go = lax.optimization_barrier(tuple(ffn_parts) + tuple(hidden_grad))[:ranks]
     ffn_arrived = send_parts("ffn_sum", ffn_go)
-    d_attended = rows_product(hidden_grad_all, out_t[None], ranks)
+    d_attended = rows_product(hidden_grad_all, out_t[None], ranks, 24)
     d_queries, d_keys, d_values = attend_back(
         me_array, query_low, key_low, value_low, bounds, attended, d_attended, lse, ranks, heads
     )
@@ -931,18 +931,22 @@
             pieces = [a + b for a, b in zip(pieces[::2], pieces[1::2])]
         return pieces[0]
 
+    gate_flow = tie(gate_flow, output, gains)
+    (down_grad,) = cut_grads(tie(down_grad, output), (hidden_cols,))
+    lift_grad = lift_grad[:, :hidden_cols].astype(F32)
+    *one_arrived, gate_flow, total, down_grad, lift_grad = lax.optimization_barrier(
+        (*one_arrived, gate_flow, gains, down_grad, lift_grad)
+    )
+    total = exchange_sum(total, "tensor", range(1, ranks), ranks)
     (gate_grad,) = last_join(
-        owner_after(last), tie(gate_flow, output), gate_near, gate_other, ring, hidden_cols, 1
-    )
-    one_arrived[-1] = tie(one_arrived[-1], output, gains, gate_grad)
+        owner_after(last), gate_flow, gate_near, gate_other, ring, hidden_cols, 1
+    )
     (tokens_grad,) = norm_back_sum(tokens, attn_gain, d_hidden, [one_parts[0]] + one_arrived, False)
-    lift_grad = lift_grad[:, :hidden_cols].astype(F32)
     query_grad, key_grad, value_grad, out_grad = cut_grads(
         attn_grad, (q_cols, kv_cols, kv_cols, q_cols)
     )
-    down_grad = down_grad[:, :hidden_cols].astype(F32)
-
-    total = exchange_sum(tie(gains, tokens_grad), "tensor", range(1, ranks), ranks)
+
+    total = tie(total, tokens_grad, gate_grad)
     total = exchange_sum(total, "dp", range(1, 2), dp_size)
     total = exchange_sum(total, "dp", range(2, dp_size, 2), dp_size)
     total = total.reshape(-1)
@@ -962,7 +966,7 @@
         total[a:b],
         gate_grad,
         lift_grad,
-        down_grad.T,
+        down_grad,
     )
 
 

time: 473 us -> 470 us (level)
  Pallas kernels: 159 us -> 178 us
  local copies, waits for them, and re-layouts: 60.1 us -> 44.3 us
  waiting for transfers between devices: 163 us -> 156 us
    unnamed x166 -> x147, local copies, waits for them, and re-layouts: 53.4 us -> 37.6 us
    pallas_call x4, Pallas kernels: 24.7 us -> 38.8 us  [product(): pl.pallas_call(functools.partial(product_kernel, tiles), grid=(tiles * le...]
    ppermute x9, waiting for transfers between devices: 75.2 us -> 69.8 us  [onward(): return lax.ppermute(v, 'dp', ring_pairs)]
  transfers between devices with their start and end apart: 53 -> 53, of which waited for: 25 -> 22; matrix products, arithmetic and copies ran while one was open for 4% -> 4% of each run, Pallas kernels for 32% -> 35%
where the time goes in v5:
time: 470 us; the launch traced here: 468 us
  Pallas kernels  178 us (38%)
  waiting for transfers between devices  156 us (33%)
  local copies, waits for them, and re-layouts  44.3 us (9%)
  starting transfers between devices  40.8 us (9%)
  matrix products  24.1 us (5%)
  between operations  14.5 us (3%)
  other arithmetic  10.2 us (2%)
    ppermute x9, waiting for transfers between devices, onward(): return lax.ppermute(v, 'dp', ring_pairs)  69.8 us
    ppermute x12, waiting for transfers between devices, send_parts(): lax.ppermute(parts[j], 'tensor', [(i, i ^ j) for i in range(ranks)])  41.2 us
    pallas_call x4, Pallas kernels, product(): pl.pallas_call(functools.partial(product_kernel, tiles), grid=(tiles * le...  38.8 us
    unnamed x147, local copies, waits for them, and re-layouts  37.6 us
    pallas_call x4, Pallas kernels, back_parts(): pl.pallas_call(functools.partial(back_parts_kernel, rows, len(lefts)), gr...  36.5 us
    dot_general x2, matrix products, mm(): return jnp.dot(left, right, preferred_element_type=F32)  24.1 us
    all_gather x1, waiting for transfers between devices, shards(): lax.all_gather(tie(jnp.stack([widen(w_down.T), widen(w_gate), widen(w_up)...  21.4 us
    pallas_call x1, Pallas kernels, attend_back(): pl.pallas_call(functools.partial(attend_back_kernel, heads, rows), grid_s...  16.7 us
  transfers between devices with their start and end apart: 53, of which 22 were waited for; matrix products, arithmetic and copies ran while one was open for 4% of the time, Pallas kernels for 35%

profile of v5, /device:TPU:0, one launch (start us, length us, event | category | flops | bytes accessed | tf_op | source)
XLA Modules:
  0.0 468.3 jit_solution(8561328598226270676)
XLA Ops:
  9.9 3.1 collective-permute-start.4
  14.4 6.5 %collective-permute-done.4.refs_2_ = bf16[192,640]{1,0:T(8,128)(2,1)S(1)} collective-permute-done((bf16[192,640]{1,0:T(8,128)(2,1)S(1)}, bf16[192,640]{1,0:T(8,128)(2,1)S(1)}, u32[]{:S(2)}, u32[]{:S(2)}) %collective-permute-start.4) | collective-permute-done | bytes 245792 | tf_op jit(solution)/shard_map/qkv_hop1/ppermute | solution.py:754
  20.9 1.5 pad_maximum_fusion
  22.5 7.4 %collective-permute-done.6.refs_4_ = bf16[192,640]{1,0:T(8,128)(2,1)S(1)} collective-permute-done((bf16[192,640]{1,0:T(8,128)(2,1)S(1)}, bf16[192,640]{1,0:T(8,128)(2,1)S(1)}, u32[]{:S(2)}, u32[]{:S(2)}) %collective-permute-start.6) | collective-permute-done | bytes 245792 | tf_op jit(solution)/shard_map/qkv_hop2/ppermute | solution.py:754
  30.8 2.3 collective-permute-start.2
  38.0 5.5 %collective-permute-done.14.refs_2_ = bf16[192,384]{1,0:T(8,128)(2,1)} collective-permute-done((bf16[192,384]{1,0:T(8,128)(2,1)S(1)}, bf16[192,384]{1,0:T(8,128)(2,1)}, u32[]{:S(2)}, u32[]{:S(2)}) %collective-permute-start.14) | collective-permute-done | bytes 147488 | tf_op jit(solution)/shard_map/out_hop1/ppermute | solution.py:754
  43.5 9.0 %collective-permute-done.8.refs_6_ = bf16[192,640]{1,0:T(8,128)(2,1)S(1)} collective-permute-done((bf16[192,640]{1,0:T(8,128)(2,1)}, bf16[192,640]{1,0:T(8,128)(2,1)S(1)}, u32[]{:S(2)}, u32[]{:S(2)}) %collective-permute-start.8) | collective-permute-done | bytes 245792 | tf_op jit(solution)/shard_map/qkv_hop3/ppermute | solution.py:754
  54.1 3.7 fusion.14
  58.8 7.7 %collective-permute-done.1.refs_2_ = bf16[256,1536]{1,0:T(8,128)(2,1)S(1)} collective-permute-done((bf16[256,1536]{1,0:T(8,128)(2,1)S(1)}, bf16[256,1536]{1,0:T(8,128)(2,1)S(1)}, u32[]{:S(2)}, u32[]{:S(2)}) %collective-permute-start.1) | collective-permute-done | bytes 786464 | tf_op jit(solution)/shard_map/one_spread/ppermute | solution.py:769
  74.0 1.6 copy-done.8
  75.6 3.5 collective-permute-done.16.refs_4_
  79.1 1.7 collective-permute-start.12
  85.6 2.9 place.2.w_ref
  88.6 5.5 %prepare.1 = (bf16[1024,384]{1,0:T(8,128)(2,1)S(1)}, bf16[1024,128]{1,0:T(8,128)(2,1)S(1)}, bf16[1024,128]{1,0:T(8,128)(2,1)S(1)}, f32[1024,512]{1,0:T(8,128)S(1)}) custom-call(bf16[1024,1536]{1,0:T(8,128)(2,1)S(1)} %get-tuple-element.171.x_ref.normed_ref, bf16[1536,640]{1,0:T(8,128)(2,1)S(1)} %place.2.w_ref, f32[1024,128]{1,0:T(8,128)S(1)} %copy-done.7, ...), custom_call_target="tpu_custom_call" | custom-call | tf_op jit(solution)/shard_map/prepare/pallas_call | solution.py:633
  97.2 12.8 %attend.1 = (bf16[1024,384]{1,0:T(8,128)(2,1)S(1)}, f32[4,2,768]{2,1,0:T(2,128)S(1)}) custom-call(s32[1]{0:T(128)} %bitcast.me_ref, bf16[1024,384]{1,0:T(8,128)(2,1)S(1)} %get-tuple-element.104.q_ref, bf16[1024,128]{1,0:T(8,128)(2,1)S(1)} %get-tuple-element.105.k_ref, bf16[1024,128]{1,0:T(8,128)(2,1)S(1)} %get-tuple-element.106.v_ref, ...), custom_call_target="tpu_custom_call" | custom-call | flops 6442450944 | bytes 33554432 | tf_op jit(solution)/shard_map/attend/pallas_call | solution.py:178
  113.8 2.3 place.3
  116.2 3.0 back_parts.4
  125.4 1.6 copy-done.10
  127.0 1.7 copy-done.15
  128.6 12.0 %collective-permute-done.20.refs_1_ = bf16[256,1536]{1,0:T(8,128)(2,1)S(1)} collective-permute-done((bf16[256,1536]{1,0:T(8,128)(2,1)S(1)}, bf16[256,1536]{1,0:T(8,128)(2,1)S(1)}, u32[]{:S(2)}, u32[]{:S(2)}) %collective-permute-start.20) | collective-permute-done | bytes 786464 | tf_op jit(solution)/shard_map/attn_sum/ppermute | solution.py:776
  140.6 17.0 %collective-permute-done.21.refs_2_ = bf16[256,1536]{1,0:T(8,128)(2,1)S(1)} collective-permute-done((bf16[256,1536]{1,0:T(8,128)(2,1)S(1)}, bf16[256,1536]{1,0:T(8,128)(2,1)S(1)}, u32[]{:S(2)}, u32[]{:S(2)}) %collective-permute-start.21) | collective-permute-done | bytes 786464 | tf_op jit(solution)/shard_map/attn_sum/ppermute | solution.py:776
  159.3 3.6 sum_up.2
  163.0 1.5 collective-permute-start.25
  164.6 1.9 collective-permute-start.23
  166.5 21.4 %all-gather.2.cloned.1.call-done.right_ref.refs_2_.refs_3_.refs_1_ = bf16[3,1536,1792]{2,1,0:T(8,128)(2,1)} async-done(((bf16[3,192,1792]{2,1,0:T(8,128)(2,1)}), bf16[3,1536,1792]{2,1,0:T(8,128)(2,1)}) %all-gather.2.cloned.1.call-update) | async-done | bytes 16515088 | tf_op jit(solution)/shard_map/all_gather | solution.py:799
  187.9 10.2 %rows_product.2 = bf16[1024,1792]{1,0:T(8,128)(2,1)} custom-call(bf16[1024,1536]{1,0:T(8,128)(2,1)} %copy-done.15, bf16[3,1536,1792]{2,1,0:T(8,128)(2,1)} %all-gather.2.cloned.1.call-done.right_ref.refs_2_.refs_3_.refs_1_), custom_call_target="tpu_custom_call" | custom-call | tf_op jit(solution)/shard_map/rows_product/pallas_call | solution.py:538
  198.9 2.5 fold.6
  202.6 10.3 %fusion.10 = bf16[1024,1792]{1,0:T(8,128)(2,1)S(1)} fusion(bf16[1024,1536]{1,0:T(8,128)(2,1)S(1)} %get-tuple-element.125, bf16[3,1536,1792]{2,1,0:T(8,128)(2,1)} %all-gather.2.cloned.1.call-done.right_ref.refs_2_.refs_3_.refs_1_), kind=kOutput, calls=%fused_computation.18 | convolution fusion | flops 5638979584 | bytes 12320768 | tf_op jit(solution)/shard_map/dot_general | solution.py:40
  213.0 13.8 %multiply_convert_fusion = (bf16[1024,1792]{1,0:T(8,128)(2,1)}, bf16[1024,1792]{1,0:T(8,128)(2,1)}, bf16[1024,1792]{1,0:T(8,128)(2,1)}) fusion(bf16[1024,1792]{1,0:T(8,128)(2,1)S(1)} %fusion.10, bf16[1024,1792]{1,0:T(8,128)(2,1)S(1)} %copy-done.57, bf16[1024,1536]{1,0:T(8,128)(2,1)S(1)} %get-tuple-element.125, ...), kind=kOutput, calls=%fused_computation.13 | convolution fusion | flops 5668339712 | bytes 27000832 | tf_op jit(solution)/shard_map/dot_general | solution.py:40
  226.8 11.0 %product.4 = bf16[1536,1792]{1,0:T(8,128)(2,1)} custom-call(bf16[1536,1024]{1,0:T(8,128)(2,1)} %copy-done.10, bf16[1024,1792]{1,0:T(8,128)(2,1)} %get-tuple-element.142.refs_0_), custom_call_target="tpu_custom_call" | custom-call | tf_op jit(solution)/shard_map/product/pallas_call | solution.py:309
  237.9 16.6 %back_parts.5 = (bf16[256,1536]{1,0:T(8,128)(2,1)S(1)}, bf16[256,1536]{1,0:T(8,128)(2,1)S(1)}, bf16[256,1536]{1,0:T(8,128)(2,1)S(1)}, bf16[256,1536]{1,0:T(8,128)(2,1)S(1)}) custom-call(bf16[1024,1792]{1,0:T(8,128)(2,1)} %get-tuple-element.135.refs_0_, bf16[1024,1792]{1,0:T(8,128)(2,1)} %get-tuple-element.137.refs_1_.refs_0_, ...), custom_call_target="tpu_custom_call" | custom-call | tf_op jit(solution)/shard_map/back_parts/pallas_call | solution.py:365
  257.3 1.5 collective-permute-start.28
  258.8 8.4 %product.5 = bf16[768,1792]{1,0:T(8,128)(2,1)} custom-call(bf16[768,1024]{1,0:T(8,128)(2,1)} %copy-done.20, bf16[1024,1792]{1,0:T(8,128)(2,1)} %get-tuple-element.135.refs_0_), custom_call_target="tpu_custom_call" | custom-call | tf_op jit(solution)/shard_map/product/pallas_call | solution.py:309
  267.2 8.3 %product.6.refs_0_.refs_1_.near_ref = bf16[768,1792]{1,0:T(8,128)(2,1)} custom-call(bf16[768,1024]{1,0:T(8,128)(2,1)} %copy-done.19, bf16[1024,1792]{1,0:T(8,128)(2,1)} %get-tuple-element.135.refs_0_), custom_call_target="tpu_custom_call" | custom-call | tf_op jit(solution)/shard_map/product/pallas_call | solution.py:309
  275.6 11.0 %product.7 = bf16[1536,1792]{1,0:T(8,128)(2,1)} custom-call(bf16[1536,1024]{1,0:T(8,128)(2,1)} %copy-done.11, bf16[1024,1792]{1,0:T(8,128)(2,1)} %get-tuple-element.137.refs_1_.refs_0_), custom_call_target="tpu_custom_call" | custom-call | tf_op jit(solution)/shard_map/product/pallas_call | solution.py:309
  286.6 6.0 %collective-permute-done.27.refs_2_ = bf16[256,1536]{1,0:T(8,128)(2,1)} collective-permute-done((bf16[256,1536]{1,0:T(8,128)(2,1)S(1)}, bf16[256,1536]{1,0:T(8,128)(2,1)}, u32[]{:S(2)}, u32[]{:S(2)}) %collective-permute-start.27) | collective-permute-done | bytes 786464 | tf_op jit(solution)/shard_map/two_sum/ppermute | solution.py:776
  292.6 4.5 norm_back_sum.2
  297.1 5.4 %reduce-scatter.4.cloned.1.call-done.grads_ref = bf16[192,1792]{1,0:T(8,128)(2,1)} async-done(((bf16[1536,1792]{1,0:T(8,128)(2,1)}), bf16[192,1792]{1,0:T(8,128)(2,1)}) %reduce-scatter.4.cloned.1.call-update) | async-done | bytes 688144 | tf_op jit(solution)/shard_map/reduce_scatter | solution.py:881
  302.7 1.5 collective-permute-start.29
  306.3 1.9 collective-permute-done.32.refs_1_.refs_2_.other_ref
  308.1 2.0 join.3
  310.2 10.5 %back_parts.6 = (bf16[256,1536]{1,0:T(8,128)(2,1)S(1)}, bf16[256,1536]{1,0:T(8,128)(2,1)}, bf16[256,1536]{1,0:T(8,128)(2,1)}, bf16[256,1536]{1,0:T(8,128)(2,1)}) custom-call(bf16[1024,1792]{1,0:T(8,128)(2,1)} %get-tuple-element.142.refs_0_, bf16[3,1536,1792]{2,1,0:T(8,128)(2,1)} %all-gather.2.cloned.1.call-done.right_ref.refs_2_.refs_3_.refs_1_), custom_call_target="tpu_custom_call" | custom-call | tf_op jit(solution)/shard_map/back_parts/pallas_call | solution.py:365
  320.7 2.8 collective-permute-done.29.refs_1_
  323.4 21.6 %collective-permute-done.33.refs_0_ = bf16[192,1792]{1,0:T(8,128)(2,1)} collective-permute-done((bf16[192,1792]{1,0:T(8,128)(2,1)}, bf16[192,1792]{1,0:T(8,128)(2,1)}, u32[]{:S(2)}, u32[]{:S(2)}) %collective-permute-start.33) | collective-permute-done | bytes 688160 | tf_op jit(solution)/shard_map/gate_grad_hop1/ppermute | solution.py:754
  345.0 2.2 join.4
  347.2 1.5 collective-permute-start.35
  348.7 1.5 collective-permute-start.36
  351.9 2.7 fold.7
  354.7 2.6 rows_product.3.do_ref
  357.4 16.7 %attend_back.1 = (f32[1024,384]{1,0:T(8,128)S(1)}, f32[1024,128]{1,0:T(8,128)S(1)}, f32[1024,128]{1,0:T(8,128)S(1)}) custom-call(s32[1]{0:T(128)} %bitcast.me_ref, bf16[1024,384]{1,0:T(8,128)(2,1)S(1)} %copy-done.23, bf16[1024,128]{1,0:T(8,128)(2,1)S(1)} %copy-done.43, bf16[1024,128]{1,0:T(8,128)(2,1)S(1)} %copy-done.45, s32[4,1,256]{2,1,0:T(1,128)S(1)} %reshape.123.lo_ref, ...), custom_call_target="tpu_custom_call" | custom-call | tf_op jit(solution)/shard_map/attend_back/pallas_call | solution.py:204
  376.8 7.7 %prepare_back.1 = (bf16[1024,640]{1,0:T(8,128)(2,1)}, f32[1,512]{1,0:T(1,128)}) custom-call(f32[1024,384]{1,0:T(8,128)} %copy-done.18, f32[1024,128]{1,0:T(8,128)} %copy-done.39, f32[1024,128]{1,0:T(8,128)} %copy-done.40, f32[1024,512]{1,0:T(8,128)} %copy-done.17, f32[1024,128]{1,0:T(8,128)} %get-tuple-element.214.cos_ref, ...), custom_call_target="tpu_custom_call" | custom-call | tf_op jit(solution)/shard_map/prepare_back/pallas_call | solution.py:687
  385.3 1.6 join.5
  387.7 6.4 %back_parts.7 = (bf16[256,1536]{1,0:T(8,128)(2,1)S(1)}, bf16[256,1536]{1,0:T(8,128)(2,1)}, bf16[256,1536]{1,0:T(8,128)(2,1)S(1)}, bf16[256,1536]{1,0:T(8,128)(2,1)S(1)}) custom-call(bf16[1024,640]{1,0:T(8,128)(2,1)S(1)} %copy-done.5, bf16[1,1536,640]{2,1,0:T(8,128)(2,1)} %bitcast.33), custom_call_target="tpu_custom_call" | custom-call | tf_op jit(solution)/shard_map/back_parts/pallas_call | solution.py:365
  395.0 5.7 %attn_products.1 = bf16[1536,1024]{1,0:T(8,128)(2,1)} custom-call(bf16[1536,1024]{1,0:T(8,128)(2,1)S(1)} %copy-done.9, bf16[1536,1024]{1,0:T(8,128)(2,1)S(1)} %get-tuple-element.153.refs_1_, bf16[1024,640]{1,0:T(8,128)(2,1)S(1)} %copy-done.5, bf16[1024,384]{1,0:T(8,128)(2,1)S(1)} %get-tuple-element.109.refs_0_.o_ref.refs_3_), custom_call_target="tpu_custom_call" | custom-call | tf_op jit(solution)/shard_map/attn_products/pallas_call | solution.py:342
  405.9 4.0 gain_parts.1
  409.9 3.5 sum_up.3
  413.4 15.7 %collective-permute-done.41.flow_ref = bf16[192,1792]{1,0:T(8,128)(2,1)S(1)} collective-permute-done((bf16[192,1792]{1,0:T(8,128)(2,1)S(1)}, bf16[192,1792]{1,0:T(8,128)(2,1)S(1)}, u32[]{:S(2)}, u32[]{:S(2)}) %collective-permute-start.41) | collective-permute-done | bytes 688160 | tf_op jit(solution)/shard_map/gate_grad_hop3/ppermute | solution.py:754
  430.6 6.3 %collective-permute-done.39.refs_2_ = bf16[256,1536]{1,0:T(8,128)(2,1)S(1)} collective-permute-done((bf16[256,1536]{1,0:T(8,128)(2,1)S(1)}, bf16[256,1536]{1,0:T(8,128)(2,1)S(1)}, u32[]{:S(2)}, u32[]{:S(2)}) %collective-permute-start.39) | collective-permute-done | bytes 786464 | tf_op jit(solution)/shard_map/one_sum/ppermute | solution.py:776
  438.4 1.5 collective-permute-start.43
  440.5 4.1 norm_back_sum.3
  444.6 2.8 last_join.1
  448.8 3.7 collective-permute-start.48
  453.2 1.6 copy.28
  454.8 2.3 collective-permute-done.47
  (259 shorter events, 69.2 us)
Async XLA Ops:
  7.2 180.7 %all-gather.2.cloned.1.call-start = ((), (), s32[]{:S(2)}) async-start(), calls=%async_computation.3 | async-start | bytes 18579456 | tf_op jit(solution)/shard_map/all_gather | solution.py:799
  9.9 11.1 %collective-permute-start.4 = (bf16[192,640]{1,0:T(8,128)(2,1)S(1)}, bf16[192,640]{1,0:T(8,128)(2,1)S(1)}, u32[]{:S(2)}, u32[]{:S(2)}) collective-permute-start(bf16[192,640]{1,0:T(8,128)(2,1)S(1)} %constant_dynamic-update-slice_fusion.refs_0_), channel_id=1, source_target_pairs={{0,8},{4,12},{8,16},{12,20},{16,24},{20,28},{24,0},{28,4},{1,9},{5... | collective-permute-start | bytes 737288 | tf_op jit(solution)/shard_map/qkv_hop1/ppermute | solution.py:754
  14.4 15.5 %copy-start.56 = (bf16[256,1536]{1,0:T(8,128)(2,1)S(1)}, bf16[256,1536]{1,0:T(8,128)(2,1)}, u32[]{:S(2)}) copy-start(bf16[256,1536]{1,0:T(8,128)(2,1)} %value_ref.1) | copy-start | bytes 2359300
  20.9 8.9 %collective-permute-start.6 = (bf16[192,640]{1,0:T(8,128)(2,1)S(1)}, bf16[192,640]{1,0:T(8,128)(2,1)S(1)}, u32[]{:S(2)}, u32[]{:S(2)}) collective-permute-start(bf16[192,640]{1,0:T(8,128)(2,1)S(1)} %collective-permute-done.4.refs_2_), channel_id=1, source_target_pairs={{0,8},{4,12},{8,16},{12,20},{16,24},{20,28},{24,0},{28,4},{1,9},{5... | collective-permute-start | bytes 737288 | tf_op jit(solution)/shard_map/qkv_hop2/ppermute | solution.py:754
  29.9 272.7 %reduce-scatter.4.cloned.1.call-start = ((), (), s32[]{:S(2)}) async-start(), calls=%async_computation.4 | async-start | bytes 6193152 | tf_op jit(solution)/shard_map/reduce_scatter | solution.py:881
  30.8 37.5 %copy-start.13 = (bf16[256,1536]{1,0:T(8,128)(2,1)}, bf16[256,1536]{1,0:T(8,128)(2,1)S(1)}, u32[]{:S(2)}) copy-start(bf16[256,1536]{1,0:T(8,128)(2,1)S(1)} %fusion.13.refs_0_) | copy-start | bytes 2359300
  30.8 21.7 %collective-permute-start.2 = (bf16[256,1536]{1,0:T(8,128)(2,1)S(1)}, bf16[256,1536]{1,0:T(8,128)(2,1)S(1)}, u32[]{:S(2)}, u32[]{:S(2)}) collective-permute-start(bf16[256,1536]{1,0:T(8,128)(2,1)S(1)} %fusion.13.refs_0_), channel_id=1, source_target_pairs={{0,3},{1,2},{2,1},{3,0},{4,7},{5,6},{6,5},{7,4},{8,11},{9,10},{10,... | collective-permute-start | bytes 2359304 | tf_op jit(solution)/shard_map/one_spread/ppermute | solution.py:769
  33.1 33.4 %collective-permute-start.1 = (bf16[256,1536]{1,0:T(8,128)(2,1)S(1)}, bf16[256,1536]{1,0:T(8,128)(2,1)S(1)}, u32[]{:S(2)}, u32[]{:S(2)}) collective-permute-start(bf16[256,1536]{1,0:T(8,128)(2,1)S(1)} %fusion.13.refs_0_), channel_id=1, source_target_pairs={{0,2},{1,3},{2,0},{3,1},{4,6},{5,7},{6,4},{7,5},{8,10},{9,11},{10,... | collective-permute-start | bytes 2359304 | tf_op jit(solution)/shard_map/one_spread/ppermute | solution.py:769
  33.6 33.7 %collective-permute-start = (bf16[256,1536]{1,0:T(8,128)(2,1)S(1)}, bf16[256,1536]{1,0:T(8,128)(2,1)S(1)}, u32[]{:S(2)}, u32[]{:S(2)}) collective-permute-start(bf16[256,1536]{1,0:T(8,128)(2,1)S(1)} %fusion.13.refs_0_), channel_id=1, source_target_pairs={{0,1},{1,0},{2,3},{3,2},{4,5},{5,4},{6,7},{7,6},{8,9},{9,8},{10,11... | collective-permute-start | bytes 2359304 | tf_op jit(solution)/shard_map/one_spread/ppermute | solution.py:769
  34.4 9.1 %collective-permute-start.14 = (bf16[192,384]{1,0:T(8,128)(2,1)S(1)}, bf16[192,384]{1,0:T(8,128)(2,1)}, u32[]{:S(2)}, u32[]{:S(2)}) collective-permute-start(bf16[192,384]{1,0:T(8,128)(2,1)S(1)} %bitcast.36), channel_id=1, source_target_pairs={{0,8},{4,12},{8,16},{12,20},{16,24},{20,28},{24,0},{28,4},{1,9},{5... | collective-permute-start | bytes 442376 | tf_op jit(solution)/shard_map/out_hop1/ppermute | solution.py:754
  37.8 14.7 %collective-permute-start.8 = (bf16[192,640]{1,0:T(8,128)(2,1)}, bf16[192,640]{1,0:T(8,128)(2,1)S(1)}, u32[]{:S(2)}, u32[]{:S(2)}) collective-permute-start(bf16[192,640]{1,0:T(8,128)(2,1)} %copy-done.48), channel_id=1, source_target_pairs={{0,8},{4,12},{8,16},{12,20},{16,24},{20,28},{24,0},{28,4},{1,9},{5... | collective-permute-start | bytes 737288 | tf_op jit(solution)/shard_map/qkv_hop3/ppermute | solution.py:754
  43.5 35.6 %collective-permute-start.3 = (bf16[192,640]{1,0:T(8,128)(2,1)S(1)}, bf16[192,640]{1,0:T(8,128)(2,1)}, u32[]{:S(2)}, u32[]{:S(2)}) collective-permute-start(bf16[192,640]{1,0:T(8,128)(2,1)S(1)} %constant_dynamic-update-slice_fusion.refs_0_), channel_id=1, source_target_pairs={{0,4},{4,0},{8,12},{12,8},{16,20},{20,16},{24,28},{28,24},{1,5},{5... | collective-permute-start | bytes 737288 | tf_op jit(solution)/shard_map/ppermute | solution.py:751
  52.5 28.3 %collective-permute-start.5 = (bf16[192,640]{1,0:T(8,128)(2,1)}, bf16[192,640]{1,0:T(8,128)(2,1)}, u32[]{:S(2)}, u32[]{:S(2)}) collective-permute-start(bf16[192,640]{1,0:T(8,128)(2,1)} %copy-done.46), channel_id=1, source_target_pairs={{0,4},{4,0},{8,12},{12,8},{16,20},{20,16},{24,28},{28,24},{1,5},{5... | collective-permute-start | bytes 737288 | tf_op jit(solution)/shard_map/ppermute | solution.py:751
  54.1 27.5 %collective-permute-start.7 = (bf16[192,640]{1,0:T(8,128)(2,1)}, bf16[192,640]{1,0:T(8,128)(2,1)}, u32[]{:S(2)}, u32[]{:S(2)}) collective-permute-start(bf16[192,640]{1,0:T(8,128)(2,1)} %copy-done.48), channel_id=1, source_target_pairs={{0,4},{4,0},{8,12},{12,8},{16,20},{20,16},{24,28},{28,24},{1,5},{5... | collective-permute-start | bytes 737288 | tf_op jit(solution)/shard_map/ppermute | solution.py:751
  58.8 29.8 %copy-start.55 = (f32[512]{0:T(512)}, f32[512]{0:T(512)S(1)}, u32[]{:S(2)}) copy-start(f32[512]{0:T(512)S(1)} %concatenate.11) | copy-start | bytes 6148
  67.3 11.7 %collective-permute-start.16 = (bf16[192,384]{1,0:T(8,128)(2,1)}, bf16[192,384]{1,0:T(8,128)(2,1)}, u32[]{:S(2)}, u32[]{:S(2)}) collective-permute-start(bf16[192,384]{1,0:T(8,128)(2,1)} %collective-permute-done.14.refs_2_), channel_id=1, source_target_pairs={{0,8},{4,12},{8,16},{12,20},{16,24},{20,28},{24,0},{28,4},{1,9},{5... | collective-permute-start | bytes 442376 | tf_op jit(solution)/shard_map/out_hop2/ppermute | solution.py:754
  68.2 14.5 %collective-permute-start.9 = (bf16[192,640]{1,0:T(8,128)(2,1)}, bf16[192,640]{1,0:T(8,128)(2,1)}, u32[]{:S(2)}, u32[]{:S(2)}) collective-permute-start(bf16[192,640]{1,0:T(8,128)(2,1)} %copy-done.50), channel_id=1, source_target_pairs={{0,4},{4,0},{8,12},{12,8},{16,20},{20,16},{24,28},{28,24},{1,5},{5... | collective-permute-start | bytes 737288 | tf_op jit(solution)/shard_map/ppermute | solution.py:751
  75.6 18.5 %copy-start.2 = (bf16[1024,1536]{1,0:T(8,128)(2,1)}, bf16[1024,1536]{1,0:T(8,128)(2,1)S(1)}, u32[]{:S(2)}) copy-start(bf16[1024,1536]{1,0:T(8,128)(2,1)S(1)} %get-tuple-element.171.x_ref.normed_ref) | copy-start | bytes 9437188
  79.1 17.7 %collective-permute-start.18 = (bf16[192,384]{1,0:T(8,128)(2,1)}, bf16[192,384]{1,0:T(8,128)(2,1)}, u32[]{:S(2)}, u32[]{:S(2)}) collective-permute-start(bf16[192,384]{1,0:T(8,128)(2,1)} %collective-permute-done.16.refs_4_), channel_id=1, source_target_pairs={{0,8},{4,12},{8,16},{12,20},{16,24},{20,28},{24,0},{28,4},{1,9},{5... | collective-permute-start | bytes 442376 | tf_op jit(solution)/shard_map/out_hop3/ppermute | solution.py:754
  79.1 37.1 %collective-permute-start.12 = (bf16[256,1536]{1,0:T(8,128)(2,1)}, bf16[256,1536]{1,0:T(8,128)(2,1)S(1)}, u32[]{:S(2)}, u32[]{:S(2)}) collective-permute-start(bf16[256,1536]{1,0:T(8,128)(2,1)} %rest_ref.1), channel_id=1, source_target_pairs={{0,3},{1,2},{2,1},{3,0},{4,7},{5,6},{6,5},{7,4},{8,11},{9,10},{10,... | collective-permute-start | bytes 2359304 | tf_op jit(solution)/shard_map/cot_spread/ppermute | solution.py:769
  80.8 35.3 %collective-permute-start.11 = (bf16[256,1536]{1,0:T(8,128)(2,1)}, bf16[256,1536]{1,0:T(8,128)(2,1)S(1)}, u32[]{:S(2)}, u32[]{:S(2)}) collective-permute-start(bf16[256,1536]{1,0:T(8,128)(2,1)} %rest_ref.1), channel_id=1, source_target_pairs={{0,2},{1,3},{2,0},{3,1},{4,6},{5,7},{6,4},{7,5},{8,10},{9,11},{10,... | collective-permute-start | bytes 2359304 | tf_op jit(solution)/shard_map/cot_spread/ppermute | solution.py:769
  81.6 34.6 %collective-permute-start.10 = (bf16[256,1536]{1,0:T(8,128)(2,1)}, bf16[256,1536]{1,0:T(8,128)(2,1)S(1)}, u32[]{:S(2)}, u32[]{:S(2)}) collective-permute-start(bf16[256,1536]{1,0:T(8,128)(2,1)} %rest_ref.1), channel_id=1, source_target_pairs={{0,1},{1,0},{2,3},{3,2},{4,5},{5,4},{6,7},{7,6},{8,9},{9,8},{10,11... | collective-permute-start | bytes 2359304 | tf_op jit(solution)/shard_map/cot_spread/ppermute | solution.py:769
  82.7 29.3 %collective-permute-start.13 = (bf16[192,384]{1,0:T(8,128)(2,1)S(1)}, bf16[192,384]{1,0:T(8,128)(2,1)S(1)}, u32[]{:S(2)}, u32[]{:S(2)}) collective-permute-start(bf16[192,384]{1,0:T(8,128)(2,1)S(1)} %bitcast.37), channel_id=1, source_target_pairs={{0,4},{4,0},{8,12},{12,8},{16,20},{20,16},{24,28},{28,24},{1,5},{5... | collective-permute-start | bytes 442376 | tf_op jit(solution)/shard_map/ppermute | solution.py:751
  96.7 13.2 %copy-start.22 = (bf16[1024,384]{1,0:T(8,128)(2,1)}, bf16[1024,384]{1,0:T(8,128)(2,1)S(1)}, u32[]{:S(2)}) copy-start(bf16[1024,384]{1,0:T(8,128)(2,1)S(1)} %get-tuple-element.104.q_ref) | copy-start | bytes 2359300
  96.7 15.3 %collective-permute-start.15 = (bf16[192,384]{1,0:T(8,128)(2,1)}, bf16[192,384]{1,0:T(8,128)(2,1)S(1)}, u32[]{:S(2)}, u32[]{:S(2)}) collective-permute-start(bf16[192,384]{1,0:T(8,128)(2,1)} %collective-permute-done.14.refs_2_), channel_id=1, source_target_pairs={{0,4},{4,0},{8,12},{12,8},{16,20},{20,16},{24,28},{28,24},{1,5},{5... | collective-permute-start | bytes 442376 | tf_op jit(solution)/shard_map/ppermute | solution.py:751
  112.0 1.6 collective-permute-start.17
  112.1 1.7 collective-permute-start.19
  120.2 20.4 %collective-permute-start.20 = (bf16[256,1536]{1,0:T(8,128)(2,1)S(1)}, bf16[256,1536]{1,0:T(8,128)(2,1)S(1)}, u32[]{:S(2)}, u32[]{:S(2)}) collective-permute-start(bf16[256,1536]{1,0:T(8,128)(2,1)S(1)} %get-tuple-element.114), channel_id=1, source_target_pairs={{0,1},{1,0},{2,3},{3,2},{4,5},{5,4},{6,7},{7,6},{8,9},{9,8},{10,11... | collective-permute-start | bytes 2359304 | tf_op jit(solution)/shard_map/attn_sum/ppermute | solution.py:776
  121.3 36.3 %collective-permute-start.21 = (bf16[256,1536]{1,0:T(8,128)(2,1)S(1)}, bf16[256,1536]{1,0:T(8,128)(2,1)S(1)}, u32[]{:S(2)}, u32[]{:S(2)}) collective-permute-start(bf16[256,1536]{1,0:T(8,128)(2,1)S(1)} %get-tuple-element.115), channel_id=1, source_target_pairs={{0,2},{1,3},{2,0},{3,1},{4,6},{5,7},{6,4},{7,5},{8,10},{9,11},{10,... | collective-permute-start | bytes 2359304 | tf_op jit(solution)/shard_map/attn_sum/ppermute | solution.py:776
  122.5 35.1 %collective-permute-start.22 = (bf16[256,1536]{1,0:T(8,128)(2,1)S(1)}, bf16[256,1536]{1,0:T(8,128)(2,1)S(1)}, u32[]{:S(2)}, u32[]{:S(2)}) collective-permute-start(bf16[256,1536]{1,0:T(8,128)(2,1)S(1)} %get-tuple-element.116), channel_id=1, source_target_pairs={{0,3},{1,2},{2,1},{3,0},{4,7},{5,6},{6,5},{7,4},{8,11},{9,10},{10,... | collective-permute-start | bytes 2359304 | tf_op jit(solution)/shard_map/attn_sum/ppermute | solution.py:776
  140.6 17.0 %copy-start.61 = (bf16[256,1536]{1,0:T(8,128)(2,1)}, bf16[256,1536]{1,0:T(8,128)(2,1)S(1)}, u32[]{:S(2)}) copy-start(bf16[256,1536]{1,0:T(8,128)(2,1)S(1)} %collective-permute-done.20.refs_1_) | copy-start | bytes 2359300
  163.0 36.0 %copy-start.35 = (bf16[256,1536]{1,0:T(8,128)(2,1)S(1)}, bf16[256,1536]{1,0:T(8,128)(2,1)}, u32[]{:S(2)}) copy-start(bf16[256,1536]{1,0:T(8,128)(2,1)} %get-tuple-element.123.refs_0_) | copy-start | bytes 2359300
  163.0 35.1 %collective-permute-start.25 = (bf16[256,1536]{1,0:T(8,128)(2,1)}, bf16[256,1536]{1,0:T(8,128)(2,1)S(1)}, u32[]{:S(2)}, u32[]{:S(2)}) collective-permute-start(bf16[256,1536]{1,0:T(8,128)(2,1)} %get-tuple-element.123.refs_0_), channel_id=1, source_target_pairs={{0,3},{1,2},{2,1},{3,0},{4,7},{5,6},{6,5},{7,4},{8,11},{9,10},{10,... | collective-permute-start | bytes 2359304 | tf_op jit(solution)/shard_map/two_spread/ppermute | solution.py:769
  164.5 34.4 %collective-permute-start.24 = (bf16[256,1536]{1,0:T(8,128)(2,1)}, bf16[256,1536]{1,0:T(8,128)(2,1)S(1)}, u32[]{:S(2)}, u32[]{:S(2)}) collective-permute-start(bf16[256,1536]{1,0:T(8,128)(2,1)} %get-tuple-element.123.refs_0_), channel_id=1, source_target_pairs={{0,2},{1,3},{2,0},{3,1},{4,6},{5,7},{6,4},{7,5},{8,10},{9,11},{10,... | collective-permute-start | bytes 2359304 | tf_op jit(solution)/shard_map/two_spread/ppermute | solution.py:769
  164.6 34.3 %collective-permute-start.23 = (bf16[256,1536]{1,0:T(8,128)(2,1)}, bf16[256,1536]{1,0:T(8,128)(2,1)}, u32[]{:S(2)}, u32[]{:S(2)}) collective-permute-start(bf16[256,1536]{1,0:T(8,128)(2,1)} %get-tuple-element.123.refs_0_), channel_id=1, source_target_pairs={{0,1},{1,0},{2,3},{3,2},{4,5},{5,4},{6,7},{7,6},{8,9},{9,8},{10,11... | collective-permute-start | bytes 2359304 | tf_op jit(solution)/shard_map/two_spread/ppermute | solution.py:769
  237.8 162.9 %reduce-scatter.6.cloned.1.call-start = ((), (), s32[]{:S(2)}) async-start(), calls=%async_computation.5 | async-start | bytes 6193152 | tf_op jit(solution)/shard_map/reduce_scatter | solution.py:895
  255.3 31.3 %collective-permute-start.26 = (bf16[256,1536]{1,0:T(8,128)(2,1)S(1)}, bf16[256,1536]{1,0:T(8,128)(2,1)}, u32[]{:S(2)}, u32[]{:S(2)}) collective-permute-start(bf16[256,1536]{1,0:T(8,128)(2,1)S(1)} %get-tuple-element.129), channel_id=1, source_target_pairs={{0,1},{1,0},{2,3},{3,2},{4,5},{5,4},{6,7},{7,6},{8,9},{9,8},{10,11... | collective-permute-start | bytes 2359304 | tf_op jit(solution)/shard_map/two_sum/ppermute | solution.py:776
  256.5 36.1 %collective-permute-start.27 = (bf16[256,1536]{1,0:T(8,128)(2,1)S(1)}, bf16[256,1536]{1,0:T(8,128)(2,1)}, u32[]{:S(2)}, u32[]{:S(2)}) collective-permute-start(bf16[256,1536]{1,0:T(8,128)(2,1)S(1)} %get-tuple-element.130), channel_id=1, source_target_pairs={{0,2},{1,3},{2,0},{3,1},{4,6},{5,7},{6,4},{7,5},{8,10},{9,11},{10,... | collective-permute-start | bytes 2359304 | tf_op jit(solution)/shard_map/two_sum/ppermute | solution.py:776
  257.3 35.3 %collective-permute-start.28 = (bf16[256,1536]{1,0:T(8,128)(2,1)S(1)}, bf16[256,1536]{1,0:T(8,128)(2,1)}, u32[]{:S(2)}, u32[]{:S(2)}) collective-permute-start(bf16[256,1536]{1,0:T(8,128)(2,1)S(1)} %get-tuple-element.131), channel_id=1, source_target_pairs={{0,3},{1,2},{2,1},{3,0},{4,7},{5,6},{6,5},{7,4},{8,11},{9,10},{10,... | collective-permute-start | bytes 2359304 | tf_op jit(solution)/shard_map/two_sum/ppermute | solution.py:776
  302.6 156.5 %reduce-scatter.8.cloned.1.call-start = ((), (), s32[]{:S(2)}) async-start(), calls=%async_computation.6 | async-start | bytes 3538944 | tf_op jit(solution)/shard_map/reduce_scatter | solution.py:921
  302.6 5.5 %collective-permute-start.32 = (bf16[768,1792]{1,0:T(8,128)(2,1)}, bf16[768,1792]{1,0:T(8,128)(2,1)}, u32[]{:S(2)}, u32[]{:S(2)}) collective-permute-start(bf16[768,1792]{1,0:T(8,128)(2,1)} %product.5), channel_id=1, source_target_pairs={{0,4},{4,0},{8,12},{12,8},{16,20},{20,16},{24,28},{28,24},{1,5},{5... | collective-permute-start | bytes 8257544 | tf_op jit(solution)/shard_map/ppermute | solution.py:751
  302.7 20.7 %collective-permute-start.29 = (bf16[256,1536]{1,0:T(8,128)(2,1)}, bf16[256,1536]{1,0:T(8,128)(2,1)}, u32[]{:S(2)}, u32[]{:S(2)}) collective-permute-start(bf16[256,1536]{1,0:T(8,128)(2,1)} %get-tuple-element.141.refs_0_), channel_id=1, source_target_pairs={{0,1},{1,0},{2,3},{3,2},{4,5},{5,4},{6,7},{7,6},{8,9},{9,8},{10,11... | collective-permute-start | bytes 2359304 | tf_op jit(solution)/shard_map/dh_spread/ppermute | solution.py:769
  304.3 43.0 %collective-permute-start.31 = (bf16[256,1536]{1,0:T(8,128)(2,1)}, bf16[256,1536]{1,0:T(8,128)(2,1)}, u32[]{:S(2)}, u32[]{:S(2)}) collective-permute-start(bf16[256,1536]{1,0:T(8,128)(2,1)} %get-tuple-element.141.refs_0_), channel_id=1, source_target_pairs={{0,3},{1,2},{2,1},{3,0},{4,7},{5,6},{6,5},{7,4},{8,11},{9,10},{10,... | collective-permute-start | bytes 2359304 | tf_op jit(solution)/shard_map/dh_spread/ppermute | solution.py:769
  305.7 41.5 %collective-permute-start.30 = (bf16[256,1536]{1,0:T(8,128)(2,1)}, bf16[256,1536]{1,0:T(8,128)(2,1)}, u32[]{:S(2)}, u32[]{:S(2)}) collective-permute-start(bf16[256,1536]{1,0:T(8,128)(2,1)} %get-tuple-element.141.refs_0_), channel_id=1, source_target_pairs={{0,2},{1,3},{2,0},{3,1},{4,6},{5,7},{6,4},{7,5},{8,10},{9,11},{10,... | collective-permute-start | bytes 2359304 | tf_op jit(solution)/shard_map/dh_spread/ppermute | solution.py:769
  310.2 34.8 %collective-permute-start.33 = (bf16[192,1792]{1,0:T(8,128)(2,1)}, bf16[192,1792]{1,0:T(8,128)(2,1)}, u32[]{:S(2)}, u32[]{:S(2)}) collective-permute-start(bf16[192,1792]{1,0:T(8,128)(2,1)} %join.3), channel_id=1, source_target_pairs={{0,8},{4,12},{8,16},{12,20},{16,24},{20,28},{24,0},{28,4},{1,9},{5... | collective-permute-start | bytes 2064392 | tf_op jit(solution)/shard_map/gate_grad_hop1/ppermute | solution.py:754
  320.7 26.5 %copy-start.21 = (bf16[256,1536]{1,0:T(8,128)(2,1)}, bf16[256,1536]{1,0:T(8,128)(2,1)S(1)}, u32[]{:S(2)}) copy-start(bf16[256,1536]{1,0:T(8,128)(2,1)S(1)} %get-tuple-element.143.refs_0_) | copy-start | bytes 2359300
  347.2 38.0 %collective-permute-start.35 = (bf16[256,1536]{1,0:T(8,128)(2,1)}, bf16[256,1536]{1,0:T(8,128)(2,1)}, u32[]{:S(2)}, u32[]{:S(2)}) collective-permute-start(bf16[256,1536]{1,0:T(8,128)(2,1)} %get-tuple-element.161), channel_id=1, source_target_pairs={{0,1},{1,0},{2,3},{3,2},{4,5},{5,4},{6,7},{7,6},{8,9},{9,8},{10,11... | collective-permute-start | bytes 2359304 | tf_op jit(solution)/shard_map/ffn_sum/ppermute | solution.py:776
  348.7 36.6 %collective-permute-start.36 = (bf16[256,1536]{1,0:T(8,128)(2,1)}, bf16[256,1536]{1,0:T(8,128)(2,1)}, u32[]{:S(2)}, u32[]{:S(2)}) collective-permute-start(bf16[256,1536]{1,0:T(8,128)(2,1)} %get-tuple-element.162), channel_id=1, source_target_pairs={{0,2},{1,3},{2,0},{3,1},{4,6},{5,7},{6,4},{7,5},{8,10},{9,11},{10,... | collective-permute-start | bytes 2359304 | tf_op jit(solution)/shard_map/ffn_sum/ppermute | solution.py:776
  350.2 35.1 %collective-permute-start.37 = (bf16[256,1536]{1,0:T(8,128)(2,1)}, bf16[256,1536]{1,0:T(8,128)(2,1)}, u32[]{:S(2)}, u32[]{:S(2)}) collective-permute-start(bf16[256,1536]{1,0:T(8,128)(2,1)} %get-tuple-element.163), channel_id=1, source_target_pairs={{0,3},{1,2},{2,1},{3,0},{4,7},{5,6},{6,5},{7,4},{8,11},{9,10},{10,... | collective-permute-start | bytes 2359304 | tf_op jit(solution)/shard_map/ffn_sum/ppermute | solution.py:776
  350.8 34.5 %collective-permute-start.34 = (bf16[192,1792]{1,0:T(8,128)(2,1)}, bf16[192,1792]{1,0:T(8,128)(2,1)}, u32[]{:S(2)}, u32[]{:S(2)}) collective-permute-start(bf16[192,1792]{1,0:T(8,128)(2,1)} %join.4), channel_id=1, source_target_pairs={{0,8},{4,12},{8,16},{12,20},{16,24},{20,28},{24,0},{28,4},{1,9},{5... | collective-permute-start | bytes 2064392 | tf_op jit(solution)/shard_map/gate_grad_hop2/ppermute | solution.py:754
  401.8 27.3 %collective-permute-start.41 = (bf16[192,1792]{1,0:T(8,128)(2,1)S(1)}, bf16[192,1792]{1,0:T(8,128)(2,1)S(1)}, u32[]{:S(2)}, u32[]{:S(2)}) collective-permute-start(bf16[192,1792]{1,0:T(8,128)(2,1)S(1)} %copy-done.38), channel_id=1, source_target_pairs={{0,8},{4,12},{8,16},{12,20},{16,24},{20,28},{24,0},{28,4},{1,9},{5... | collective-permute-start | bytes 2064392 | tf_op jit(solution)/shard_map/gate_grad_hop3/ppermute | solution.py:754
  401.8 28.8 %collective-permute-start.38 = (bf16[256,1536]{1,0:T(8,128)(2,1)}, bf16[256,1536]{1,0:T(8,128)(2,1)S(1)}, u32[]{:S(2)}, u32[]{:S(2)}) collective-permute-start(bf16[256,1536]{1,0:T(8,128)(2,1)} %get-tuple-element.167.refs_1_), channel_id=1, source_target_pairs={{0,1},{1,0},{2,3},{3,2},{4,5},{5,4},{6,7},{7,6},{8,9},{9,8},{10,11... | collective-permute-start | bytes 2359304 | tf_op jit(solution)/shard_map/one_sum/ppermute | solution.py:776
  403.2 33.7 %collective-permute-start.39 = (bf16[256,1536]{1,0:T(8,128)(2,1)S(1)}, bf16[256,1536]{1,0:T(8,128)(2,1)S(1)}, u32[]{:S(2)}, u32[]{:S(2)}) collective-permute-start(bf16[256,1536]{1,0:T(8,128)(2,1)S(1)} %get-tuple-element.168.refs_2_), channel_id=1, source_target_pairs={{0,2},{1,3},{2,0},{3,1},{4,6},{5,7},{6,4},{7,5},{8,10},{9,11},{10,... | collective-permute-start | bytes 2359304 | tf_op jit(solution)/shard_map/one_sum/ppermute | solution.py:776
  404.7 32.2 %collective-permute-start.40 = (bf16[256,1536]{1,0:T(8,128)(2,1)S(1)}, bf16[256,1536]{1,0:T(8,128)(2,1)S(1)}, u32[]{:S(2)}, u32[]{:S(2)}) collective-permute-start(bf16[256,1536]{1,0:T(8,128)(2,1)S(1)} %get-tuple-element.169.refs_3_), channel_id=1, source_target_pairs={{0,3},{1,2},{2,1},{3,0},{4,7},{5,6},{6,5},{7,4},{8,11},{9,10},{10,... | collective-permute-start | bytes 2359304 | tf_op jit(solution)/shard_map/one_sum/ppermute | solution.py:776
  409.9 19.2 %copy-start.36 = (bf16[192,1792]{1,0:T(8,128)(2,1)S(1)}, bf16[192,1792]{1,0:T(8,128)(2,1)}, u32[]{:S(2)}) copy-start(bf16[192,1792]{1,0:T(8,128)(2,1)} %reduce-scatter.4.cloned.1.call-done.grads_ref) | copy-start | bytes 2064388
  409.9 19.5 %copy-start.65 = (bf16[192,1792]{1,0:T(8,128)(2,1)S(1)}, bf16[192,1792]{1,0:T(8,128)(2,1)}, u32[]{:S(2)}) copy-start(bf16[192,1792]{1,0:T(8,128)(2,1)} %reduce-scatter.6.cloned.1.call-done) | copy-start | bytes 2064388
  413.4 23.5 %copy-start.67 = (f32[1,3584]{1,0:T(1,128)S(1)}, f32[1,3584]{1,0:T(1,128)}, u32[]{:S(2)}) copy-start(f32[1,3584]{1,0:T(1,128)} %gain_parts.1) | copy-start | bytes 43012
  436.9 10.5 %collective-permute-start.44 = (f32[1,3584]{1,0:T(1,128)S(1)}, f32[1,3584]{1,0:T(1,128)S(1)}, u32[]{:S(2)}, u32[]{:S(2)}) collective-permute-start(f32[1,3584]{1,0:T(1,128)S(1)} %copy-done.67), channel_id=1, source_target_pairs={{0,3},{1,2},{2,1},{3,0},{4,7},{5,6},{6,5},{7,4},{8,11},{9,10},{10,... | collective-permute-start | bytes 43016 | tf_op jit(solution)/shard_map/ppermute | solution.py:929
  438.4 9.1 %collective-permute-start.43 = (f32[1,3584]{1,0:T(1,128)S(1)}, f32[1,3584]{1,0:T(1,128)S(1)}, u32[]{:S(2)}, u32[]{:S(2)}) collective-permute-start(f32[1,3584]{1,0:T(1,128)S(1)} %copy-done.67), channel_id=1, source_target_pairs={{0,2},{1,3},{2,0},{3,1},{4,6},{5,7},{6,4},{7,5},{8,10},{9,11},{10,... | collective-permute-start | bytes 43016 | tf_op jit(solution)/shard_map/ppermute | solution.py:929
  439.8 7.6 %collective-permute-start.42 = (f32[1,3584]{1,0:T(1,128)S(1)}, f32[1,3584]{1,0:T(1,128)S(1)}, u32[]{:S(2)}, u32[]{:S(2)}) collective-permute-start(f32[1,3584]{1,0:T(1,128)S(1)} %copy-done.67), channel_id=1, source_target_pairs={{0,1},{1,0},{2,3},{3,2},{4,5},{5,4},{6,7},{7,6},{8,9},{9,8},{10,11... | collective-permute-start | bytes 43016 | tf_op jit(solution)/shard_map/ppermute | solution.py:929
  447.5 1.2 collective-permute-start.45
  448.8 6.1 %collective-permute-start.48 = (f32[1,3584]{1,0:T(1,128)S(1)}, f32[1,3584]{1,0:T(1,128)S(1)}, u32[]{:S(2)}, u32[]{:S(2)}) collective-permute-start(f32[1,3584]{1,0:T(1,128)S(1)} %add.119), channel_id=1, source_target_pairs={{0,24},{4,28},{8,16},{12,20},{16,8},{20,12},{24,0},{28,4},{1,25},{... | collective-permute-start | bytes 43016 | tf_op jit(solution)/shard_map/ppermute | solution.py:929
  452.5 4.6 collective-permute-start.47
  452.7 4.4 collective-permute-start.46
  (60 other events, 236.3 us)
Sparse Core Ops, SparseCore 0:
  30.0 157.8 all-gather.1
  237.9 64.5 reduce-scatter.3
  304.9 90.2 reduce-scatter.5
  400.8 48.1 reduce-scatter.7

commit v6 on v5

--- a/solution.py
+++ b/solution.py
@@ -142,14 +142,17 @@
         )
         lse = lse_ref[0, head : head + 1, :]
 
-        def step(other, acc, q3=q3, do3=do3, cols=cols, inner=inner, lse=lse):
+        def step(other, acc, q3=q3, do3=do3, cols=cols, inner=inner, lse=lse, own=False):
             first = pl.multiple_of((other ^ me) * rows, rows)
             place = pl.ds(first, rows)
             keys = k_ref[place, cols]
             vals = v_ref[place, cols]
             ids = other * rows + lax.broadcasted_iota(jnp.int32, (rows, 1), 0)
             scores = kdot(keys, q3, NT)
-            scores = jnp.where((ids <= row_ids) & (ids >= low_bound), scores, NEGATIVE_FILL)
+            allowed = ids >= low_bound
+            if own:
+                allowed = allowed & (ids <= row_ids)
+            scores = jnp.where(allowed, scores, NEGATIVE_FILL)
             probs = jnp.exp(scores - lse)
             d_probs = kdot(vals, do3, NT)
             d_scores = (probs * (d_probs - inner)).astype(LOW)
@@ -157,7 +160,8 @@
             dv_ref[place, cols] += kdot(probs.astype(LOW), do3, NN)
             return acc + kdot(keys, d_scores, TN)
 
-        acc = lax.fori_loop(0, block + 1, step, jnp.zeros((HEAD_SIZE, width), F32))
+        acc = step(block, jnp.zeros((HEAD_SIZE, width), F32), own=True)
+        acc = lax.fori_loop(0, block, step, acc)
         pieces += [acc[:, g * rows : (g + 1) * rows] for g in range(GROUP)]
     dq_ref[...] = jnp.concatenate(pieces, axis=0).T * SCALE
 
@@ -361,7 +365,7 @@
     length, cols = lefts[0].shape
     width = weights.shape[1]
     rows = length // ranks
-    tile = 256
+    tile = 512
     return pl.pallas_call(
         functools.partial(back_parts_kernel, rows, len(lefts)),
         grid=(width // tile,),

time: 470 us -> 472 us (level)
  transfers between devices with their start and end apart: 53 -> 53, of which waited for: 22 -> 23; matrix products, arithmetic and copies ran while one was open for 4% -> 4% of each run, Pallas kernels for 35% -> 34%
where the time goes in v6:
time: 472 us; the launch traced here: 467 us
  Pallas kernels  174 us (37%)
  waiting for transfers between devices  158 us (33%)
  local copies, waits for them, and re-layouts  44.2 us (9%)
  starting transfers between devices  41.2 us (9%)
  matrix products  24.1 us (5%)
  between operations  15 us (3%)
  other arithmetic  10.2 us (2%)
    ppermute x9, waiting for transfers between devices, onward(): return lax.ppermute(v, 'dp', ring_pairs)  72.4 us
    ppermute x12, waiting for transfers between devices, send_parts(): lax.ppermute(parts[j], 'tensor', [(i, i ^ j) for i in range(ranks)])  40 us
    pallas_call x4, Pallas kernels, product(): pl.pallas_call(functools.partial(product_kernel, tiles), grid=(tiles * le...  38.8 us
    unnamed x147, local copies, waits for them, and re-layouts  37.5 us
    pallas_call x4, Pallas kernels, back_parts(): pl.pallas_call(functools.partial(back_parts_kernel, rows, len(lefts)), gr...  33.8 us
    dot_general x2, matrix products, mm(): return jnp.dot(left, right, preferred_element_type=F32)  24.1 us
    all_gather x1, waiting for transfers between devices, shards(): lax.all_gather(tie(jnp.stack([widen(w_down.T), widen(w_gate), widen(w_up)...  21.8 us
    pallas_call x1, Pallas kernels, attend_back(): pl.pallas_call(functools.partial(attend_back_kernel, heads, rows), grid_s...  15.6 us
  transfers between devices with their start and end apart: 53, of which 23 were waited for; matrix products, arithmetic and copies ran while one was open for 4% of the time, Pallas kernels for 34%

profile of v6, /device:TPU:0, one launch (start us, length us, event | category | flops | bytes accessed | tf_op | source)
XLA Modules:
  0.0 467.0 jit_solution(11474687583416098916)
XLA Ops:
  9.9 3.1 collective-permute-start.4
  14.4 6.5 %collective-permute-done.4.refs_2_ = bf16[192,640]{1,0:T(8,128)(2,1)S(1)} collective-permute-done((bf16[192,640]{1,0:T(8,128)(2,1)S(1)}, bf16[192,640]{1,0:T(8,128)(2,1)S(1)}, u32[]{:S(2)}, u32[]{:S(2)}) %collective-permute-start.4) | collective-permute-done | bytes 245792 | tf_op jit(solution)/shard_map/qkv_hop1/ppermute | solution.py:758
  20.9 1.5 pad_maximum_fusion
  22.5 7.4 %collective-permute-done.6.refs_4_ = bf16[192,640]{1,0:T(8,128)(2,1)S(1)} collective-permute-done((bf16[192,640]{1,0:T(8,128)(2,1)S(1)}, bf16[192,640]{1,0:T(8,128)(2,1)S(1)}, u32[]{:S(2)}, u32[]{:S(2)}) %collective-permute-start.6) | collective-permute-done | bytes 245792 | tf_op jit(solution)/shard_map/qkv_hop2/ppermute | solution.py:758
  30.8 2.3 collective-permute-start.2
  38.0 5.5 %collective-permute-done.14.refs_2_ = bf16[192,384]{1,0:T(8,128)(2,1)} collective-permute-done((bf16[192,384]{1,0:T(8,128)(2,1)S(1)}, bf16[192,384]{1,0:T(8,128)(2,1)}, u32[]{:S(2)}, u32[]{:S(2)}) %collective-permute-start.14) | collective-permute-done | bytes 147488 | tf_op jit(solution)/shard_map/out_hop1/ppermute | solution.py:758
  43.5 9.0 %collective-permute-done.8.refs_6_ = bf16[192,640]{1,0:T(8,128)(2,1)S(1)} collective-permute-done((bf16[192,640]{1,0:T(8,128)(2,1)}, bf16[192,640]{1,0:T(8,128)(2,1)S(1)}, u32[]{:S(2)}, u32[]{:S(2)}) %collective-permute-start.8) | collective-permute-done | bytes 245792 | tf_op jit(solution)/shard_map/qkv_hop3/ppermute | solution.py:758
  54.1 3.7 fusion.14
  58.8 7.7 %collective-permute-done.1.refs_2_ = bf16[256,1536]{1,0:T(8,128)(2,1)S(1)} collective-permute-done((bf16[256,1536]{1,0:T(8,128)(2,1)S(1)}, bf16[256,1536]{1,0:T(8,128)(2,1)S(1)}, u32[]{:S(2)}, u32[]{:S(2)}) %collective-permute-start.1) | collective-permute-done | bytes 786464 | tf_op jit(solution)/shard_map/one_spread/ppermute | solution.py:773
  74.0 1.6 copy-done.8
  75.6 3.5 collective-permute-done.16.refs_4_
  79.3 1.7 collective-permute-start.12
  85.8 2.9 place.2.w_ref
  88.7 5.5 %prepare.1 = (bf16[1024,384]{1,0:T(8,128)(2,1)S(1)}, bf16[1024,128]{1,0:T(8,128)(2,1)S(1)}, bf16[1024,128]{1,0:T(8,128)(2,1)S(1)}, f32[1024,512]{1,0:T(8,128)S(1)}) custom-call(bf16[1024,1536]{1,0:T(8,128)(2,1)S(1)} %get-tuple-element.171.x_ref.normed_ref, bf16[1536,640]{1,0:T(8,128)(2,1)S(1)} %place.2.w_ref, f32[1024,128]{1,0:T(8,128)S(1)} %copy-done.7, ...), custom_call_target="tpu_custom_call" | custom-call | tf_op jit(solution)/shard_map/prepare/pallas_call | solution.py:637
  97.4 12.8 %attend.1 = (bf16[1024,384]{1,0:T(8,128)(2,1)S(1)}, f32[4,2,768]{2,1,0:T(2,128)S(1)}) custom-call(s32[1]{0:T(128)} %bitcast.me_ref, bf16[1024,384]{1,0:T(8,128)(2,1)S(1)} %get-tuple-element.104.q_ref, bf16[1024,128]{1,0:T(8,128)(2,1)S(1)} %get-tuple-element.105.k_ref, bf16[1024,128]{1,0:T(8,128)(2,1)S(1)} %get-tuple-element.106.v_ref, ...), custom_call_target="tpu_custom_call" | custom-call | flops 6442450944 | bytes 33554432 | tf_op jit(solution)/shard_map/attend/pallas_call | solution.py:182
  114.0 2.3 place.3
  116.4 2.4 back_parts.4
  124.9 1.6 copy-done.10
  126.6 1.7 copy-done.15
  128.2 12.0 %collective-permute-done.20.refs_1_ = bf16[256,1536]{1,0:T(8,128)(2,1)S(1)} collective-permute-done((bf16[256,1536]{1,0:T(8,128)(2,1)S(1)}, bf16[256,1536]{1,0:T(8,128)(2,1)S(1)}, u32[]{:S(2)}, u32[]{:S(2)}) %collective-permute-start.20) | collective-permute-done | bytes 786464 | tf_op jit(solution)/shard_map/attn_sum/ppermute | solution.py:780
  140.2 16.9 %collective-permute-done.21.refs_2_ = bf16[256,1536]{1,0:T(8,128)(2,1)S(1)} collective-permute-done((bf16[256,1536]{1,0:T(8,128)(2,1)S(1)}, bf16[256,1536]{1,0:T(8,128)(2,1)S(1)}, u32[]{:S(2)}, u32[]{:S(2)}) %collective-permute-start.21) | collective-permute-done | bytes 786464 | tf_op jit(solution)/shard_map/attn_sum/ppermute | solution.py:780
  158.9 3.6 sum_up.2
  162.5 1.5 collective-permute-start.25
  164.2 1.8 collective-permute-start.23
  166.0 21.8 %all-gather.2.cloned.1.call-done.right_ref.refs_2_.refs_3_.refs_1_ = bf16[3,1536,1792]{2,1,0:T(8,128)(2,1)} async-done(((bf16[3,192,1792]{2,1,0:T(8,128)(2,1)}), bf16[3,1536,1792]{2,1,0:T(8,128)(2,1)}) %all-gather.2.cloned.1.call-update) | async-done | bytes 16515088 | tf_op jit(solution)/shard_map/all_gather | solution.py:803
  187.9 10.2 %rows_product.2 = bf16[1024,1792]{1,0:T(8,128)(2,1)} custom-call(bf16[1024,1536]{1,0:T(8,128)(2,1)} %copy-done.15, bf16[3,1536,1792]{2,1,0:T(8,128)(2,1)} %all-gather.2.cloned.1.call-done.right_ref.refs_2_.refs_3_.refs_1_), custom_call_target="tpu_custom_call" | custom-call | tf_op jit(solution)/shard_map/rows_product/pallas_call | solution.py:542
  198.5 2.5 fold.6
  202.2 10.3 %fusion.10 = bf16[1024,1792]{1,0:T(8,128)(2,1)S(1)} fusion(bf16[1024,1536]{1,0:T(8,128)(2,1)S(1)} %get-tuple-element.125, bf16[3,1536,1792]{2,1,0:T(8,128)(2,1)} %all-gather.2.cloned.1.call-done.right_ref.refs_2_.refs_3_.refs_1_), kind=kOutput, calls=%fused_computation.18 | convolution fusion | flops 5638979584 | bytes 12320768 | tf_op jit(solution)/shard_map/dot_general | solution.py:40
  212.6 13.8 %multiply_convert_fusion = (bf16[1024,1792]{1,0:T(8,128)(2,1)}, bf16[1024,1792]{1,0:T(8,128)(2,1)}, bf16[1024,1792]{1,0:T(8,128)(2,1)}) fusion(bf16[1024,1792]{1,0:T(8,128)(2,1)S(1)} %fusion.10, bf16[1024,1792]{1,0:T(8,128)(2,1)S(1)} %copy-done.57, bf16[1024,1536]{1,0:T(8,128)(2,1)S(1)} %get-tuple-element.125, ...), kind=kOutput, calls=%fused_computation.13 | convolution fusion | flops 5668339712 | bytes 27000832 | tf_op jit(solution)/shard_map/dot_general | solution.py:40
  226.3 11.0 %product.4 = bf16[1536,1792]{1,0:T(8,128)(2,1)} custom-call(bf16[1536,1024]{1,0:T(8,128)(2,1)} %copy-done.10, bf16[1024,1792]{1,0:T(8,128)(2,1)} %get-tuple-element.142.refs_0_), custom_call_target="tpu_custom_call" | custom-call | tf_op jit(solution)/shard_map/product/pallas_call | solution.py:313
  237.4 16.4 %back_parts.5 = (bf16[256,1536]{1,0:T(8,128)(2,1)S(1)}, bf16[256,1536]{1,0:T(8,128)(2,1)S(1)}, bf16[256,1536]{1,0:T(8,128)(2,1)S(1)}, bf16[256,1536]{1,0:T(8,128)(2,1)S(1)}) custom-call(bf16[1024,1792]{1,0:T(8,128)(2,1)} %get-tuple-element.135.refs_0_, bf16[1024,1792]{1,0:T(8,128)(2,1)} %get-tuple-element.137.refs_1_.refs_0_, ...), custom_call_target="tpu_custom_call" | custom-call | tf_op jit(solution)/shard_map/back_parts/pallas_call | solution.py:369
  258.2 8.4 %product.5 = bf16[768,1792]{1,0:T(8,128)(2,1)} custom-call(bf16[768,1024]{1,0:T(8,128)(2,1)} %copy-done.20, bf16[1024,1792]{1,0:T(8,128)(2,1)} %get-tuple-element.135.refs_0_), custom_call_target="tpu_custom_call" | custom-call | tf_op jit(solution)/shard_map/product/pallas_call | solution.py:313
  266.5 8.4 %product.6.refs_0_.refs_1_.near_ref = bf16[768,1792]{1,0:T(8,128)(2,1)} custom-call(bf16[768,1024]{1,0:T(8,128)(2,1)} %copy-done.19, bf16[1024,1792]{1,0:T(8,128)(2,1)} %get-tuple-element.135.refs_0_), custom_call_target="tpu_custom_call" | custom-call | tf_op jit(solution)/shard_map/product/pallas_call | solution.py:313
  274.9 11.0 %product.7 = bf16[1536,1792]{1,0:T(8,128)(2,1)} custom-call(bf16[1536,1024]{1,0:T(8,128)(2,1)} %copy-done.11, bf16[1024,1792]{1,0:T(8,128)(2,1)} %get-tuple-element.137.refs_1_.refs_0_), custom_call_target="tpu_custom_call" | custom-call | tf_op jit(solution)/shard_map/product/pallas_call | solution.py:313
  285.9 6.1 %collective-permute-done.27.refs_2_ = bf16[256,1536]{1,0:T(8,128)(2,1)} collective-permute-done((bf16[256,1536]{1,0:T(8,128)(2,1)S(1)}, bf16[256,1536]{1,0:T(8,128)(2,1)}, u32[]{:S(2)}, u32[]{:S(2)}) %collective-permute-start.27) | collective-permute-done | bytes 786464 | tf_op jit(solution)/shard_map/two_sum/ppermute | solution.py:780
  292.0 4.5 norm_back_sum.2
  296.6 5.6 %reduce-scatter.4.cloned.1.call-done.grads_ref = bf16[192,1792]{1,0:T(8,128)(2,1)} async-done(((bf16[1536,1792]{1,0:T(8,128)(2,1)}), bf16[192,1792]{1,0:T(8,128)(2,1)}) %reduce-scatter.4.cloned.1.call-update) | async-done | bytes 688144 | tf_op jit(solution)/shard_map/reduce_scatter | solution.py:885
  302.3 1.5 collective-permute-start.29
  305.8 1.9 collective-permute-done.32.refs_1_.refs_2_.other_ref
  307.7 2.1 join.3
  309.8 9.8 %back_parts.6 = (bf16[256,1536]{1,0:T(8,128)(2,1)S(1)}, bf16[256,1536]{1,0:T(8,128)(2,1)}, bf16[256,1536]{1,0:T(8,128)(2,1)}, bf16[256,1536]{1,0:T(8,128)(2,1)}) custom-call(bf16[1024,1792]{1,0:T(8,128)(2,1)} %get-tuple-element.142.refs_0_, bf16[3,1536,1792]{2,1,0:T(8,128)(2,1)} %all-gather.2.cloned.1.call-done.right_ref.refs_2_.refs_3_.refs_1_), custom_call_target="tpu_custom_call" | custom-call | tf_op jit(solution)/shard_map/back_parts/pallas_call | solution.py:369
  319.6 3.4 collective-permute-done.29.refs_1_
  323.0 21.6 %collective-permute-done.33.refs_0_ = bf16[192,1792]{1,0:T(8,128)(2,1)} collective-permute-done((bf16[192,1792]{1,0:T(8,128)(2,1)}, bf16[192,1792]{1,0:T(8,128)(2,1)}, u32[]{:S(2)}, u32[]{:S(2)}) %collective-permute-start.33) | collective-permute-done | bytes 688160 | tf_op jit(solution)/shard_map/gate_grad_hop1/ppermute | solution.py:758
  344.6 2.2 join.4
  348.2 1.5 collective-permute-start.36
  351.7 2.7 fold.7
  354.5 2.3 rows_product.3.do_ref
  356.9 15.6 %attend_back.1 = (f32[1024,384]{1,0:T(8,128)S(1)}, f32[1024,128]{1,0:T(8,128)S(1)}, f32[1024,128]{1,0:T(8,128)S(1)}) custom-call(s32[1]{0:T(128)} %bitcast.me_ref, bf16[1024,384]{1,0:T(8,128)(2,1)S(1)} %copy-done.23, bf16[1024,128]{1,0:T(8,128)(2,1)S(1)} %copy-done.43, bf16[1024,128]{1,0:T(8,128)(2,1)S(1)} %copy-done.45, s32[4,1,256]{2,1,0:T(1,128)S(1)} %reshape.123.lo_ref, ...), custom_call_target="tpu_custom_call" | custom-call | tf_op jit(solution)/shard_map/attend_back/pallas_call | solution.py:208
  375.3 7.7 %prepare_back.1 = (bf16[1024,640]{1,0:T(8,128)(2,1)}, f32[1,512]{1,0:T(1,128)}) custom-call(f32[1024,384]{1,0:T(8,128)} %copy-done.18, f32[1024,128]{1,0:T(8,128)} %copy-done.39, f32[1024,128]{1,0:T(8,128)} %copy-done.40, f32[1024,512]{1,0:T(8,128)} %copy-done.17, f32[1024,128]{1,0:T(8,128)} %get-tuple-element.214.cos_ref, ...), custom_call_target="tpu_custom_call" | custom-call | tf_op jit(solution)/shard_map/prepare_back/pallas_call | solution.py:691
  383.0 2.0 collective-permute-done.34.refs_0_
  385.1 1.6 join.5
  387.5 5.2 %back_parts.7 = (bf16[256,1536]{1,0:T(8,128)(2,1)S(1)}, bf16[256,1536]{1,0:T(8,128)(2,1)}, bf16[256,1536]{1,0:T(8,128)(2,1)S(1)}, bf16[256,1536]{1,0:T(8,128)(2,1)S(1)}) custom-call(bf16[1024,640]{1,0:T(8,128)(2,1)S(1)} %copy-done.5, bf16[1,1536,640]{2,1,0:T(8,128)(2,1)} %bitcast.33), custom_call_target="tpu_custom_call" | custom-call | tf_op jit(solution)/shard_map/back_parts/pallas_call | solution.py:369
  393.5 5.7 %attn_products.1 = bf16[1536,1024]{1,0:T(8,128)(2,1)} custom-call(bf16[1536,1024]{1,0:T(8,128)(2,1)S(1)} %copy-done.9, bf16[1536,1024]{1,0:T(8,128)(2,1)S(1)} %get-tuple-element.153.refs_1_, bf16[1024,640]{1,0:T(8,128)(2,1)S(1)} %copy-done.5, bf16[1024,384]{1,0:T(8,128)(2,1)S(1)} %get-tuple-element.109.refs_0_.o_ref.refs_3_), custom_call_target="tpu_custom_call" | custom-call | tf_op jit(solution)/shard_map/attn_products/pallas_call | solution.py:346
  401.7 1.5 collective-permute-start.39
  404.4 3.8 gain_parts.1
  408.2 3.5 sum_up.3
  411.7 17.0 %collective-permute-done.41.flow_ref = bf16[192,1792]{1,0:T(8,128)(2,1)S(1)} collective-permute-done((bf16[192,1792]{1,0:T(8,128)(2,1)S(1)}, bf16[192,1792]{1,0:T(8,128)(2,1)S(1)}, u32[]{:S(2)}, u32[]{:S(2)}) %collective-permute-start.41) | collective-permute-done | bytes 688160 | tf_op jit(solution)/shard_map/gate_grad_hop3/ppermute | solution.py:758
  430.2 4.1 collective-permute-done.39.refs_2_
  435.3 1.5 collective-permute-start.44
  438.8 4.1 norm_back_sum.3
  443.0 2.8 last_join.1
  447.1 3.7 collective-permute-start.48
  451.5 1.6 copy.28
  453.2 2.2 collective-permute-done.47
  (259 shorter events, 70.8 us)
Async XLA Ops:
  7.2 180.7 %all-gather.2.cloned.1.call-start = ((), (), s32[]{:S(2)}) async-start(), calls=%async_computation.3 | async-start | bytes 18579456 | tf_op jit(solution)/shard_map/all_gather | solution.py:803
  9.9 11.1 %collective-permute-start.4 = (bf16[192,640]{1,0:T(8,128)(2,1)S(1)}, bf16[192,640]{1,0:T(8,128)(2,1)S(1)}, u32[]{:S(2)}, u32[]{:S(2)}) collective-permute-start(bf16[192,640]{1,0:T(8,128)(2,1)S(1)} %constant_dynamic-update-slice_fusion.refs_0_), channel_id=1, source_target_pairs={{0,8},{4,12},{8,16},{12,20},{16,24},{20,28},{24,0},{28,4},{1,9},{5... | collective-permute-start | bytes 737288 | tf_op jit(solution)/shard_map/qkv_hop1/ppermute | solution.py:758
  14.4 15.5 %copy-start.56 = (bf16[256,1536]{1,0:T(8,128)(2,1)S(1)}, bf16[256,1536]{1,0:T(8,128)(2,1)}, u32[]{:S(2)}) copy-start(bf16[256,1536]{1,0:T(8,128)(2,1)} %value_ref.1) | copy-start | bytes 2359300
  20.9 8.9 %collective-permute-start.6 = (bf16[192,640]{1,0:T(8,128)(2,1)S(1)}, bf16[192,640]{1,0:T(8,128)(2,1)S(1)}, u32[]{:S(2)}, u32[]{:S(2)}) collective-permute-start(bf16[192,640]{1,0:T(8,128)(2,1)S(1)} %collective-permute-done.4.refs_2_), channel_id=1, source_target_pairs={{0,8},{4,12},{8,16},{12,20},{16,24},{20,28},{24,0},{28,4},{1,9},{5... | collective-permute-start | bytes 737288 | tf_op jit(solution)/shard_map/qkv_hop2/ppermute | solution.py:758
  29.9 272.2 %reduce-scatter.4.cloned.1.call-start = ((), (), s32[]{:S(2)}) async-start(), calls=%async_computation.4 | async-start | bytes 6193152 | tf_op jit(solution)/shard_map/reduce_scatter | solution.py:885
  30.8 37.5 %copy-start.13 = (bf16[256,1536]{1,0:T(8,128)(2,1)}, bf16[256,1536]{1,0:T(8,128)(2,1)S(1)}, u32[]{:S(2)}) copy-start(bf16[256,1536]{1,0:T(8,128)(2,1)S(1)} %fusion.13.refs_0_) | copy-start | bytes 2359300
  30.8 21.7 %collective-permute-start.2 = (bf16[256,1536]{1,0:T(8,128)(2,1)S(1)}, bf16[256,1536]{1,0:T(8,128)(2,1)S(1)}, u32[]{:S(2)}, u32[]{:S(2)}) collective-permute-start(bf16[256,1536]{1,0:T(8,128)(2,1)S(1)} %fusion.13.refs_0_), channel_id=1, source_target_pairs={{0,3},{1,2},{2,1},{3,0},{4,7},{5,6},{6,5},{7,4},{8,11},{9,10},{10,... | collective-permute-start | bytes 2359304 | tf_op jit(solution)/shard_map/one_spread/ppermute | solution.py:773
  33.1 33.4 %collective-permute-start.1 = (bf16[256,1536]{1,0:T(8,128)(2,1)S(1)}, bf16[256,1536]{1,0:T(8,128)(2,1)S(1)}, u32[]{:S(2)}, u32[]{:S(2)}) collective-permute-start(bf16[256,1536]{1,0:T(8,128)(2,1)S(1)} %fusion.13.refs_0_), channel_id=1, source_target_pairs={{0,2},{1,3},{2,0},{3,1},{4,6},{5,7},{6,4},{7,5},{8,10},{9,11},{10,... | collective-permute-start | bytes 2359304 | tf_op jit(solution)/shard_map/one_spread/ppermute | solution.py:773
  33.6 33.7 %collective-permute-start = (bf16[256,1536]{1,0:T(8,128)(2,1)S(1)}, bf16[256,1536]{1,0:T(8,128)(2,1)S(1)}, u32[]{:S(2)}, u32[]{:S(2)}) collective-permute-start(bf16[256,1536]{1,0:T(8,128)(2,1)S(1)} %fusion.13.refs_0_), channel_id=1, source_target_pairs={{0,1},{1,0},{2,3},{3,2},{4,5},{5,4},{6,7},{7,6},{8,9},{9,8},{10,11... | collective-permute-start | bytes 2359304 | tf_op jit(solution)/shard_map/one_spread/ppermute | solution.py:773
  34.4 9.1 %collective-permute-start.14 = (bf16[192,384]{1,0:T(8,128)(2,1)S(1)}, bf16[192,384]{1,0:T(8,128)(2,1)}, u32[]{:S(2)}, u32[]{:S(2)}) collective-permute-start(bf16[192,384]{1,0:T(8,128)(2,1)S(1)} %bitcast.36), channel_id=1, source_target_pairs={{0,8},{4,12},{8,16},{12,20},{16,24},{20,28},{24,0},{28,4},{1,9},{5... | collective-permute-start | bytes 442376 | tf_op jit(solution)/shard_map/out_hop1/ppermute | solution.py:758
  37.8 14.7 %collective-permute-start.8 = (bf16[192,640]{1,0:T(8,128)(2,1)}, bf16[192,640]{1,0:T(8,128)(2,1)S(1)}, u32[]{:S(2)}, u32[]{:S(2)}) collective-permute-start(bf16[192,640]{1,0:T(8,128)(2,1)} %copy-done.48), channel_id=1, source_target_pairs={{0,8},{4,12},{8,16},{12,20},{16,24},{20,28},{24,0},{28,4},{1,9},{5... | collective-permute-start | bytes 737288 | tf_op jit(solution)/shard_map/qkv_hop3/ppermute | solution.py:758
  43.5 35.8 %collective-permute-start.3 = (bf16[192,640]{1,0:T(8,128)(2,1)S(1)}, bf16[192,640]{1,0:T(8,128)(2,1)}, u32[]{:S(2)}, u32[]{:S(2)}) collective-permute-start(bf16[192,640]{1,0:T(8,128)(2,1)S(1)} %constant_dynamic-update-slice_fusion.refs_0_), channel_id=1, source_target_pairs={{0,4},{4,0},{8,12},{12,8},{16,20},{20,16},{24,28},{28,24},{1,5},{5... | collective-permute-start | bytes 737288 | tf_op jit(solution)/shard_map/ppermute | solution.py:755
  52.5 28.5 %collective-permute-start.5 = (bf16[192,640]{1,0:T(8,128)(2,1)}, bf16[192,640]{1,0:T(8,128)(2,1)}, u32[]{:S(2)}, u32[]{:S(2)}) collective-permute-start(bf16[192,640]{1,0:T(8,128)(2,1)} %copy-done.46), channel_id=1, source_target_pairs={{0,4},{4,0},{8,12},{12,8},{16,20},{20,16},{24,28},{28,24},{1,5},{5... | collective-permute-start | bytes 737288 | tf_op jit(solution)/shard_map/ppermute | solution.py:755
  54.1 27.7 %collective-permute-start.7 = (bf16[192,640]{1,0:T(8,128)(2,1)}, bf16[192,640]{1,0:T(8,128)(2,1)}, u32[]{:S(2)}, u32[]{:S(2)}) collective-permute-start(bf16[192,640]{1,0:T(8,128)(2,1)} %copy-done.48), channel_id=1, source_target_pairs={{0,4},{4,0},{8,12},{12,8},{16,20},{20,16},{24,28},{28,24},{1,5},{5... | collective-permute-start | bytes 737288 | tf_op jit(solution)/shard_map/ppermute | solution.py:755
  58.8 29.9 %copy-start.55 = (f32[512]{0:T(512)}, f32[512]{0:T(512)S(1)}, u32[]{:S(2)}) copy-start(f32[512]{0:T(512)S(1)} %concatenate.11) | copy-start | bytes 6148
  67.3 11.7 %collective-permute-start.16 = (bf16[192,384]{1,0:T(8,128)(2,1)}, bf16[192,384]{1,0:T(8,128)(2,1)}, u32[]{:S(2)}, u32[]{:S(2)}) collective-permute-start(bf16[192,384]{1,0:T(8,128)(2,1)} %collective-permute-done.14.refs_2_), channel_id=1, source_target_pairs={{0,8},{4,12},{8,16},{12,20},{16,24},{20,28},{24,0},{28,4},{1,9},{5... | collective-permute-start | bytes 442376 | tf_op jit(solution)/shard_map/out_hop2/ppermute | solution.py:758
  68.2 14.7 %collective-permute-start.9 = (bf16[192,640]{1,0:T(8,128)(2,1)}, bf16[192,640]{1,0:T(8,128)(2,1)}, u32[]{:S(2)}, u32[]{:S(2)}) collective-permute-start(bf16[192,640]{1,0:T(8,128)(2,1)} %copy-done.50), channel_id=1, source_target_pairs={{0,4},{4,0},{8,12},{12,8},{16,20},{20,16},{24,28},{28,24},{1,5},{5... | collective-permute-start | bytes 737288 | tf_op jit(solution)/shard_map/ppermute | solution.py:755
  75.6 18.7 %copy-start.2 = (bf16[1024,1536]{1,0:T(8,128)(2,1)}, bf16[1024,1536]{1,0:T(8,128)(2,1)S(1)}, u32[]{:S(2)}) copy-start(bf16[1024,1536]{1,0:T(8,128)(2,1)S(1)} %get-tuple-element.171.x_ref.normed_ref) | copy-start | bytes 9437188
  79.1 17.8 %collective-permute-start.18 = (bf16[192,384]{1,0:T(8,128)(2,1)}, bf16[192,384]{1,0:T(8,128)(2,1)}, u32[]{:S(2)}, u32[]{:S(2)}) collective-permute-start(bf16[192,384]{1,0:T(8,128)(2,1)} %collective-permute-done.16.refs_4_), channel_id=1, source_target_pairs={{0,8},{4,12},{8,16},{12,20},{16,24},{20,28},{24,0},{28,4},{1,9},{5... | collective-permute-start | bytes 442376 | tf_op jit(solution)/shard_map/out_hop3/ppermute | solution.py:758
  79.3 37.1 %collective-permute-start.12 = (bf16[256,1536]{1,0:T(8,128)(2,1)}, bf16[256,1536]{1,0:T(8,128)(2,1)S(1)}, u32[]{:S(2)}, u32[]{:S(2)}) collective-permute-start(bf16[256,1536]{1,0:T(8,128)(2,1)} %rest_ref.1), channel_id=1, source_target_pairs={{0,3},{1,2},{2,1},{3,0},{4,7},{5,6},{6,5},{7,4},{8,11},{9,10},{10,... | collective-permute-start | bytes 2359304 | tf_op jit(solution)/shard_map/cot_spread/ppermute | solution.py:773
  81.0 35.3 %collective-permute-start.11 = (bf16[256,1536]{1,0:T(8,128)(2,1)}, bf16[256,1536]{1,0:T(8,128)(2,1)S(1)}, u32[]{:S(2)}, u32[]{:S(2)}) collective-permute-start(bf16[256,1536]{1,0:T(8,128)(2,1)} %rest_ref.1), channel_id=1, source_target_pairs={{0,2},{1,3},{2,0},{3,1},{4,6},{5,7},{6,4},{7,5},{8,10},{9,11},{10,... | collective-permute-start | bytes 2359304 | tf_op jit(solution)/shard_map/cot_spread/ppermute | solution.py:773
  81.8 34.6 %collective-permute-start.10 = (bf16[256,1536]{1,0:T(8,128)(2,1)}, bf16[256,1536]{1,0:T(8,128)(2,1)S(1)}, u32[]{:S(2)}, u32[]{:S(2)}) collective-permute-start(bf16[256,1536]{1,0:T(8,128)(2,1)} %rest_ref.1), channel_id=1, source_target_pairs={{0,1},{1,0},{2,3},{3,2},{4,5},{5,4},{6,7},{7,6},{8,9},{9,8},{10,11... | collective-permute-start | bytes 2359304 | tf_op jit(solution)/shard_map/cot_spread/ppermute | solution.py:773
  82.9 29.3 %collective-permute-start.13 = (bf16[192,384]{1,0:T(8,128)(2,1)S(1)}, bf16[192,384]{1,0:T(8,128)(2,1)S(1)}, u32[]{:S(2)}, u32[]{:S(2)}) collective-permute-start(bf16[192,384]{1,0:T(8,128)(2,1)S(1)} %bitcast.37), channel_id=1, source_target_pairs={{0,4},{4,0},{8,12},{12,8},{16,20},{20,16},{24,28},{28,24},{1,5},{5... | collective-permute-start | bytes 442376 | tf_op jit(solution)/shard_map/ppermute | solution.py:755
  96.9 13.3 %copy-start.22 = (bf16[1024,384]{1,0:T(8,128)(2,1)}, bf16[1024,384]{1,0:T(8,128)(2,1)S(1)}, u32[]{:S(2)}) copy-start(bf16[1024,384]{1,0:T(8,128)(2,1)S(1)} %get-tuple-element.104.q_ref) | copy-start | bytes 2359300
  96.9 15.3 %collective-permute-start.15 = (bf16[192,384]{1,0:T(8,128)(2,1)}, bf16[192,384]{1,0:T(8,128)(2,1)S(1)}, u32[]{:S(2)}, u32[]{:S(2)}) collective-permute-start(bf16[192,384]{1,0:T(8,128)(2,1)} %collective-permute-done.14.refs_2_), channel_id=1, source_target_pairs={{0,4},{4,0},{8,12},{12,8},{16,20},{20,16},{24,28},{28,24},{1,5},{5... | collective-permute-start | bytes 442376 | tf_op jit(solution)/shard_map/ppermute | solution.py:755
  112.2 1.6 collective-permute-start.17
  112.2 1.8 collective-permute-start.19
  119.8 20.4 %collective-permute-start.20 = (bf16[256,1536]{1,0:T(8,128)(2,1)S(1)}, bf16[256,1536]{1,0:T(8,128)(2,1)S(1)}, u32[]{:S(2)}, u32[]{:S(2)}) collective-permute-start(bf16[256,1536]{1,0:T(8,128)(2,1)S(1)} %get-tuple-element.114), channel_id=1, source_target_pairs={{0,1},{1,0},{2,3},{3,2},{4,5},{5,4},{6,7},{7,6},{8,9},{9,8},{10,11... | collective-permute-start | bytes 2359304 | tf_op jit(solution)/shard_map/attn_sum/ppermute | solution.py:780
  120.8 36.3 %collective-permute-start.21 = (bf16[256,1536]{1,0:T(8,128)(2,1)S(1)}, bf16[256,1536]{1,0:T(8,128)(2,1)S(1)}, u32[]{:S(2)}, u32[]{:S(2)}) collective-permute-start(bf16[256,1536]{1,0:T(8,128)(2,1)S(1)} %get-tuple-element.115), channel_id=1, source_target_pairs={{0,2},{1,3},{2,0},{3,1},{4,6},{5,7},{6,4},{7,5},{8,10},{9,11},{10,... | collective-permute-start | bytes 2359304 | tf_op jit(solution)/shard_map/attn_sum/ppermute | solution.py:780
  122.1 35.1 %collective-permute-start.22 = (bf16[256,1536]{1,0:T(8,128)(2,1)S(1)}, bf16[256,1536]{1,0:T(8,128)(2,1)S(1)}, u32[]{:S(2)}, u32[]{:S(2)}) collective-permute-start(bf16[256,1536]{1,0:T(8,128)(2,1)S(1)} %get-tuple-element.116), channel_id=1, source_target_pairs={{0,3},{1,2},{2,1},{3,0},{4,7},{5,6},{6,5},{7,4},{8,11},{9,10},{10,... | collective-permute-start | bytes 2359304 | tf_op jit(solution)/shard_map/attn_sum/ppermute | solution.py:780
  140.2 16.9 %copy-start.61 = (bf16[256,1536]{1,0:T(8,128)(2,1)}, bf16[256,1536]{1,0:T(8,128)(2,1)S(1)}, u32[]{:S(2)}) copy-start(bf16[256,1536]{1,0:T(8,128)(2,1)S(1)} %collective-permute-done.20.refs_1_) | copy-start | bytes 2359300
  162.5 36.0 %copy-start.35 = (bf16[256,1536]{1,0:T(8,128)(2,1)S(1)}, bf16[256,1536]{1,0:T(8,128)(2,1)}, u32[]{:S(2)}) copy-start(bf16[256,1536]{1,0:T(8,128)(2,1)} %get-tuple-element.123.refs_0_) | copy-start | bytes 2359300
  162.5 35.5 %collective-permute-start.25 = (bf16[256,1536]{1,0:T(8,128)(2,1)}, bf16[256,1536]{1,0:T(8,128)(2,1)S(1)}, u32[]{:S(2)}, u32[]{:S(2)}) collective-permute-start(bf16[256,1536]{1,0:T(8,128)(2,1)} %get-tuple-element.123.refs_0_), channel_id=1, source_target_pairs={{0,3},{1,2},{2,1},{3,0},{4,7},{5,6},{6,5},{7,4},{8,11},{9,10},{10,... | collective-permute-start | bytes 2359304 | tf_op jit(solution)/shard_map/two_spread/ppermute | solution.py:773
  164.0 34.4 %collective-permute-start.24 = (bf16[256,1536]{1,0:T(8,128)(2,1)}, bf16[256,1536]{1,0:T(8,128)(2,1)S(1)}, u32[]{:S(2)}, u32[]{:S(2)}) collective-permute-start(bf16[256,1536]{1,0:T(8,128)(2,1)} %get-tuple-element.123.refs_0_), channel_id=1, source_target_pairs={{0,2},{1,3},{2,0},{3,1},{4,6},{5,7},{6,4},{7,5},{8,10},{9,11},{10,... | collective-permute-start | bytes 2359304 | tf_op jit(solution)/shard_map/two_spread/ppermute | solution.py:773
  164.2 34.3 %collective-permute-start.23 = (bf16[256,1536]{1,0:T(8,128)(2,1)}, bf16[256,1536]{1,0:T(8,128)(2,1)}, u32[]{:S(2)}, u32[]{:S(2)}) collective-permute-start(bf16[256,1536]{1,0:T(8,128)(2,1)} %get-tuple-element.123.refs_0_), channel_id=1, source_target_pairs={{0,1},{1,0},{2,3},{3,2},{4,5},{5,4},{6,7},{7,6},{8,9},{9,8},{10,11... | collective-permute-start | bytes 2359304 | tf_op jit(solution)/shard_map/two_spread/ppermute | solution.py:773
  237.3 161.9 %reduce-scatter.6.cloned.1.call-start = ((), (), s32[]{:S(2)}) async-start(), calls=%async_computation.5 | async-start | bytes 6193152 | tf_op jit(solution)/shard_map/reduce_scatter | solution.py:899
  254.7 31.3 %collective-permute-start.26 = (bf16[256,1536]{1,0:T(8,128)(2,1)S(1)}, bf16[256,1536]{1,0:T(8,128)(2,1)}, u32[]{:S(2)}, u32[]{:S(2)}) collective-permute-start(bf16[256,1536]{1,0:T(8,128)(2,1)S(1)} %get-tuple-element.129), channel_id=1, source_target_pairs={{0,1},{1,0},{2,3},{3,2},{4,5},{5,4},{6,7},{7,6},{8,9},{9,8},{10,11... | collective-permute-start | bytes 2359304 | tf_op jit(solution)/shard_map/two_sum/ppermute | solution.py:780
  255.9 36.1 %collective-permute-start.27 = (bf16[256,1536]{1,0:T(8,128)(2,1)S(1)}, bf16[256,1536]{1,0:T(8,128)(2,1)}, u32[]{:S(2)}, u32[]{:S(2)}) collective-permute-start(bf16[256,1536]{1,0:T(8,128)(2,1)S(1)} %get-tuple-element.130), channel_id=1, source_target_pairs={{0,2},{1,3},{2,0},{3,1},{4,6},{5,7},{6,4},{7,5},{8,10},{9,11},{10,... | collective-permute-start | bytes 2359304 | tf_op jit(solution)/shard_map/two_sum/ppermute | solution.py:780
  257.0 35.0 %collective-permute-start.28 = (bf16[256,1536]{1,0:T(8,128)(2,1)S(1)}, bf16[256,1536]{1,0:T(8,128)(2,1)}, u32[]{:S(2)}, u32[]{:S(2)}) collective-permute-start(bf16[256,1536]{1,0:T(8,128)(2,1)S(1)} %get-tuple-element.131), channel_id=1, source_target_pairs={{0,3},{1,2},{2,1},{3,0},{4,7},{5,6},{6,5},{7,4},{8,11},{9,10},{10,... | collective-permute-start | bytes 2359304 | tf_op jit(solution)/shard_map/two_sum/ppermute | solution.py:780
  302.1 155.2 %reduce-scatter.8.cloned.1.call-start = ((), (), s32[]{:S(2)}) async-start(), calls=%async_computation.6 | async-start | bytes 3538944 | tf_op jit(solution)/shard_map/reduce_scatter | solution.py:925
  302.2 5.5 %collective-permute-start.32 = (bf16[768,1792]{1,0:T(8,128)(2,1)}, bf16[768,1792]{1,0:T(8,128)(2,1)}, u32[]{:S(2)}, u32[]{:S(2)}) collective-permute-start(bf16[768,1792]{1,0:T(8,128)(2,1)} %product.5), channel_id=1, source_target_pairs={{0,4},{4,0},{8,12},{12,8},{16,20},{20,16},{24,28},{28,24},{1,5},{5... | collective-permute-start | bytes 8257544 | tf_op jit(solution)/shard_map/ppermute | solution.py:755
  302.3 20.7 %collective-permute-start.29 = (bf16[256,1536]{1,0:T(8,128)(2,1)}, bf16[256,1536]{1,0:T(8,128)(2,1)}, u32[]{:S(2)}, u32[]{:S(2)}) collective-permute-start(bf16[256,1536]{1,0:T(8,128)(2,1)} %get-tuple-element.141.refs_0_), channel_id=1, source_target_pairs={{0,1},{1,0},{2,3},{3,2},{4,5},{5,4},{6,7},{7,6},{8,9},{9,8},{10,11... | collective-permute-start | bytes 2359304 | tf_op jit(solution)/shard_map/dh_spread/ppermute | solution.py:773
  303.8 43.0 %collective-permute-start.31 = (bf16[256,1536]{1,0:T(8,128)(2,1)}, bf16[256,1536]{1,0:T(8,128)(2,1)}, u32[]{:S(2)}, u32[]{:S(2)}) collective-permute-start(bf16[256,1536]{1,0:T(8,128)(2,1)} %get-tuple-element.141.refs_0_), channel_id=1, source_target_pairs={{0,3},{1,2},{2,1},{3,0},{4,7},{5,6},{6,5},{7,4},{8,11},{9,10},{10,... | collective-permute-start | bytes 2359304 | tf_op jit(solution)/shard_map/dh_spread/ppermute | solution.py:773
  305.3 41.5 %collective-permute-start.30 = (bf16[256,1536]{1,0:T(8,128)(2,1)}, bf16[256,1536]{1,0:T(8,128)(2,1)}, u32[]{:S(2)}, u32[]{:S(2)}) collective-permute-start(bf16[256,1536]{1,0:T(8,128)(2,1)} %get-tuple-element.141.refs_0_), channel_id=1, source_target_pairs={{0,2},{1,3},{2,0},{3,1},{4,6},{5,7},{6,4},{7,5},{8,10},{9,11},{10,... | collective-permute-start | bytes 2359304 | tf_op jit(solution)/shard_map/dh_spread/ppermute | solution.py:773
  309.8 34.8 %collective-permute-start.33 = (bf16[192,1792]{1,0:T(8,128)(2,1)}, bf16[192,1792]{1,0:T(8,128)(2,1)}, u32[]{:S(2)}, u32[]{:S(2)}) collective-permute-start(bf16[192,1792]{1,0:T(8,128)(2,1)} %join.3), channel_id=1, source_target_pairs={{0,8},{4,12},{8,16},{12,20},{16,24},{20,28},{24,0},{28,4},{1,9},{5... | collective-permute-start | bytes 2064392 | tf_op jit(solution)/shard_map/gate_grad_hop1/ppermute | solution.py:758
  319.6 27.2 %copy-start.21 = (bf16[256,1536]{1,0:T(8,128)(2,1)}, bf16[256,1536]{1,0:T(8,128)(2,1)S(1)}, u32[]{:S(2)}) copy-start(bf16[256,1536]{1,0:T(8,128)(2,1)S(1)} %get-tuple-element.143.refs_0_) | copy-start | bytes 2359300
  346.8 38.3 %collective-permute-start.35 = (bf16[256,1536]{1,0:T(8,128)(2,1)}, bf16[256,1536]{1,0:T(8,128)(2,1)}, u32[]{:S(2)}, u32[]{:S(2)}) collective-permute-start(bf16[256,1536]{1,0:T(8,128)(2,1)} %get-tuple-element.161), channel_id=1, source_target_pairs={{0,1},{1,0},{2,3},{3,2},{4,5},{5,4},{6,7},{7,6},{8,9},{9,8},{10,11... | collective-permute-start | bytes 2359304 | tf_op jit(solution)/shard_map/ffn_sum/ppermute | solution.py:780
  348.2 36.8 %collective-permute-start.36 = (bf16[256,1536]{1,0:T(8,128)(2,1)}, bf16[256,1536]{1,0:T(8,128)(2,1)}, u32[]{:S(2)}, u32[]{:S(2)}) collective-permute-start(bf16[256,1536]{1,0:T(8,128)(2,1)} %get-tuple-element.162), channel_id=1, source_target_pairs={{0,2},{1,3},{2,0},{3,1},{4,6},{5,7},{6,4},{7,5},{8,10},{9,11},{10,... | collective-permute-start | bytes 2359304 | tf_op jit(solution)/shard_map/ffn_sum/ppermute | solution.py:780
  349.7 35.3 %collective-permute-start.37 = (bf16[256,1536]{1,0:T(8,128)(2,1)}, bf16[256,1536]{1,0:T(8,128)(2,1)}, u32[]{:S(2)}, u32[]{:S(2)}) collective-permute-start(bf16[256,1536]{1,0:T(8,128)(2,1)} %get-tuple-element.163), channel_id=1, source_target_pairs={{0,3},{1,2},{2,1},{3,0},{4,7},{5,6},{6,5},{7,4},{8,11},{9,10},{10,... | collective-permute-start | bytes 2359304 | tf_op jit(solution)/shard_map/ffn_sum/ppermute | solution.py:780
  350.3 34.7 %collective-permute-start.34 = (bf16[192,1792]{1,0:T(8,128)(2,1)}, bf16[192,1792]{1,0:T(8,128)(2,1)}, u32[]{:S(2)}, u32[]{:S(2)}) collective-permute-start(bf16[192,1792]{1,0:T(8,128)(2,1)} %join.4), channel_id=1, source_target_pairs={{0,8},{4,12},{8,16},{12,20},{16,24},{20,28},{24,0},{28,4},{1,9},{5... | collective-permute-start | bytes 2064392 | tf_op jit(solution)/shard_map/gate_grad_hop2/ppermute | solution.py:758
  400.3 28.4 %collective-permute-start.41 = (bf16[192,1792]{1,0:T(8,128)(2,1)S(1)}, bf16[192,1792]{1,0:T(8,128)(2,1)S(1)}, u32[]{:S(2)}, u32[]{:S(2)}) collective-permute-start(bf16[192,1792]{1,0:T(8,128)(2,1)S(1)} %copy-done.38), channel_id=1, source_target_pairs={{0,8},{4,12},{8,16},{12,20},{16,24},{20,28},{24,0},{28,4},{1,9},{5... | collective-permute-start | bytes 2064392 | tf_op jit(solution)/shard_map/gate_grad_hop3/ppermute | solution.py:758
  400.3 29.9 %collective-permute-start.38 = (bf16[256,1536]{1,0:T(8,128)(2,1)}, bf16[256,1536]{1,0:T(8,128)(2,1)S(1)}, u32[]{:S(2)}, u32[]{:S(2)}) collective-permute-start(bf16[256,1536]{1,0:T(8,128)(2,1)} %get-tuple-element.167.refs_1_), channel_id=1, source_target_pairs={{0,1},{1,0},{2,3},{3,2},{4,5},{5,4},{6,7},{7,6},{8,9},{9,8},{10,11... | collective-permute-start | bytes 2359304 | tf_op jit(solution)/shard_map/one_sum/ppermute | solution.py:780
  401.7 32.7 %collective-permute-start.39 = (bf16[256,1536]{1,0:T(8,128)(2,1)S(1)}, bf16[256,1536]{1,0:T(8,128)(2,1)S(1)}, u32[]{:S(2)}, u32[]{:S(2)}) collective-permute-start(bf16[256,1536]{1,0:T(8,128)(2,1)S(1)} %get-tuple-element.168.refs_2_), channel_id=1, source_target_pairs={{0,2},{1,3},{2,0},{3,1},{4,6},{5,7},{6,4},{7,5},{8,10},{9,11},{10,... | collective-permute-start | bytes 2359304 | tf_op jit(solution)/shard_map/one_sum/ppermute | solution.py:780
  403.2 32.1 %collective-permute-start.40 = (bf16[256,1536]{1,0:T(8,128)(2,1)S(1)}, bf16[256,1536]{1,0:T(8,128)(2,1)S(1)}, u32[]{:S(2)}, u32[]{:S(2)}) collective-permute-start(bf16[256,1536]{1,0:T(8,128)(2,1)S(1)} %get-tuple-element.169.refs_3_), channel_id=1, source_target_pairs={{0,3},{1,2},{2,1},{3,0},{4,7},{5,6},{6,5},{7,4},{8,11},{9,10},{10,... | collective-permute-start | bytes 2359304 | tf_op jit(solution)/shard_map/one_sum/ppermute | solution.py:780
  408.2 20.5 %copy-start.36 = (bf16[192,1792]{1,0:T(8,128)(2,1)S(1)}, bf16[192,1792]{1,0:T(8,128)(2,1)}, u32[]{:S(2)}) copy-start(bf16[192,1792]{1,0:T(8,128)(2,1)} %reduce-scatter.4.cloned.1.call-done.grads_ref) | copy-start | bytes 2064388
  408.2 20.9 %copy-start.65 = (bf16[192,1792]{1,0:T(8,128)(2,1)S(1)}, bf16[192,1792]{1,0:T(8,128)(2,1)}, u32[]{:S(2)}) copy-start(bf16[192,1792]{1,0:T(8,128)(2,1)} %reduce-scatter.6.cloned.1.call-done) | copy-start | bytes 2064388
  411.7 23.6 %copy-start.67 = (f32[1,3584]{1,0:T(1,128)S(1)}, f32[1,3584]{1,0:T(1,128)}, u32[]{:S(2)}) copy-start(f32[1,3584]{1,0:T(1,128)} %gain_parts.1) | copy-start | bytes 43012
  435.3 10.5 %collective-permute-start.44 = (f32[1,3584]{1,0:T(1,128)S(1)}, f32[1,3584]{1,0:T(1,128)S(1)}, u32[]{:S(2)}, u32[]{:S(2)}) collective-permute-start(f32[1,3584]{1,0:T(1,128)S(1)} %copy-done.67), channel_id=1, source_target_pairs={{0,3},{1,2},{2,1},{3,0},{4,7},{5,6},{6,5},{7,4},{8,11},{9,10},{10,... | collective-permute-start | bytes 43016 | tf_op jit(solution)/shard_map/ppermute | solution.py:933
  436.8 9.0 %collective-permute-start.43 = (f32[1,3584]{1,0:T(1,128)S(1)}, f32[1,3584]{1,0:T(1,128)S(1)}, u32[]{:S(2)}, u32[]{:S(2)}) collective-permute-start(f32[1,3584]{1,0:T(1,128)S(1)} %copy-done.67), channel_id=1, source_target_pairs={{0,2},{1,3},{2,0},{3,1},{4,6},{5,7},{6,4},{7,5},{8,10},{9,11},{10,... | collective-permute-start | bytes 43016 | tf_op jit(solution)/shard_map/ppermute | solution.py:933
  438.2 7.6 %collective-permute-start.42 = (f32[1,3584]{1,0:T(1,128)S(1)}, f32[1,3584]{1,0:T(1,128)S(1)}, u32[]{:S(2)}, u32[]{:S(2)}) collective-permute-start(f32[1,3584]{1,0:T(1,128)S(1)} %copy-done.67), channel_id=1, source_target_pairs={{0,1},{1,0},{2,3},{3,2},{4,5},{5,4},{6,7},{7,6},{8,9},{9,8},{10,11... | collective-permute-start | bytes 43016 | tf_op jit(solution)/shard_map/ppermute | solution.py:933
  445.8 1.2 collective-permute-start.45
  447.1 6.1 %collective-permute-start.48 = (f32[1,3584]{1,0:T(1,128)S(1)}, f32[1,3584]{1,0:T(1,128)S(1)}, u32[]{:S(2)}, u32[]{:S(2)}) collective-permute-start(f32[1,3584]{1,0:T(1,128)S(1)} %add.119), channel_id=1, source_target_pairs={{0,24},{4,28},{8,16},{12,20},{16,8},{20,12},{24,0},{28,4},{1,25},{... | collective-permute-start | bytes 43016 | tf_op jit(solution)/shard_map/ppermute | solution.py:933
  450.8 4.6 collective-permute-start.47
  450.8 4.6 collective-permute-start.46
  (60 other events, 231.2 us)
Sparse Core Ops, SparseCore 0:
  30.0 157.8 all-gather.1
  237.5 64.6 reduce-scatter.3
  304.4 90.1 reduce-scatter.5
  399.4 47.9 reduce-scatter.7

commit v7 on v6

--- a/solution.py
+++ b/solution.py
@@ -365,7 +365,7 @@
     length, cols = lefts[0].shape
     width = weights.shape[1]
     rows = length // ranks
-    tile = 512
+    tile = 256
     return pl.pallas_call(
         functools.partial(back_parts_kernel, rows, len(lefts)),
         grid=(width // tile,),

time: 472 us -> 474 us (level)
  transfers between devices with their start and end apart: 53 -> 53, of which waited for: 23 -> 23; matrix products, arithmetic and copies ran while one was open for 4% -> 4% of each run, Pallas kernels for 34% -> 35%
where the time goes in v7:
time: 474 us; the launch traced here: 469 us
  Pallas kernels  177 us (37%)
  waiting for transfers between devices  157 us (33%)
  local copies, waits for them, and re-layouts  44.3 us (9%)
  starting transfers between devices  40.9 us (9%)
  matrix products  24.1 us (5%)
  between operations  15 us (3%)
  other arithmetic  10.2 us (2%)
    ppermute x9, waiting for transfers between devices, onward(): return lax.ppermute(v, 'dp', ring_pairs)  71.8 us
    ppermute x12, waiting for transfers between devices, send_parts(): lax.ppermute(parts[j], 'tensor', [(i, i ^ j) for i in range(ranks)])  40.2 us
    pallas_call x4, Pallas kernels, product(): pl.pallas_call(functools.partial(product_kernel, tiles), grid=(tiles * le...  38.8 us
    unnamed x147, local copies, waits for them, and re-layouts  37.6 us
    pallas_call x4, Pallas kernels, back_parts(): pl.pallas_call(functools.partial(back_parts_kernel, rows, len(lefts)), gr...  36.5 us
    dot_general x2, matrix products, mm(): return jnp.dot(left, right, preferred_element_type=F32)  24.1 us
    all_gather x1, waiting for transfers between devices, shards(): lax.all_gather(tie(jnp.stack([widen(w_down.T), widen(w_gate), widen(w_up)...  21.2 us
    pallas_call x1, Pallas kernels, attend_back(): pl.pallas_call(functools.partial(attend_back_kernel, heads, rows), grid_s...  15.6 us
  transfers between devices with their start and end apart: 53, of which 23 were waited for; matrix products, arithmetic and copies ran while one was open for 4% of the time, Pallas kernels for 35%

profile of v7, /device:TPU:0, one launch (start us, length us, event | category | flops | bytes accessed | tf_op | source)
XLA Modules:
  0.0 468.5 jit_solution(281082133370623212)
XLA Ops:
  9.9 3.1 collective-permute-start.4
  14.4 6.5 %collective-permute-done.4.refs_2_ = bf16[192,640]{1,0:T(8,128)(2,1)S(1)} collective-permute-done((bf16[192,640]{1,0:T(8,128)(2,1)S(1)}, bf16[192,640]{1,0:T(8,128)(2,1)S(1)}, u32[]{:S(2)}, u32[]{:S(2)}) %collective-permute-start.4) | collective-permute-done | bytes 245792 | tf_op jit(solution)/shard_map/qkv_hop1/ppermute | solution.py:758
  20.9 1.5 pad_maximum_fusion
  22.5 7.4 %collective-permute-done.6.refs_4_ = bf16[192,640]{1,0:T(8,128)(2,1)S(1)} collective-permute-done((bf16[192,640]{1,0:T(8,128)(2,1)S(1)}, bf16[192,640]{1,0:T(8,128)(2,1)S(1)}, u32[]{:S(2)}, u32[]{:S(2)}) %collective-permute-start.6) | collective-permute-done | bytes 245792 | tf_op jit(solution)/shard_map/qkv_hop2/ppermute | solution.py:758
  30.8 2.3 collective-permute-start.2
  38.0 5.5 %collective-permute-done.14.refs_2_ = bf16[192,384]{1,0:T(8,128)(2,1)} collective-permute-done((bf16[192,384]{1,0:T(8,128)(2,1)S(1)}, bf16[192,384]{1,0:T(8,128)(2,1)}, u32[]{:S(2)}, u32[]{:S(2)}) %collective-permute-start.14) | collective-permute-done | bytes 147488 | tf_op jit(solution)/shard_map/out_hop1/ppermute | solution.py:758
  43.5 9.0 %collective-permute-done.8.refs_6_ = bf16[192,640]{1,0:T(8,128)(2,1)S(1)} collective-permute-done((bf16[192,640]{1,0:T(8,128)(2,1)}, bf16[192,640]{1,0:T(8,128)(2,1)S(1)}, u32[]{:S(2)}, u32[]{:S(2)}) %collective-permute-start.8) | collective-permute-done | bytes 245792 | tf_op jit(solution)/shard_map/qkv_hop3/ppermute | solution.py:758
  54.1 3.7 fusion.14
  58.8 7.7 %collective-permute-done.1.refs_2_ = bf16[256,1536]{1,0:T(8,128)(2,1)S(1)} collective-permute-done((bf16[256,1536]{1,0:T(8,128)(2,1)S(1)}, bf16[256,1536]{1,0:T(8,128)(2,1)S(1)}, u32[]{:S(2)}, u32[]{:S(2)}) %collective-permute-start.1) | collective-permute-done | bytes 786464 | tf_op jit(solution)/shard_map/one_spread/ppermute | solution.py:773
  74.0 1.6 copy-done.8
  75.6 3.5 collective-permute-done.16.refs_4_
  79.3 1.7 collective-permute-start.12
  85.8 2.9 place.2.w_ref
  88.7 5.5 %prepare.1 = (bf16[1024,384]{1,0:T(8,128)(2,1)S(1)}, bf16[1024,128]{1,0:T(8,128)(2,1)S(1)}, bf16[1024,128]{1,0:T(8,128)(2,1)S(1)}, f32[1024,512]{1,0:T(8,128)S(1)}) custom-call(bf16[1024,1536]{1,0:T(8,128)(2,1)S(1)} %get-tuple-element.171.x_ref.normed_ref, bf16[1536,640]{1,0:T(8,128)(2,1)S(1)} %place.2.w_ref, f32[1024,128]{1,0:T(8,128)S(1)} %copy-done.7, ...), custom_call_target="tpu_custom_call" | custom-call | tf_op jit(solution)/shard_map/prepare/pallas_call | solution.py:637
  97.4 12.8 %attend.1 = (bf16[1024,384]{1,0:T(8,128)(2,1)S(1)}, f32[4,2,768]{2,1,0:T(2,128)S(1)}) custom-call(s32[1]{0:T(128)} %bitcast.me_ref, bf16[1024,384]{1,0:T(8,128)(2,1)S(1)} %get-tuple-element.104.q_ref, bf16[1024,128]{1,0:T(8,128)(2,1)S(1)} %get-tuple-element.105.k_ref, bf16[1024,128]{1,0:T(8,128)(2,1)S(1)} %get-tuple-element.106.v_ref, ...), custom_call_target="tpu_custom_call" | custom-call | flops 6442450944 | bytes 33554432 | tf_op jit(solution)/shard_map/attend/pallas_call | solution.py:182
  114.0 2.3 place.3
  116.4 3.0 back_parts.4
  125.6 1.6 copy-done.10
  127.2 1.7 copy-done.15
  128.8 12.0 %collective-permute-done.20.refs_1_ = bf16[256,1536]{1,0:T(8,128)(2,1)S(1)} collective-permute-done((bf16[256,1536]{1,0:T(8,128)(2,1)S(1)}, bf16[256,1536]{1,0:T(8,128)(2,1)S(1)}, u32[]{:S(2)}, u32[]{:S(2)}) %collective-permute-start.20) | collective-permute-done | bytes 786464 | tf_op jit(solution)/shard_map/attn_sum/ppermute | solution.py:780
  140.8 16.9 %collective-permute-done.21.refs_2_ = bf16[256,1536]{1,0:T(8,128)(2,1)S(1)} collective-permute-done((bf16[256,1536]{1,0:T(8,128)(2,1)S(1)}, bf16[256,1536]{1,0:T(8,128)(2,1)S(1)}, u32[]{:S(2)}, u32[]{:S(2)}) %collective-permute-start.21) | collective-permute-done | bytes 786464 | tf_op jit(solution)/shard_map/attn_sum/ppermute | solution.py:780
  159.5 3.6 sum_up.2
  163.1 1.5 collective-permute-start.25
  164.8 1.8 collective-permute-start.23
  166.6 21.2 %all-gather.2.cloned.1.call-done.right_ref.refs_2_.refs_3_.refs_1_ = bf16[3,1536,1792]{2,1,0:T(8,128)(2,1)} async-done(((bf16[3,192,1792]{2,1,0:T(8,128)(2,1)}), bf16[3,1536,1792]{2,1,0:T(8,128)(2,1)}) %all-gather.2.cloned.1.call-update) | async-done | bytes 16515088 | tf_op jit(solution)/shard_map/all_gather | solution.py:803
  187.9 10.2 %rows_product.2 = bf16[1024,1792]{1,0:T(8,128)(2,1)} custom-call(bf16[1024,1536]{1,0:T(8,128)(2,1)} %copy-done.15, bf16[3,1536,1792]{2,1,0:T(8,128)(2,1)} %all-gather.2.cloned.1.call-done.right_ref.refs_2_.refs_3_.refs_1_), custom_call_target="tpu_custom_call" | custom-call | tf_op jit(solution)/shard_map/rows_product/pallas_call | solution.py:542
  199.1 2.5 fold.6
  202.8 10.3 %fusion.10 = bf16[1024,1792]{1,0:T(8,128)(2,1)S(1)} fusion(bf16[1024,1536]{1,0:T(8,128)(2,1)S(1)} %get-tuple-element.125, bf16[3,1536,1792]{2,1,0:T(8,128)(2,1)} %all-gather.2.cloned.1.call-done.right_ref.refs_2_.refs_3_.refs_1_), kind=kOutput, calls=%fused_computation.18 | convolution fusion | flops 5638979584 | bytes 12320768 | tf_op jit(solution)/shard_map/dot_general | solution.py:40
  213.2 13.8 %multiply_convert_fusion = (bf16[1024,1792]{1,0:T(8,128)(2,1)}, bf16[1024,1792]{1,0:T(8,128)(2,1)}, bf16[1024,1792]{1,0:T(8,128)(2,1)}) fusion(bf16[1024,1792]{1,0:T(8,128)(2,1)S(1)} %fusion.10, bf16[1024,1792]{1,0:T(8,128)(2,1)S(1)} %copy-done.57, bf16[1024,1536]{1,0:T(8,128)(2,1)S(1)} %get-tuple-element.125, ...), kind=kOutput, calls=%fused_computation.13 | convolution fusion | flops 5668339712 | bytes 27000832 | tf_op jit(solution)/shard_map/dot_general | solution.py:40
  226.9 11.0 %product.4 = bf16[1536,1792]{1,0:T(8,128)(2,1)} custom-call(bf16[1536,1024]{1,0:T(8,128)(2,1)} %copy-done.10, bf16[1024,1792]{1,0:T(8,128)(2,1)} %get-tuple-element.142.refs_0_), custom_call_target="tpu_custom_call" | custom-call | tf_op jit(solution)/shard_map/product/pallas_call | solution.py:313
  238.0 16.6 %back_parts.5 = (bf16[256,1536]{1,0:T(8,128)(2,1)S(1)}, bf16[256,1536]{1,0:T(8,128)(2,1)S(1)}, bf16[256,1536]{1,0:T(8,128)(2,1)S(1)}, bf16[256,1536]{1,0:T(8,128)(2,1)S(1)}) custom-call(bf16[1024,1792]{1,0:T(8,128)(2,1)} %get-tuple-element.135.refs_0_, bf16[1024,1792]{1,0:T(8,128)(2,1)} %get-tuple-element.137.refs_1_.refs_0_, ...), custom_call_target="tpu_custom_call" | custom-call | tf_op jit(solution)/shard_map/back_parts/pallas_call | solution.py:369
  257.5 1.5 collective-permute-start.28
  259.0 8.4 %product.5 = bf16[768,1792]{1,0:T(8,128)(2,1)} custom-call(bf16[768,1024]{1,0:T(8,128)(2,1)} %copy-done.20, bf16[1024,1792]{1,0:T(8,128)(2,1)} %get-tuple-element.135.refs_0_), custom_call_target="tpu_custom_call" | custom-call | tf_op jit(solution)/shard_map/product/pallas_call | solution.py:313
  267.4 8.3 %product.6.refs_0_.refs_1_.near_ref = bf16[768,1792]{1,0:T(8,128)(2,1)} custom-call(bf16[768,1024]{1,0:T(8,128)(2,1)} %copy-done.19, bf16[1024,1792]{1,0:T(8,128)(2,1)} %get-tuple-element.135.refs_0_), custom_call_target="tpu_custom_call" | custom-call | tf_op jit(solution)/shard_map/product/pallas_call | solution.py:313
  275.7 11.0 %product.7 = bf16[1536,1792]{1,0:T(8,128)(2,1)} custom-call(bf16[1536,1024]{1,0:T(8,128)(2,1)} %copy-done.11, bf16[1024,1792]{1,0:T(8,128)(2,1)} %get-tuple-element.137.refs_1_.refs_0_), custom_call_target="tpu_custom_call" | custom-call | tf_op jit(solution)/shard_map/product/pallas_call | solution.py:313
  286.7 6.1 %collective-permute-done.27.refs_2_ = bf16[256,1536]{1,0:T(8,128)(2,1)} collective-permute-done((bf16[256,1536]{1,0:T(8,128)(2,1)S(1)}, bf16[256,1536]{1,0:T(8,128)(2,1)}, u32[]{:S(2)}, u32[]{:S(2)}) %collective-permute-start.27) | collective-permute-done | bytes 786464 | tf_op jit(solution)/shard_map/two_sum/ppermute | solution.py:780
  292.8 4.5 norm_back_sum.2
  297.3 5.4 %reduce-scatter.4.cloned.1.call-done.grads_ref = bf16[192,1792]{1,0:T(8,128)(2,1)} async-done(((bf16[1536,1792]{1,0:T(8,128)(2,1)}), bf16[192,1792]{1,0:T(8,128)(2,1)}) %reduce-scatter.4.cloned.1.call-update) | async-done | bytes 688144 | tf_op jit(solution)/shard_map/reduce_scatter | solution.py:885
  302.9 1.5 collective-permute-start.29
  306.4 1.9 collective-permute-done.32.refs_1_.refs_2_.other_ref
  308.3 2.1 join.3
  310.4 10.5 %back_parts.6 = (bf16[256,1536]{1,0:T(8,128)(2,1)S(1)}, bf16[256,1536]{1,0:T(8,128)(2,1)}, bf16[256,1536]{1,0:T(8,128)(2,1)}, bf16[256,1536]{1,0:T(8,128)(2,1)}) custom-call(bf16[1024,1792]{1,0:T(8,128)(2,1)} %get-tuple-element.142.refs_0_, bf16[3,1536,1792]{2,1,0:T(8,128)(2,1)} %all-gather.2.cloned.1.call-done.right_ref.refs_2_.refs_3_.refs_1_), custom_call_target="tpu_custom_call" | custom-call | tf_op jit(solution)/shard_map/back_parts/pallas_call | solution.py:369
  320.8 2.8 collective-permute-done.29.refs_1_
  323.6 21.6 %collective-permute-done.33.refs_0_ = bf16[192,1792]{1,0:T(8,128)(2,1)} collective-permute-done((bf16[192,1792]{1,0:T(8,128)(2,1)}, bf16[192,1792]{1,0:T(8,128)(2,1)}, u32[]{:S(2)}, u32[]{:S(2)}) %collective-permute-start.33) | collective-permute-done | bytes 688160 | tf_op jit(solution)/shard_map/gate_grad_hop1/ppermute | solution.py:758
  345.2 2.2 join.4
  348.8 1.5 collective-permute-start.36
  352.1 2.7 fold.7
  354.9 2.6 rows_product.3.do_ref
  357.5 15.6 %attend_back.1 = (f32[1024,384]{1,0:T(8,128)S(1)}, f32[1024,128]{1,0:T(8,128)S(1)}, f32[1024,128]{1,0:T(8,128)S(1)}) custom-call(s32[1]{0:T(128)} %bitcast.me_ref, bf16[1024,384]{1,0:T(8,128)(2,1)S(1)} %copy-done.23, bf16[1024,128]{1,0:T(8,128)(2,1)S(1)} %copy-done.43, bf16[1024,128]{1,0:T(8,128)(2,1)S(1)} %copy-done.45, s32[4,1,256]{2,1,0:T(1,128)S(1)} %reshape.123.lo_ref, ...), custom_call_target="tpu_custom_call" | custom-call | tf_op jit(solution)/shard_map/attend_back/pallas_call | solution.py:208
  375.9 7.8 %prepare_back.1 = (bf16[1024,640]{1,0:T(8,128)(2,1)}, f32[1,512]{1,0:T(1,128)}) custom-call(f32[1024,384]{1,0:T(8,128)} %copy-done.18, f32[1024,128]{1,0:T(8,128)} %copy-done.39, f32[1024,128]{1,0:T(8,128)} %copy-done.40, f32[1024,512]{1,0:T(8,128)} %copy-done.17, f32[1024,128]{1,0:T(8,128)} %get-tuple-element.214.cos_ref, ...), custom_call_target="tpu_custom_call" | custom-call | tf_op jit(solution)/shard_map/prepare_back/pallas_call | solution.py:691
  383.7 1.7 collective-permute-done.34.refs_0_
  385.4 1.6 join.5
  387.9 6.4 %back_parts.7 = (bf16[256,1536]{1,0:T(8,128)(2,1)S(1)}, bf16[256,1536]{1,0:T(8,128)(2,1)}, bf16[256,1536]{1,0:T(8,128)(2,1)S(1)}, bf16[256,1536]{1,0:T(8,128)(2,1)S(1)}) custom-call(bf16[1024,640]{1,0:T(8,128)(2,1)S(1)} %copy-done.5, bf16[1,1536,640]{2,1,0:T(8,128)(2,1)} %bitcast.33), custom_call_target="tpu_custom_call" | custom-call | tf_op jit(solution)/shard_map/back_parts/pallas_call | solution.py:369
  395.2 5.7 %attn_products.1 = bf16[1536,1024]{1,0:T(8,128)(2,1)} custom-call(bf16[1536,1024]{1,0:T(8,128)(2,1)S(1)} %copy-done.9, bf16[1536,1024]{1,0:T(8,128)(2,1)S(1)} %get-tuple-element.153.refs_1_, bf16[1024,640]{1,0:T(8,128)(2,1)S(1)} %copy-done.5, bf16[1024,384]{1,0:T(8,128)(2,1)S(1)} %get-tuple-element.109.refs_0_.o_ref.refs_3_), custom_call_target="tpu_custom_call" | custom-call | tf_op jit(solution)/shard_map/attn_products/pallas_call | solution.py:346
  406.0 3.9 gain_parts.1
  409.9 3.5 sum_up.3
  413.4 16.7 %collective-permute-done.41.flow_ref = bf16[192,1792]{1,0:T(8,128)(2,1)S(1)} collective-permute-done((bf16[192,1792]{1,0:T(8,128)(2,1)S(1)}, bf16[192,1792]{1,0:T(8,128)(2,1)S(1)}, u32[]{:S(2)}, u32[]{:S(2)}) %collective-permute-start.41) | collective-permute-done | bytes 688160 | tf_op jit(solution)/shard_map/gate_grad_hop3/ppermute | solution.py:758
  431.6 4.4 collective-permute-done.39.refs_2_
  436.8 1.5 collective-permute-start.44
  440.4 4.1 norm_back_sum.3
  444.5 2.8 last_join.1
  448.7 3.7 collective-permute-start.48
  453.1 1.6 copy.28
  454.7 2.3 collective-permute-done.47
  (259 shorter events, 71.0 us)
Async XLA Ops:
  7.2 180.7 %all-gather.2.cloned.1.call-start = ((), (), s32[]{:S(2)}) async-start(), calls=%async_computation.3 | async-start | bytes 18579456 | tf_op jit(solution)/shard_map/all_gather | solution.py:803
  9.9 11.1 %collective-permute-start.4 = (bf16[192,640]{1,0:T(8,128)(2,1)S(1)}, bf16[192,640]{1,0:T(8,128)(2,1)S(1)}, u32[]{:S(2)}, u32[]{:S(2)}) collective-permute-start(bf16[192,640]{1,0:T(8,128)(2,1)S(1)} %constant_dynamic-update-slice_fusion.refs_0_), channel_id=1, source_target_pairs={{0,8},{4,12},{8,16},{12,20},{16,24},{20,28},{24,0},{28,4},{1,9},{5... | collective-permute-start | bytes 737288 | tf_op jit(solution)/shard_map/qkv_hop1/ppermute | solution.py:758
  14.4 15.5 %copy-start.56 = (bf16[256,1536]{1,0:T(8,128)(2,1)S(1)}, bf16[256,1536]{1,0:T(8,128)(2,1)}, u32[]{:S(2)}) copy-start(bf16[256,1536]{1,0:T(8,128)(2,1)} %value_ref.1) | copy-start | bytes 2359300
  20.9 8.9 %collective-permute-start.6 = (bf16[192,640]{1,0:T(8,128)(2,1)S(1)}, bf16[192,640]{1,0:T(8,128)(2,1)S(1)}, u32[]{:S(2)}, u32[]{:S(2)}) collective-permute-start(bf16[192,640]{1,0:T(8,128)(2,1)S(1)} %collective-permute-done.4.refs_2_), channel_id=1, source_target_pairs={{0,8},{4,12},{8,16},{12,20},{16,24},{20,28},{24,0},{28,4},{1,9},{5... | collective-permute-start | bytes 737288 | tf_op jit(solution)/shard_map/qkv_hop2/ppermute | solution.py:758
  29.9 272.8 %reduce-scatter.4.cloned.1.call-start = ((), (), s32[]{:S(2)}) async-start(), calls=%async_computation.4 | async-start | bytes 6193152 | tf_op jit(solution)/shard_map/reduce_scatter | solution.py:885
  30.8 37.5 %copy-start.13 = (bf16[256,1536]{1,0:T(8,128)(2,1)}, bf16[256,1536]{1,0:T(8,128)(2,1)S(1)}, u32[]{:S(2)}) copy-start(bf16[256,1536]{1,0:T(8,128)(2,1)S(1)} %fusion.13.refs_0_) | copy-start | bytes 2359300
  30.8 21.7 %collective-permute-start.2 = (bf16[256,1536]{1,0:T(8,128)(2,1)S(1)}, bf16[256,1536]{1,0:T(8,128)(2,1)S(1)}, u32[]{:S(2)}, u32[]{:S(2)}) collective-permute-start(bf16[256,1536]{1,0:T(8,128)(2,1)S(1)} %fusion.13.refs_0_), channel_id=1, source_target_pairs={{0,3},{1,2},{2,1},{3,0},{4,7},{5,6},{6,5},{7,4},{8,11},{9,10},{10,... | collective-permute-start | bytes 2359304 | tf_op jit(solution)/shard_map/one_spread/ppermute | solution.py:773
  33.1 33.4 %collective-permute-start.1 = (bf16[256,1536]{1,0:T(8,128)(2,1)S(1)}, bf16[256,1536]{1,0:T(8,128)(2,1)S(1)}, u32[]{:S(2)}, u32[]{:S(2)}) collective-permute-start(bf16[256,1536]{1,0:T(8,128)(2,1)S(1)} %fusion.13.refs_0_), channel_id=1, source_target_pairs={{0,2},{1,3},{2,0},{3,1},{4,6},{5,7},{6,4},{7,5},{8,10},{9,11},{10,... | collective-permute-start | bytes 2359304 | tf_op jit(solution)/shard_map/one_spread/ppermute | solution.py:773
  33.6 33.7 %collective-permute-start = (bf16[256,1536]{1,0:T(8,128)(2,1)S(1)}, bf16[256,1536]{1,0:T(8,128)(2,1)S(1)}, u32[]{:S(2)}, u32[]{:S(2)}) collective-permute-start(bf16[256,1536]{1,0:T(8,128)(2,1)S(1)} %fusion.13.refs_0_), channel_id=1, source_target_pairs={{0,1},{1,0},{2,3},{3,2},{4,5},{5,4},{6,7},{7,6},{8,9},{9,8},{10,11... | collective-permute-start | bytes 2359304 | tf_op jit(solution)/shard_map/one_spread/ppermute | solution.py:773
  34.4 9.1 %collective-permute-start.14 = (bf16[192,384]{1,0:T(8,128)(2,1)S(1)}, bf16[192,384]{1,0:T(8,128)(2,1)}, u32[]{:S(2)}, u32[]{:S(2)}) collective-permute-start(bf16[192,384]{1,0:T(8,128)(2,1)S(1)} %bitcast.36), channel_id=1, source_target_pairs={{0,8},{4,12},{8,16},{12,20},{16,24},{20,28},{24,0},{28,4},{1,9},{5... | collective-permute-start | bytes 442376 | tf_op jit(solution)/shard_map/out_hop1/ppermute | solution.py:758
  37.8 14.7 %collective-permute-start.8 = (bf16[192,640]{1,0:T(8,128)(2,1)}, bf16[192,640]{1,0:T(8,128)(2,1)S(1)}, u32[]{:S(2)}, u32[]{:S(2)}) collective-permute-start(bf16[192,640]{1,0:T(8,128)(2,1)} %copy-done.48), channel_id=1, source_target_pairs={{0,8},{4,12},{8,16},{12,20},{16,24},{20,28},{24,0},{28,4},{1,9},{5... | collective-permute-start | bytes 737288 | tf_op jit(solution)/shard_map/qkv_hop3/ppermute | solution.py:758
  43.5 35.8 %collective-permute-start.3 = (bf16[192,640]{1,0:T(8,128)(2,1)S(1)}, bf16[192,640]{1,0:T(8,128)(2,1)}, u32[]{:S(2)}, u32[]{:S(2)}) collective-permute-start(bf16[192,640]{1,0:T(8,128)(2,1)S(1)} %constant_dynamic-update-slice_fusion.refs_0_), channel_id=1, source_target_pairs={{0,4},{4,0},{8,12},{12,8},{16,20},{20,16},{24,28},{28,24},{1,5},{5... | collective-permute-start | bytes 737288 | tf_op jit(solution)/shard_map/ppermute | solution.py:755
  52.5 28.5 %collective-permute-start.5 = (bf16[192,640]{1,0:T(8,128)(2,1)}, bf16[192,640]{1,0:T(8,128)(2,1)}, u32[]{:S(2)}, u32[]{:S(2)}) collective-permute-start(bf16[192,640]{1,0:T(8,128)(2,1)} %copy-done.46), channel_id=1, source_target_pairs={{0,4},{4,0},{8,12},{12,8},{16,20},{20,16},{24,28},{28,24},{1,5},{5... | collective-permute-start | bytes 737288 | tf_op jit(solution)/shard_map/ppermute | solution.py:755
  54.1 27.7 %collective-permute-start.7 = (bf16[192,640]{1,0:T(8,128)(2,1)}, bf16[192,640]{1,0:T(8,128)(2,1)}, u32[]{:S(2)}, u32[]{:S(2)}) collective-permute-start(bf16[192,640]{1,0:T(8,128)(2,1)} %copy-done.48), channel_id=1, source_target_pairs={{0,4},{4,0},{8,12},{12,8},{16,20},{20,16},{24,28},{28,24},{1,5},{5... | collective-permute-start | bytes 737288 | tf_op jit(solution)/shard_map/ppermute | solution.py:755
  58.8 29.9 %copy-start.55 = (f32[512]{0:T(512)}, f32[512]{0:T(512)S(1)}, u32[]{:S(2)}) copy-start(f32[512]{0:T(512)S(1)} %concatenate.11) | copy-start | bytes 6148
  67.3 11.7 %collective-permute-start.16 = (bf16[192,384]{1,0:T(8,128)(2,1)}, bf16[192,384]{1,0:T(8,128)(2,1)}, u32[]{:S(2)}, u32[]{:S(2)}) collective-permute-start(bf16[192,384]{1,0:T(8,128)(2,1)} %collective-permute-done.14.refs_2_), channel_id=1, source_target_pairs={{0,8},{4,12},{8,16},{12,20},{16,24},{20,28},{24,0},{28,4},{1,9},{5... | collective-permute-start | bytes 442376 | tf_op jit(solution)/shard_map/out_hop2/ppermute | solution.py:758
  68.2 14.7 %collective-permute-start.9 = (bf16[192,640]{1,0:T(8,128)(2,1)}, bf16[192,640]{1,0:T(8,128)(2,1)}, u32[]{:S(2)}, u32[]{:S(2)}) collective-permute-start(bf16[192,640]{1,0:T(8,128)(2,1)} %copy-done.50), channel_id=1, source_target_pairs={{0,4},{4,0},{8,12},{12,8},{16,20},{20,16},{24,28},{28,24},{1,5},{5... | collective-permute-start | bytes 737288 | tf_op jit(solution)/shard_map/ppermute | solution.py:755
  75.6 18.7 %copy-start.2 = (bf16[1024,1536]{1,0:T(8,128)(2,1)}, bf16[1024,1536]{1,0:T(8,128)(2,1)S(1)}, u32[]{:S(2)}) copy-start(bf16[1024,1536]{1,0:T(8,128)(2,1)S(1)} %get-tuple-element.171.x_ref.normed_ref) | copy-start | bytes 9437188
  79.1 17.8 %collective-permute-start.18 = (bf16[192,384]{1,0:T(8,128)(2,1)}, bf16[192,384]{1,0:T(8,128)(2,1)}, u32[]{:S(2)}, u32[]{:S(2)}) collective-permute-start(bf16[192,384]{1,0:T(8,128)(2,1)} %collective-permute-done.16.refs_4_), channel_id=1, source_target_pairs={{0,8},{4,12},{8,16},{12,20},{16,24},{20,28},{24,0},{28,4},{1,9},{5... | collective-permute-start | bytes 442376 | tf_op jit(solution)/shard_map/out_hop3/ppermute | solution.py:758
  79.3 37.1 %collective-permute-start.12 = (bf16[256,1536]{1,0:T(8,128)(2,1)}, bf16[256,1536]{1,0:T(8,128)(2,1)S(1)}, u32[]{:S(2)}, u32[]{:S(2)}) collective-permute-start(bf16[256,1536]{1,0:T(8,128)(2,1)} %rest_ref.1), channel_id=1, source_target_pairs={{0,3},{1,2},{2,1},{3,0},{4,7},{5,6},{6,5},{7,4},{8,11},{9,10},{10,... | collective-permute-start | bytes 2359304 | tf_op jit(solution)/shard_map/cot_spread/ppermute | solution.py:773
  81.0 35.3 %collective-permute-start.11 = (bf16[256,1536]{1,0:T(8,128)(2,1)}, bf16[256,1536]{1,0:T(8,128)(2,1)S(1)}, u32[]{:S(2)}, u32[]{:S(2)}) collective-permute-start(bf16[256,1536]{1,0:T(8,128)(2,1)} %rest_ref.1), channel_id=1, source_target_pairs={{0,2},{1,3},{2,0},{3,1},{4,6},{5,7},{6,4},{7,5},{8,10},{9,11},{10,... | collective-permute-start | bytes 2359304 | tf_op jit(solution)/shard_map/cot_spread/ppermute | solution.py:773
  81.8 34.6 %collective-permute-start.10 = (bf16[256,1536]{1,0:T(8,128)(2,1)}, bf16[256,1536]{1,0:T(8,128)(2,1)S(1)}, u32[]{:S(2)}, u32[]{:S(2)}) collective-permute-start(bf16[256,1536]{1,0:T(8,128)(2,1)} %rest_ref.1), channel_id=1, source_target_pairs={{0,1},{1,0},{2,3},{3,2},{4,5},{5,4},{6,7},{7,6},{8,9},{9,8},{10,11... | collective-permute-start | bytes 2359304 | tf_op jit(solution)/shard_map/cot_spread/ppermute | solution.py:773
  82.9 29.3 %collective-permute-start.13 = (bf16[192,384]{1,0:T(8,128)(2,1)S(1)}, bf16[192,384]{1,0:T(8,128)(2,1)S(1)}, u32[]{:S(2)}, u32[]{:S(2)}) collective-permute-start(bf16[192,384]{1,0:T(8,128)(2,1)S(1)} %bitcast.37), channel_id=1, source_target_pairs={{0,4},{4,0},{8,12},{12,8},{16,20},{20,16},{24,28},{28,24},{1,5},{5... | collective-permute-start | bytes 442376 | tf_op jit(solution)/shard_map/ppermute | solution.py:755
  96.9 13.3 %copy-start.22 = (bf16[1024,384]{1,0:T(8,128)(2,1)}, bf16[1024,384]{1,0:T(8,128)(2,1)S(1)}, u32[]{:S(2)}) copy-start(bf16[1024,384]{1,0:T(8,128)(2,1)S(1)} %get-tuple-element.104.q_ref) | copy-start | bytes 2359300
  96.9 15.3 %collective-permute-start.15 = (bf16[192,384]{1,0:T(8,128)(2,1)}, bf16[192,384]{1,0:T(8,128)(2,1)S(1)}, u32[]{:S(2)}, u32[]{:S(2)}) collective-permute-start(bf16[192,384]{1,0:T(8,128)(2,1)} %collective-permute-done.14.refs_2_), channel_id=1, source_target_pairs={{0,4},{4,0},{8,12},{12,8},{16,20},{20,16},{24,28},{28,24},{1,5},{5... | collective-permute-start | bytes 442376 | tf_op jit(solution)/shard_map/ppermute | solution.py:755
  112.2 1.6 collective-permute-start.17
  112.2 1.8 collective-permute-start.19
  120.4 20.4 %collective-permute-start.20 = (bf16[256,1536]{1,0:T(8,128)(2,1)S(1)}, bf16[256,1536]{1,0:T(8,128)(2,1)S(1)}, u32[]{:S(2)}, u32[]{:S(2)}) collective-permute-start(bf16[256,1536]{1,0:T(8,128)(2,1)S(1)} %get-tuple-element.114), channel_id=1, source_target_pairs={{0,1},{1,0},{2,3},{3,2},{4,5},{5,4},{6,7},{7,6},{8,9},{9,8},{10,11... | collective-permute-start | bytes 2359304 | tf_op jit(solution)/shard_map/attn_sum/ppermute | solution.py:780
  121.4 36.3 %collective-permute-start.21 = (bf16[256,1536]{1,0:T(8,128)(2,1)S(1)}, bf16[256,1536]{1,0:T(8,128)(2,1)S(1)}, u32[]{:S(2)}, u32[]{:S(2)}) collective-permute-start(bf16[256,1536]{1,0:T(8,128)(2,1)S(1)} %get-tuple-element.115), channel_id=1, source_target_pairs={{0,2},{1,3},{2,0},{3,1},{4,6},{5,7},{6,4},{7,5},{8,10},{9,11},{10,... | collective-permute-start | bytes 2359304 | tf_op jit(solution)/shard_map/attn_sum/ppermute | solution.py:780
  122.7 35.0 %collective-permute-start.22 = (bf16[256,1536]{1,0:T(8,128)(2,1)S(1)}, bf16[256,1536]{1,0:T(8,128)(2,1)S(1)}, u32[]{:S(2)}, u32[]{:S(2)}) collective-permute-start(bf16[256,1536]{1,0:T(8,128)(2,1)S(1)} %get-tuple-element.116), channel_id=1, source_target_pairs={{0,3},{1,2},{2,1},{3,0},{4,7},{5,6},{6,5},{7,4},{8,11},{9,10},{10,... | collective-permute-start | bytes 2359304 | tf_op jit(solution)/shard_map/attn_sum/ppermute | solution.py:780
  140.8 16.9 %copy-start.61 = (bf16[256,1536]{1,0:T(8,128)(2,1)}, bf16[256,1536]{1,0:T(8,128)(2,1)S(1)}, u32[]{:S(2)}) copy-start(bf16[256,1536]{1,0:T(8,128)(2,1)S(1)} %collective-permute-done.20.refs_1_) | copy-start | bytes 2359300
  163.1 36.0 %copy-start.35 = (bf16[256,1536]{1,0:T(8,128)(2,1)S(1)}, bf16[256,1536]{1,0:T(8,128)(2,1)}, u32[]{:S(2)}) copy-start(bf16[256,1536]{1,0:T(8,128)(2,1)} %get-tuple-element.123.refs_0_) | copy-start | bytes 2359300
  163.1 34.9 %collective-permute-start.25 = (bf16[256,1536]{1,0:T(8,128)(2,1)}, bf16[256,1536]{1,0:T(8,128)(2,1)S(1)}, u32[]{:S(2)}, u32[]{:S(2)}) collective-permute-start(bf16[256,1536]{1,0:T(8,128)(2,1)} %get-tuple-element.123.refs_0_), channel_id=1, source_target_pairs={{0,3},{1,2},{2,1},{3,0},{4,7},{5,6},{6,5},{7,4},{8,11},{9,10},{10,... | collective-permute-start | bytes 2359304 | tf_op jit(solution)/shard_map/two_spread/ppermute | solution.py:773
  164.6 34.4 %collective-permute-start.24 = (bf16[256,1536]{1,0:T(8,128)(2,1)}, bf16[256,1536]{1,0:T(8,128)(2,1)S(1)}, u32[]{:S(2)}, u32[]{:S(2)}) collective-permute-start(bf16[256,1536]{1,0:T(8,128)(2,1)} %get-tuple-element.123.refs_0_), channel_id=1, source_target_pairs={{0,2},{1,3},{2,0},{3,1},{4,6},{5,7},{6,4},{7,5},{8,10},{9,11},{10,... | collective-permute-start | bytes 2359304 | tf_op jit(solution)/shard_map/two_spread/ppermute | solution.py:773
  164.8 34.3 %collective-permute-start.23 = (bf16[256,1536]{1,0:T(8,128)(2,1)}, bf16[256,1536]{1,0:T(8,128)(2,1)}, u32[]{:S(2)}, u32[]{:S(2)}) collective-permute-start(bf16[256,1536]{1,0:T(8,128)(2,1)} %get-tuple-element.123.refs_0_), channel_id=1, source_target_pairs={{0,1},{1,0},{2,3},{3,2},{4,5},{5,4},{6,7},{7,6},{8,9},{9,8},{10,11... | collective-permute-start | bytes 2359304 | tf_op jit(solution)/shard_map/two_spread/ppermute | solution.py:773
  238.0 162.9 %reduce-scatter.6.cloned.1.call-start = ((), (), s32[]{:S(2)}) async-start(), calls=%async_computation.5 | async-start | bytes 6193152 | tf_op jit(solution)/shard_map/reduce_scatter | solution.py:899
  255.5 31.3 %collective-permute-start.26 = (bf16[256,1536]{1,0:T(8,128)(2,1)S(1)}, bf16[256,1536]{1,0:T(8,128)(2,1)}, u32[]{:S(2)}, u32[]{:S(2)}) collective-permute-start(bf16[256,1536]{1,0:T(8,128)(2,1)S(1)} %get-tuple-element.129), channel_id=1, source_target_pairs={{0,1},{1,0},{2,3},{3,2},{4,5},{5,4},{6,7},{7,6},{8,9},{9,8},{10,11... | collective-permute-start | bytes 2359304 | tf_op jit(solution)/shard_map/two_sum/ppermute | solution.py:780
  256.7 36.1 %collective-permute-start.27 = (bf16[256,1536]{1,0:T(8,128)(2,1)S(1)}, bf16[256,1536]{1,0:T(8,128)(2,1)}, u32[]{:S(2)}, u32[]{:S(2)}) collective-permute-start(bf16[256,1536]{1,0:T(8,128)(2,1)S(1)} %get-tuple-element.130), channel_id=1, source_target_pairs={{0,2},{1,3},{2,0},{3,1},{4,6},{5,7},{6,4},{7,5},{8,10},{9,11},{10,... | collective-permute-start | bytes 2359304 | tf_op jit(solution)/shard_map/two_sum/ppermute | solution.py:780
  257.5 35.3 %collective-permute-start.28 = (bf16[256,1536]{1,0:T(8,128)(2,1)S(1)}, bf16[256,1536]{1,0:T(8,128)(2,1)}, u32[]{:S(2)}, u32[]{:S(2)}) collective-permute-start(bf16[256,1536]{1,0:T(8,128)(2,1)S(1)} %get-tuple-element.131), channel_id=1, source_target_pairs={{0,3},{1,2},{2,1},{3,0},{4,7},{5,6},{6,5},{7,4},{8,11},{9,10},{10,... | collective-permute-start | bytes 2359304 | tf_op jit(solution)/shard_map/two_sum/ppermute | solution.py:780
  302.8 156.1 %reduce-scatter.8.cloned.1.call-start = ((), (), s32[]{:S(2)}) async-start(), calls=%async_computation.6 | async-start | bytes 3538944 | tf_op jit(solution)/shard_map/reduce_scatter | solution.py:925
  302.8 5.5 %collective-permute-start.32 = (bf16[768,1792]{1,0:T(8,128)(2,1)}, bf16[768,1792]{1,0:T(8,128)(2,1)}, u32[]{:S(2)}, u32[]{:S(2)}) collective-permute-start(bf16[768,1792]{1,0:T(8,128)(2,1)} %product.5), channel_id=1, source_target_pairs={{0,4},{4,0},{8,12},{12,8},{16,20},{20,16},{24,28},{28,24},{1,5},{5... | collective-permute-start | bytes 8257544 | tf_op jit(solution)/shard_map/ppermute | solution.py:755
  302.9 20.7 %collective-permute-start.29 = (bf16[256,1536]{1,0:T(8,128)(2,1)}, bf16[256,1536]{1,0:T(8,128)(2,1)}, u32[]{:S(2)}, u32[]{:S(2)}) collective-permute-start(bf16[256,1536]{1,0:T(8,128)(2,1)} %get-tuple-element.141.refs_0_), channel_id=1, source_target_pairs={{0,1},{1,0},{2,3},{3,2},{4,5},{5,4},{6,7},{7,6},{8,9},{9,8},{10,11... | collective-permute-start | bytes 2359304 | tf_op jit(solution)/shard_map/dh_spread/ppermute | solution.py:773
  304.4 43.0 %collective-permute-start.31 = (bf16[256,1536]{1,0:T(8,128)(2,1)}, bf16[256,1536]{1,0:T(8,128)(2,1)}, u32[]{:S(2)}, u32[]{:S(2)}) collective-permute-start(bf16[256,1536]{1,0:T(8,128)(2,1)} %get-tuple-element.141.refs_0_), channel_id=1, source_target_pairs={{0,3},{1,2},{2,1},{3,0},{4,7},{5,6},{6,5},{7,4},{8,11},{9,10},{10,... | collective-permute-start | bytes 2359304 | tf_op jit(solution)/shard_map/dh_spread/ppermute | solution.py:773
  305.9 41.5 %collective-permute-start.30 = (bf16[256,1536]{1,0:T(8,128)(2,1)}, bf16[256,1536]{1,0:T(8,128)(2,1)}, u32[]{:S(2)}, u32[]{:S(2)}) collective-permute-start(bf16[256,1536]{1,0:T(8,128)(2,1)} %get-tuple-element.141.refs_0_), channel_id=1, source_target_pairs={{0,2},{1,3},{2,0},{3,1},{4,6},{5,7},{6,4},{7,5},{8,10},{9,11},{10,... | collective-permute-start | bytes 2359304 | tf_op jit(solution)/shard_map/dh_spread/ppermute | solution.py:773
  310.4 34.8 %collective-permute-start.33 = (bf16[192,1792]{1,0:T(8,128)(2,1)}, bf16[192,1792]{1,0:T(8,128)(2,1)}, u32[]{:S(2)}, u32[]{:S(2)}) collective-permute-start(bf16[192,1792]{1,0:T(8,128)(2,1)} %join.3), channel_id=1, source_target_pairs={{0,8},{4,12},{8,16},{12,20},{16,24},{20,28},{24,0},{28,4},{1,9},{5... | collective-permute-start | bytes 2064392 | tf_op jit(solution)/shard_map/gate_grad_hop1/ppermute | solution.py:758
  320.8 26.5 %copy-start.21 = (bf16[256,1536]{1,0:T(8,128)(2,1)}, bf16[256,1536]{1,0:T(8,128)(2,1)S(1)}, u32[]{:S(2)}) copy-start(bf16[256,1536]{1,0:T(8,128)(2,1)S(1)} %get-tuple-element.143.refs_0_) | copy-start | bytes 2359300
  347.4 38.0 %collective-permute-start.35 = (bf16[256,1536]{1,0:T(8,128)(2,1)}, bf16[256,1536]{1,0:T(8,128)(2,1)}, u32[]{:S(2)}, u32[]{:S(2)}) collective-permute-start(bf16[256,1536]{1,0:T(8,128)(2,1)} %get-tuple-element.161), channel_id=1, source_target_pairs={{0,1},{1,0},{2,3},{3,2},{4,5},{5,4},{6,7},{7,6},{8,9},{9,8},{10,11... | collective-permute-start | bytes 2359304 | tf_op jit(solution)/shard_map/ffn_sum/ppermute | solution.py:780
  348.8 36.6 %collective-permute-start.36 = (bf16[256,1536]{1,0:T(8,128)(2,1)}, bf16[256,1536]{1,0:T(8,128)(2,1)}, u32[]{:S(2)}, u32[]{:S(2)}) collective-permute-start(bf16[256,1536]{1,0:T(8,128)(2,1)} %get-tuple-element.162), channel_id=1, source_target_pairs={{0,2},{1,3},{2,0},{3,1},{4,6},{5,7},{6,4},{7,5},{8,10},{9,11},{10,... | collective-permute-start | bytes 2359304 | tf_op jit(solution)/shard_map/ffn_sum/ppermute | solution.py:780
  350.3 35.1 %collective-permute-start.37 = (bf16[256,1536]{1,0:T(8,128)(2,1)}, bf16[256,1536]{1,0:T(8,128)(2,1)}, u32[]{:S(2)}, u32[]{:S(2)}) collective-permute-start(bf16[256,1536]{1,0:T(8,128)(2,1)} %get-tuple-element.163), channel_id=1, source_target_pairs={{0,3},{1,2},{2,1},{3,0},{4,7},{5,6},{6,5},{7,4},{8,11},{9,10},{10,... | collective-permute-start | bytes 2359304 | tf_op jit(solution)/shard_map/ffn_sum/ppermute | solution.py:780
  350.9 34.5 %collective-permute-start.34 = (bf16[192,1792]{1,0:T(8,128)(2,1)}, bf16[192,1792]{1,0:T(8,128)(2,1)}, u32[]{:S(2)}, u32[]{:S(2)}) collective-permute-start(bf16[192,1792]{1,0:T(8,128)(2,1)} %join.4), channel_id=1, source_target_pairs={{0,8},{4,12},{8,16},{12,20},{16,24},{20,28},{24,0},{28,4},{1,9},{5... | collective-permute-start | bytes 2064392 | tf_op jit(solution)/shard_map/gate_grad_hop2/ppermute | solution.py:758
  401.9 28.1 %collective-permute-start.41 = (bf16[192,1792]{1,0:T(8,128)(2,1)S(1)}, bf16[192,1792]{1,0:T(8,128)(2,1)S(1)}, u32[]{:S(2)}, u32[]{:S(2)}) collective-permute-start(bf16[192,1792]{1,0:T(8,128)(2,1)S(1)} %copy-done.38), channel_id=1, source_target_pairs={{0,8},{4,12},{8,16},{12,20},{16,24},{20,28},{24,0},{28,4},{1,9},{5... | collective-permute-start | bytes 2064392 | tf_op jit(solution)/shard_map/gate_grad_hop3/ppermute | solution.py:758
  401.9 29.6 %collective-permute-start.38 = (bf16[256,1536]{1,0:T(8,128)(2,1)}, bf16[256,1536]{1,0:T(8,128)(2,1)S(1)}, u32[]{:S(2)}, u32[]{:S(2)}) collective-permute-start(bf16[256,1536]{1,0:T(8,128)(2,1)} %get-tuple-element.167.refs_1_), channel_id=1, source_target_pairs={{0,1},{1,0},{2,3},{3,2},{4,5},{5,4},{6,7},{7,6},{8,9},{9,8},{10,11... | collective-permute-start | bytes 2359304 | tf_op jit(solution)/shard_map/one_sum/ppermute | solution.py:780
  403.3 32.7 %collective-permute-start.39 = (bf16[256,1536]{1,0:T(8,128)(2,1)S(1)}, bf16[256,1536]{1,0:T(8,128)(2,1)S(1)}, u32[]{:S(2)}, u32[]{:S(2)}) collective-permute-start(bf16[256,1536]{1,0:T(8,128)(2,1)S(1)} %get-tuple-element.168.refs_2_), channel_id=1, source_target_pairs={{0,2},{1,3},{2,0},{3,1},{4,6},{5,7},{6,4},{7,5},{8,10},{9,11},{10,... | collective-permute-start | bytes 2359304 | tf_op jit(solution)/shard_map/one_sum/ppermute | solution.py:780
  404.8 32.0 %collective-permute-start.40 = (bf16[256,1536]{1,0:T(8,128)(2,1)S(1)}, bf16[256,1536]{1,0:T(8,128)(2,1)S(1)}, u32[]{:S(2)}, u32[]{:S(2)}) collective-permute-start(bf16[256,1536]{1,0:T(8,128)(2,1)S(1)} %get-tuple-element.169.refs_3_), channel_id=1, source_target_pairs={{0,3},{1,2},{2,1},{3,0},{4,7},{5,6},{6,5},{7,4},{8,11},{9,10},{10,... | collective-permute-start | bytes 2359304 | tf_op jit(solution)/shard_map/one_sum/ppermute | solution.py:780
  409.9 20.2 %copy-start.36 = (bf16[192,1792]{1,0:T(8,128)(2,1)S(1)}, bf16[192,1792]{1,0:T(8,128)(2,1)}, u32[]{:S(2)}) copy-start(bf16[192,1792]{1,0:T(8,128)(2,1)} %reduce-scatter.4.cloned.1.call-done.grads_ref) | copy-start | bytes 2064388
  409.9 20.5 %copy-start.65 = (bf16[192,1792]{1,0:T(8,128)(2,1)S(1)}, bf16[192,1792]{1,0:T(8,128)(2,1)}, u32[]{:S(2)}) copy-start(bf16[192,1792]{1,0:T(8,128)(2,1)} %reduce-scatter.6.cloned.1.call-done) | copy-start | bytes 2064388
  413.4 23.5 %copy-start.67 = (f32[1,3584]{1,0:T(1,128)S(1)}, f32[1,3584]{1,0:T(1,128)}, u32[]{:S(2)}) copy-start(f32[1,3584]{1,0:T(1,128)} %gain_parts.1) | copy-start | bytes 43012
  436.8 10.5 %collective-permute-start.44 = (f32[1,3584]{1,0:T(1,128)S(1)}, f32[1,3584]{1,0:T(1,128)S(1)}, u32[]{:S(2)}, u32[]{:S(2)}) collective-permute-start(f32[1,3584]{1,0:T(1,128)S(1)} %copy-done.67), channel_id=1, source_target_pairs={{0,3},{1,2},{2,1},{3,0},{4,7},{5,6},{6,5},{7,4},{8,11},{9,10},{10,... | collective-permute-start | bytes 43016 | tf_op jit(solution)/shard_map/ppermute | solution.py:933
  438.4 9.0 %collective-permute-start.43 = (f32[1,3584]{1,0:T(1,128)S(1)}, f32[1,3584]{1,0:T(1,128)S(1)}, u32[]{:S(2)}, u32[]{:S(2)}) collective-permute-start(f32[1,3584]{1,0:T(1,128)S(1)} %copy-done.67), channel_id=1, source_target_pairs={{0,2},{1,3},{2,0},{3,1},{4,6},{5,7},{6,4},{7,5},{8,10},{9,11},{10,... | collective-permute-start | bytes 43016 | tf_op jit(solution)/shard_map/ppermute | solution.py:933
  439.8 7.5 %collective-permute-start.42 = (f32[1,3584]{1,0:T(1,128)S(1)}, f32[1,3584]{1,0:T(1,128)S(1)}, u32[]{:S(2)}, u32[]{:S(2)}) collective-permute-start(f32[1,3584]{1,0:T(1,128)S(1)} %copy-done.67), channel_id=1, source_target_pairs={{0,1},{1,0},{2,3},{3,2},{4,5},{5,4},{6,7},{7,6},{8,9},{9,8},{10,11... | collective-permute-start | bytes 43016 | tf_op jit(solution)/shard_map/ppermute | solution.py:933
  447.4 1.2 collective-permute-start.45
  448.7 6.1 %collective-permute-start.48 = (f32[1,3584]{1,0:T(1,128)S(1)}, f32[1,3584]{1,0:T(1,128)S(1)}, u32[]{:S(2)}, u32[]{:S(2)}) collective-permute-start(f32[1,3584]{1,0:T(1,128)S(1)} %add.119), channel_id=1, source_target_pairs={{0,24},{4,28},{8,16},{12,20},{16,8},{20,12},{24,0},{28,4},{1,25},{... | collective-permute-start | bytes 43016 | tf_op jit(solution)/shard_map/ppermute | solution.py:933
  452.3 4.6 collective-permute-start.47
  452.3 4.6 collective-permute-start.46
  (60 other events, 235.1 us)
Sparse Core Ops, SparseCore 0:
  30.0 157.8 all-gather.1
  238.1 64.6 reduce-scatter.3
  305.1 90.1 reduce-scatter.5
  401.0 47.9 reduce-scatter.7
